TPU v7x, 32 devices: a whole 2x2x4 slice. The times are simulated.
32 devices in a mesh: req: 8 (over z, y), tp: 4 (over x, core).
Axes of the slice: x: 2, y: 2, z: 4, core: 2. Of those that a mesh axis runs over, the one named last changes fastest.
Arguments:
- query: bfloat16 [32, 2048], P('req', 'tp'), may hold values from -8 to 8
- key_new: bfloat16 [32, 2048], P('req', 'tp'), may hold values from -4 to 4
- value_new: bfloat16 [32, 2048], P('req', 'tp'), may hold values from -4 to 4
- resid: bfloat16 [32, 2048], P('req', 'tp'), may hold values from -6 to 6
- lengths: int32 [32], replicated, may hold values from 1 to 512, as said below
- owner: int32 [32], replicated, may hold values from 0 to 7, as said below
- page_table: int32 [32, 16], replicated, may hold values from 0 to 21, as said below
- kv_pool: bfloat16 [2, 176, 32, 2048], P(None, 'req', None, 'tp'), may hold values from -4 to 4
- out_weight: bfloat16 [2048, 2048], P('tp'), may hold values from -0.125 to 0.125
- out_bias: bfloat16 [2048], P('tp'), may hold values from -3 to 3
- norm_gain: bfloat16 [2048], P('tp'), may hold values from 0.099609375 to 1.8984375
- norm_bias: bfloat16 [2048], P('tp'), may hold values from -3 to 3
- up_weight_t: bfloat16 [8192, 2048], P('req', 'tp'), may hold values from -0.125 to 0.125
- up_bias: bfloat16 [8192], P('req'), may hold values from -3 to 3
- down_weight: bfloat16 [8192, 2048], P('req', 'tp'), may hold values from -0.0625 to 0.0625
- down_bias: bfloat16 [2048], P('tp'), may hold values from -3 to 3
- order: int32 [32], replicated, may hold values from 0 to 31, each once
Outputs:
- layer_out: bfloat16 [32, 2048], P('req', 'tp')
Inputs may be any that keep to these rules, and one draw needn't show every extreme that they name: `lengths`: one request in 32 (at least one) is long, with a length from 256 to 512; the others have at most 63 positions. `owner`: every index of req owns exactly 4 requests, at most one of them long, and no two of them among the 4 rows that one index of req holds. `page_table`: entry j of request r for j < ceil(lengths[r] / 32) names a page of the owner's pool that no other entry of that owner's requests below that bound names; later entries are arbitrary pages.
All inputs are finite; a program needn't handle non-finite values.
Results may differ from a plain program's by a relative error of at most 0.015.
Values may be sent and summed in bfloat16 or wider, within the bound.
No kernel may reach another device: no remote copies, remote signals or barrier semaphores. Data moves between devices by JAX's collectives and lax.ppermute only.
A program may use at most 64 MiB of HBM per device.

v0:
```python
import math

import jax
import jax.numpy as jnp
from jax import lax
from jax.sharding import PartitionSpec as P

D = 2048
HEAD_DIM = 128


norm_eps = 1e-05


def per_device(
    query,
    key_new,
    value_new,
    resid,
    lengths,
    owner,
    page_table,
    kv_pool,
    out_weight,
    out_bias,
    norm_gain,
    norm_bias,
    up_weight_t,
    up_bias,
    down_weight,
    down_bias,
    order,
):
    owned_count = query.shape[0]
    local_heads = query.shape[1] // HEAD_DIM
    pool_pages = kv_pool.shape[1]
    page_len = kv_pool.shape[2]
    max_pages = page_table.shape[1]
    request_count = lengths.shape[0]
    devices = lax.axis_size("req")
    device_index = lax.axis_index("req")
    score_scale = 1.0 / math.sqrt(HEAD_DIM)
    highest = lax.Precision.HIGHEST
    owner_hot = (owner[:, None] == jnp.arange(devices, dtype=jnp.int32)[None, :]).astype(jnp.int32)
    owner_rank = jnp.sum((jnp.cumsum(owner_hot, axis=0) - 1) * owner_hot, axis=1)
    slot_pos = owner * owned_count + owner_rank
    picker = (owner[None, :] == device_index) & (
        owner_rank[None, :] == jnp.arange(owned_count, dtype=jnp.int32)[:, None]
    )
    own_ids = jnp.sum(
        picker.astype(jnp.int32) * jnp.arange(request_count, dtype=jnp.int32)[None, :], axis=1
    )
    query_all, key_all, value_all, resid_all = (
        lax.all_gather(query, "req", axis=0, tiled=True),
        lax.all_gather(key_new, "req", axis=0, tiled=True),
        lax.all_gather(value_new, "req", axis=0, tiled=True),
        lax.all_gather(resid, "req", axis=0, tiled=True),
    )
    pick_matrix = picker.astype(jnp.bfloat16)

    def pick_rows(source_rows):
        return jnp.dot(pick_matrix, source_rows, preferred_element_type=jnp.float32).astype(
            jnp.bfloat16
        )

    query_own = pick_rows(query_all)
    key_own = pick_rows(key_all)
    value_own = pick_rows(value_all)
    resid_own = pick_rows(resid_all)
    own_len = lengths[own_ids]
    own_table = page_table[own_ids]
    own_pages = (own_len + page_len - 1) // page_len
    page_used = jnp.arange(max_pages, dtype=jnp.int32)[None, :] < own_pages[:, None]
    page_match = (
        own_table[:, :, None] == jnp.arange(pool_pages, dtype=jnp.int32)[None, None, :]
    ) & page_used[:, :, None]
    page_hot = jnp.any(page_match, axis=1).T
    page_index = jnp.sum(
        page_match.astype(jnp.int32) * jnp.arange(max_pages, dtype=jnp.int32)[None, :, None],
        axis=(0, 1),
    )
    page_limit = jnp.sum(page_hot.astype(jnp.int32) * own_len[None, :], axis=1)
    query_page = jnp.dot(
        page_hot.astype(jnp.bfloat16), query_own, preferred_element_type=jnp.float32
    ).astype(jnp.bfloat16)
    query_page = query_page.reshape(pool_pages, local_heads, HEAD_DIM)
    page_keys = kv_pool[0].reshape(pool_pages, page_len, local_heads, HEAD_DIM)
    page_values = kv_pool[1].reshape(pool_pages, page_len, local_heads, HEAD_DIM)
    scores = (
        jnp.einsum("phd,pthd->pht", query_page, page_keys, preferred_element_type=jnp.float32)
        * score_scale
    )
    position = page_index[:, None] * page_len + jnp.arange(page_len, dtype=jnp.int32)[None, :]
    valid_mask = (position < page_limit[:, None])[:, None, :]
    scores = jnp.where(valid_mask, scores, -jnp.inf)
    query_heads = query_own.astype(jnp.float32).reshape(owned_count, local_heads, HEAD_DIM)
    key_heads = key_own.astype(jnp.float32).reshape(owned_count, local_heads, HEAD_DIM)
    self_score = jnp.sum(query_heads * key_heads, axis=-1) * score_scale
    page_top = jnp.max(scores, axis=2)
    slot_top = jnp.max(jnp.where(page_hot[:, :, None], page_top[:, None, :], -jnp.inf), axis=0)
    slot_top = jnp.maximum(slot_top, self_score)
    page_ref = jnp.sum(jnp.where(page_hot[:, :, None], slot_top[None, :, :], 0.0), axis=1)
    weights = jnp.where(valid_mask, jnp.exp(scores - page_ref[:, :, None]), 0.0)
    page_total = jnp.sum(weights, axis=2)
    self_weight = jnp.exp(self_score - slot_top)
    slot_total = (
        jnp.sum(jnp.where(page_hot[:, :, None], page_total[:, None, :], 0.0), axis=0) + self_weight
    )
    page_numer = jnp.einsum(
        "pht,pthd->phd",
        weights.astype(jnp.bfloat16),
        page_values,
        preferred_element_type=jnp.float32,
    )
    slot_numer = jnp.einsum(
        "pr,phd->rhd", page_hot.astype(jnp.float32), page_numer, precision=highest
    )
    value_heads = value_own.astype(jnp.float32).reshape(owned_count, local_heads, HEAD_DIM)
    slot_numer = (
        slot_numer + self_weight.astype(jnp.bfloat16).astype(jnp.float32)[:, :, None] * value_heads
    )
    attn = (
        (slot_numer / slot_total[:, :, None])
        .astype(jnp.bfloat16)
        .reshape(owned_count, local_heads * HEAD_DIM)
    )
    projected = lax.psum_scatter(
        lax.dot_general(
            out_weight, attn, (((0,), (1,)), ((), ())), preferred_element_type=jnp.float32
        ),
        "tp",
        scatter_dimension=0,
        tiled=True,
    )
    bias_row = out_bias.astype(jnp.float32)[None, :]
    stream_own = (resid_own.astype(jnp.float32) + projected.T + bias_row).astype(jnp.bfloat16)
    own_f = stream_own.astype(jnp.float32)
    row_sum, row_square = lax.psum((jnp.sum(own_f, axis=1), jnp.sum(own_f * own_f, axis=1)), "tp")
    mean_own = row_sum / D
    inverse_own = lax.rsqrt(row_square / D - mean_own * mean_own + norm_eps)
    stream_all = lax.all_gather(stream_own, "req", axis=0, tiled=True)
    mean_all, inverse_all = (
        lax.all_gather(mean_own, "req", axis=0, tiled=True),
        lax.all_gather(inverse_own, "req", axis=0, tiled=True),
    )
    stream_f = stream_all.astype(jnp.float32)
    normed = (
        (stream_f - mean_all[:, None])
        * inverse_all[:, None]
        * norm_gain.astype(jnp.float32)[None, :]
        + norm_bias.astype(jnp.float32)[None, :]
    ).astype(jnp.bfloat16)
    partial_value = lax.dot_general(
        up_weight_t, normed, (((1,), (1,)), ((), ())), preferred_element_type=jnp.float32
    )
    bias_col = up_bias.astype(jnp.float32)[:, None]
    summed = lax.psum(partial_value.astype(jnp.bfloat16), "tp").astype(jnp.float32)
    activated = jax.nn.gelu(summed + bias_col, approximate=False).astype(jnp.bfloat16)
    activated_out = jnp.take(activated, slot_pos[order], axis=1)
    feed_rows = lax.psum_scatter(
        lax.dot_general(
            activated_out, down_weight, (((0,), (0,)), ((), ())), preferred_element_type=jnp.float32
        ),
        "req",
        scatter_dimension=0,
        tiled=True,
    )
    order_mine = lax.dynamic_slice_in_dim(order, device_index * owned_count, owned_count)
    residual_rows = jnp.take(stream_all, slot_pos[order_mine], axis=0)
    combined = (
        residual_rows.astype(jnp.float32) + feed_rows + down_bias.astype(jnp.float32)[None, :]
    )
    return combined.astype(jnp.bfloat16)


def solution(mesh):
    in_specs = (
        P("req", "tp"),
        P("req", "tp"),
        P("req", "tp"),
        P("req", "tp"),
        P(),
        P(),
        P(),
        P(None, "req", None, "tp"),
        P("tp", None),
        P("tp"),
        P("tp"),
        P("tp"),
        P("req", "tp"),
        P("req"),
        P("req", "tp"),
        P("tp"),
        P(),
    )
    out_specs = P("req", "tp")
    return jax.shard_map(
        per_device, mesh=mesh, in_specs=in_specs, out_specs=out_specs, check_vma=False
    )
```

profile of v0, /device:TPU:0, one launch (start us, length us, event | category | flops | bytes accessed | tf_op | source)
XLA Modules:
  0.0 322.6 jit_solution(4653431069971478999)
XLA Ops:
  6.5 0.9 fusion.44
  7.4 0.7 broadcast_compare_fusion
  8.1 0.8 select_reduce_fusion.1
  9.1 1.3 gather_fusion.2
  10.5 0.8 copy.28
  13.2 32.3 %all-gather.1 = bf16[8,4,512]{2,1,0:T(4,128)(2,1)S(1)} all-gather(bf16[1,4,512]{2,1,0:T(4,128)(2,1)} %bitcast.72), channel_id=1, replica_groups=mesh['req'=8,'tp'=4] {'req'}, dimensions={0}, use_global_device_ids=true | all-gather | bytes 36864 | tf_op jit(solution)/shard_map/all_gather | solution.py:54
  46.5 1.4 fusion.57
  48.0 1.0 reshape_squeeze.6
  49.0 0.8 add_compare_fusion
  49.7 1.6 fusion.15
  51.6 30.4 %all-gather.2 = bf16[8,4,512]{2,1,0:T(4,128)(2,1)S(1)} all-gather(bf16[1,4,512]{2,1,0:T(4,128)(2,1)S(1)} %bitcast.73), channel_id=1, replica_groups=mesh['req'=8,'tp'=4] {'req'}, dimensions={0}, use_global_device_ids=true | all-gather | bytes 36864 | tf_op jit(solution)/shard_map/all_gather | solution.py:55
  83.1 0.7 fusion.45
  84.0 0.7 select_reduce_fusion.2
  84.7 0.7 fusion.54
  85.5 30.5 %all-gather.3 = bf16[8,4,512]{2,1,0:T(4,128)(2,1)S(1)} all-gather(bf16[1,4,512]{2,1,0:T(4,128)(2,1)} %bitcast.74), channel_id=1, replica_groups=mesh['req'=8,'tp'=4] {'req'}, dimensions={0}, use_global_device_ids=true | all-gather | bytes 36864 | tf_op jit(solution)/shard_map/all_gather | solution.py:56
  116.1 1.0 fusion.13
  117.1 0.7 fusion.11
  117.9 0.8 fusion.12
  119.1 1.4 copy.40
  120.6 0.7 gather_fusion.4
  122.1 30.4 %all-gather = bf16[8,4,512]{2,1,0:T(4,128)(2,1)S(1)} all-gather(bf16[1,4,512]{2,1,0:T(4,128)(2,1)S(1)} %bitcast.75), channel_id=1, replica_groups=mesh['req'=8,'tp'=4] {'req'}, dimensions={0}, use_global_device_ids=true | all-gather | bytes 36864 | tf_op jit(solution)/shard_map/all_gather | solution.py:57
  152.6 0.7 fusion.58
  154.0 1.1 copy.41
  155.3 30.4 %all-gather.4 = bf16[8,4,512]{2,1,0:T(4,128)(2,1)S(1)} all-gather(bf16[1,4,512]{2,1,0:T(4,128)(2,1)S(1)} %bitcast.68), channel_id=1, replica_groups=mesh['req'=8,'tp'=4] {'req'}, dimensions={0}, use_global_device_ids=true | all-gather | bytes 36864 | tf_op jit(solution)/shard_map/all_gather | solution.py:141
  185.8 5.7 %all-reduce.4 = (f32[4]{0:T(128)S(1)}, f32[4]{0:T(128)S(1)}) all-reduce(f32[4]{0:T(128)S(1)} %get-tuple-element.6, f32[4]{0:T(128)S(1)} %get-tuple-element.5), channel_id=1, replica_groups=mesh['req'=8,'tp'=4] {'tp'}, use_global_device_ids=true, to_apply=%region_16.17 | all-reduce | flops 8 | bytes 64 | tf_op jit(solution)/shard_map/psum | solution.py:138
  191.6 21.3 %all-reduce.3 = (f32[32]{0:T(128)S(1)}, f32[32]{0:T(128)S(1)}) all-reduce(f32[32]{0:T(128)S(1)} %rsqrt_dynamic-update-slice_fusion, f32[32]{0:T(128)S(1)} %multiply_dynamic-update-slice_fusion), channel_id=1, replica_groups=mesh['req'=8,'tp'=4] {'req'}, use_global_device_ids=true, to_apply=%add.1 | all-reduce | flops 64 | bytes 512
  212.9 1.0 fusion
  214.8 27.9 %all-reduce.8.cloned.1.call-done = bf16[1024,32]{0,1:T(8,128)(2,1)} async-done(((bf16[1024,32]{0,1:T(8,128)(2,1)}), bf16[1024,32]{0,1:T(8,128)(2,1)}) %all-reduce.8.cloned.1.call-update) | async-done | bytes 65552 | tf_op jit(solution)/shard_map/psum | solution.py:157
  242.7 1.1 fusion.19
  244.5 0.9 fusion.30
  246.0 68.6 %all-reduce.10.cloned.1.call-done = f32[32,512]{1,0:T(8,128)} async-done(((f32[32,512]{1,0:T(8,128)}), f32[32,512]{1,0:T(8,128)}) %all-reduce.10.cloned.1.call-update) | async-done | bytes 65552
  314.7 1.4 fusion.48
  (102 shorter events, 8.0 us)
Async XLA Ops:
  6.5 112.1 %copy-start = (bf16[512,2048]{1,0:T(8,128)(2,1)S(1)}, bf16[512,2048]{1,0:T(8,128)(2,1)}, u32[]{:S(2)}) copy-start(bf16[512,2048]{1,0:T(8,128)(2,1)} %param.25) | copy-start | bytes 6291460
  6.5 147.5 %reduce-scatter.4.cloned.1.call-start = ((), (), s32[]{:S(2)}) async-start(), calls=%async_computation.2 | async-start | bytes 1310720
  9.0 4.3 %copy-start.12 = (s32[32]{0:T(128)}, s32[32]{0:T(128)S(1)}, u32[]{:S(2)}) copy-start(s32[32]{0:T(128)S(1)} %select_reduce_fusion.1) | copy-start | bytes 388
  9.1 72.9 %copy-start.5 = (pred[4,32]{1,0:T(4,128)(4,1)}, pred[4,32]{1,0:T(4,128)(4,1)S(1)}, u32[]{:S(2)}) copy-start(pred[4,32]{1,0:T(4,128)(4,1)S(1)} %get-tuple-element.12) | copy-start | bytes 388
  11.9 70.4 %copy-start.4 = (pred[4,22]{1,0:T(4,128)(4,1)}, pred[4,22]{1,0:T(4,128)(4,1)S(1)}, u32[]{:S(2)}) copy-start(pred[4,22]{1,0:T(4,128)(4,1)S(1)} %fusion.43) | copy-start | bytes 268
  46.5 5.0 %copy-start.7 = (bf16[4,512]{1,0:T(4,128)(2,1)S(1)}, bf16[4,512]{1,0:T(4,128)(2,1)}, u32[]{:S(2)}) copy-start(bf16[4,512]{1,0:T(4,128)(2,1)} %param.18) | copy-start | bytes 12292
  82.3 0.6 copy-start.3
  118.7 1.9 copy-start.10
  118.7 1.9 copy-start.13
  118.7 1.9 copy-start.18
  119.1 3.0 copy-start.8
  119.1 33.5 %copy-start.14 = (bf16[512]{0:T(512)(128)(2,1)S(1)}, bf16[512]{0:T(512)(128)(2,1)}, u32[]{:S(2)}) copy-start(bf16[512]{0:T(512)(128)(2,1)} %param.26) | copy-start | bytes 3076
  119.1 33.5 %copy-start.15 = (bf16[512]{0:T(512)(128)(2,1)S(1)}, bf16[512]{0:T(512)(128)(2,1)}, u32[]{:S(2)}) copy-start(bf16[512]{0:T(512)(128)(2,1)} %param.27) | copy-start | bytes 3076
  119.1 33.5 %copy-start.16 = (bf16[512]{0:T(512)(128)(2,1)S(1)}, bf16[512]{0:T(512)(128)(2,1)}, u32[]{:S(2)}) copy-start(bf16[512]{0:T(512)(128)(2,1)} %param.28) | copy-start | bytes 3076
  119.1 33.5 %copy-start.11 = (u32[32]{0:T(128)S(1)}, u32[32]{0:T(128)}, u32[]{:S(2)}) copy-start(u32[32]{0:T(128)} %constant.150) | copy-start | bytes 388
  119.1 36.0 %copy-start.6 = (pred[4,32]{1,0:T(4,128)(4,1)S(1)}, pred[4,32]{1,0:T(4,128)(4,1)}, u32[]{:S(2)}) copy-start(pred[4,32]{1,0:T(4,128)(4,1)} %copy-done.5) | copy-start | bytes 388
  119.1 93.8 %copy-start.1 = (bf16[1024,512]{1,0:T(8,128)(2,1)S(1)}, bf16[1024,512]{1,0:T(8,128)(2,1)}, u32[]{:S(2)}) copy-start(bf16[1024,512]{1,0:T(8,128)(2,1)} %param.29) | copy-start | bytes 3145732
  120.5 93.6 %copy-start.9 = (bf16[1024]{0:T(1024)(128)(2,1)S(1)}, bf16[1024]{0:T(1024)(128)(2,1)}, u32[]{:S(2)}) copy-start(bf16[1024]{0:T(1024)(128)(2,1)} %param.30) | copy-start | bytes 6148
  120.5 93.6 %copy-start.17 = (bf16[512]{0:T(512)(128)(2,1)S(1)}, bf16[512]{0:T(512)(128)(2,1)}, u32[]{:S(2)}) copy-start(bf16[512]{0:T(512)(128)(2,1)} %param.32) | copy-start | bytes 3076
  120.5 122.2 %all-reduce.8.cloned.1.call-start = ((), (), s32[]{:S(2)}) async-start(), calls=%async_computation.1 | async-start | bytes 131072 | tf_op jit(solution)/shard_map/psum | solution.py:157
  214.0 30.5 %copy-start.2 = (bf16[1024,512]{1,0:T(8,128)(2,1)S(1)}, bf16[1024,512]{1,0:T(8,128)(2,1)}, u32[]{:S(2)}) copy-start(bf16[1024,512]{1,0:T(8,128)(2,1)} %param.31) | copy-start | bytes 3145732
  214.0 100.7 %all-reduce.10.cloned.1.call-start = ((), (), s32[]{:S(2)}) async-start(), calls=%async_computation.3 | async-start | bytes 131072
Sparse Core Ops, SparseCore 0:
  120.6 25.7 reduce-scatter.3
  214.1 28.5 all-reduce.7
  246.1 68.4 all-reduce.9
where the time goes:
time: 323 us
  blocking collectives  181 us (56%)
  waiting for transfers between devices  96.6 us (30%)
  between operations  14.9 us (5%)
  local copies, waits for them, and re-layouts  12.7 us (4%)
  other arithmetic  10.1 us (3%)
  matrix products  7.19 us (2%)
    unnamed x5, waiting for transfers between devices  68.7 us
    all_gather x1, blocking collectives, per_device(): lax.all_gather(query, 'req', axis=0, tiled=True)  32.3 us
    all_gather x1, blocking collectives, per_device(): lax.all_gather(value_new, 'req', axis=0, tiled=True)  30.5 us
    all_gather x1, blocking collectives, per_device(): lax.all_gather(resid, 'req', axis=0, tiled=True)  30.4 us
    all_gather x1, blocking collectives, per_device(): stream_all = lax.all_gather(stream_own, 'req', axis=0, tiled=True)  30.4 us
    all_gather x1, blocking collectives, per_device(): lax.all_gather(key_new, 'req', axis=0, tiled=True)  30.4 us
    psum x1, waiting for transfers between devices, per_device(): lax.psum(partial_value.astype(jnp.bfloat16), 'tp').astype(jnp.float32)  27.9 us
    unnamed x1, blocking collectives  21.3 us
  transfers between devices with their start and end apart: 3, of which 2 were waited for; matrix products, arithmetic and copies ran while one was open for 1% of the time, Pallas kernels for 0%

commit v1 on v0

v1 whole, which is shorter than its diff:
```python
import math

import jax
import jax.numpy as jnp
from jax import lax
from jax.sharding import PartitionSpec as P

HEAD_DIM = 128
NORM_EPS = 1e-05
DIRECT = 16


def swap(x, axis, n, step):
    if step == 0:
        return x
    return lax.ppermute(x, axis, [(i, i ^ step) for i in range(n)])


def trade(blocks, axis, n):
    if n <= DIRECT:
        return [swap(blocks[s], axis, n, s) for s in range(n)]
    me = lax.axis_index(axis)
    pos = jnp.arange(n, dtype=jnp.int32) ^ me
    stacked = jnp.stack(blocks)[pos]
    moved = lax.all_to_all(stacked, axis, 0, 0, tiled=True)
    moved = moved[pos]
    return [moved[s] for s in range(n)]


def spread(x, axis, n):
    if n <= DIRECT:
        return [swap(x, axis, n, s) for s in range(n)]
    me = lax.axis_index(axis)
    pos = jnp.arange(n, dtype=jnp.int32) ^ me
    whole = lax.all_gather(x, axis, axis=0)[pos]
    return [whole[s] for s in range(n)]


def per_device(
    query,
    key_new,
    value_new,
    resid,
    lengths,
    owner,
    page_table,
    kv_pool,
    out_weight,
    out_bias,
    norm_gain,
    norm_bias,
    up_weight_t,
    up_bias,
    down_weight,
    down_bias,
    order,
):
    f32, bf16, i32 = jnp.float32, jnp.bfloat16, jnp.int32
    n_req = lax.axis_size("req")
    n_tp = lax.axis_size("tp")
    me = lax.axis_index("req")
    me_tp = lax.axis_index("tp")
    rows, cols = query.shape
    width = cols * n_tp
    heads = cols // HEAD_DIM
    pool_pages, page_len = kv_pool.shape[1], kv_pool.shape[2]
    positions = pool_pages * page_len
    scale = 1.0 / math.sqrt(HEAD_DIM)

    steps = jnp.arange(n_req, dtype=i32)
    my_owner = lax.dynamic_slice_in_dim(owner, me * rows, rows)
    send_hot = (my_owner[None, :] == (steps ^ me)[:, None]).astype(bf16)
    packed = jnp.concatenate([query, key_new, value_new, resid], axis=1)
    outgoing = jnp.dot(send_hot, packed, preferred_element_type=f32).astype(bf16)
    arrived = jnp.concatenate(
        trade([outgoing[s : s + 1] for s in range(n_req)], "req", n_req), axis=0
    )

    owner2 = owner.reshape(n_req, rows)
    same = owner[:, None] == owner[None, :]
    ids = jnp.arange(owner.shape[0], dtype=i32)
    rank = jnp.sum((same & (ids[None, :] < ids[:, None])).astype(i32), axis=1)
    slots = jnp.arange(rows, dtype=i32)
    mine = (owner == me)[None, :] & (rank[None, :] == slots[:, None])
    mine_i = mine.astype(i32)
    own_len = jnp.sum(mine_i * lengths[None, :], axis=1)
    own_table = jnp.sum(mine_i[:, :, None] * page_table[None], axis=1)
    own_src = jnp.sum(mine_i * (ids // rows)[None, :], axis=1)
    take_hot = (own_src[:, None] == (steps ^ me)[None, :]).astype(bf16)
    own = jnp.dot(take_hot, arrived, preferred_element_type=f32).astype(bf16)
    query_own, key_own, value_own, resid_own = (own[:, i * cols : (i + 1) * cols] for i in range(4))

    pos = jnp.arange(positions, dtype=i32)
    page, within = pos // page_len, pos % page_len
    entry = jnp.arange(page_table.shape[1], dtype=i32)
    start = entry * page_len
    hit = (own_table[:, :, None] == page[None, None, :]) & (
        start[None, :, None] + within[None, None, :] < own_len[:, None, None]
    )
    valid = jnp.any(hit, axis=1)

    keys = kv_pool[0].reshape(positions, cols)
    values = kv_pool[1].reshape(positions, cols)
    head_of = jnp.arange(cols, dtype=i32) // HEAD_DIM
    head_mask = head_of[None, :] == jnp.arange(heads, dtype=i32)[:, None]
    spread_q = jnp.where(head_mask[:, None, :], query_own[None], 0).reshape(heads * rows, cols)
    scores = (
        lax.dot_general(spread_q, keys, (((1,), (1,)), ((), ())), preferred_element_type=f32) * scale
    ).reshape(heads, rows, positions)
    scores = jnp.where(valid[None], scores, -jnp.inf)
    self_score = (
        jnp.sum(
            (query_own.astype(f32) * key_own.astype(f32)).reshape(rows, heads, HEAD_DIM), axis=-1
        ).T
        * scale
    )
    top = jnp.maximum(jnp.max(scores, axis=2), self_score)
    weights = jnp.exp(scores - top[:, :, None])
    self_weight = jnp.exp(self_score - top)
    total = jnp.sum(weights, axis=2) + self_weight
    numer = jnp.dot(
        weights.astype(bf16).reshape(heads * rows, positions), values, preferred_element_type=f32
    ).reshape(heads, rows, cols)
    numer = numer + self_weight.astype(bf16).astype(f32)[:, :, None] * value_own.astype(f32)[None]
    attn = jnp.sum(
        jnp.where(head_mask[:, None, :], numer / total[:, :, None], 0.0), axis=0
    ).astype(bf16)

    extra = resid_own.astype(f32) + out_bias.astype(f32)[None, :]
    partial = jnp.dot(attn, out_weight, preferred_element_type=f32)
    place = (jnp.arange(n_tp, dtype=i32) == me_tp)[None, :, None]
    partial = (
        partial.reshape(rows, n_tp, cols) + jnp.where(place, extra[:, None, :], 0.0)
    ).reshape(rows, width)
    stream = sum(spread(partial, "tp", n_tp)).astype(bf16)
    stream_f = stream.astype(f32)
    mean = jnp.mean(stream_f, axis=1, keepdims=True)
    var = jnp.mean((stream_f - mean) ** 2, axis=1, keepdims=True)
    inverse = lax.rsqrt(var + NORM_EPS)
    stream_own = lax.dynamic_slice_in_dim(stream, me_tp * cols, cols, axis=1)
    normed = (
        (stream_own.astype(f32) - mean) * inverse * norm_gain.astype(f32)[None, :]
        + norm_bias.astype(f32)[None, :]
    ).astype(bf16)

    normed_all = jnp.concatenate(spread(normed, "req", n_req), axis=0)
    order_rel = order.reshape(n_req, rows)[steps ^ me].reshape(-1)
    slot_rel = (owner ^ me) * rows + rank
    place_hot = (slot_rel[order_rel][:, None] == ids[None, :]).astype(bf16)
    normed_out = jnp.dot(place_hot, normed_all, preferred_element_type=f32).astype(bf16)
    hidden = lax.dot_general(
        normed_out, up_weight_t, (((1,), (1,)), ((), ())), preferred_element_type=f32
    ).astype(bf16)
    summed = sum(h.astype(f32) for h in spread(hidden, "tp", n_tp))
    activated = jax.nn.gelu(summed + up_bias.astype(f32)[None, :], approximate=False).astype(bf16)
    feed = jnp.dot(activated, down_weight, preferred_element_type=f32)
    feed = feed + jnp.dot(place_hot[:, :rows], stream_own, preferred_element_type=f32)
    pieces = trade([feed[s * rows : (s + 1) * rows] for s in range(n_req)], "req", n_req)
    return (sum(pieces) + down_bias.astype(f32)[None, :]).astype(bf16)


def solution(mesh):
    in_specs = (
        P("req", "tp"),
        P("req", "tp"),
        P("req", "tp"),
        P("req", "tp"),
        P(),
        P(),
        P(),
        P(None, "req", None, "tp"),
        P("tp", None),
        P("tp"),
        P("tp"),
        P("tp"),
        P("req", "tp"),
        P("req"),
        P("req", "tp"),
        P("tp"),
        P(),
    )
    out_specs = P("req", "tp")
    return jax.shard_map(
        per_device, mesh=mesh, in_specs=in_specs, out_specs=out_specs, check_vma=False
    )
```

time: 323 us -> 74.3 us (0.23)
  blocking collectives: 181 us -> 0 us
  waiting for transfers between devices: 96.6 us -> 19.2 us
  starting transfers between devices: 0.09 us -> 38.7 us
  between operations: 14.9 us -> 0.39 us
  local copies, waits for them, and re-layouts: 12.7 us -> 5.88 us
  other arithmetic: 10.1 us -> 4.25 us
    all_gather x5 -> x0, blocking collectives: 154 us -> none  [the longest x1 32.3 us: per_device(): lax.all_gather(query, 'req', axis=0, tiled=True)]
    unnamed x5 -> x0, waiting for transfers between devices: 68.7 us -> none
    ppermute x0 -> x27, starting transfers between devices: none -> 38.7 us  [swap(): return lax.ppermute(x, axis, [(i, i ^ step) for i in range(n)])]
    psum x1 -> x0, waiting for transfers between devices: 27.9 us -> none  [per_device(): lax.psum(partial_value.astype(jnp.bfloat16), 'tp').astype(jnp.float32)]
    unnamed x1 -> x0, blocking collectives: 21.3 us -> none
    ppermute x0 -> x27, waiting for transfers between devices: none -> 19.2 us  [swap(): return lax.ppermute(x, axis, [(i, i ^ step) for i in range(n)])]
    psum x1 -> x0, blocking collectives: 5.67 us -> none  [per_device(): lax.psum((jnp.sum(own_f, axis=1), jnp.sum(own_f * own_f, axis=1)), 'tp')]
    unnamed x49 -> x24, local copies, waits for them, and re-layouts: 4.57 us -> 0.17 us
  transfers between devices with their start and end apart: 3 -> 27, of which waited for: 2 -> 9; matrix products, arithmetic and copies ran while one was open for 1% -> 9% of each run, Pallas kernels for 0% -> 0%
where the time goes in v1:
time: 74.3 us; the launch traced here: 74 us
  starting transfers between devices  38.7 us (52%)
  waiting for transfers between devices  19.2 us (26%)
  local copies, waits for them, and re-layouts  5.88 us (8%)
  matrix products  5.59 us (8%)
  other arithmetic  4.25 us (6%)
    ppermute x27, starting transfers between devices, swap(): return lax.ppermute(x, axis, [(i, i ^ step) for i in range(n)])  38.7 us
    ppermute x27, waiting for transfers between devices, swap(): return lax.ppermute(x, axis, [(i, i ^ step) for i in range(n)])  19.2 us
    slice x1, local copies, waits for them, and re-layouts, per_device(): values = kv_pool[1].reshape(positions, cols)  2.35 us
    dot_general x1, matrix products, per_device(): feed = jnp.dot(activated, down_weight, preferred_element_type=f32)  1.69 us
  transfers between devices with their start and end apart: 27, of which 9 were waited for; matrix products, arithmetic and copies ran while one was open for 9% of the time, Pallas kernels for 0%

profile of v1, /device:TPU:0, one launch (start us, length us, event | category | flops | bytes accessed | tf_op | source)
XLA Modules:
  0.0 74.0 jit_solution(11291133617068577108)
XLA Ops:
  0.0 0.9 %dynamic_slice.6 = s32[4]{0:T(128)S(1)} dynamic-slice(s32[32]{0:T(128)} %param.22, s32[]{:T(128)S(6)} %select_n.102), dynamic_slice_sizes={4} | dynamic-slice | bytes 36 | tf_op jit(solution)/shard_map/dynamic_slice | solution.py:71
  0.9 0.9 %convolution_convert_fusion = bf16[8,2048]{1,0:T(8,128)(2,1)S(1)} fusion(bf16[4,512]{1,0:T(4,128)(2,1)} %param.20, bf16[4,512]{1,0:T(4,128)(2,1)} %param.19, bf16[4,512]{1,0:T(4,128)(2,1)} %param.18, bf16[4,512]{1,0:T(4,128)(2,1)} %param.17, s32[4]{0:T(128)S(1)} %dynamic_slice.6, s32[8]{0:T(128)S(1)} %iota_xor_fusion), kind=kOutput, calls=%fused_computation.2 | convolution fusion | flops 213024 | bytes 49200 | tf_op jit(solution)/shard_map/dot_general | solution.py:74
  1.9 3.0 %collective-permute-start = (bf16[1,2048]{1,0:T(2,128)(2,1)S(1)}, bf16[1,2048]{1,0:T(2,128)(2,1)S(1)}, u32[]{:S(2)}, u32[]{:S(2)}) collective-permute-start(bf16[1,2048]{1,0:T(2,128)(2,1)S(1)} %get-tuple-element.26), channel_id=1, source_target_pairs={{0,4},{4,0},{8,12},{12,8},{16,20},{20,16},{24,28},{28,24},{1,5},{5... | collective-permute-start | bytes 12296 | tf_op jit(solution)/shard_map/ppermute | solution.py:16
  4.9 1.6 %collective-permute-start.1 = (bf16[1,2048]{1,0:T(2,128)(2,1)S(1)}, bf16[1,2048]{1,0:T(2,128)(2,1)S(1)}, u32[]{:S(2)}, u32[]{:S(2)}) collective-permute-start(bf16[1,2048]{1,0:T(2,128)(2,1)S(1)} %get-tuple-element.25), channel_id=1, source_target_pairs={{0,8},{4,12},{8,0},{12,4},{16,24},{20,28},{24,16},{28,20},{1,9},{5... | collective-permute-start | bytes 12296 | tf_op jit(solution)/shard_map/ppermute | solution.py:16
  6.5 3.0 %collective-permute-start.3 = (bf16[1,2048]{1,0:T(2,128)(2,1)S(1)}, bf16[1,2048]{1,0:T(2,128)(2,1)S(1)}, u32[]{:S(2)}, u32[]{:S(2)}) collective-permute-start(bf16[1,2048]{1,0:T(2,128)(2,1)S(1)} %get-tuple-element.23), channel_id=1, source_target_pairs={{0,16},{4,20},{8,24},{12,28},{16,0},{20,4},{24,8},{28,12},{1,17},{... | collective-permute-start | bytes 12296 | tf_op jit(solution)/shard_map/ppermute | solution.py:16
  9.5 1.3 %collective-permute-start.4 = (bf16[1,2048]{1,0:T(2,128)(2,1)S(1)}, bf16[1,2048]{1,0:T(2,128)(2,1)S(1)}, u32[]{:S(2)}, u32[]{:S(2)}) collective-permute-start(bf16[1,2048]{1,0:T(2,128)(2,1)S(1)} %get-tuple-element.22), channel_id=1, source_target_pairs={{0,20},{4,16},{8,28},{12,24},{16,4},{20,0},{24,12},{28,8},{1,21},{... | collective-permute-start | bytes 12296 | tf_op jit(solution)/shard_map/ppermute | solution.py:16
  11.4 0.9 %convert_reduce_fusion.1 = s32[32]{0:T(128)S(1)} fusion(s32[32]{0:T(128)} %param.22), kind=kLoop, calls=%fused_computation.86 | loop fusion | flops 5088 | bytes 256 | tf_op jit(solution)/shard_map/reduce_sum | solution.py:82
  12.4 0.7 multiply_add_fusion
  13.1 2.3 %fusion.124 = (bf16[1,22,32,512]{3,2,1,0:T(8,128)(2,1)}, bf16[1,22,32,512]{3,2,1,0:T(8,128)(2,1)S(1)}) fusion(bf16[2,22,32,512]{3,2,1,0:T(8,128)(2,1)} %param.24), kind=kLoop, calls=%fused_computation.191 | loop fusion | bytes 2883584 | tf_op jit(solution)/shard_map/slice | solution.py:103
  16.0 3.7 %collective-permute-start.5 = (bf16[1,2048]{1,0:T(2,128)(2,1)S(1)}, bf16[1,2048]{1,0:T(2,128)(2,1)S(1)}, u32[]{:S(2)}, u32[]{:S(2)}) collective-permute-start(bf16[1,2048]{1,0:T(2,128)(2,1)S(1)} %get-tuple-element.21), channel_id=1, source_target_pairs={{0,24},{4,28},{8,16},{12,20},{16,8},{20,12},{24,0},{28,4},{1,25},{... | collective-permute-start | bytes 12296 | tf_op jit(solution)/shard_map/ppermute | solution.py:16
  19.9 1.7 %collective-permute-done.5 = bf16[1,2048]{1,0:T(2,128)(2,1)S(1)} collective-permute-done((bf16[1,2048]{1,0:T(2,128)(2,1)S(1)}, bf16[1,2048]{1,0:T(2,128)(2,1)S(1)}, u32[]{:S(2)}, u32[]{:S(2)}) %collective-permute-start.5) | collective-permute-done | bytes 4128 | tf_op jit(solution)/shard_map/ppermute | solution.py:16
  21.6 4.5 %collective-permute-done.6 = bf16[1,2048]{1,0:T(2,128)(2,1)S(1)} collective-permute-done((bf16[1,2048]{1,0:T(2,128)(2,1)S(1)}, bf16[1,2048]{1,0:T(2,128)(2,1)S(1)}, u32[]{:S(2)}, u32[]{:S(2)}) %collective-permute-start.6) | collective-permute-done | bytes 4128 | tf_op jit(solution)/shard_map/ppermute | solution.py:16
  28.0 1.3 %fusion.3 = bf16[4,512]{1,0:T(4,128)(2,1)S(1)} fusion(bf16[4,4,704]{2,1,0:T(4,128)(2,1)S(1)} %dot_general.32, bf16[704,512,1]{1,0,2:T(8,128)(2,1)} %bitcast.38, f32[4,4]{1,0:T(4,128)S(1)} %copy.30, f32[4,512]{1,0:T(4,128)S(1)} %get-tuple-element.28, f32[4,4]{1,0:T(4,128)S(1)} %copy.28, pred[4,512]{1,0:T(4,128)(4,1)S(1)} %iota_compare_fusion.2), kind=kOutput, calls=%fused_computation.13 | convolution fusion | flops 11573248 | bytes 757888 | tf_op jit(solution)/shard_map/dot_general | solution.py:121
  29.8 1.5 %collective-permute-start.8 = (f32[4,2048]{1,0:T(4,128)S(1)}, f32[4,2048]{1,0:T(4,128)S(1)}, u32[]{:S(2)}, u32[]{:S(2)}) collective-permute-start(f32[4,2048]{1,0:T(4,128)S(1)} %convolution_add_fusion), channel_id=1, source_target_pairs={{0,2},{1,3},{2,0},{3,1},{4,6},{5,7},{6,4},{7,5},{8,10},{9,11},{10,... | collective-permute-start | bytes 98312 | tf_op jit(solution)/shard_map/ppermute | solution.py:16
  32.4 1.3 %collective-permute-done.8 = f32[4,2048]{1,0:T(4,128)S(1)} collective-permute-done((f32[4,2048]{1,0:T(4,128)S(1)}, f32[4,2048]{1,0:T(4,128)S(1)}, u32[]{:S(2)}, u32[]{:S(2)}) %collective-permute-start.8) | collective-permute-done | bytes 32800 | tf_op jit(solution)/shard_map/ppermute | solution.py:16
  33.7 0.9 %collective-permute-done.9 = f32[4,2048]{1,0:T(4,128)S(1)} collective-permute-done((f32[4,2048]{1,0:T(4,128)S(1)}, f32[4,2048]{1,0:T(4,128)S(1)}, u32[]{:S(2)}, u32[]{:S(2)}) %collective-permute-start.9) | collective-permute-done | bytes 32800 | tf_op jit(solution)/shard_map/ppermute | solution.py:16
  35.6 3.0 %collective-permute-start.12 = (bf16[4,512]{1,0:T(4,128)(2,1)S(1)}, bf16[4,512]{1,0:T(4,128)(2,1)S(1)}, u32[]{:S(2)}, u32[]{:S(2)}) collective-permute-start(bf16[4,512]{1,0:T(4,128)(2,1)S(1)} %add_convert_fusion.1), channel_id=1, source_target_pairs={{0,12},{4,8},{8,4},{12,0},{16,28},{20,24},{24,20},{28,16},{1,13},{... | collective-permute-start | bytes 12296 | tf_op jit(solution)/shard_map/ppermute | solution.py:16
  38.6 2.9 %collective-permute-start.14 = (bf16[4,512]{1,0:T(4,128)(2,1)S(1)}, bf16[4,512]{1,0:T(4,128)(2,1)S(1)}, u32[]{:S(2)}, u32[]{:S(2)}) collective-permute-start(bf16[4,512]{1,0:T(4,128)(2,1)S(1)} %add_convert_fusion.1), channel_id=1, source_target_pairs={{0,20},{4,16},{8,28},{12,24},{16,4},{20,0},{24,12},{28,8},{1,21},{... | collective-permute-start | bytes 12296 | tf_op jit(solution)/shard_map/ppermute | solution.py:16
  41.7 4.6 %collective-permute-start.16 = (bf16[4,512]{1,0:T(4,128)(2,1)S(1)}, bf16[4,512]{1,0:T(4,128)(2,1)S(1)}, u32[]{:S(2)}, u32[]{:S(2)}) collective-permute-start(bf16[4,512]{1,0:T(4,128)(2,1)S(1)} %add_convert_fusion.1), channel_id=1, source_target_pairs={{0,28},{4,24},{8,20},{12,16},{16,12},{20,8},{24,4},{28,0},{1,29},{... | collective-permute-start | bytes 12296 | tf_op jit(solution)/shard_map/ppermute | solution.py:16
  46.2 0.7 gather_fusion.1
  47.0 1.0 %collective-permute-done.16 = bf16[4,512]{1,0:T(4,128)(2,1)S(1)} collective-permute-done((bf16[4,512]{1,0:T(4,128)(2,1)S(1)}, bf16[4,512]{1,0:T(4,128)(2,1)S(1)}, u32[]{:S(2)}, u32[]{:S(2)}) %collective-permute-start.16) | collective-permute-done | bytes 4128 | tf_op jit(solution)/shard_map/ppermute | solution.py:16
  48.7 0.9 %collective-permute-start.18 = (bf16[32,1024]{1,0:T(8,128)(2,1)S(1)}, bf16[32,1024]{1,0:T(8,128)(2,1)S(1)}, u32[]{:S(2)}, u32[]{:S(2)}) collective-permute-start(bf16[32,1024]{1,0:T(8,128)(2,1)S(1)} %convolution_convert_fusion.2), channel_id=1, source_target_pairs={{0,2},{1,3},{2,0},{3,1},{4,6},{5,7},{6,4},{7,5},{8,10},{9,11},{10,... | collective-permute-start | bytes 196616 | tf_op jit(solution)/shard_map/ppermute | solution.py:16
  49.6 1.0 %collective-permute-start.19 = (bf16[32,1024]{1,0:T(8,128)(2,1)S(1)}, bf16[32,1024]{1,0:T(8,128)(2,1)S(1)}, u32[]{:S(2)}, u32[]{:S(2)}) collective-permute-start(bf16[32,1024]{1,0:T(8,128)(2,1)S(1)} %convolution_convert_fusion.2), channel_id=1, source_target_pairs={{0,3},{1,2},{2,1},{3,0},{4,7},{5,6},{6,5},{7,4},{8,11},{9,10},{10,... | collective-permute-start | bytes 196616 | tf_op jit(solution)/shard_map/ppermute | solution.py:16
  50.7 3.0 %collective-permute-done.18 = bf16[32,1024]{1,0:T(8,128)(2,1)S(1)} collective-permute-done((bf16[32,1024]{1,0:T(8,128)(2,1)S(1)}, bf16[32,1024]{1,0:T(8,128)(2,1)S(1)}, u32[]{:S(2)}, u32[]{:S(2)}) %collective-permute-start.18) | collective-permute-done | bytes 65568 | tf_op jit(solution)/shard_map/ppermute | solution.py:16
  54.2 1.7 %fusion.14 = f32[32,512]{1,0:T(8,128)S(1)} fusion(bf16[1024,512]{1,0:T(8,128)(2,1)} %param.31, bf16[32,1024]{1,0:T(8,128)(2,1)S(1)} %collective-permute-done.19, bf16[32,1024]{1,0:T(8,128)(2,1)S(1)} %collective-permute-done.18, bf16[32,1024]{1,0:T(8,128)(2,1)S(1)} %collective-permute-done.17, bf16[32,1024]{1,0:T(8,128)(2,1)S(1)} %convolution_convert_fusion.2, ...), kind=kOutput, calls=%fused_computation.35 | convolution fusion | flops 35946496 | bytes 1380352 | tf_op jit(solution)/shard_map/dot_general | solution.py:156
  56.0 1.6 %collective-permute-start.20 = (f32[4,512]{1,0:T(4,128)S(1)}, f32[4,512]{1,0:T(4,128)S(1)}, u32[]{:S(2)}, u32[]{:S(2)}) collective-permute-start(f32[4,512]{1,0:T(4,128)S(1)} %get-tuple-element.11), channel_id=1, source_target_pairs={{0,4},{4,0},{8,12},{12,8},{16,20},{20,16},{24,28},{28,24},{1,5},{5... | collective-permute-start | bytes 24584 | tf_op jit(solution)/shard_map/ppermute | solution.py:16
  57.6 2.0 %collective-permute-start.22 = (f32[4,512]{1,0:T(4,128)S(1)}, f32[4,512]{1,0:T(4,128)S(1)}, u32[]{:S(2)}, u32[]{:S(2)}) collective-permute-start(f32[4,512]{1,0:T(4,128)S(1)} %get-tuple-element.16), channel_id=1, source_target_pairs={{0,12},{4,8},{8,4},{12,0},{16,28},{20,24},{24,20},{28,16},{1,13},{... | collective-permute-start | bytes 24584 | tf_op jit(solution)/shard_map/ppermute | solution.py:16
  59.5 2.2 %collective-permute-start.23 = (f32[4,512]{1,0:T(4,128)S(1)}, f32[4,512]{1,0:T(4,128)S(1)}, u32[]{:S(2)}, u32[]{:S(2)}) collective-permute-start(f32[4,512]{1,0:T(4,128)S(1)} %get-tuple-element.15), channel_id=1, source_target_pairs={{0,16},{4,20},{8,24},{12,28},{16,0},{20,4},{24,8},{28,12},{1,17},{... | collective-permute-start | bytes 24584 | tf_op jit(solution)/shard_map/ppermute | solution.py:16
  61.8 1.7 %collective-permute-start.24 = (f32[4,512]{1,0:T(4,128)S(1)}, f32[4,512]{1,0:T(4,128)S(1)}, u32[]{:S(2)}, u32[]{:S(2)}) collective-permute-start(f32[4,512]{1,0:T(4,128)S(1)} %get-tuple-element.14), channel_id=1, source_target_pairs={{0,20},{4,16},{8,28},{12,24},{16,4},{20,0},{24,12},{28,8},{1,21},{... | collective-permute-start | bytes 24584 | tf_op jit(solution)/shard_map/ppermute | solution.py:16
  63.4 3.6 %collective-permute-start.25 = (f32[4,512]{1,0:T(4,128)S(1)}, f32[4,512]{1,0:T(4,128)S(1)}, u32[]{:S(2)}, u32[]{:S(2)}) collective-permute-start(f32[4,512]{1,0:T(4,128)S(1)} %get-tuple-element.13), channel_id=1, source_target_pairs={{0,24},{4,28},{8,16},{12,20},{16,8},{20,12},{24,0},{28,4},{1,25},{... | collective-permute-start | bytes 24584 | tf_op jit(solution)/shard_map/ppermute | solution.py:16
  67.2 1.6 %collective-permute-done.25 = f32[4,512]{1,0:T(4,128)S(1)} collective-permute-done((f32[4,512]{1,0:T(4,128)S(1)}, f32[4,512]{1,0:T(4,128)S(1)}, u32[]{:S(2)}, u32[]{:S(2)}) %collective-permute-start.25) | collective-permute-done | bytes 8224 | tf_op jit(solution)/shard_map/ppermute | solution.py:16
  68.9 4.5 %collective-permute-done.26 = f32[4,512]{1,0:T(4,128)S(1)} collective-permute-done((f32[4,512]{1,0:T(4,128)S(1)}, f32[4,512]{1,0:T(4,128)S(1)}, u32[]{:S(2)}, u32[]{:S(2)}) %collective-permute-start.26) | collective-permute-done | bytes 8224 | tf_op jit(solution)/shard_map/ppermute | solution.py:16
  (116 shorter events, 8.2 us)
Async XLA Ops:
  0.0 29.4 %copy-start = (bf16[512,2048]{1,0:T(8,128)(2,1)S(1)}, bf16[512,2048]{1,0:T(8,128)(2,1)}, u32[]{:S(2)}) copy-start(bf16[512,2048]{1,0:T(8,128)(2,1)} %param.25) | copy-start | bytes 6291460
  0.0 19.8 %copy-start.4 = (bf16[512]{0:T(512)(128)(2,1)S(1)}, bf16[512]{0:T(512)(128)(2,1)}, u32[]{:S(2)}) copy-start(bf16[512]{0:T(512)(128)(2,1)} %param.26) | copy-start | bytes 3076
  1.9 14.1 %collective-permute-start = (bf16[1,2048]{1,0:T(2,128)(2,1)S(1)}, bf16[1,2048]{1,0:T(2,128)(2,1)S(1)}, u32[]{:S(2)}, u32[]{:S(2)}) collective-permute-start(bf16[1,2048]{1,0:T(2,128)(2,1)S(1)} %get-tuple-element.26), channel_id=1, source_target_pairs={{0,4},{4,0},{8,12},{12,8},{16,20},{20,16},{24,28},{28,24},{1,5},{5... | collective-permute-start | bytes 12296 | tf_op jit(solution)/shard_map/ppermute | solution.py:16
  4.9 14.8 %collective-permute-start.1 = (bf16[1,2048]{1,0:T(2,128)(2,1)S(1)}, bf16[1,2048]{1,0:T(2,128)(2,1)S(1)}, u32[]{:S(2)}, u32[]{:S(2)}) collective-permute-start(bf16[1,2048]{1,0:T(2,128)(2,1)S(1)} %get-tuple-element.25), channel_id=1, source_target_pairs={{0,8},{4,12},{8,0},{12,4},{16,24},{20,28},{24,16},{28,20},{1,9},{5... | collective-permute-start | bytes 12296 | tf_op jit(solution)/shard_map/ppermute | solution.py:16
  6.5 13.3 %collective-permute-start.2 = (bf16[1,2048]{1,0:T(2,128)(2,1)S(1)}, bf16[1,2048]{1,0:T(2,128)(2,1)S(1)}, u32[]{:S(2)}, u32[]{:S(2)}) collective-permute-start(bf16[1,2048]{1,0:T(2,128)(2,1)S(1)} %get-tuple-element.24), channel_id=1, source_target_pairs={{0,12},{4,8},{8,4},{12,0},{16,28},{20,24},{24,20},{28,16},{1,13},{... | collective-permute-start | bytes 12296 | tf_op jit(solution)/shard_map/ppermute | solution.py:16
  6.5 13.3 %collective-permute-start.3 = (bf16[1,2048]{1,0:T(2,128)(2,1)S(1)}, bf16[1,2048]{1,0:T(2,128)(2,1)S(1)}, u32[]{:S(2)}, u32[]{:S(2)}) collective-permute-start(bf16[1,2048]{1,0:T(2,128)(2,1)S(1)} %get-tuple-element.23), channel_id=1, source_target_pairs={{0,16},{4,20},{8,24},{12,28},{16,0},{20,4},{24,8},{28,12},{1,17},{... | collective-permute-start | bytes 12296 | tf_op jit(solution)/shard_map/ppermute | solution.py:16
  9.5 10.3 %collective-permute-start.4 = (bf16[1,2048]{1,0:T(2,128)(2,1)S(1)}, bf16[1,2048]{1,0:T(2,128)(2,1)S(1)}, u32[]{:S(2)}, u32[]{:S(2)}) collective-permute-start(bf16[1,2048]{1,0:T(2,128)(2,1)S(1)} %get-tuple-element.22), channel_id=1, source_target_pairs={{0,20},{4,16},{8,28},{12,24},{16,4},{20,0},{24,12},{28,8},{1,21},{... | collective-permute-start | bytes 12296 | tf_op jit(solution)/shard_map/ppermute | solution.py:16
  16.0 5.5 %collective-permute-start.5 = (bf16[1,2048]{1,0:T(2,128)(2,1)S(1)}, bf16[1,2048]{1,0:T(2,128)(2,1)S(1)}, u32[]{:S(2)}, u32[]{:S(2)}) collective-permute-start(bf16[1,2048]{1,0:T(2,128)(2,1)S(1)} %get-tuple-element.21), channel_id=1, source_target_pairs={{0,24},{4,28},{8,16},{12,20},{16,8},{20,12},{24,0},{28,4},{1,25},{... | collective-permute-start | bytes 12296 | tf_op jit(solution)/shard_map/ppermute | solution.py:16
  19.7 6.3 %collective-permute-start.6 = (bf16[1,2048]{1,0:T(2,128)(2,1)S(1)}, bf16[1,2048]{1,0:T(2,128)(2,1)S(1)}, u32[]{:S(2)}, u32[]{:S(2)}) collective-permute-start(bf16[1,2048]{1,0:T(2,128)(2,1)S(1)} %get-tuple-element.20), channel_id=1, source_target_pairs={{0,28},{4,24},{8,20},{12,16},{16,12},{20,8},{24,4},{28,0},{1,29},{... | collective-permute-start | bytes 12296 | tf_op jit(solution)/shard_map/ppermute | solution.py:16
  26.9 21.2 %copy-start.1 = (bf16[1024,512]{1,0:T(8,128)(2,1)S(1)}, bf16[1024,512]{1,0:T(8,128)(2,1)}, u32[]{:S(2)}) copy-start(bf16[1024,512]{1,0:T(8,128)(2,1)} %param.29) | copy-start | bytes 3145732
  29.4 21.3 %copy-start.3 = (bf16[1024]{0:T(1024)(128)(2,1)S(1)}, bf16[1024]{0:T(1024)(128)(2,1)}, u32[]{:S(2)}) copy-start(bf16[1024]{0:T(1024)(128)(2,1)} %param.30) | copy-start | bytes 6148
  29.8 2.6 %collective-permute-start.7 = (f32[4,2048]{1,0:T(4,128)S(1)}, f32[4,2048]{1,0:T(4,128)S(1)}, u32[]{:S(2)}, u32[]{:S(2)}) collective-permute-start(f32[4,2048]{1,0:T(4,128)S(1)} %convolution_add_fusion), channel_id=1, source_target_pairs={{0,1},{1,0},{2,3},{3,2},{4,5},{5,4},{6,7},{7,6},{8,9},{9,8},{10,11... | collective-permute-start | bytes 98312 | tf_op jit(solution)/shard_map/ppermute | solution.py:16
  29.8 4.0 %collective-permute-start.8 = (f32[4,2048]{1,0:T(4,128)S(1)}, f32[4,2048]{1,0:T(4,128)S(1)}, u32[]{:S(2)}, u32[]{:S(2)}) collective-permute-start(f32[4,2048]{1,0:T(4,128)S(1)} %convolution_add_fusion), channel_id=1, source_target_pairs={{0,2},{1,3},{2,0},{3,1},{4,6},{5,7},{6,4},{7,5},{8,10},{9,11},{10,... | collective-permute-start | bytes 98312 | tf_op jit(solution)/shard_map/ppermute | solution.py:16
  31.3 3.3 %collective-permute-start.9 = (f32[4,2048]{1,0:T(4,128)S(1)}, f32[4,2048]{1,0:T(4,128)S(1)}, u32[]{:S(2)}, u32[]{:S(2)}) collective-permute-start(f32[4,2048]{1,0:T(4,128)S(1)} %convolution_add_fusion), channel_id=1, source_target_pairs={{0,3},{1,2},{2,1},{3,0},{4,7},{5,6},{6,5},{7,4},{8,11},{9,10},{10,... | collective-permute-start | bytes 98312 | tf_op jit(solution)/shard_map/ppermute | solution.py:16
  35.1 6.4 %collective-permute-start.10 = (bf16[4,512]{1,0:T(4,128)(2,1)S(1)}, bf16[4,512]{1,0:T(4,128)(2,1)S(1)}, u32[]{:S(2)}, u32[]{:S(2)}) collective-permute-start(bf16[4,512]{1,0:T(4,128)(2,1)S(1)} %add_convert_fusion.1), channel_id=1, source_target_pairs={{0,4},{4,0},{8,12},{12,8},{16,20},{20,16},{24,28},{28,24},{1,5},{5... | collective-permute-start | bytes 12296 | tf_op jit(solution)/shard_map/ppermute | solution.py:16
  35.6 6.1 %collective-permute-start.11 = (bf16[4,512]{1,0:T(4,128)(2,1)S(1)}, bf16[4,512]{1,0:T(4,128)(2,1)S(1)}, u32[]{:S(2)}, u32[]{:S(2)}) collective-permute-start(bf16[4,512]{1,0:T(4,128)(2,1)S(1)} %add_convert_fusion.1), channel_id=1, source_target_pairs={{0,8},{4,12},{8,0},{12,4},{16,24},{20,28},{24,16},{28,20},{1,9},{5... | collective-permute-start | bytes 12296 | tf_op jit(solution)/shard_map/ppermute | solution.py:16
  35.6 11.3 %collective-permute-start.12 = (bf16[4,512]{1,0:T(4,128)(2,1)S(1)}, bf16[4,512]{1,0:T(4,128)(2,1)S(1)}, u32[]{:S(2)}, u32[]{:S(2)}) collective-permute-start(bf16[4,512]{1,0:T(4,128)(2,1)S(1)} %add_convert_fusion.1), channel_id=1, source_target_pairs={{0,12},{4,8},{8,4},{12,0},{16,28},{20,24},{24,20},{28,16},{1,13},{... | collective-permute-start | bytes 12296 | tf_op jit(solution)/shard_map/ppermute | solution.py:16
  38.6 8.4 %collective-permute-start.13 = (bf16[4,512]{1,0:T(4,128)(2,1)S(1)}, bf16[4,512]{1,0:T(4,128)(2,1)S(1)}, u32[]{:S(2)}, u32[]{:S(2)}) collective-permute-start(bf16[4,512]{1,0:T(4,128)(2,1)S(1)} %add_convert_fusion.1), channel_id=1, source_target_pairs={{0,16},{4,20},{8,24},{12,28},{16,0},{20,4},{24,8},{28,12},{1,17},{... | collective-permute-start | bytes 12296 | tf_op jit(solution)/shard_map/ppermute | solution.py:16
  38.6 8.4 %collective-permute-start.14 = (bf16[4,512]{1,0:T(4,128)(2,1)S(1)}, bf16[4,512]{1,0:T(4,128)(2,1)S(1)}, u32[]{:S(2)}, u32[]{:S(2)}) collective-permute-start(bf16[4,512]{1,0:T(4,128)(2,1)S(1)} %add_convert_fusion.1), channel_id=1, source_target_pairs={{0,20},{4,16},{8,28},{12,24},{16,4},{20,0},{24,12},{28,8},{1,21},{... | collective-permute-start | bytes 12296 | tf_op jit(solution)/shard_map/ppermute | solution.py:16
  41.5 5.5 %collective-permute-start.15 = (bf16[4,512]{1,0:T(4,128)(2,1)S(1)}, bf16[4,512]{1,0:T(4,128)(2,1)S(1)}, u32[]{:S(2)}, u32[]{:S(2)}) collective-permute-start(bf16[4,512]{1,0:T(4,128)(2,1)S(1)} %add_convert_fusion.1), channel_id=1, source_target_pairs={{0,24},{4,28},{8,16},{12,20},{16,8},{20,12},{24,0},{28,4},{1,25},{... | collective-permute-start | bytes 12296 | tf_op jit(solution)/shard_map/ppermute | solution.py:16
  41.7 6.3 %collective-permute-start.16 = (bf16[4,512]{1,0:T(4,128)(2,1)S(1)}, bf16[4,512]{1,0:T(4,128)(2,1)S(1)}, u32[]{:S(2)}, u32[]{:S(2)}) collective-permute-start(bf16[4,512]{1,0:T(4,128)(2,1)S(1)} %add_convert_fusion.1), channel_id=1, source_target_pairs={{0,28},{4,24},{8,20},{12,16},{16,12},{20,8},{24,4},{28,0},{1,29},{... | collective-permute-start | bytes 12296 | tf_op jit(solution)/shard_map/ppermute | solution.py:16
  48.6 18.6 %copy-start.7 = (bf16[512]{0:T(512)(128)(2,1)S(1)}, bf16[512]{0:T(512)(128)(2,1)}, u32[]{:S(2)}) copy-start(bf16[512]{0:T(512)(128)(2,1)} %param.32) | copy-start | bytes 3076
  48.6 2.0 %collective-permute-start.17 = (bf16[32,1024]{1,0:T(8,128)(2,1)S(1)}, bf16[32,1024]{1,0:T(8,128)(2,1)S(1)}, u32[]{:S(2)}, u32[]{:S(2)}) collective-permute-start(bf16[32,1024]{1,0:T(8,128)(2,1)S(1)} %convolution_convert_fusion.2), channel_id=1, source_target_pairs={{0,1},{1,0},{2,3},{3,2},{4,5},{5,4},{6,7},{7,6},{8,9},{9,8},{10,11... | collective-permute-start | bytes 196616 | tf_op jit(solution)/shard_map/ppermute | solution.py:16
  48.7 5.0 %collective-permute-start.18 = (bf16[32,1024]{1,0:T(8,128)(2,1)S(1)}, bf16[32,1024]{1,0:T(8,128)(2,1)S(1)}, u32[]{:S(2)}, u32[]{:S(2)}) collective-permute-start(bf16[32,1024]{1,0:T(8,128)(2,1)S(1)} %convolution_convert_fusion.2), channel_id=1, source_target_pairs={{0,2},{1,3},{2,0},{3,1},{4,6},{5,7},{6,4},{7,5},{8,10},{9,11},{10,... | collective-permute-start | bytes 196616 | tf_op jit(solution)/shard_map/ppermute | solution.py:16
  49.6 4.6 %collective-permute-start.19 = (bf16[32,1024]{1,0:T(8,128)(2,1)S(1)}, bf16[32,1024]{1,0:T(8,128)(2,1)S(1)}, u32[]{:S(2)}, u32[]{:S(2)}) collective-permute-start(bf16[32,1024]{1,0:T(8,128)(2,1)S(1)} %convolution_convert_fusion.2), channel_id=1, source_target_pairs={{0,3},{1,2},{2,1},{3,0},{4,7},{5,6},{6,5},{7,4},{8,11},{9,10},{10,... | collective-permute-start | bytes 196616 | tf_op jit(solution)/shard_map/ppermute | solution.py:16
  56.0 7.4 %collective-permute-start.20 = (f32[4,512]{1,0:T(4,128)S(1)}, f32[4,512]{1,0:T(4,128)S(1)}, u32[]{:S(2)}, u32[]{:S(2)}) collective-permute-start(f32[4,512]{1,0:T(4,128)S(1)} %get-tuple-element.11), channel_id=1, source_target_pairs={{0,4},{4,0},{8,12},{12,8},{16,20},{20,16},{24,28},{28,24},{1,5},{5... | collective-permute-start | bytes 24584 | tf_op jit(solution)/shard_map/ppermute | solution.py:16
  57.6 9.5 %collective-permute-start.21 = (f32[4,512]{1,0:T(4,128)S(1)}, f32[4,512]{1,0:T(4,128)S(1)}, u32[]{:S(2)}, u32[]{:S(2)}) collective-permute-start(f32[4,512]{1,0:T(4,128)S(1)} %get-tuple-element.17), channel_id=1, source_target_pairs={{0,8},{4,12},{8,0},{12,4},{16,24},{20,28},{24,16},{28,20},{1,9},{5... | collective-permute-start | bytes 24584 | tf_op jit(solution)/shard_map/ppermute | solution.py:16
  57.6 9.6 %collective-permute-start.22 = (f32[4,512]{1,0:T(4,128)S(1)}, f32[4,512]{1,0:T(4,128)S(1)}, u32[]{:S(2)}, u32[]{:S(2)}) collective-permute-start(f32[4,512]{1,0:T(4,128)S(1)} %get-tuple-element.16), channel_id=1, source_target_pairs={{0,12},{4,8},{8,4},{12,0},{16,28},{20,24},{24,20},{28,16},{1,13},{... | collective-permute-start | bytes 24584 | tf_op jit(solution)/shard_map/ppermute | solution.py:16
  59.5 7.7 %collective-permute-start.23 = (f32[4,512]{1,0:T(4,128)S(1)}, f32[4,512]{1,0:T(4,128)S(1)}, u32[]{:S(2)}, u32[]{:S(2)}) collective-permute-start(f32[4,512]{1,0:T(4,128)S(1)} %get-tuple-element.15), channel_id=1, source_target_pairs={{0,16},{4,20},{8,24},{12,28},{16,0},{20,4},{24,8},{28,12},{1,17},{... | collective-permute-start | bytes 24584 | tf_op jit(solution)/shard_map/ppermute | solution.py:16
  61.8 5.5 %collective-permute-start.24 = (f32[4,512]{1,0:T(4,128)S(1)}, f32[4,512]{1,0:T(4,128)S(1)}, u32[]{:S(2)}, u32[]{:S(2)}) collective-permute-start(f32[4,512]{1,0:T(4,128)S(1)} %get-tuple-element.14), channel_id=1, source_target_pairs={{0,20},{4,16},{8,28},{12,24},{16,4},{20,0},{24,12},{28,8},{1,21},{... | collective-permute-start | bytes 24584 | tf_op jit(solution)/shard_map/ppermute | solution.py:16
  63.4 5.4 %collective-permute-start.25 = (f32[4,512]{1,0:T(4,128)S(1)}, f32[4,512]{1,0:T(4,128)S(1)}, u32[]{:S(2)}, u32[]{:S(2)}) collective-permute-start(f32[4,512]{1,0:T(4,128)S(1)} %get-tuple-element.13), channel_id=1, source_target_pairs={{0,24},{4,28},{8,16},{12,20},{16,8},{20,12},{24,0},{28,4},{1,25},{... | collective-permute-start | bytes 24584 | tf_op jit(solution)/shard_map/ppermute | solution.py:16
  67.0 6.3 %collective-permute-start.26 = (f32[4,512]{1,0:T(4,128)S(1)}, f32[4,512]{1,0:T(4,128)S(1)}, u32[]{:S(2)}, u32[]{:S(2)}) collective-permute-start(f32[4,512]{1,0:T(4,128)S(1)} %get-tuple-element.12), channel_id=1, source_target_pairs={{0,28},{4,24},{8,20},{12,16},{16,12},{20,8},{24,4},{28,0},{1,29},{... | collective-permute-start | bytes 24584 | tf_op jit(solution)/shard_map/ppermute | solution.py:16
  (5 other events, 46.9 us)

commit v2 on v1

--- a/solution.py
+++ b/solution.py
@@ -7,33 +7,14 @@
 
 HEAD_DIM = 128
 NORM_EPS = 1e-05
-DIRECT = 16
 
 
-def swap(x, axis, n, step):
-    if step == 0:
-        return x
-    return lax.ppermute(x, axis, [(i, i ^ step) for i in range(n)])
+def trade(blocks, axis):
+    return lax.all_to_all(blocks, axis, 0, 0, tiled=True)
 
 
-def trade(blocks, axis, n):
-    if n <= DIRECT:
-        return [swap(blocks[s], axis, n, s) for s in range(n)]
-    me = lax.axis_index(axis)
-    pos = jnp.arange(n, dtype=jnp.int32) ^ me
-    stacked = jnp.stack(blocks)[pos]
-    moved = lax.all_to_all(stacked, axis, 0, 0, tiled=True)
-    moved = moved[pos]
-    return [moved[s] for s in range(n)]
-
-
-def spread(x, axis, n):
-    if n <= DIRECT:
-        return [swap(x, axis, n, s) for s in range(n)]
-    me = lax.axis_index(axis)
-    pos = jnp.arange(n, dtype=jnp.int32) ^ me
-    whole = lax.all_gather(x, axis, axis=0)[pos]
-    return [whole[s] for s in range(n)]
+def spread(x, axis):
+    return trade(jnp.broadcast_to(x[None], (lax.axis_size(axis),) + x.shape), axis)
 
 
 def per_device(
@@ -69,14 +50,11 @@
 
     steps = jnp.arange(n_req, dtype=i32)
     my_owner = lax.dynamic_slice_in_dim(owner, me * rows, rows)
-    send_hot = (my_owner[None, :] == (steps ^ me)[:, None]).astype(bf16)
+    send_hot = (my_owner[None, :] == steps[:, None]).astype(bf16)
     packed = jnp.concatenate([query, key_new, value_new, resid], axis=1)
     outgoing = jnp.dot(send_hot, packed, preferred_element_type=f32).astype(bf16)
-    arrived = jnp.concatenate(
-        trade([outgoing[s : s + 1] for s in range(n_req)], "req", n_req), axis=0
-    )
+    arrived = trade(outgoing[:, None], "req")[:, 0]
 
-    owner2 = owner.reshape(n_req, rows)
     same = owner[:, None] == owner[None, :]
     ids = jnp.arange(owner.shape[0], dtype=i32)
     rank = jnp.sum((same & (ids[None, :] < ids[:, None])).astype(i32), axis=1)
@@ -86,7 +64,7 @@
     own_len = jnp.sum(mine_i * lengths[None, :], axis=1)
     own_table = jnp.sum(mine_i[:, :, None] * page_table[None], axis=1)
     own_src = jnp.sum(mine_i * (ids // rows)[None, :], axis=1)
-    take_hot = (own_src[:, None] == (steps ^ me)[None, :]).astype(bf16)
+    take_hot = (own_src[:, None] == steps[None, :]).astype(bf16)
     own = jnp.dot(take_hot, arrived, preferred_element_type=f32).astype(bf16)
     query_own, key_own, value_own, resid_own = (own[:, i * cols : (i + 1) * cols] for i in range(4))
 
@@ -132,7 +110,7 @@
     partial = (
         partial.reshape(rows, n_tp, cols) + jnp.where(place, extra[:, None, :], 0.0)
     ).reshape(rows, width)
-    stream = sum(spread(partial, "tp", n_tp)).astype(bf16)
+    stream = jnp.sum(spread(partial, "tp"), axis=0).astype(bf16)
     stream_f = stream.astype(f32)
     mean = jnp.mean(stream_f, axis=1, keepdims=True)
     var = jnp.mean((stream_f - mean) ** 2, axis=1, keepdims=True)
@@ -143,20 +121,20 @@
         + norm_bias.astype(f32)[None, :]
     ).astype(bf16)
 
-    normed_all = jnp.concatenate(spread(normed, "req", n_req), axis=0)
-    order_rel = order.reshape(n_req, rows)[steps ^ me].reshape(-1)
-    slot_rel = (owner ^ me) * rows + rank
-    place_hot = (slot_rel[order_rel][:, None] == ids[None, :]).astype(bf16)
+    normed_all = spread(normed, "req").reshape(-1, cols)
+    slot_of = owner * rows + rank
+    place_hot = (slot_of[order][:, None] == ids[None, :]).astype(bf16)
+    mine_hot = (slot_of[order][:, None] == (me * rows + slots)[None, :]).astype(bf16)
     normed_out = jnp.dot(place_hot, normed_all, preferred_element_type=f32).astype(bf16)
     hidden = lax.dot_general(
         normed_out, up_weight_t, (((1,), (1,)), ((), ())), preferred_element_type=f32
     ).astype(bf16)
-    summed = sum(h.astype(f32) for h in spread(hidden, "tp", n_tp))
+    summed = jnp.sum(spread(hidden, "tp").astype(f32), axis=0)
     activated = jax.nn.gelu(summed + up_bias.astype(f32)[None, :], approximate=False).astype(bf16)
     feed = jnp.dot(activated, down_weight, preferred_element_type=f32)
-    feed = feed + jnp.dot(place_hot[:, :rows], stream_own, preferred_element_type=f32)
-    pieces = trade([feed[s * rows : (s + 1) * rows] for s in range(n_req)], "req", n_req)
-    return (sum(pieces) + down_bias.astype(f32)[None, :]).astype(bf16)
+    feed = feed + jnp.dot(mine_hot, stream_own, preferred_element_type=f32)
+    pieces = trade(feed.reshape(n_req, rows, cols), "req")
+    return (jnp.sum(pieces, axis=0) + down_bias.astype(f32)[None, :]).astype(bf16)
 
 
 def solution(mesh):

time: 74.3 us -> 66.9 us (0.900)
  starting transfers between devices: 38.7 us -> 22 us
  waiting for transfers between devices: 19.2 us -> 24.7 us
  local copies, waits for them, and re-layouts: 5.88 us -> 8.67 us
    ppermute x27 -> x0, starting transfers between devices: 38.7 us -> none  [swap(): return lax.ppermute(x, axis, [(i, i ^ step) for i in range(n)])]
    all_to_all x0 -> x5, waiting for transfers between devices: none -> 24.7 us  [trade(): return lax.all_to_all(blocks, axis, 0, 0, tiled=True)]
    all_to_all x0 -> x5, starting transfers between devices: none -> 22 us  [trade(): return lax.all_to_all(blocks, axis, 0, 0, tiled=True)]
    ppermute x27 -> x0, waiting for transfers between devices: 19.2 us -> none  [swap(): return lax.ppermute(x, axis, [(i, i ^ step) for i in range(n)])]
    broadcast_in_dim x0 -> x4, local copies, waits for them, and re-layouts: none -> 2.53 us  [the longest x3 2.02 us: spread(): jnp.broadcast_to(x[None], (lax.axis_size(axis),) + x.shape)]
  transfers between devices with their start and end apart: 27 -> 5, of which waited for: 9 -> 5; matrix products, arithmetic and copies ran while one was open for 9% -> 9% of each run, Pallas kernels for 0% -> 0%
where the time goes in v2:
time: 66.9 us; the launch traced here: 66.3 us
  waiting for transfers between devices  24.7 us (37%)
  starting transfers between devices  22 us (33%)
  local copies, waits for them, and re-layouts  8.67 us (13%)
  matrix products  5.68 us (8%)
  other arithmetic  4.91 us (7%)
    all_to_all x5, waiting for transfers between devices, trade(): return lax.all_to_all(blocks, axis, 0, 0, tiled=True)  24.7 us
    all_to_all x5, starting transfers between devices, trade(): return lax.all_to_all(blocks, axis, 0, 0, tiled=True)  22 us
    slice x1, local copies, waits for them, and re-layouts, per_device(): values = kv_pool[1].reshape(positions, cols)  2.3 us
    broadcast_in_dim x3, local copies, waits for them, and re-layouts, spread(): jnp.broadcast_to(x[None], (lax.axis_size(axis),) + x.shape)  2.02 us
    dot_general x1, matrix products, per_device(): feed = jnp.dot(activated, down_weight, preferred_element_type=f32)  1.69 us
    dot_general x1, matrix products, per_device(): jnp.dot(weights.astype(bf16).reshape(heads * rows, positions), values, pr...  1.43 us
  transfers between devices with their start and end apart: 5, of which 5 were waited for; matrix products, arithmetic and copies ran while one was open for 9% of the time, Pallas kernels for 0%

profile of v2, /device:TPU:0, one launch (start us, length us, event | category | flops | bytes accessed | tf_op | source)
XLA Modules:
  0.0 66.3 jit_solution(225656848863793629)
XLA Ops:
  0.0 0.9 %dynamic_slice.6 = s32[4]{0:T(128)S(1)} dynamic-slice(s32[32]{0:T(128)} %param.22, s32[]{:T(128)S(6)} %select_n.86), dynamic_slice_sizes={4} | dynamic-slice | bytes 36 | tf_op jit(solution)/shard_map/dynamic_slice | solution.py:52
  0.9 0.9 %fusion = bf16[8,1,2048]{2,0,1:T(8,128)(2,1)S(1)} fusion(bf16[4,512]{1,0:T(4,128)(2,1)} %param.20, bf16[4,512]{1,0:T(4,128)(2,1)} %param.19, bf16[4,512]{1,0:T(4,128)(2,1)} %param.18, bf16[4,512]{1,0:T(4,128)(2,1)} %param.17, s32[4]{0:T(128)S(1)} %dynamic_slice.6), kind=kOutput, calls=%fused_computation.2 | convolution fusion | flops 213024 | bytes 49168 | tf_op jit(solution)/shard_map/dot_general | solution.py:55
  1.8 0.5 broadcast.302
  2.3 0.7 reduce.2
  2.9 0.6 reshape.232
  3.6 7.3 %all-to-all-start = ((bf16[8,2,1024]{2,1,0:T(2,128)(2,1)}), bf16[8,2,1024]{2,1,0:T(2,128)(2,1)S(1)}, u32[]{:S(2)}, u32[]{:S(2)}) async-start(bf16[8,2,1024]{2,1,0:T(2,128)(2,1)} %reshape.232), calls=%async_computation | async-start | bytes 65536 | tf_op jit(solution)/shard_map/all_to_all | solution.py:13
  10.8 0.7 broadcast_compare_fusion
  11.5 0.9 %convert_reduce_fusion.2 = s32[32]{0:T(128)S(1)} fusion(s32[32]{0:T(128)} %param.22), kind=kLoop, calls=%fused_computation.87 | loop fusion | flops 5088 | bytes 256 | tf_op jit(solution)/shard_map/reduce_sum | solution.py:60
  12.5 0.7 multiply_add_fusion
  13.1 2.3 %fusion.117 = (bf16[1,22,32,512]{3,2,1,0:T(8,128)(2,1)}, bf16[1,22,32,512]{3,2,1,0:T(8,128)(2,1)S(1)}) fusion(bf16[2,22,32,512]{3,2,1,0:T(8,128)(2,1)} %param.24), kind=kLoop, calls=%fused_computation.181 | loop fusion | bytes 2883584 | tf_op jit(solution)/shard_map/slice | solution.py:81
  16.1 1.4 %all-to-all-done = bf16[8,2,1024]{2,1,0:T(2,128)(2,1)S(1)} async-done(((bf16[8,2,1024]{2,1,0:T(2,128)(2,1)}), bf16[8,2,1024]{2,1,0:T(2,128)(2,1)S(1)}, u32[]{:S(2)}, u32[]{:S(2)}) %all-to-all-start) | async-done | bytes 32800 | tf_op jit(solution)/shard_map/all_to_all | solution.py:13
  17.8 0.4 fusion.118
  18.7 0.2 fusion.48
  19.4 1.4 %fusion.4 = bf16[4,512]{1,0:T(4,128)(2,1)S(1)} fusion(bf16[4,4,704]{2,1,0:T(4,128)(2,1)S(1)} %dot_general.32, bf16[704,512,1]{1,0,2:T(8,128)(2,1)} %bitcast.38, f32[4,4]{1,0:T(4,128)S(1)} %copy.39, f32[4,512]{1,0:T(4,128)S(1)} %get-tuple-element.11, f32[4,4]{1,0:T(4,128)S(1)} %copy.37, pred[4,512]{1,0:T(4,128)(4,1)S(1)} %iota_compare_fusion.4), kind=kOutput, calls=%fused_computation.13 | convolution fusion | flops 11573248 | bytes 757888 | tf_op jit(solution)/shard_map/dot_general | solution.py:99
  20.9 0.4 convolution_add_fusion
  21.2 0.7 broadcast_in_dim.97
  21.9 3.3 %all-to-all-start.1 = ((f32[4,4,2048]{2,1,0:T(4,128)}), f32[4,4,2048]{2,1,0:T(4,128)S(1)}, u32[]{:S(2)}, u32[]{:S(2)}) async-start(f32[4,4,2048]{2,1,0:T(4,128)} %broadcast_in_dim.97), calls=%async_computation.1 | async-start | bytes 262144 | tf_op jit(solution)/shard_map/all_to_all | solution.py:13
  25.3 4.5 %all-to-all-done.1 = f32[4,4,2048]{2,1,0:T(4,128)S(1)} async-done(((f32[4,4,2048]{2,1,0:T(4,128)}), f32[4,4,2048]{2,1,0:T(4,128)S(1)}, u32[]{:S(2)}, u32[]{:S(2)}) %all-to-all-start.1) | async-done | bytes 131104 | tf_op jit(solution)/shard_map/all_to_all | solution.py:13
  30.0 0.2 fusion.51
  30.3 0.6 broadcast_in_dim.98
  30.9 4.6 %all-to-all-start.2 = ((bf16[8,4,512]{2,1,0:T(4,128)(2,1)}), bf16[8,4,512]{2,1,0:T(4,128)(2,1)S(1)}, u32[]{:S(2)}, u32[]{:S(2)}) async-start(bf16[8,4,512]{2,1,0:T(4,128)(2,1)} %broadcast_in_dim.98), calls=%async_computation.2 | async-start | bytes 65536 | tf_op jit(solution)/shard_map/all_to_all | solution.py:13
  35.5 0.7 %gather_fusion = s32[32]{0:T(128)S(1)} fusion(s32[32]{0:T(128)S(1)} %multiply_add_fusion, s32[1024]{0:T(1024)S(1)} %pad_clamp_fusion), kind=kCustom, calls=%fused_computation | custom fusion | bytes 384 | tf_op jit(solution)/shard_map/gather | solution.py:126
  36.2 6.0 %all-to-all-done.2 = bf16[8,4,512]{2,1,0:T(4,128)(2,1)S(1)} async-done(((bf16[8,4,512]{2,1,0:T(4,128)(2,1)}), bf16[8,4,512]{2,1,0:T(4,128)(2,1)S(1)}, u32[]{:S(2)}, u32[]{:S(2)}) %all-to-all-start.2) | async-done | bytes 32800 | tf_op jit(solution)/shard_map/all_to_all | solution.py:13
  42.2 0.5 convolution_convert_fusion.2
  42.7 0.7 %broadcast_in_dim.99 = bf16[4,32,1024]{2,1,0:T(8,128)(2,1)} broadcast(bf16[32,1024]{1,0:T(8,128)(2,1)S(1)} %convolution_convert_fusion.2), dimensions={1,2} | broadcast | bytes 327680 | tf_op jit(solution)/shard_map/broadcast_in_dim | solution.py:17
  43.5 3.4 %all-to-all-start.3 = ((bf16[4,32,1024]{2,1,0:T(8,128)(2,1)}), bf16[4,32,1024]{2,1,0:T(8,128)(2,1)S(1)}, u32[]{:S(2)}, u32[]{:S(2)}) async-start(bf16[4,32,1024]{2,1,0:T(8,128)(2,1)} %broadcast_in_dim.99), calls=%async_computation.3 | async-start | bytes 524288 | tf_op jit(solution)/shard_map/all_to_all | solution.py:13
  46.9 6.0 %all-to-all-done.3 = bf16[4,32,1024]{2,1,0:T(8,128)(2,1)S(1)} async-done(((bf16[4,32,1024]{2,1,0:T(8,128)(2,1)}), bf16[4,32,1024]{2,1,0:T(8,128)(2,1)S(1)}, u32[]{:S(2)}, u32[]{:S(2)}) %all-to-all-start.3) | async-done | bytes 262176 | tf_op jit(solution)/shard_map/all_to_all | solution.py:13
  52.9 1.7 %fusion.15 = f32[32,512]{1,0:T(8,128)S(1)} fusion(bf16[1024,512]{1,0:T(8,128)(2,1)} %param.31, f32[32,1024]{1,0:T(8,128)S(1)} %convert_reduce_fusion, f32[1024]{0:T(1024)S(1)} %convert_element_type.111), kind=kOutput, calls=%fused_computation.35 | convolution fusion | flops 35717120 | bytes 1249280 | tf_op jit(solution)/shard_map/dot_general | solution.py:134
  54.8 0.6 reshape.221
  55.5 3.3 %all-to-all-start.4 = ((f32[8,4,512]{2,1,0:T(4,128)}), f32[8,4,512]{2,1,0:T(4,128)S(1)}, u32[]{:S(2)}, u32[]{:S(2)}) async-start(f32[8,4,512]{2,1,0:T(4,128)} %reshape.221), calls=%async_computation.4 | async-start | bytes 131072 | tf_op jit(solution)/shard_map/all_to_all | solution.py:13
  58.8 6.8 %all-to-all-done.4 = f32[8,4,512]{2,1,0:T(4,128)S(1)} async-done(((f32[8,4,512]{2,1,0:T(4,128)}), f32[8,4,512]{2,1,0:T(4,128)S(1)}, u32[]{:S(2)}, u32[]{:S(2)}) %all-to-all-start.4) | async-done | bytes 65568 | tf_op jit(solution)/shard_map/all_to_all | solution.py:13
  65.7 0.6 add_convert_fusion
  (74 shorter events, 2.4 us)
Async XLA Ops:
  0.0 20.8 %copy-start = (bf16[512,2048]{1,0:T(8,128)(2,1)S(1)}, bf16[512,2048]{1,0:T(8,128)(2,1)}, u32[]{:S(2)}) copy-start(bf16[512,2048]{1,0:T(8,128)(2,1)} %param.25) | copy-start | bytes 6291460
  0.0 15.5 %copy-start.8 = (s32[32]{0:T(128)S(1)}, s32[32]{0:T(128)}, u32[]{:S(2)}) copy-start(s32[32]{0:T(128)} %param.21) | copy-start | bytes 388
  0.0 15.7 %copy-start.2 = (s32[32,16]{0,1:T(8,128)S(1)}, s32[32,16]{0,1:T(8,128)}, u32[]{:S(2)}) copy-start(s32[32,16]{0,1:T(8,128)} %param.23) | copy-start | bytes 6148
  0.0 16.1 %copy-start.4 = (bf16[512]{0:T(512)(128)(2,1)S(1)}, bf16[512]{0:T(512)(128)(2,1)}, u32[]{:S(2)}) copy-start(bf16[512]{0:T(512)(128)(2,1)} %param.26) | copy-start | bytes 3076
  3.6 14.0 %all-to-all-start = ((bf16[8,2,1024]{2,1,0:T(2,128)(2,1)}), bf16[8,2,1024]{2,1,0:T(2,128)(2,1)S(1)}, u32[]{:S(2)}, u32[]{:S(2)}) async-start(bf16[8,2,1024]{2,1,0:T(2,128)(2,1)} %reshape.232), calls=%async_computation | async-start | bytes 65536 | tf_op jit(solution)/shard_map/all_to_all | solution.py:13
  17.8 7.4 %copy-start.9 = (s32[32]{0:T(128)S(1)}, s32[32]{0:T(128)}, u32[]{:S(2)}) copy-start(s32[32]{0:T(128)} %param.33) | copy-start | bytes 388
  17.8 7.4 %copy-start.5 = (bf16[512]{0:T(512)(128)(2,1)S(1)}, bf16[512]{0:T(512)(128)(2,1)}, u32[]{:S(2)}) copy-start(bf16[512]{0:T(512)(128)(2,1)} %param.27) | copy-start | bytes 3076
  17.8 7.5 %copy-start.6 = (bf16[512]{0:T(512)(128)(2,1)S(1)}, bf16[512]{0:T(512)(128)(2,1)}, u32[]{:S(2)}) copy-start(bf16[512]{0:T(512)(128)(2,1)} %param.28) | copy-start | bytes 3076
  19.4 22.8 %copy-start.1 = (bf16[1024,512]{1,0:T(8,128)(2,1)S(1)}, bf16[1024,512]{1,0:T(8,128)(2,1)}, u32[]{:S(2)}) copy-start(bf16[1024,512]{1,0:T(8,128)(2,1)} %param.29) | copy-start | bytes 3145732
  21.2 25.7 %copy-start.3 = (bf16[1024]{0:T(1024)(128)(2,1)S(1)}, bf16[1024]{0:T(1024)(128)(2,1)}, u32[]{:S(2)}) copy-start(bf16[1024]{0:T(1024)(128)(2,1)} %param.30) | copy-start | bytes 6148
  21.9 7.9 %all-to-all-start.1 = ((f32[4,4,2048]{2,1,0:T(4,128)}), f32[4,4,2048]{2,1,0:T(4,128)S(1)}, u32[]{:S(2)}, u32[]{:S(2)}) async-start(f32[4,4,2048]{2,1,0:T(4,128)} %broadcast_in_dim.97), calls=%async_computation.1 | async-start | bytes 262144 | tf_op jit(solution)/shard_map/all_to_all | solution.py:13
  30.9 11.3 %all-to-all-start.2 = ((bf16[8,4,512]{2,1,0:T(4,128)(2,1)}), bf16[8,4,512]{2,1,0:T(4,128)(2,1)S(1)}, u32[]{:S(2)}, u32[]{:S(2)}) async-start(bf16[8,4,512]{2,1,0:T(4,128)(2,1)} %broadcast_in_dim.98), calls=%async_computation.2 | async-start | bytes 65536 | tf_op jit(solution)/shard_map/all_to_all | solution.py:13
  43.5 9.4 %all-to-all-start.3 = ((bf16[4,32,1024]{2,1,0:T(8,128)(2,1)}), bf16[4,32,1024]{2,1,0:T(8,128)(2,1)S(1)}, u32[]{:S(2)}, u32[]{:S(2)}) async-start(bf16[4,32,1024]{2,1,0:T(8,128)(2,1)} %broadcast_in_dim.99), calls=%async_computation.3 | async-start | bytes 524288 | tf_op jit(solution)/shard_map/all_to_all | solution.py:13
  52.9 5.9 %copy-start.7 = (bf16[512]{0:T(512)(128)(2,1)S(1)}, bf16[512]{0:T(512)(128)(2,1)}, u32[]{:S(2)}) copy-start(bf16[512]{0:T(512)(128)(2,1)} %param.32) | copy-start | bytes 3076
  55.5 10.2 %all-to-all-start.4 = ((f32[8,4,512]{2,1,0:T(4,128)}), f32[8,4,512]{2,1,0:T(4,128)S(1)}, u32[]{:S(2)}, u32[]{:S(2)}) async-start(f32[8,4,512]{2,1,0:T(4,128)} %reshape.221), calls=%async_computation.4 | async-start | bytes 131072 | tf_op jit(solution)/shard_map/all_to_all | solution.py:13

commit v3 on v2

--- a/solution.py
+++ b/solution.py
@@ -7,14 +7,56 @@
 
 HEAD_DIM = 128
 NORM_EPS = 1e-05
-
-
-def trade(blocks, axis):
-    return lax.all_to_all(blocks, axis, 0, 0, tiled=True)
-
-
-def spread(x, axis):
-    return trade(jnp.broadcast_to(x[None], (lax.axis_size(axis),) + x.shape), axis)
+PAIRWISE = 16
+
+
+def swap(x, axis, step):
+    n = lax.axis_size(axis)
+    return lax.ppermute(x, axis, [(i, i ^ step) for i in range(n)])
+
+
+def origins(axis):
+    n, me = lax.axis_size(axis), lax.axis_index(axis)
+    if n > PAIRWISE:
+        return jnp.arange(n, dtype=jnp.int32)
+    offsets = [0]
+    step = n // 2
+    while step:
+        offsets = offsets + [o ^ step for o in offsets]
+        step //= 2
+    return jnp.array(offsets, dtype=jnp.int32) ^ me
+
+
+def gather_rows(x, axis):
+    n = lax.axis_size(axis)
+    if n > PAIRWISE:
+        return lax.all_gather(x, axis, axis=0, tiled=True)
+    step = n // 2
+    while step:
+        x = jnp.concatenate([x, swap(x, axis, step)], axis=0)
+        step //= 2
+    return x
+
+
+def fold_rows(x, axis):
+    n = lax.axis_size(axis)
+    if n > PAIRWISE:
+        return lax.psum_scatter(x, axis, scatter_dimension=0, tiled=True)
+    step = 1
+    while step < n:
+        half = x.shape[0] // 2
+        x = x[:half] + swap(x[half:], axis, step)
+        step *= 2
+    return x
+
+
+def sum_pairs(x, axis):
+    n = lax.axis_size(axis)
+    step = 1
+    while step < n:
+        x = (x.astype(jnp.float32) + swap(x, axis, step).astype(jnp.float32)).astype(x.dtype)
+        step *= 2
+    return x
 
 
 def per_device(
@@ -48,12 +90,9 @@
     positions = pool_pages * page_len
     scale = 1.0 / math.sqrt(HEAD_DIM)
 
-    steps = jnp.arange(n_req, dtype=i32)
-    my_owner = lax.dynamic_slice_in_dim(owner, me * rows, rows)
-    send_hot = (my_owner[None, :] == steps[:, None]).astype(bf16)
+    origin = origins("req")
     packed = jnp.concatenate([query, key_new, value_new, resid], axis=1)
-    outgoing = jnp.dot(send_hot, packed, preferred_element_type=f32).astype(bf16)
-    arrived = trade(outgoing[:, None], "req")[:, 0]
+    arrived = gather_rows(packed, "req")
 
     same = owner[:, None] == owner[None, :]
     ids = jnp.arange(owner.shape[0], dtype=i32)
@@ -63,8 +102,9 @@
     mine_i = mine.astype(i32)
     own_len = jnp.sum(mine_i * lengths[None, :], axis=1)
     own_table = jnp.sum(mine_i[:, :, None] * page_table[None], axis=1)
-    own_src = jnp.sum(mine_i * (ids // rows)[None, :], axis=1)
-    take_hot = (own_src[:, None] == steps[None, :]).astype(bf16)
+    origin_ids = (origin[:, None] * rows + slots[None, :]).reshape(-1)
+    own_id = jnp.sum(mine_i * ids[None, :], axis=1)
+    take_hot = (own_id[:, None] == origin_ids[None, :]).astype(bf16)
     own = jnp.dot(take_hot, arrived, preferred_element_type=f32).astype(bf16)
     query_own, key_own, value_own, resid_own = (own[:, i * cols : (i + 1) * cols] for i in range(4))
 
@@ -110,7 +150,7 @@
     partial = (
         partial.reshape(rows, n_tp, cols) + jnp.where(place, extra[:, None, :], 0.0)
     ).reshape(rows, width)
-    stream = jnp.sum(spread(partial, "tp"), axis=0).astype(bf16)
+    stream = sum_pairs(partial, "tp").astype(bf16)
     stream_f = stream.astype(f32)
     mean = jnp.mean(stream_f, axis=1, keepdims=True)
     var = jnp.mean((stream_f - mean) ** 2, axis=1, keepdims=True)
@@ -121,20 +161,21 @@
         + norm_bias.astype(f32)[None, :]
     ).astype(bf16)
 
-    normed_all = spread(normed, "req").reshape(-1, cols)
+    normed_all = gather_rows(normed, "req")
     slot_of = owner * rows + rank
-    place_hot = (slot_of[order][:, None] == ids[None, :]).astype(bf16)
-    mine_hot = (slot_of[order][:, None] == (me * rows + slots)[None, :]).astype(bf16)
+    wanted = slot_of[order[origin_ids]]
+    place_hot = (wanted[:, None] == origin_ids[None, :]).astype(bf16)
+    mine_hot = (wanted[:, None] == (me * rows + slots)[None, :]).astype(bf16)
     normed_out = jnp.dot(place_hot, normed_all, preferred_element_type=f32).astype(bf16)
     hidden = lax.dot_general(
         normed_out, up_weight_t, (((1,), (1,)), ((), ())), preferred_element_type=f32
     ).astype(bf16)
-    summed = jnp.sum(spread(hidden, "tp").astype(f32), axis=0)
+    summed = sum_pairs(hidden, "tp").astype(f32)
     activated = jax.nn.gelu(summed + up_bias.astype(f32)[None, :], approximate=False).astype(bf16)
     feed = jnp.dot(activated, down_weight, preferred_element_type=f32)
     feed = feed + jnp.dot(mine_hot, stream_own, preferred_element_type=f32)
-    pieces = trade(feed.reshape(n_req, rows, cols), "req")
-    return (jnp.sum(pieces, axis=0) + down_bias.astype(f32)[None, :]).astype(bf16)
+    mixed = fold_rows(feed, "req")
+    return (mixed + down_bias.astype(f32)[None, :]).astype(bf16)
 
 
 def solution(mesh):

time: 66.9 us -> 63.3 us (0.946)
  starting transfers between devices: 22 us -> 17 us
  waiting for transfers between devices: 24.7 us -> 28.7 us
  local copies, waits for them, and re-layouts: 8.67 us -> 7.77 us
  matrix products: 5.68 us -> 4.81 us
    ppermute x0 -> x13, waiting for transfers between devices: none -> 28.7 us  [swap(): return lax.ppermute(x, axis, [(i, i ^ step) for i in range(n)])]
    all_to_all x5 -> x0, waiting for transfers between devices: 24.7 us -> none  [trade(): return lax.all_to_all(blocks, axis, 0, 0, tiled=True)]
    all_to_all x5 -> x0, starting transfers between devices: 22 us -> none  [trade(): return lax.all_to_all(blocks, axis, 0, 0, tiled=True)]
    ppermute x0 -> x13, starting transfers between devices: none -> 17 us  [swap(): return lax.ppermute(x, axis, [(i, i ^ step) for i in range(n)])]
    broadcast_in_dim x4 -> x0, local copies, waits for them, and re-layouts: 2.53 us -> none  [the longest x3 2.02 us: spread(): jnp.broadcast_to(x[None], (lax.axis_size(axis),) + x.shape)]
    unnamed x26 -> x29, local copies, waits for them, and re-layouts: 0.8 us -> 2.4 us
    dynamic_slice x1 -> x0, local copies, waits for them, and re-layouts: 0.88 us -> none  [per_device(): my_owner = lax.dynamic_slice_in_dim(owner, me * rows, rows)]
    dot_general x1 -> x0, matrix products: 0.86 us -> none  [per_device(): jnp.dot(send_hot, packed, preferred_element_type=f32).astype(bf16)]
  transfers between devices with their start and end apart: 5 -> 13, of which waited for: 5 -> 12; matrix products, arithmetic and copies ran while one was open for 9% -> 11% of each run, Pallas kernels for 0% -> 0%
where the time goes in v3:
time: 63.3 us; the launch traced here: 62.9 us
  waiting for transfers between devices  28.7 us (45%)
  starting transfers between devices  17 us (27%)
  local copies, waits for them, and re-layouts  7.77 us (12%)
  matrix products  4.81 us (8%)
  other arithmetic  4.36 us (7%)
    ppermute x13, waiting for transfers between devices, swap(): return lax.ppermute(x, axis, [(i, i ^ step) for i in range(n)])  28.7 us
    ppermute x13, starting transfers between devices, swap(): return lax.ppermute(x, axis, [(i, i ^ step) for i in range(n)])  17 us
    unnamed x29, local copies, waits for them, and re-layouts  2.4 us
    slice x1, local copies, waits for them, and re-layouts, per_device(): values = kv_pool[1].reshape(positions, cols)  2.3 us
    dot_general x1, matrix products, per_device(): feed = jnp.dot(activated, down_weight, preferred_element_type=f32)  1.69 us
    dot_general x1, matrix products, per_device(): jnp.dot(weights.astype(bf16).reshape(heads * rows, positions), values, pr...  1.43 us
    gather x2, local copies, waits for them, and re-layouts, per_device(): wanted = slot_of[order[origin_ids]]  1.39 us
  transfers between devices with their start and end apart: 13, of which 12 were waited for; matrix products, arithmetic and copies ran while one was open for 11% of the time, Pallas kernels for 0%

profile of v3, /device:TPU:0, one launch (start us, length us, event | category | flops | bytes accessed | tf_op | source)
XLA Modules:
  0.0 62.9 jit_solution(15108813765209268054)
XLA Ops:
  0.0 0.8 %constant_dynamic-update-slice_fusion.3 = bf16[4,2048]{1,0:T(4,128)(2,1)S(1)} fusion(bf16[4,512]{1,0:T(4,128)(2,1)} %param.18), kind=kLoop, calls=%fused_computation.112 | loop fusion | bytes 8192
  0.9 0.7 %constant_dynamic-update-slice_fusion.2 = bf16[4,2048]{1,0:T(4,128)(2,1)S(1)} fusion(bf16[4,2048]{1,0:T(4,128)(2,1)S(1)} %constant_dynamic-update-slice_fusion.3, bf16[4,512]{1,0:T(4,128)(2,1)} %param.19), kind=kLoop, calls=%fused_computation.111 | loop fusion | bytes 8192
  1.5 0.7 %constant_dynamic-update-slice_fusion.1 = bf16[4,2048]{1,0:T(4,128)(2,1)S(1)} fusion(bf16[4,2048]{1,0:T(4,128)(2,1)S(1)} %constant_dynamic-update-slice_fusion.2, bf16[4,512]{1,0:T(4,128)(2,1)} %param.20), kind=kLoop, calls=%fused_computation.110 | loop fusion | bytes 8192
  2.2 0.7 %constant_dynamic-update-slice_fusion = bf16[4,2048]{1,0:T(4,128)(2,1)S(1)} fusion(bf16[4,2048]{1,0:T(4,128)(2,1)S(1)} %constant_dynamic-update-slice_fusion.1, bf16[4,512]{1,0:T(4,128)(2,1)} %param.21), kind=kLoop, calls=%fused_computation.109 | loop fusion | bytes 8192 | tf_op jit(solution)/shard_map/concatenate | solution.py:94
  2.9 4.0 %collective-permute-start = (bf16[4,2048]{1,0:T(4,128)(2,1)S(1)}, bf16[4,2048]{1,0:T(4,128)(2,1)S(1)}, u32[]{:S(2)}, u32[]{:S(2)}) collective-permute-start(bf16[4,2048]{1,0:T(4,128)(2,1)S(1)} %constant_dynamic-update-slice_fusion), channel_id=1, source_target_pairs={{0,16},{4,20},{8,24},{12,28},{16,0},{20,4},{24,8},{28,12},{1,17},{... | collective-permute-start | bytes 49160 | tf_op jit(solution)/shard_map/ppermute | solution.py:15
  7.0 0.9 %convert_reduce_fusion.1 = s32[32]{0:T(128)S(1)} fusion(s32[32]{0:T(128)} %param.23), kind=kLoop, calls=%fused_computation.100 | loop fusion | flops 5088 | bytes 256 | tf_op jit(solution)/shard_map/reduce_sum | solution.py:99
  7.9 0.7 %broadcast_compare_fusion = pred[32]{0:T(512)(128)(4,1)S(1)} fusion(s32[32]{0:T(128)} %param.23, s32[]{:T(128)S(6)} %axis_index.27), kind=kLoop, calls=%fused_computation.170 | loop fusion | flops 32 | bytes 164 | tf_op jit(solution)/shard_map/eq | solution.py:101
  9.3 2.3 %fusion.142 = (bf16[1,22,32,512]{3,2,1,0:T(8,128)(2,1)}, bf16[1,22,32,512]{3,2,1,0:T(8,128)(2,1)S(1)}) fusion(bf16[2,22,32,512]{3,2,1,0:T(8,128)(2,1)} %param.25), kind=kLoop, calls=%fused_computation.205 | loop fusion | bytes 2883584 | tf_op jit(solution)/shard_map/slice | solution.py:121
  12.1 1.6 %collective-permute-start.1 = (bf16[8,2048]{1,0:T(8,128)(2,1)S(1)}, bf16[8,2048]{1,0:T(8,128)(2,1)S(1)}, u32[]{:S(2)}, u32[]{:S(2)}) collective-permute-start(bf16[8,2048]{1,0:T(8,128)(2,1)S(1)} %pad_maximum_fusion.1), channel_id=1, source_target_pairs={{0,8},{4,12},{8,0},{12,4},{16,24},{20,28},{24,16},{28,20},{1,9},{5... | collective-permute-start | bytes 98312 | tf_op jit(solution)/shard_map/ppermute | solution.py:15
  13.8 2.3 %collective-permute-done.1 = bf16[8,2048]{1,0:T(8,128)(2,1)S(1)} collective-permute-done((bf16[8,2048]{1,0:T(8,128)(2,1)S(1)}, bf16[8,2048]{1,0:T(8,128)(2,1)S(1)}, u32[]{:S(2)}, u32[]{:S(2)}) %collective-permute-start.1) | collective-permute-done | bytes 32800 | tf_op jit(solution)/shard_map/ppermute | solution.py:15
  16.1 1.6 %collective-permute-start.2 = (bf16[16,2048]{1,0:T(8,128)(2,1)S(1)}, bf16[16,2048]{1,0:T(8,128)(2,1)S(1)}, u32[]{:S(2)}, u32[]{:S(2)}) collective-permute-start(bf16[16,2048]{1,0:T(8,128)(2,1)S(1)} %pad_maximum_fusion), channel_id=1, source_target_pairs={{0,4},{4,0},{8,12},{12,8},{16,20},{20,16},{24,28},{28,24},{1,5},{5... | collective-permute-start | bytes 196616 | tf_op jit(solution)/shard_map/ppermute | solution.py:15
  17.9 2.5 %collective-permute-done.2 = bf16[16,2048]{1,0:T(8,128)(2,1)S(1)} collective-permute-done((bf16[16,2048]{1,0:T(8,128)(2,1)S(1)}, bf16[16,2048]{1,0:T(8,128)(2,1)S(1)}, u32[]{:S(2)}, u32[]{:S(2)}) %collective-permute-start.2) | collective-permute-done | bytes 65568 | tf_op jit(solution)/shard_map/ppermute | solution.py:15
  22.3 1.4 %fusion.3 = bf16[4,512]{1,0:T(4,128)(2,1)S(1)} fusion(bf16[4,4,704]{2,1,0:T(4,128)(2,1)S(1)} %dot_general.28, bf16[704,512,1]{1,0,2:T(8,128)(2,1)} %bitcast.38, f32[4,4]{1,0:T(4,128)S(1)} %copy.31, f32[4,512]{1,0:T(4,128)S(1)} %get-tuple-element.13, f32[4,4]{1,0:T(4,128)S(1)} %copy.29, pred[4,512]{1,0:T(4,128)(4,1)S(1)} %iota_compare_fusion.1), kind=kOutput, calls=%fused_computation.12 | convolution fusion | flops 11573248 | bytes 757888 | tf_op jit(solution)/shard_map/dot_general | solution.py:139
  24.3 1.1 %collective-permute-done.3 = f32[4,2048]{1,0:T(4,128)S(1)} collective-permute-done((f32[4,2048]{1,0:T(4,128)S(1)}, f32[4,2048]{1,0:T(4,128)S(1)}, u32[]{:S(2)}, u32[]{:S(2)}) %collective-permute-start.3) | collective-permute-done | bytes 32800 | tf_op jit(solution)/shard_map/ppermute | solution.py:15
  25.4 1.6 %collective-permute-start.4 = (f32[4,2048]{1,0:T(4,128)S(1)}, f32[4,2048]{1,0:T(4,128)S(1)}, u32[]{:S(2)}, u32[]{:S(2)}) collective-permute-start(f32[4,2048]{1,0:T(4,128)S(1)} %add.196), channel_id=1, source_target_pairs={{0,2},{1,3},{2,0},{3,1},{4,6},{5,7},{6,4},{7,5},{8,10},{9,11},{10,... | collective-permute-start | bytes 98312 | tf_op jit(solution)/shard_map/ppermute | solution.py:15
  27.0 2.4 %collective-permute-done.4 = f32[4,2048]{1,0:T(4,128)S(1)} collective-permute-done((f32[4,2048]{1,0:T(4,128)S(1)}, f32[4,2048]{1,0:T(4,128)S(1)}, u32[]{:S(2)}, u32[]{:S(2)}) %collective-permute-start.4) | collective-permute-done | bytes 32800 | tf_op jit(solution)/shard_map/ppermute | solution.py:15
  29.9 0.7 %gather_fusion = s32[32]{0:T(128)S(1)} fusion(s32[32]{0:T(128)S(1)} %copy-done.1, s32[1024]{0:T(1024)S(1)} %pad_clamp_fusion.1), kind=kCustom, calls=%fused_computation | custom fusion | bytes 384 | tf_op jit(solution)/shard_map/gather | solution.py:166
  30.6 3.8 %collective-permute-done.5 = bf16[4,512]{1,0:T(4,128)(2,1)S(1)} collective-permute-done((bf16[4,512]{1,0:T(4,128)(2,1)S(1)}, bf16[4,512]{1,0:T(4,128)(2,1)S(1)}, u32[]{:S(2)}, u32[]{:S(2)}) %collective-permute-start.5) | collective-permute-done | bytes 4128 | tf_op jit(solution)/shard_map/ppermute | solution.py:15
  34.3 1.6 %collective-permute-start.6 = (bf16[8,512]{1,0:T(8,128)(2,1)S(1)}, bf16[8,512]{1,0:T(8,128)(2,1)S(1)}, u32[]{:S(2)}, u32[]{:S(2)}) collective-permute-start(bf16[8,512]{1,0:T(8,128)(2,1)S(1)} %pad_maximum_fusion.3), channel_id=1, source_target_pairs={{0,8},{4,12},{8,0},{12,4},{16,24},{20,28},{24,16},{28,20},{1,9},{5... | collective-permute-start | bytes 24584 | tf_op jit(solution)/shard_map/ppermute | solution.py:15
  36.0 2.1 %collective-permute-done.6 = bf16[8,512]{1,0:T(8,128)(2,1)S(1)} collective-permute-done((bf16[8,512]{1,0:T(8,128)(2,1)S(1)}, bf16[8,512]{1,0:T(8,128)(2,1)S(1)}, u32[]{:S(2)}, u32[]{:S(2)}) %collective-permute-start.6) | collective-permute-done | bytes 8224 | tf_op jit(solution)/shard_map/ppermute | solution.py:15
  38.1 1.6 %collective-permute-start.7 = (bf16[16,512]{1,0:T(8,128)(2,1)S(1)}, bf16[16,512]{1,0:T(8,128)(2,1)S(1)}, u32[]{:S(2)}, u32[]{:S(2)}) collective-permute-start(bf16[16,512]{1,0:T(8,128)(2,1)S(1)} %pad_maximum_fusion.2), channel_id=1, source_target_pairs={{0,4},{4,0},{8,12},{12,8},{16,20},{20,16},{24,28},{28,24},{1,5},{5... | collective-permute-start | bytes 49160 | tf_op jit(solution)/shard_map/ppermute | solution.py:15
  39.7 0.7 %gather_fusion.1 = s32[32]{0:T(128)S(1)} fusion(s32[32]{0:T(128)S(1)} %multiply_add_fusion, s32[1024]{0:T(1024)S(1)} %pad_clamp_fusion), kind=kCustom, calls=%fused_computation.1 | custom fusion | bytes 384 | tf_op jit(solution)/shard_map/gather | solution.py:166
  40.4 1.5 %collective-permute-done.7 = bf16[16,512]{1,0:T(8,128)(2,1)S(1)} collective-permute-done((bf16[16,512]{1,0:T(8,128)(2,1)S(1)}, bf16[16,512]{1,0:T(8,128)(2,1)S(1)}, u32[]{:S(2)}, u32[]{:S(2)}) %collective-permute-start.7) | collective-permute-done | bytes 16416 | tf_op jit(solution)/shard_map/ppermute | solution.py:15
  42.5 1.2 %collective-permute-done.8 = bf16[32,1024]{1,0:T(8,128)(2,1)S(1)} collective-permute-done((bf16[32,1024]{1,0:T(8,128)(2,1)S(1)}, bf16[32,1024]{1,0:T(8,128)(2,1)S(1)}, u32[]{:S(2)}, u32[]{:S(2)}) %collective-permute-start.8) | collective-permute-done | bytes 65568 | tf_op jit(solution)/shard_map/ppermute | solution.py:15
  43.7 1.6 %collective-permute-start.9 = (bf16[32,1024]{1,0:T(8,128)(2,1)S(1)}, bf16[32,1024]{1,0:T(8,128)(2,1)S(1)}, u32[]{:S(2)}, u32[]{:S(2)}) collective-permute-start(bf16[32,1024]{1,0:T(8,128)(2,1)S(1)} %add_convert_fusion.1), channel_id=1, source_target_pairs={{0,2},{1,3},{2,0},{3,1},{4,6},{5,7},{6,4},{7,5},{8,10},{9,11},{10,... | collective-permute-start | bytes 196616 | tf_op jit(solution)/shard_map/ppermute | solution.py:15
  45.3 2.8 %collective-permute-done.9 = bf16[32,1024]{1,0:T(8,128)(2,1)S(1)} collective-permute-done((bf16[32,1024]{1,0:T(8,128)(2,1)S(1)}, bf16[32,1024]{1,0:T(8,128)(2,1)S(1)}, u32[]{:S(2)}, u32[]{:S(2)}) %collective-permute-start.9) | collective-permute-done | bytes 65568 | tf_op jit(solution)/shard_map/ppermute | solution.py:15
  48.0 1.7 %fusion.24 = f32[32,512]{1,0:T(8,128)S(1)} fusion(bf16[1024,512]{1,0:T(8,128)(2,1)} %param.32, bf16[32,1024]{1,0:T(8,128)(2,1)S(1)} %collective-permute-done.9, bf16[32,1024]{1,0:T(8,128)(2,1)S(1)} %add_convert_fusion.1, f32[1024]{0:T(1024)S(1)} %convert_element_type.130), kind=kOutput, calls=%fused_computation.45 | convolution fusion | flops 35880960 | bytes 1249280 | tf_op jit(solution)/shard_map/dot_general | solution.py:175
  49.9 1.6 %collective-permute-start.10 = (f32[16,512]{1,0:T(8,128)S(1)}, f32[16,512]{1,0:T(8,128)S(1)}, u32[]{:S(2)}, u32[]{:S(2)}) collective-permute-start(f32[16,512]{1,0:T(8,128)S(1)} %slice.57), channel_id=1, source_target_pairs={{0,4},{4,0},{8,12},{12,8},{16,20},{20,16},{24,28},{28,24},{1,5},{5... | collective-permute-start | bytes 98312 | tf_op jit(solution)/shard_map/ppermute | solution.py:15
  51.5 2.4 %collective-permute-done.10 = f32[16,512]{1,0:T(8,128)S(1)} collective-permute-done((f32[16,512]{1,0:T(8,128)S(1)}, f32[16,512]{1,0:T(8,128)S(1)}, u32[]{:S(2)}, u32[]{:S(2)}) %collective-permute-start.10) | collective-permute-done | bytes 32800 | tf_op jit(solution)/shard_map/ppermute | solution.py:15
  53.9 1.6 %collective-permute-start.11 = (f32[8,512]{1,0:T(8,128)S(1)}, f32[8,512]{1,0:T(8,128)S(1)}, u32[]{:S(2)}, u32[]{:S(2)}) collective-permute-start(f32[8,512]{1,0:T(8,128)S(1)} %slice.59), channel_id=1, source_target_pairs={{0,8},{4,12},{8,0},{12,4},{16,24},{20,28},{24,16},{28,20},{1,9},{5... | collective-permute-start | bytes 49160 | tf_op jit(solution)/shard_map/ppermute | solution.py:15
  55.6 2.2 %collective-permute-done.11 = f32[8,512]{1,0:T(8,128)S(1)} collective-permute-done((f32[8,512]{1,0:T(8,128)S(1)}, f32[8,512]{1,0:T(8,128)S(1)}, u32[]{:S(2)}, u32[]{:S(2)}) %collective-permute-start.11) | collective-permute-done | bytes 16416 | tf_op jit(solution)/shard_map/ppermute | solution.py:15
  57.8 4.5 %collective-permute-done.12 = f32[4,512]{1,0:T(4,128)S(1)} collective-permute-done((f32[4,512]{1,0:T(4,128)S(1)}, f32[4,512]{1,0:T(4,128)S(1)}, u32[]{:S(2)}, u32[]{:S(2)}) %collective-permute-start.12) | collective-permute-done | bytes 8224 | tf_op jit(solution)/shard_map/ppermute | solution.py:15
  (99 shorter events, 5.8 us)
Async XLA Ops:
  0.0 23.8 %copy-start = (bf16[512,2048]{1,0:T(8,128)(2,1)S(1)}, bf16[512,2048]{1,0:T(8,128)(2,1)}, u32[]{:S(2)}) copy-start(bf16[512,2048]{1,0:T(8,128)(2,1)} %param.26) | copy-start | bytes 6291460
  0.0 11.7 %copy-start.3 = (s32[32,16]{0,1:T(8,128)S(1)}, s32[32,16]{0,1:T(8,128)}, u32[]{:S(2)}) copy-start(s32[32,16]{0,1:T(8,128)} %param.24) | copy-start | bytes 6148
  0.0 11.9 %copy-start.9 = (s32[32]{0:T(128)S(1)}, s32[32]{0:T(128)}, u32[]{:S(2)}) copy-start(s32[32]{0:T(128)} %param.22) | copy-start | bytes 388
  0.0 17.9 %copy-start.5 = (bf16[512]{0:T(512)(128)(2,1)S(1)}, bf16[512]{0:T(512)(128)(2,1)}, u32[]{:S(2)}) copy-start(bf16[512]{0:T(512)(128)(2,1)} %param.27) | copy-start | bytes 3076
  2.9 9.1 %collective-permute-start = (bf16[4,2048]{1,0:T(4,128)(2,1)S(1)}, bf16[4,2048]{1,0:T(4,128)(2,1)S(1)}, u32[]{:S(2)}, u32[]{:S(2)}) collective-permute-start(bf16[4,2048]{1,0:T(4,128)(2,1)S(1)} %constant_dynamic-update-slice_fusion), channel_id=1, source_target_pairs={{0,16},{4,20},{8,24},{12,28},{16,0},{20,4},{24,8},{28,12},{1,17},{... | collective-permute-start | bytes 49160 | tf_op jit(solution)/shard_map/ppermute | solution.py:15
  12.1 4.0 %collective-permute-start.1 = (bf16[8,2048]{1,0:T(8,128)(2,1)S(1)}, bf16[8,2048]{1,0:T(8,128)(2,1)S(1)}, u32[]{:S(2)}, u32[]{:S(2)}) collective-permute-start(bf16[8,2048]{1,0:T(8,128)(2,1)S(1)} %pad_maximum_fusion.1), channel_id=1, source_target_pairs={{0,8},{4,12},{8,0},{12,4},{16,24},{20,28},{24,16},{28,20},{1,9},{5... | collective-permute-start | bytes 98312 | tf_op jit(solution)/shard_map/ppermute | solution.py:15
  16.1 4.3 %collective-permute-start.2 = (bf16[16,2048]{1,0:T(8,128)(2,1)S(1)}, bf16[16,2048]{1,0:T(8,128)(2,1)S(1)}, u32[]{:S(2)}, u32[]{:S(2)}) collective-permute-start(bf16[16,2048]{1,0:T(8,128)(2,1)S(1)} %pad_maximum_fusion), channel_id=1, source_target_pairs={{0,4},{4,0},{8,12},{12,8},{16,20},{20,16},{24,28},{28,24},{1,5},{5... | collective-permute-start | bytes 196616 | tf_op jit(solution)/shard_map/ppermute | solution.py:15
  20.7 3.5 %copy-start.10 = (s32[32]{0:T(128)S(1)}, s32[32]{0:T(128)}, u32[]{:S(2)}) copy-start(s32[32]{0:T(128)} %param.23) | copy-start | bytes 388
  20.7 6.2 %copy-start.6 = (bf16[512]{0:T(512)(128)(2,1)S(1)}, bf16[512]{0:T(512)(128)(2,1)}, u32[]{:S(2)}) copy-start(bf16[512]{0:T(512)(128)(2,1)} %param.28) | copy-start | bytes 3076
  20.7 6.2 %copy-start.7 = (bf16[512]{0:T(512)(128)(2,1)S(1)}, bf16[512]{0:T(512)(128)(2,1)}, u32[]{:S(2)}) copy-start(bf16[512]{0:T(512)(128)(2,1)} %param.29) | copy-start | bytes 3076
  20.8 9.1 %copy-start.1 = (s32[32]{0:T(128)S(1)}, s32[32]{0:T(128)}, u32[]{:S(2)}) copy-start(s32[32]{0:T(128)} %param.34) | copy-start | bytes 388
  22.3 19.6 %copy-start.2 = (bf16[1024,512]{1,0:T(8,128)(2,1)S(1)}, bf16[1024,512]{1,0:T(8,128)(2,1)}, u32[]{:S(2)}) copy-start(bf16[1024,512]{1,0:T(8,128)(2,1)} %param.30) | copy-start | bytes 3145732
  23.8 18.7 %copy-start.4 = (bf16[1024]{0:T(1024)(128)(2,1)S(1)}, bf16[1024]{0:T(1024)(128)(2,1)}, u32[]{:S(2)}) copy-start(bf16[1024]{0:T(1024)(128)(2,1)} %param.31) | copy-start | bytes 6148
  24.2 1.2 %collective-permute-start.3 = (f32[4,2048]{1,0:T(4,128)S(1)}, f32[4,2048]{1,0:T(4,128)S(1)}, u32[]{:S(2)}, u32[]{:S(2)}) collective-permute-start(f32[4,2048]{1,0:T(4,128)S(1)} %convolution_add_fusion), channel_id=1, source_target_pairs={{0,1},{1,0},{2,3},{3,2},{4,5},{5,4},{6,7},{7,6},{8,9},{9,8},{10,11... | collective-permute-start | bytes 98312 | tf_op jit(solution)/shard_map/ppermute | solution.py:15
  25.4 4.0 %collective-permute-start.4 = (f32[4,2048]{1,0:T(4,128)S(1)}, f32[4,2048]{1,0:T(4,128)S(1)}, u32[]{:S(2)}, u32[]{:S(2)}) collective-permute-start(f32[4,2048]{1,0:T(4,128)S(1)} %add.196), channel_id=1, source_target_pairs={{0,2},{1,3},{2,0},{3,1},{4,6},{5,7},{6,4},{7,5},{8,10},{9,11},{10,... | collective-permute-start | bytes 98312 | tf_op jit(solution)/shard_map/ppermute | solution.py:15
  29.8 4.5 %collective-permute-start.5 = (bf16[4,512]{1,0:T(4,128)(2,1)S(1)}, bf16[4,512]{1,0:T(4,128)(2,1)S(1)}, u32[]{:S(2)}, u32[]{:S(2)}) collective-permute-start(bf16[4,512]{1,0:T(4,128)(2,1)S(1)} %add_convert_fusion.4), channel_id=1, source_target_pairs={{0,16},{4,20},{8,24},{12,28},{16,0},{20,4},{24,8},{28,12},{1,17},{... | collective-permute-start | bytes 12296 | tf_op jit(solution)/shard_map/ppermute | solution.py:15
  34.3 3.7 %collective-permute-start.6 = (bf16[8,512]{1,0:T(8,128)(2,1)S(1)}, bf16[8,512]{1,0:T(8,128)(2,1)S(1)}, u32[]{:S(2)}, u32[]{:S(2)}) collective-permute-start(bf16[8,512]{1,0:T(8,128)(2,1)S(1)} %pad_maximum_fusion.3), channel_id=1, source_target_pairs={{0,8},{4,12},{8,0},{12,4},{16,24},{20,28},{24,16},{28,20},{1,9},{5... | collective-permute-start | bytes 24584 | tf_op jit(solution)/shard_map/ppermute | solution.py:15
  38.1 3.8 %collective-permute-start.7 = (bf16[16,512]{1,0:T(8,128)(2,1)S(1)}, bf16[16,512]{1,0:T(8,128)(2,1)S(1)}, u32[]{:S(2)}, u32[]{:S(2)}) collective-permute-start(bf16[16,512]{1,0:T(8,128)(2,1)S(1)} %pad_maximum_fusion.2), channel_id=1, source_target_pairs={{0,4},{4,0},{8,12},{12,8},{16,20},{20,16},{24,28},{28,24},{1,5},{5... | collective-permute-start | bytes 49160 | tf_op jit(solution)/shard_map/ppermute | solution.py:15
  42.4 1.3 %collective-permute-start.8 = (bf16[32,1024]{1,0:T(8,128)(2,1)S(1)}, bf16[32,1024]{1,0:T(8,128)(2,1)S(1)}, u32[]{:S(2)}, u32[]{:S(2)}) collective-permute-start(bf16[32,1024]{1,0:T(8,128)(2,1)S(1)} %convolution_convert_fusion.1), channel_id=1, source_target_pairs={{0,1},{1,0},{2,3},{3,2},{4,5},{5,4},{6,7},{7,6},{8,9},{9,8},{10,11... | collective-permute-start | bytes 196616 | tf_op jit(solution)/shard_map/ppermute | solution.py:15
  42.5 15.4 %copy-start.8 = (bf16[512]{0:T(512)(128)(2,1)S(1)}, bf16[512]{0:T(512)(128)(2,1)}, u32[]{:S(2)}) copy-start(bf16[512]{0:T(512)(128)(2,1)} %param.33) | copy-start | bytes 3076
  43.7 4.3 %collective-permute-start.9 = (bf16[32,1024]{1,0:T(8,128)(2,1)S(1)}, bf16[32,1024]{1,0:T(8,128)(2,1)S(1)}, u32[]{:S(2)}, u32[]{:S(2)}) collective-permute-start(bf16[32,1024]{1,0:T(8,128)(2,1)S(1)} %add_convert_fusion.1), channel_id=1, source_target_pairs={{0,2},{1,3},{2,0},{3,1},{4,6},{5,7},{6,4},{7,5},{8,10},{9,11},{10,... | collective-permute-start | bytes 196616 | tf_op jit(solution)/shard_map/ppermute | solution.py:15
  49.9 4.0 %collective-permute-start.10 = (f32[16,512]{1,0:T(8,128)S(1)}, f32[16,512]{1,0:T(8,128)S(1)}, u32[]{:S(2)}, u32[]{:S(2)}) collective-permute-start(f32[16,512]{1,0:T(8,128)S(1)} %slice.57), channel_id=1, source_target_pairs={{0,4},{4,0},{8,12},{12,8},{16,20},{20,16},{24,28},{28,24},{1,5},{5... | collective-permute-start | bytes 98312 | tf_op jit(solution)/shard_map/ppermute | solution.py:15
  53.9 3.8 %collective-permute-start.11 = (f32[8,512]{1,0:T(8,128)S(1)}, f32[8,512]{1,0:T(8,128)S(1)}, u32[]{:S(2)}, u32[]{:S(2)}) collective-permute-start(f32[8,512]{1,0:T(8,128)S(1)} %slice.59), channel_id=1, source_target_pairs={{0,8},{4,12},{8,0},{12,4},{16,24},{20,28},{24,16},{28,20},{1,9},{5... | collective-permute-start | bytes 49160 | tf_op jit(solution)/shard_map/ppermute | solution.py:15
  57.7 4.6 %collective-permute-start.12 = (f32[4,512]{1,0:T(4,128)S(1)}, f32[4,512]{1,0:T(4,128)S(1)}, u32[]{:S(2)}, u32[]{:S(2)}) collective-permute-start(f32[4,512]{1,0:T(4,128)S(1)} %slice.61), channel_id=1, source_target_pairs={{0,16},{4,20},{8,24},{12,28},{16,0},{20,4},{24,8},{28,12},{1,17},{... | collective-permute-start | bytes 24584 | tf_op jit(solution)/shard_map/ppermute | solution.py:15

commit v4 on v3

--- a/solution.py
+++ b/solution.py
@@ -1,13 +1,337 @@
+import functools
 import math
 
 import jax
 import jax.numpy as jnp
 from jax import lax
+from jax.experimental import pallas as pl
+from jax.experimental.pallas import tpu as pltpu
 from jax.sharding import PartitionSpec as P
 
 HEAD_DIM = 128
 NORM_EPS = 1e-05
 PAIRWISE = 16
+
+REQ, TP = 8, 4
+Z_STEPS = (0, 2, 4, 6)
+Y_STEPS = (0, 1)
+F32, BF16, I32 = jnp.float32, jnp.bfloat16, jnp.int32
+VMEM = pl.BlockSpec(memory_space=pltpu.VMEM)
+SMEM = pl.BlockSpec(memory_space=pltpu.SMEM)
+
+
+def send(x, from_odd, req_step, tp_step):
+    pairs = [
+        (q * TP + t, (q ^ req_step) * TP + (t ^ tp_step))
+        for q in range(REQ)
+        for t in range(TP)
+        if t % 2 == from_odd
+    ]
+    return lax.ppermute(x, ("req", "tp"), pairs)
+
+
+def iota(shape, dim):
+    return lax.broadcasted_iota(I32, shape, dim)
+
+
+def onto_mxu(a, b):
+    return jnp.dot(a, b, preferred_element_type=F32)
+
+
+def nt_dot(a, b):
+    return lax.dot_general(a, b, (((1,), (1,)), ((), ())), preferred_element_type=F32)
+
+
+def hot(condition):
+    return jnp.where(condition, 1.0, 0.0).astype(BF16)
+
+
+def pack_kernel(query, key, value, resid, out):
+    rows = query.shape[0]
+    for i, ref in enumerate((query, key, value, resid)):
+        out[i * rows : (i + 1) * rows, :] = ref[...]
+
+
+def index_kernel(place, owner, order, lengths, table, pick1, pick2, valid, arrange, *, page_len):
+    me = place[0]
+    count = owner.shape[1]
+    rows = count // REQ
+    square = (count, count)
+    down, across = iota(square, 0), iota(square, 1)
+    same_place = down == across
+    owner_row = owner[...]
+    owner_col = jnp.sum(jnp.where(same_place, owner_row, 0), axis=1, keepdims=True)
+    same_owner = owner_col == owner_row
+    rank_row = jnp.sum(jnp.where(same_owner & (down < across), 1, 0), axis=0, keepdims=True)
+    rank_col = jnp.sum(jnp.where(same_owner & (across < down), 1, 0), axis=1, keepdims=True)
+
+    source = me ^ (across // (4 * rows))
+    here = hot((down // rows == source) & (down % rows == across % rows))
+    owner_there = onto_mxu(owner_row.astype(F32).astype(BF16), here).astype(I32)
+    target = me ^ (2 * (down // (2 * rows)))
+    pick1[...] = hot(
+        ((down // rows) % 2 == across // (4 * rows))
+        & (down % rows == (across // rows) % rows)
+        & (owner_there == target)
+    )
+
+    half = (4 * rows, count)
+    down_h, across_h = iota(half, 0), iota(half, 1)
+    mine = hot((owner_row == me) & (rank_row == down_h % rows))
+    came_from = me ^ (2 * (across // (2 * rows))) ^ ((across // rows) % 2)
+    from_there = onto_mxu(mine, hot(down // rows == came_from))
+    pick2[...] = hot((from_there > 0.5) & (down_h // rows == across_h % rows))
+
+    shape = valid.shape
+    slot = iota((shape[0], count), 0) % rows
+    mine_v = hot((owner_row == me) & (rank_row == slot))
+    table_v = onto_mxu(mine_v, table[...].astype(F32).astype(BF16)).astype(I32)
+    length_v = jnp.sum(jnp.where(mine_v > 0.5, lengths[...], 0), axis=1, keepdims=True)
+    position = iota(shape, 1)
+    page, within = position // page_len, position % page_len
+    seen = jnp.zeros(shape, F32)
+    for j in range(table.shape[1]):
+        inside = (table_v[:, j : j + 1] == page) & (within + j * page_len < length_v)
+        seen = jnp.where(inside, 1.0, seen)
+    valid[...] = seen
+
+    row_at = me ^ (down // (4 * rows)) ^ (2 * ((down // rows) % 4))
+    there = (across // rows == row_at) & (across % rows == down % rows)
+    wanted = jnp.sum(jnp.where(there, order[...], 0), axis=1, keepdims=True)
+    owner_at = me ^ (2 * (across // (2 * rows))) ^ ((across // rows) % 2)
+    holds = (owner_col == owner_at) & (rank_col == across % rows)
+    arrange[...] = onto_mxu(hot(wanted == across), hot(holds)).astype(BF16)
+
+
+def route_kernel(place, pick, own, sibling, far_even, far_odd, *outs):
+    @pl.when(place[1] == 1)
+    def _():
+        near = jnp.concatenate([sibling[...], own[...]], axis=1)
+        far = jnp.concatenate([far_even[...], far_odd[...]], axis=1)
+        moved = onto_mxu(pick[...], jnp.concatenate([near, far], axis=0)).astype(BF16)
+        each = moved.shape[0] // len(outs)
+        for i, out in enumerate(outs):
+            out[...] = moved[i * each : (i + 1) * each]
+
+
+def collect_kernel(place, pick, first, second, third, fourth, gain, bias, kept, passed):
+    @pl.when(place[1] == 0)
+    def _():
+        rows = jnp.concatenate([first[...], second[...], third[...], fourth[...]], axis=0)
+        own = onto_mxu(pick[...], rows).astype(BF16)
+        half = kept.shape[1]
+        used = own.shape[0]
+        kept[...] = own[:, :half]
+        passed[:used, :] = own[:, half:]
+        passed[used : used + 1, :] = gain[...]
+        passed[used + 1 : used + 2, :] = bias[...]
+
+
+def attention_kernel(place, kept, passed, valid, pool, weight, out_bias, partial, *, rows):
+    cols = kept.shape[1]
+    heads = cols // HEAD_DIM
+    used = 4 * rows
+    scale = 1.0 / math.sqrt(HEAD_DIM)
+    own = jnp.where(place[1] == 0, kept[...].astype(F32), passed[:used, :].astype(F32))
+    query, key, value, resid = (own[i * rows : (i + 1) * rows] for i in range(4))
+
+    def tile(x):
+        return jnp.concatenate([x] * heads, axis=0)
+
+    shape = (heads * rows, cols)
+    in_head = iota(shape, 0) // rows == iota(shape, 1) // HEAD_DIM
+    wide = jnp.where(in_head, tile(query), 0.0)
+    positions = valid.shape[1]
+    keys = pool[0].reshape(positions, cols)
+    values = pool[1].reshape(positions, cols)
+    scores = nt_dot(wide.astype(BF16), keys) * scale
+    scores = jnp.where(valid[...] > 0.5, scores, -jnp.inf)
+    self_score = jnp.sum(wide * tile(key), axis=1, keepdims=True) * scale
+    top = jnp.maximum(jnp.max(scores, axis=1, keepdims=True), self_score)
+    weights = jnp.exp(scores - top)
+    self_weight = jnp.exp(self_score - top)
+    total = jnp.sum(weights, axis=1, keepdims=True) + self_weight
+    numer = onto_mxu(weights.astype(BF16), values)
+    numer = numer + self_weight.astype(BF16).astype(F32) * tile(value)
+    numer = jnp.where(in_head, numer / total, 0.0)
+    attn = sum(numer[i * rows : (i + 1) * rows] for i in range(heads))
+    attn = jnp.concatenate([attn, jnp.zeros_like(attn)], axis=0).astype(BF16)
+    partial[...] = onto_mxu(attn, weight[...])[:rows]
+    mine = pl.ds(pl.multiple_of(place[2] * cols, cols), cols)
+    partial[:, mine] += resid + out_bias[...].astype(F32)
+
+
+def norm_kernel(place, own, sibling, far_even, far_odd, passed, gain, bias, out, *, used):
+    @pl.when(place[1] == 1)
+    def _():
+        whole = (sibling[...] + own[...]) + (far_even[...] + far_odd[...])
+        stream = whole.astype(BF16).astype(F32)
+        rows, width = stream.shape
+        mean = jnp.sum(stream, axis=1, keepdims=True) / width
+        var = jnp.sum((stream - mean) ** 2, axis=1, keepdims=True) / width
+        mine = jnp.where(place[2] // 2 == 0, stream[:, : width // 2], stream[:, width // 2 :])
+        gains = jnp.concatenate([passed[used : used + 1, :], gain[...]], axis=1).astype(F32)
+        biases = jnp.concatenate([passed[used + 1 : used + 2, :], bias[...]], axis=1).astype(F32)
+        normed = (mine - mean) * lax.rsqrt(var + NORM_EPS) * gains + biases
+        out[...] = jnp.concatenate([normed, mine], axis=0).astype(BF16)
+
+
+def up_kernel(place, arrange, first, second, third, fourth, moved, weight, out):
+    @pl.when(place[1] == 1)
+    def _():
+        rows = jnp.concatenate([first[...], second[...], third[...], fourth[...]], axis=0)
+        ordered = onto_mxu(arrange[...], rows).astype(BF16)
+        half = moved.shape[1]
+        hidden = nt_dot(ordered[:, :half], moved[...]) + nt_dot(ordered[:, half:], weight[...])
+        out[...] = hidden.astype(BF16)
+
+
+def down_kernel(place, arrange, near, far, up_bias, stream, weight, moved, first, second, *, rows):
+    @pl.when(place[1] == 0)
+    def _():
+        hidden = near[...].astype(F32) + far[...].astype(F32) + up_bias[...].astype(F32)
+        activated = (0.5 * hidden * (1.0 + lax.erf(hidden * math.sqrt(0.5)))).astype(BF16)
+        kept = onto_mxu(arrange[:, :rows], stream[rows:, :])
+        feed = jnp.concatenate(
+            [onto_mxu(activated, weight[...]), onto_mxu(activated, moved[...])], axis=1
+        )
+        feed = feed + kept
+        half = feed.shape[0] // 2
+        first[...] = feed[:half]
+        second[...] = feed[half:]
+
+
+def call(kernel, shapes, args, smem, flops=0, **fixed):
+    moved = sum(a.size * a.dtype.itemsize for a in args)
+    return pl.pallas_call(
+        functools.partial(kernel, **fixed) if fixed else kernel,
+        out_shape=shapes,
+        in_specs=[SMEM] * smem + [VMEM] * (len(args) - smem),
+        out_specs=[VMEM] * len(shapes),
+        compiler_params=pltpu.CompilerParams(vmem_limit_bytes=24 * 2**20),
+        cost_estimate=pl.CostEstimate(flops=flops, bytes_accessed=moved, transcendentals=0),
+    )(*args)
+
+
+def on_pairs(
+    query,
+    key_new,
+    value_new,
+    resid,
+    lengths,
+    owner,
+    page_table,
+    kv_pool,
+    out_weight,
+    out_bias,
+    norm_gain,
+    norm_bias,
+    up_weight_t,
+    up_bias,
+    down_weight,
+    down_bias,
+    order,
+):
+    rows, cols = query.shape
+    width = cols * TP
+    pool_pages, page_len = kv_pool.shape[1], kv_pool.shape[2]
+    positions = pool_pages * page_len
+    heads = cols // HEAD_DIM
+    count = owner.shape[0]
+    hidden = up_bias.shape[0]
+    used = 4 * rows
+
+    def arr(shape, dtype=BF16):
+        return jax.ShapeDtypeStruct(shape, dtype)
+
+    me, me_tp = lax.axis_index("req").astype(I32), lax.axis_index("tp").astype(I32)
+    place = jnp.stack([me, me_tp % 2, me_tp])
+    gain, bias = norm_gain[None, :], norm_bias[None, :]
+
+    (packed,) = call(pack_kernel, [arr((used, cols))], [query, key_new, value_new, resid], 0)
+    from_sibling = send(packed, 0, 0, 1)
+    from_far_even = send(packed, 0, 1, 1)
+    from_far_odd = send(packed, 1, 1, 0)
+    up_moved = send(up_weight_t, 0, 0, 1)
+    down_moved = send(down_weight, 1, 0, 1)
+    pick1, pick2, valid, arrange = call(
+        functools.partial(index_kernel, page_len=page_len),
+        [
+            arr((count, count)),
+            arr((used, count)),
+            arr((heads * rows, positions), F32),
+            arr((count, count)),
+        ],
+        [place, owner[None, :], order[None, :], lengths[None, :], page_table],
+        1,
+    )
+    outgoing = call(
+        route_kernel,
+        [arr((2 * rows, 2 * cols))] * len(Z_STEPS),
+        [place, pick1, packed, from_sibling, from_far_even, from_far_odd],
+        1,
+    )
+    arrived = [send(x, 1, step, 1) for x, step in zip(outgoing, Z_STEPS)]
+    kept, passed = call(
+        collect_kernel,
+        [arr((used, cols)), arr((2 * used, cols))],
+        [place, pick2, *arrived, gain, bias],
+        1,
+    )
+    passed = send(passed, 0, 0, 1)
+
+    (partial,) = call(
+        attention_kernel,
+        [arr((rows, width), F32)],
+        [place, kept, passed, valid, kv_pool, out_weight, out_bias[None, :]],
+        1,
+        rows=rows,
+    )
+    (normed,) = call(
+        norm_kernel,
+        [arr((2 * rows, 2 * cols))],
+        [
+            place,
+            partial,
+            send(partial, 0, 0, 1),
+            send(partial, 0, 0, 3),
+            send(partial, 1, 0, 2),
+            passed,
+            gain,
+            bias,
+        ],
+        1,
+        used=used,
+    )
+
+    along_y = [send(normed, 1, step, 1) for step in Y_STEPS]
+    two = jnp.concatenate([x[:rows] for x in along_y], axis=0)
+    along_z = [send(two, 0, step, 1) for step in Z_STEPS]
+    (partial_hidden,) = call(
+        up_kernel,
+        [arr((count, hidden))],
+        [place, arrange, *along_z, up_moved, up_weight_t],
+        1,
+    )
+    near = send(partial_hidden, 1, 0, 1)
+    far = send(partial_hidden, 1, 0, 3)
+    feeds = call(
+        down_kernel,
+        [arr((count // 2, 2 * cols), F32)] * 2,
+        [place, arrange, near, far, up_bias[None, :], along_y[0], down_weight, down_moved],
+        1,
+        rows=rows,
+    )
+
+    halves = [send(x, 0, step, 1) for x, step in zip(feeds, Y_STEPS)]
+    summed = halves[0] + halves[1]
+    blocks = [
+        send(summed[i * rows : (i + 1) * rows], 1, step, 1) for i, step in enumerate(Z_STEPS)
+    ]
+    final = (blocks[0] + blocks[1]) + (blocks[2] + blocks[3])
+    other = send(final[:, cols:], 0, 0, 1)
+    mine = jnp.where(place[1] == 0, final[:, :cols], other)
+    return (mine + down_bias.astype(F32)[None, :]).astype(BF16)
 
 
 def swap(x, axis, step):
@@ -59,7 +383,7 @@
     return x
 
 
-def per_device(
+def on_any_mesh(
     query,
     key_new,
     value_new,
@@ -179,6 +503,8 @@
 
 
 def solution(mesh):
+    pairs = mesh.shape["req"] == REQ and mesh.shape["tp"] == TP
+    per_device = on_pairs if pairs else on_any_mesh
     in_specs = (
         P("req", "tp"),
         P("req", "tp"),

time: 63.3 us -> 88.8 us (1.40)
  starting transfers between devices: 17 us -> 45.9 us
  Pallas kernels: 0 us -> 5.97 us
  matrix products: 4.81 us -> 0 us
  waiting for transfers between devices: 28.7 us -> 24.3 us
  other arithmetic: 4.36 us -> 0.71 us
  local copies, waits for them, and re-layouts: 7.77 us -> 10.5 us
    ppermute x13 -> x28, starting transfers between devices: 17 us -> 45.9 us  [send(): return lax.ppermute(x, ('req', 'tp'), pairs)]
    unnamed x29 -> x27, local copies, waits for them, and re-layouts: 2.4 us -> 8.44 us
    pallas_call x0 -> x8, Pallas kernels: none -> 5.97 us  [call(): pl.pallas_call(functools.partial(kernel, **fixed) if fixed else kernel, o...]
    dot_general x7 -> x0, matrix products: 4.81 us -> none  [the longest x1 1.69 us: per_device(): feed = jnp.dot(activated, down_weight, preferred_element_type=f32)]
    ppermute x13 -> x28, waiting for transfers between devices: 28.7 us -> 24.3 us  [send(): return lax.ppermute(x, ('req', 'tp'), pairs)]
    slice x4, local copies, waits for them, and re-layouts: 2.32 us -> 0.03 us  [the longest x1 0.01 us: on_pairs(): summed[i * rows:(i + 1) * rows]]
    broadcast_in_dim x2 -> x4, local copies, waits for them, and re-layouts: 0.03 us -> 2.06 us  [the longest x2 1.37 us: on_pairs(): gain, bias = (norm_gain[None, :], norm_bias[None, :])]
    reduce_sum x7 -> x0, other arithmetic: 1.83 us -> none  [the longest x1 0.91 us: per_device(): rank = jnp.sum((same & (ids[None, :] < ids[:, None])).astype(i32), axis=1)]
  transfers between devices with their start and end apart: 13 -> 28, of which waited for: 12 -> 14; matrix products, arithmetic and copies ran while one was open for 11% -> 3% of each run, Pallas kernels for 0% -> 6%
where the time goes in v4:
time: 88.8 us; the launch traced here: 87.9 us
  starting transfers between devices  45.9 us (52%)
  waiting for transfers between devices  24.3 us (27%)
  local copies, waits for them, and re-layouts  10.5 us (12%)
  Pallas kernels  5.97 us (7%)
    ppermute x28, starting transfers between devices, send(): return lax.ppermute(x, ('req', 'tp'), pairs)  45.9 us
    ppermute x28, waiting for transfers between devices, send(): return lax.ppermute(x, ('req', 'tp'), pairs)  24.3 us
    unnamed x27, local copies, waits for them, and re-layouts  8.44 us
    pallas_call x8, Pallas kernels, call(): pl.pallas_call(functools.partial(kernel, **fixed) if fixed else kernel, o...  5.97 us
  transfers between devices with their start and end apart: 28, of which 14 were waited for; matrix products, arithmetic and copies ran while one was open for 3% of the time, Pallas kernels for 6%

profile of v4, /device:TPU:0, one launch (start us, length us, event | category | flops | bytes accessed | tf_op | source)
XLA Modules:
  0.0 87.9 jit_solution(11180076663719692128)
XLA Ops:
  0.0 2.4 %collective-permute-start.17 = (bf16[1024,512]{1,0:T(8,128)(2,1)}, bf16[1024,512]{1,0:T(8,128)(2,1)S(1)}, u32[]{:S(2)}, u32[]{:S(2)}) collective-permute-start(bf16[1024,512]{1,0:T(8,128)(2,1)} %weight.4), channel_id=1, source_target_pairs={{0,1},{2,3},{4,5},{6,7},{8,9},{10,11},{12,13},{14,15},{16,17},{18,... | collective-permute-start | bytes 3145736 | tf_op jit(solution)/shard_map/ppermute | solution.py:30
  2.4 1.3 %collective-permute-start.20 = (bf16[1024,512]{1,0:T(8,128)(2,1)}, bf16[1024,512]{1,0:T(8,128)(2,1)S(1)}, u32[]{:S(2)}, u32[]{:S(2)}) collective-permute-start(bf16[1024,512]{1,0:T(8,128)(2,1)} %weight.5), channel_id=1, source_target_pairs={{1,0},{3,2},{5,4},{7,6},{9,8},{11,10},{13,12},{15,14},{17,16},{19,... | collective-permute-start | bytes 3145736 | tf_op jit(solution)/shard_map/ppermute | solution.py:30
  6.5 3.1 %collective-permute-start = (bf16[16,512]{1,0:T(8,128)(2,1)S(1)}, bf16[16,512]{1,0:T(8,128)(2,1)S(1)}, u32[]{:S(2)}, u32[]{:S(2)}) collective-permute-start(bf16[16,512]{1,0:T(8,128)(2,1)S(1)} %shard_map.164.own), channel_id=1, source_target_pairs={{0,1},{2,3},{4,5},{6,7},{8,9},{10,11},{12,13},{14,15},{16,17},{18,... | collective-permute-start | bytes 49160 | tf_op jit(solution)/shard_map/ppermute | solution.py:30
  9.6 3.2 %collective-permute-start.1 = (bf16[16,512]{1,0:T(8,128)(2,1)S(1)}, bf16[16,512]{1,0:T(8,128)(2,1)S(1)}, u32[]{:S(2)}, u32[]{:S(2)}) collective-permute-start(bf16[16,512]{1,0:T(8,128)(2,1)S(1)} %shard_map.164.own), channel_id=1, source_target_pairs={{0,5},{2,7},{4,1},{6,3},{8,13},{10,15},{12,9},{14,11},{16,21},{18,... | collective-permute-start | bytes 49160 | tf_op jit(solution)/shard_map/ppermute | solution.py:30
  17.9 1.3 %collective-permute-start.3 = (bf16[8,1024]{1,0:T(8,128)(2,1)S(1)}, bf16[8,1024]{1,0:T(8,128)(2,1)S(1)}, u32[]{:S(2)}, u32[]{:S(2)}) collective-permute-start(bf16[8,1024]{1,0:T(8,128)(2,1)S(1)} %get-tuple-element.20), channel_id=1, source_target_pairs={{1,0},{3,2},{5,4},{7,6},{9,8},{11,10},{13,12},{15,14},{17,16},{19,... | collective-permute-start | bytes 49160 | tf_op jit(solution)/shard_map/ppermute | solution.py:30
  19.2 1.3 %collective-permute-start.4 = (bf16[8,1024]{1,0:T(8,128)(2,1)S(1)}, bf16[8,1024]{1,0:T(8,128)(2,1)S(1)}, u32[]{:S(2)}, u32[]{:S(2)}) collective-permute-start(bf16[8,1024]{1,0:T(8,128)(2,1)S(1)} %get-tuple-element.21), channel_id=1, source_target_pairs={{1,8},{3,10},{5,12},{7,14},{9,0},{11,2},{13,4},{15,6},{17,24},{19,... | collective-permute-start | bytes 49160 | tf_op jit(solution)/shard_map/ppermute | solution.py:30
  20.5 1.3 %collective-permute-start.5 = (bf16[8,1024]{1,0:T(8,128)(2,1)S(1)}, bf16[8,1024]{1,0:T(8,128)(2,1)S(1)}, u32[]{:S(2)}, u32[]{:S(2)}) collective-permute-start(bf16[8,1024]{1,0:T(8,128)(2,1)S(1)} %get-tuple-element.22), channel_id=1, source_target_pairs={{1,16},{3,18},{5,20},{7,22},{9,24},{11,26},{13,28},{15,30},{17,0},... | collective-permute-start | bytes 49160 | tf_op jit(solution)/shard_map/ppermute | solution.py:30
  21.8 1.3 %collective-permute-start.6 = (bf16[8,1024]{1,0:T(8,128)(2,1)S(1)}, bf16[8,1024]{1,0:T(8,128)(2,1)S(1)}, u32[]{:S(2)}, u32[]{:S(2)}) collective-permute-start(bf16[8,1024]{1,0:T(8,128)(2,1)S(1)} %get-tuple-element.23), channel_id=1, source_target_pairs={{1,24},{3,26},{5,28},{7,30},{9,16},{11,18},{13,20},{15,22},{17,8},... | collective-permute-start | bytes 49160 | tf_op jit(solution)/shard_map/ppermute | solution.py:30
  24.5 3.3 %collective-permute-done.5.third = bf16[8,1024]{1,0:T(8,128)(2,1)S(1)} collective-permute-done((bf16[8,1024]{1,0:T(8,128)(2,1)S(1)}, bf16[8,1024]{1,0:T(8,128)(2,1)S(1)}, u32[]{:S(2)}, u32[]{:S(2)}) %collective-permute-start.5) | collective-permute-done | bytes 16416 | tf_op jit(solution)/shard_map/ppermute | solution.py:30
  29.6 1.7 %collective-permute-start.7 = (bf16[32,512]{1,0:T(8,128)(2,1)S(1)}, bf16[32,512]{1,0:T(8,128)(2,1)S(1)}, u32[]{:S(2)}, u32[]{:S(2)}) collective-permute-start(bf16[32,512]{1,0:T(8,128)(2,1)S(1)} %get-tuple-element.25), channel_id=1, source_target_pairs={{0,1},{2,3},{4,5},{6,7},{8,9},{10,11},{12,13},{14,15},{16,17},{18,... | collective-permute-start | bytes 98312 | tf_op jit(solution)/shard_map/ppermute | solution.py:30
  32.2 1.6 %copy-done = bf16[512,2048]{1,0:T(8,128)(2,1)S(1)} copy-done((bf16[512,2048]{1,0:T(8,128)(2,1)S(1)}, bf16[512,2048]{1,0:T(8,128)(2,1)}, u32[]{:S(2)}) %copy-start) | copy-done | bytes 2097176
  33.7 1.4 %copy-done.1 = bf16[2,22,32,512]{3,2,1,0:T(8,128)(2,1)S(1)} copy-done((bf16[2,22,32,512]{3,2,1,0:T(8,128)(2,1)S(1)}, bf16[2,22,32,512]{3,2,1,0:T(8,128)(2,1)}, u32[]{:S(2)}) %copy-start.1) | copy-done | bytes 1441816
  35.1 1.6 %shard_map.167.own = f32[4,2048]{1,0:T(4,128)S(1)} custom-call(s32[3]{0:T(128)S(1)} %pad_add_fusion.place, bf16[16,512]{1,0:T(8,128)(2,1)S(1)} %get-tuple-element.24.kept, bf16[32,512]{1,0:T(8,128)(2,1)S(1)} %collective-permute-done.7.passed, f32[16,704]{1,0:T(8,128)S(1)} %get-tuple-element.26.valid, bf16[2,22,32,512]{3,2,1,0:T(8,128)(2,1)S(1)} %copy-done.1, ...), custom_call_target="tpu_custom_call" | custom-call | bytes 3634188 | tf_op jit(solution)/shard_map/pallas_call | solution.py:206
  37.6 4.7 %collective-permute-start.8 = (f32[4,2048]{1,0:T(4,128)S(1)}, f32[4,2048]{1,0:T(4,128)S(1)}, u32[]{:S(2)}, u32[]{:S(2)}) collective-permute-start(f32[4,2048]{1,0:T(4,128)S(1)} %shard_map.167.own), channel_id=1, source_target_pairs={{0,1},{2,3},{4,5},{6,7},{8,9},{10,11},{12,13},{14,15},{16,17},{18,... | collective-permute-start | bytes 98312 | tf_op jit(solution)/shard_map/ppermute | solution.py:30
  42.3 1.4 %collective-permute-start.9 = (f32[4,2048]{1,0:T(4,128)S(1)}, f32[4,2048]{1,0:T(4,128)S(1)}, u32[]{:S(2)}, u32[]{:S(2)}) collective-permute-start(f32[4,2048]{1,0:T(4,128)S(1)} %shard_map.167.own), channel_id=1, source_target_pairs={{0,3},{2,1},{4,7},{6,5},{8,11},{10,9},{12,15},{14,13},{16,19},{18,... | collective-permute-start | bytes 98312 | tf_op jit(solution)/shard_map/ppermute | solution.py:30
  43.7 1.6 %collective-permute-done.9.far_even = f32[4,2048]{1,0:T(4,128)S(1)} collective-permute-done((f32[4,2048]{1,0:T(4,128)S(1)}, f32[4,2048]{1,0:T(4,128)S(1)}, u32[]{:S(2)}, u32[]{:S(2)}) %collective-permute-start.9) | collective-permute-done | bytes 32800 | tf_op jit(solution)/shard_map/ppermute | solution.py:30
  45.8 1.3 %collective-permute-start.11 = (bf16[8,1024]{1,0:T(8,128)(2,1)S(1)}, bf16[8,1024]{1,0:T(8,128)(2,1)S(1)}, u32[]{:S(2)}, u32[]{:S(2)}) collective-permute-start(bf16[8,1024]{1,0:T(8,128)(2,1)S(1)} %shard_map.168), channel_id=1, source_target_pairs={{1,0},{3,2},{5,4},{7,6},{9,8},{11,10},{13,12},{15,14},{17,16},{19,... | collective-permute-start | bytes 49160 | tf_op jit(solution)/shard_map/ppermute | solution.py:30
  47.1 1.3 %collective-permute-start.12 = (bf16[8,1024]{1,0:T(8,128)(2,1)S(1)}, bf16[8,1024]{1,0:T(8,128)(2,1)S(1)}, u32[]{:S(2)}, u32[]{:S(2)}) collective-permute-start(bf16[8,1024]{1,0:T(8,128)(2,1)S(1)} %shard_map.168), channel_id=1, source_target_pairs={{1,4},{3,6},{5,0},{7,2},{9,12},{11,14},{13,8},{15,10},{17,20},{19,... | collective-permute-start | bytes 49160 | tf_op jit(solution)/shard_map/ppermute | solution.py:30
  49.6 2.6 %collective-permute-done.12 = bf16[8,1024]{1,0:T(8,128)(2,1)S(1)} collective-permute-done((bf16[8,1024]{1,0:T(8,128)(2,1)S(1)}, bf16[8,1024]{1,0:T(8,128)(2,1)S(1)}, u32[]{:S(2)}, u32[]{:S(2)}) %collective-permute-start.12) | collective-permute-done | bytes 16416 | tf_op jit(solution)/shard_map/ppermute | solution.py:30
  54.8 1.5 %collective-permute-start.15 = (bf16[8,1024]{1,0:T(8,128)(2,1)S(1)}, bf16[8,1024]{1,0:T(8,128)(2,1)S(1)}, u32[]{:S(2)}, u32[]{:S(2)}) collective-permute-start(bf16[8,1024]{1,0:T(8,128)(2,1)S(1)} %pad_maximum_fusion), channel_id=1, source_target_pairs={{0,17},{2,19},{4,21},{6,23},{8,25},{10,27},{12,29},{14,31},{16,1},... | collective-permute-start | bytes 49160 | tf_op jit(solution)/shard_map/ppermute | solution.py:30
  56.4 3.1 %collective-permute-start.16 = (bf16[8,1024]{1,0:T(8,128)(2,1)S(1)}, bf16[8,1024]{1,0:T(8,128)(2,1)S(1)}, u32[]{:S(2)}, u32[]{:S(2)}) collective-permute-start(bf16[8,1024]{1,0:T(8,128)(2,1)S(1)} %pad_maximum_fusion), channel_id=1, source_target_pairs={{0,25},{2,27},{4,29},{6,31},{8,17},{10,19},{12,21},{14,23},{16,9},... | collective-permute-start | bytes 49160 | tf_op jit(solution)/shard_map/ppermute | solution.py:30
  59.5 1.4 %collective-permute-done.16.fourth = bf16[8,1024]{1,0:T(8,128)(2,1)S(1)} collective-permute-done((bf16[8,1024]{1,0:T(8,128)(2,1)S(1)}, bf16[8,1024]{1,0:T(8,128)(2,1)S(1)}, u32[]{:S(2)}, u32[]{:S(2)}) %collective-permute-start.16) | collective-permute-done | bytes 16416 | tf_op jit(solution)/shard_map/ppermute | solution.py:30
  65.2 3.6 %collective-permute-done.19.far = bf16[32,1024]{1,0:T(8,128)(2,1)S(1)} collective-permute-done((bf16[32,1024]{1,0:T(8,128)(2,1)S(1)}, bf16[32,1024]{1,0:T(8,128)(2,1)S(1)}, u32[]{:S(2)}, u32[]{:S(2)}) %collective-permute-start.19) | collective-permute-done | bytes 65568 | tf_op jit(solution)/shard_map/ppermute | solution.py:30
  69.9 1.3 %collective-permute-start.21 = (f32[16,1024]{1,0:T(8,128)S(1)}, f32[16,1024]{1,0:T(8,128)S(1)}, u32[]{:S(2)}, u32[]{:S(2)}) collective-permute-start(f32[16,1024]{1,0:T(8,128)S(1)} %get-tuple-element.27), channel_id=1, source_target_pairs={{0,1},{2,3},{4,5},{6,7},{8,9},{10,11},{12,13},{14,15},{16,17},{18,... | collective-permute-start | bytes 196616 | tf_op jit(solution)/shard_map/ppermute | solution.py:30
  71.2 1.3 %collective-permute-start.22 = (f32[16,1024]{1,0:T(8,128)S(1)}, f32[16,1024]{1,0:T(8,128)S(1)}, u32[]{:S(2)}, u32[]{:S(2)}) collective-permute-start(f32[16,1024]{1,0:T(8,128)S(1)} %get-tuple-element.28), channel_id=1, source_target_pairs={{0,5},{2,7},{4,1},{6,3},{8,13},{10,15},{12,9},{14,11},{16,21},{18,... | collective-permute-start | bytes 196616 | tf_op jit(solution)/shard_map/ppermute | solution.py:30
  72.5 1.9 %collective-permute-done.22 = f32[16,1024]{1,0:T(8,128)S(1)} collective-permute-done((f32[16,1024]{1,0:T(8,128)S(1)}, f32[16,1024]{1,0:T(8,128)S(1)}, u32[]{:S(2)}, u32[]{:S(2)}) %collective-permute-start.22) | collective-permute-done | bytes 65568 | tf_op jit(solution)/shard_map/ppermute | solution.py:30
  74.4 1.3 %collective-permute-start.23 = (f32[4,1024]{1,0:T(4,128)S(1)}, f32[4,1024]{1,0:T(4,128)S(1)}, u32[]{:S(2)}, u32[]{:S(2)}) collective-permute-start(f32[4,1024]{1,0:T(4,128)S(1)} %get-tuple-element.32), channel_id=1, source_target_pairs={{1,0},{3,2},{5,4},{7,6},{9,8},{11,10},{13,12},{15,14},{17,16},{19,... | collective-permute-start | bytes 49160 | tf_op jit(solution)/shard_map/ppermute | solution.py:30
  75.7 1.3 %collective-permute-start.24 = (f32[4,1024]{1,0:T(4,128)S(1)}, f32[4,1024]{1,0:T(4,128)S(1)}, u32[]{:S(2)}, u32[]{:S(2)}) collective-permute-start(f32[4,1024]{1,0:T(4,128)S(1)} %get-tuple-element.29), channel_id=1, source_target_pairs={{1,8},{3,10},{5,12},{7,14},{9,0},{11,2},{13,4},{15,6},{17,24},{19,... | collective-permute-start | bytes 49160 | tf_op jit(solution)/shard_map/ppermute | solution.py:30
  77.0 1.3 %collective-permute-start.25 = (f32[4,1024]{1,0:T(4,128)S(1)}, f32[4,1024]{1,0:T(4,128)S(1)}, u32[]{:S(2)}, u32[]{:S(2)}) collective-permute-start(f32[4,1024]{1,0:T(4,128)S(1)} %get-tuple-element.31), channel_id=1, source_target_pairs={{1,16},{3,18},{5,20},{7,22},{9,24},{11,26},{13,28},{15,30},{17,0},... | collective-permute-start | bytes 49160 | tf_op jit(solution)/shard_map/ppermute | solution.py:30
  78.3 1.3 %collective-permute-start.26 = (f32[4,1024]{1,0:T(4,128)S(1)}, f32[4,1024]{1,0:T(4,128)S(1)}, u32[]{:S(2)}, u32[]{:S(2)}) collective-permute-start(f32[4,1024]{1,0:T(4,128)S(1)} %get-tuple-element.30), channel_id=1, source_target_pairs={{1,24},{3,26},{5,28},{7,30},{9,16},{11,18},{13,20},{15,22},{17,8},... | collective-permute-start | bytes 49160 | tf_op jit(solution)/shard_map/ppermute | solution.py:30
  80.7 2.4 %collective-permute-done.25 = f32[4,1024]{1,0:T(4,128)S(1)} collective-permute-done((f32[4,1024]{1,0:T(4,128)S(1)}, f32[4,1024]{1,0:T(4,128)S(1)}, u32[]{:S(2)}, u32[]{:S(2)}) %collective-permute-start.25) | collective-permute-done | bytes 16416 | tf_op jit(solution)/shard_map/ppermute | solution.py:30
  83.2 2.0 %collective-permute-done.26 = f32[4,1024]{1,0:T(4,128)S(1)} collective-permute-done((f32[4,1024]{1,0:T(4,128)S(1)}, f32[4,1024]{1,0:T(4,128)S(1)}, u32[]{:S(2)}, u32[]{:S(2)}) %collective-permute-start.26) | collective-permute-done | bytes 16416 | tf_op jit(solution)/shard_map/ppermute | solution.py:30
  (73 shorter events, 26.1 us)
Async XLA Ops:
  0.0 60.9 %collective-permute-start.17 = (bf16[1024,512]{1,0:T(8,128)(2,1)}, bf16[1024,512]{1,0:T(8,128)(2,1)S(1)}, u32[]{:S(2)}, u32[]{:S(2)}) collective-permute-start(bf16[1024,512]{1,0:T(8,128)(2,1)} %weight.4), channel_id=1, source_target_pairs={{0,1},{2,3},{4,5},{6,7},{8,9},{10,11},{12,13},{14,15},{16,17},{18,... | collective-permute-start | bytes 3145736 | tf_op jit(solution)/shard_map/ppermute | solution.py:30
  2.4 61.7 %collective-permute-start.20 = (bf16[1024,512]{1,0:T(8,128)(2,1)}, bf16[1024,512]{1,0:T(8,128)(2,1)S(1)}, u32[]{:S(2)}, u32[]{:S(2)}) collective-permute-start(bf16[1024,512]{1,0:T(8,128)(2,1)} %weight.5), channel_id=1, source_target_pairs={{1,0},{3,2},{5,4},{7,6},{9,8},{11,10},{13,12},{15,14},{17,16},{19,... | collective-permute-start | bytes 3145736 | tf_op jit(solution)/shard_map/ppermute | solution.py:30
  6.5 10.8 %collective-permute-start = (bf16[16,512]{1,0:T(8,128)(2,1)S(1)}, bf16[16,512]{1,0:T(8,128)(2,1)S(1)}, u32[]{:S(2)}, u32[]{:S(2)}) collective-permute-start(bf16[16,512]{1,0:T(8,128)(2,1)S(1)} %shard_map.164.own), channel_id=1, source_target_pairs={{0,1},{2,3},{4,5},{6,7},{8,9},{10,11},{12,13},{14,15},{16,17},{18,... | collective-permute-start | bytes 49160 | tf_op jit(solution)/shard_map/ppermute | solution.py:30
  9.6 7.8 %collective-permute-start.1 = (bf16[16,512]{1,0:T(8,128)(2,1)S(1)}, bf16[16,512]{1,0:T(8,128)(2,1)S(1)}, u32[]{:S(2)}, u32[]{:S(2)}) collective-permute-start(bf16[16,512]{1,0:T(8,128)(2,1)S(1)} %shard_map.164.own), channel_id=1, source_target_pairs={{0,5},{2,7},{4,1},{6,3},{8,13},{10,15},{12,9},{14,11},{16,21},{18,... | collective-permute-start | bytes 49160 | tf_op jit(solution)/shard_map/ppermute | solution.py:30
  12.8 4.5 %collective-permute-start.2 = (bf16[16,512]{1,0:T(8,128)(2,1)S(1)}, bf16[16,512]{1,0:T(8,128)(2,1)S(1)}, u32[]{:S(2)}, u32[]{:S(2)}) collective-permute-start(bf16[16,512]{1,0:T(8,128)(2,1)S(1)} %shard_map.164.own), channel_id=1, source_target_pairs={{1,5},{3,7},{5,1},{7,3},{9,13},{11,15},{13,9},{15,11},{17,21},{19,... | collective-permute-start | bytes 49160 | tf_op jit(solution)/shard_map/ppermute | solution.py:30
  17.9 3.9 %collective-permute-start.3 = (bf16[8,1024]{1,0:T(8,128)(2,1)S(1)}, bf16[8,1024]{1,0:T(8,128)(2,1)S(1)}, u32[]{:S(2)}, u32[]{:S(2)}) collective-permute-start(bf16[8,1024]{1,0:T(8,128)(2,1)S(1)} %get-tuple-element.20), channel_id=1, source_target_pairs={{1,0},{3,2},{5,4},{7,6},{9,8},{11,10},{13,12},{15,14},{17,16},{19,... | collective-permute-start | bytes 49160 | tf_op jit(solution)/shard_map/ppermute | solution.py:30
  19.2 5.3 %collective-permute-start.4 = (bf16[8,1024]{1,0:T(8,128)(2,1)S(1)}, bf16[8,1024]{1,0:T(8,128)(2,1)S(1)}, u32[]{:S(2)}, u32[]{:S(2)}) collective-permute-start(bf16[8,1024]{1,0:T(8,128)(2,1)S(1)} %get-tuple-element.21), channel_id=1, source_target_pairs={{1,8},{3,10},{5,12},{7,14},{9,0},{11,2},{13,4},{15,6},{17,24},{19,... | collective-permute-start | bytes 49160 | tf_op jit(solution)/shard_map/ppermute | solution.py:30
  20.5 7.3 %collective-permute-start.5 = (bf16[8,1024]{1,0:T(8,128)(2,1)S(1)}, bf16[8,1024]{1,0:T(8,128)(2,1)S(1)}, u32[]{:S(2)}, u32[]{:S(2)}) collective-permute-start(bf16[8,1024]{1,0:T(8,128)(2,1)S(1)} %get-tuple-element.22), channel_id=1, source_target_pairs={{1,16},{3,18},{5,20},{7,22},{9,24},{11,26},{13,28},{15,30},{17,0},... | collective-permute-start | bytes 49160 | tf_op jit(solution)/shard_map/ppermute | solution.py:30
  21.8 7.1 %collective-permute-start.6 = (bf16[8,1024]{1,0:T(8,128)(2,1)S(1)}, bf16[8,1024]{1,0:T(8,128)(2,1)S(1)}, u32[]{:S(2)}, u32[]{:S(2)}) collective-permute-start(bf16[8,1024]{1,0:T(8,128)(2,1)S(1)} %get-tuple-element.23), channel_id=1, source_target_pairs={{1,24},{3,26},{5,28},{7,30},{9,16},{11,18},{13,20},{15,22},{17,8},... | collective-permute-start | bytes 49160 | tf_op jit(solution)/shard_map/ppermute | solution.py:30
  29.6 2.6 %collective-permute-start.7 = (bf16[32,512]{1,0:T(8,128)(2,1)S(1)}, bf16[32,512]{1,0:T(8,128)(2,1)S(1)}, u32[]{:S(2)}, u32[]{:S(2)}) collective-permute-start(bf16[32,512]{1,0:T(8,128)(2,1)S(1)} %get-tuple-element.25), channel_id=1, source_target_pairs={{0,1},{2,3},{4,5},{6,7},{8,9},{10,11},{12,13},{14,15},{16,17},{18,... | collective-permute-start | bytes 98312 | tf_op jit(solution)/shard_map/ppermute | solution.py:30
  35.1 25.8 %copy-start.2 = (bf16[1024,512]{1,0:T(8,128)(2,1)S(1)}, bf16[1024,512]{1,0:T(8,128)(2,1)}, u32[]{:S(2)}) copy-start(bf16[1024,512]{1,0:T(8,128)(2,1)} %weight.4) | copy-start | bytes 3145732
  36.7 27.3 %copy-start.11 = (bf16[1024]{0:T(1024)(128)(2,1)S(1)}, bf16[1024]{0:T(1024)(128)(2,1)}, u32[]{:S(2)}) copy-start(bf16[1024]{0:T(1024)(128)(2,1)} %param.30) | copy-start | bytes 6148
  36.7 32.1 %copy-start.3 = (bf16[1024,512]{1,0:T(8,128)(2,1)S(1)}, bf16[1024,512]{1,0:T(8,128)(2,1)}, u32[]{:S(2)}) copy-start(bf16[1024,512]{1,0:T(8,128)(2,1)} %weight.5) | copy-start | bytes 3145732
  36.7 7.0 %collective-permute-start.10 = (f32[4,2048]{1,0:T(4,128)S(1)}, f32[4,2048]{1,0:T(4,128)S(1)}, u32[]{:S(2)}, u32[]{:S(2)}) collective-permute-start(f32[4,2048]{1,0:T(4,128)S(1)} %shard_map.167.own), channel_id=1, source_target_pairs={{1,3},{3,1},{5,7},{7,5},{9,11},{11,9},{13,15},{15,13},{17,19},{19,... | collective-permute-start | bytes 98312 | tf_op jit(solution)/shard_map/ppermute | solution.py:30
  37.6 6.2 %collective-permute-start.8 = (f32[4,2048]{1,0:T(4,128)S(1)}, f32[4,2048]{1,0:T(4,128)S(1)}, u32[]{:S(2)}, u32[]{:S(2)}) collective-permute-start(f32[4,2048]{1,0:T(4,128)S(1)} %shard_map.167.own), channel_id=1, source_target_pairs={{0,1},{2,3},{4,5},{6,7},{8,9},{10,11},{12,13},{14,15},{16,17},{18,... | collective-permute-start | bytes 98312 | tf_op jit(solution)/shard_map/ppermute | solution.py:30
  42.3 3.0 %collective-permute-start.9 = (f32[4,2048]{1,0:T(4,128)S(1)}, f32[4,2048]{1,0:T(4,128)S(1)}, u32[]{:S(2)}, u32[]{:S(2)}) collective-permute-start(f32[4,2048]{1,0:T(4,128)S(1)} %shard_map.167.own), channel_id=1, source_target_pairs={{0,3},{2,1},{4,7},{6,5},{8,11},{10,9},{12,15},{14,13},{16,19},{18,... | collective-permute-start | bytes 98312 | tf_op jit(solution)/shard_map/ppermute | solution.py:30
  45.8 3.7 %collective-permute-start.11 = (bf16[8,1024]{1,0:T(8,128)(2,1)S(1)}, bf16[8,1024]{1,0:T(8,128)(2,1)S(1)}, u32[]{:S(2)}, u32[]{:S(2)}) collective-permute-start(bf16[8,1024]{1,0:T(8,128)(2,1)S(1)} %shard_map.168), channel_id=1, source_target_pairs={{1,0},{3,2},{5,4},{7,6},{9,8},{11,10},{13,12},{15,14},{17,16},{19,... | collective-permute-start | bytes 49160 | tf_op jit(solution)/shard_map/ppermute | solution.py:30
  47.1 5.1 %collective-permute-start.12 = (bf16[8,1024]{1,0:T(8,128)(2,1)S(1)}, bf16[8,1024]{1,0:T(8,128)(2,1)S(1)}, u32[]{:S(2)}, u32[]{:S(2)}) collective-permute-start(bf16[8,1024]{1,0:T(8,128)(2,1)S(1)} %shard_map.168), channel_id=1, source_target_pairs={{1,4},{3,6},{5,0},{7,2},{9,12},{11,14},{13,8},{15,10},{17,20},{19,... | collective-permute-start | bytes 49160 | tf_op jit(solution)/shard_map/ppermute | solution.py:30
  52.2 4.1 %collective-permute-start.13 = (bf16[8,1024]{1,0:T(8,128)(2,1)S(1)}, bf16[8,1024]{1,0:T(8,128)(2,1)S(1)}, u32[]{:S(2)}, u32[]{:S(2)}) collective-permute-start(bf16[8,1024]{1,0:T(8,128)(2,1)S(1)} %pad_maximum_fusion), channel_id=1, source_target_pairs={{0,1},{2,3},{4,5},{6,7},{8,9},{10,11},{12,13},{14,15},{16,17},{18,... | collective-permute-start | bytes 49160 | tf_op jit(solution)/shard_map/ppermute | solution.py:30
  53.5 5.9 %collective-permute-start.14 = (bf16[8,1024]{1,0:T(8,128)(2,1)S(1)}, bf16[8,1024]{1,0:T(8,128)(2,1)S(1)}, u32[]{:S(2)}, u32[]{:S(2)}) collective-permute-start(bf16[8,1024]{1,0:T(8,128)(2,1)S(1)} %pad_maximum_fusion), channel_id=1, source_target_pairs={{0,9},{2,11},{4,13},{6,15},{8,1},{10,3},{12,5},{14,7},{16,25},{18,... | collective-permute-start | bytes 49160 | tf_op jit(solution)/shard_map/ppermute | solution.py:30
  54.8 4.7 %collective-permute-start.15 = (bf16[8,1024]{1,0:T(8,128)(2,1)S(1)}, bf16[8,1024]{1,0:T(8,128)(2,1)S(1)}, u32[]{:S(2)}, u32[]{:S(2)}) collective-permute-start(bf16[8,1024]{1,0:T(8,128)(2,1)S(1)} %pad_maximum_fusion), channel_id=1, source_target_pairs={{0,17},{2,19},{4,21},{6,23},{8,25},{10,27},{12,29},{14,31},{16,1},... | collective-permute-start | bytes 49160 | tf_op jit(solution)/shard_map/ppermute | solution.py:30
  56.4 4.5 %collective-permute-start.16 = (bf16[8,1024]{1,0:T(8,128)(2,1)S(1)}, bf16[8,1024]{1,0:T(8,128)(2,1)S(1)}, u32[]{:S(2)}, u32[]{:S(2)}) collective-permute-start(bf16[8,1024]{1,0:T(8,128)(2,1)S(1)} %pad_maximum_fusion), channel_id=1, source_target_pairs={{0,25},{2,27},{4,29},{6,31},{8,17},{10,19},{12,21},{14,23},{16,9},... | collective-permute-start | bytes 49160 | tf_op jit(solution)/shard_map/ppermute | solution.py:30
  60.9 25.6 %copy-start.12 = (bf16[512]{0:T(512)(128)(2,1)S(1)}, bf16[512]{0:T(512)(128)(2,1)}, u32[]{:S(2)}) copy-start(bf16[512]{0:T(512)(128)(2,1)} %param.32) | copy-start | bytes 3076
  61.5 3.8 %collective-permute-start.18 = (bf16[32,1024]{1,0:T(8,128)(2,1)S(1)}, bf16[32,1024]{1,0:T(8,128)(2,1)S(1)}, u32[]{:S(2)}, u32[]{:S(2)}) collective-permute-start(bf16[32,1024]{1,0:T(8,128)(2,1)S(1)} %shard_map.169), channel_id=1, source_target_pairs={{1,0},{3,2},{5,4},{7,6},{9,8},{11,10},{13,12},{15,14},{17,16},{19,... | collective-permute-start | bytes 196616 | tf_op jit(solution)/shard_map/ppermute | solution.py:30
  62.8 6.1 %collective-permute-start.19 = (bf16[32,1024]{1,0:T(8,128)(2,1)S(1)}, bf16[32,1024]{1,0:T(8,128)(2,1)S(1)}, u32[]{:S(2)}, u32[]{:S(2)}) collective-permute-start(bf16[32,1024]{1,0:T(8,128)(2,1)S(1)} %shard_map.169), channel_id=1, source_target_pairs={{1,2},{3,0},{5,6},{7,4},{9,10},{11,8},{13,14},{15,12},{17,18},{19,... | collective-permute-start | bytes 196616 | tf_op jit(solution)/shard_map/ppermute | solution.py:30
  69.9 2.6 %collective-permute-start.21 = (f32[16,1024]{1,0:T(8,128)S(1)}, f32[16,1024]{1,0:T(8,128)S(1)}, u32[]{:S(2)}, u32[]{:S(2)}) collective-permute-start(f32[16,1024]{1,0:T(8,128)S(1)} %get-tuple-element.27), channel_id=1, source_target_pairs={{0,1},{2,3},{4,5},{6,7},{8,9},{10,11},{12,13},{14,15},{16,17},{18,... | collective-permute-start | bytes 196616 | tf_op jit(solution)/shard_map/ppermute | solution.py:30
  71.2 3.2 %collective-permute-start.22 = (f32[16,1024]{1,0:T(8,128)S(1)}, f32[16,1024]{1,0:T(8,128)S(1)}, u32[]{:S(2)}, u32[]{:S(2)}) collective-permute-start(f32[16,1024]{1,0:T(8,128)S(1)} %get-tuple-element.28), channel_id=1, source_target_pairs={{0,5},{2,7},{4,1},{6,3},{8,13},{10,15},{12,9},{14,11},{16,21},{18,... | collective-permute-start | bytes 196616 | tf_op jit(solution)/shard_map/ppermute | solution.py:30
  74.4 5.2 %collective-permute-start.23 = (f32[4,1024]{1,0:T(4,128)S(1)}, f32[4,1024]{1,0:T(4,128)S(1)}, u32[]{:S(2)}, u32[]{:S(2)}) collective-permute-start(f32[4,1024]{1,0:T(4,128)S(1)} %get-tuple-element.32), channel_id=1, source_target_pairs={{1,0},{3,2},{5,4},{7,6},{9,8},{11,10},{13,12},{15,14},{17,16},{19,... | collective-permute-start | bytes 49160 | tf_op jit(solution)/shard_map/ppermute | solution.py:30
  75.7 5.1 %collective-permute-start.24 = (f32[4,1024]{1,0:T(4,128)S(1)}, f32[4,1024]{1,0:T(4,128)S(1)}, u32[]{:S(2)}, u32[]{:S(2)}) collective-permute-start(f32[4,1024]{1,0:T(4,128)S(1)} %get-tuple-element.29), channel_id=1, source_target_pairs={{1,8},{3,10},{5,12},{7,14},{9,0},{11,2},{13,4},{15,6},{17,24},{19,... | collective-permute-start | bytes 49160 | tf_op jit(solution)/shard_map/ppermute | solution.py:30
  77.0 6.2 %collective-permute-start.25 = (f32[4,1024]{1,0:T(4,128)S(1)}, f32[4,1024]{1,0:T(4,128)S(1)}, u32[]{:S(2)}, u32[]{:S(2)}) collective-permute-start(f32[4,1024]{1,0:T(4,128)S(1)} %get-tuple-element.31), channel_id=1, source_target_pairs={{1,16},{3,18},{5,20},{7,22},{9,24},{11,26},{13,28},{15,30},{17,0},... | collective-permute-start | bytes 49160 | tf_op jit(solution)/shard_map/ppermute | solution.py:30
  78.3 6.9 %collective-permute-start.26 = (f32[4,1024]{1,0:T(4,128)S(1)}, f32[4,1024]{1,0:T(4,128)S(1)}, u32[]{:S(2)}, u32[]{:S(2)}) collective-permute-start(f32[4,1024]{1,0:T(4,128)S(1)} %get-tuple-element.30), channel_id=1, source_target_pairs={{1,24},{3,26},{5,28},{7,30},{9,16},{11,18},{13,20},{15,22},{17,8},... | collective-permute-start | bytes 49160 | tf_op jit(solution)/shard_map/ppermute | solution.py:30
  85.2 2.1 %collective-permute-start.27 = (f32[4,512]{1,0:T(4,128)S(1)}, f32[4,512]{1,0:T(4,128)S(1)}, u32[]{:S(2)}, u32[]{:S(2)}) collective-permute-start(f32[4,512]{1,0:T(4,128)S(1)} %slice.39), channel_id=1, source_target_pairs={{0,1},{2,3},{4,5},{6,7},{8,9},{10,11},{12,13},{14,15},{16,17},{18,... | collective-permute-start | bytes 24584 | tf_op jit(solution)/shard_map/ppermute | solution.py:30
  (9 other events, 7.7 us)

commit v5 on v3

--- a/solution.py
+++ b/solution.py
@@ -54,9 +54,25 @@
     n = lax.axis_size(axis)
     step = 1
     while step < n:
-        x = (x.astype(jnp.float32) + swap(x, axis, step).astype(jnp.float32)).astype(x.dtype)
+        x = (x.astype(jnp.float32) + swap(x, axis, 2 * step - 1).astype(jnp.float32)).astype(x.dtype)
         step *= 2
     return x
+
+
+def gather_by_odd(x, even_cols):
+    n_req, n_tp = lax.axis_size("req"), lax.axis_size("tp")
+    odd = lax.axis_index("tp") % 2 == 1
+    step = n_req // 2
+    while step:
+        pairs = [
+            (q * n_tp + t, (q ^ step if t % 2 else q) * n_tp + t)
+            for q in range(n_req)
+            for t in range(n_tp)
+        ]
+        x = jnp.concatenate([x, lax.ppermute(x, ("req", "tp"), pairs)], axis=0)
+        step //= 2
+    passed = swap(x[:, :even_cols], "tp", 1)
+    return jnp.where(odd, x[:, even_cols:], passed)
 
 
 def per_device(
@@ -156,12 +172,21 @@
     var = jnp.mean((stream_f - mean) ** 2, axis=1, keepdims=True)
     inverse = lax.rsqrt(var + NORM_EPS)
     stream_own = lax.dynamic_slice_in_dim(stream, me_tp * cols, cols, axis=1)
+    stream_pair = lax.dynamic_slice_in_dim(stream, (me_tp // 2) * 2 * cols, 2 * cols, axis=1)
+    gain_pair, bias_pair = (
+        jnp.concatenate([jnp.where(me_tp % 2 == 0, v, w), jnp.where(me_tp % 2 == 0, w, v)])
+        for v, w in ((v, swap(v, "tp", 1)) for v in (norm_gain, norm_bias))
+    )
     normed = (
-        (stream_own.astype(f32) - mean) * inverse * norm_gain.astype(f32)[None, :]
-        + norm_bias.astype(f32)[None, :]
+        (stream_pair.astype(f32) - mean) * inverse * gain_pair.astype(f32)[None, :]
+        + bias_pair.astype(f32)[None, :]
     ).astype(bf16)
 
-    normed_all = gather_rows(normed, "req")
+    if n_req > PAIRWISE:
+        own = lax.dynamic_slice_in_dim(normed, (me_tp % 2) * cols, cols, axis=1)
+        normed_all = gather_rows(own, "req")
+    else:
+        normed_all = gather_by_odd(normed, cols)
     slot_of = owner * rows + rank
     wanted = slot_of[order[origin_ids]]
     place_hot = (wanted[:, None] == origin_ids[None, :]).astype(bf16)

time: 63.3 us -> 87.8 us (1.39)
  other arithmetic: 4.36 us -> 18 us
  waiting for transfers between devices: 28.7 us -> 17.4 us
  starting transfers between devices: 17 us -> 27.3 us
  local copies, waits for them, and re-layouts: 7.77 us -> 15.4 us
  matrix products: 4.81 us -> 8.22 us
    ppermute x13, waiting for transfers between devices: 28.7 us -> 17.4 us  [swap(): return lax.ppermute(x, axis, [(i, i ^ step) for i in range(n)])]
    ppermute x13, starting transfers between devices: 17 us -> 25.3 us  [swap(): return lax.ppermute(x, axis, [(i, i ^ step) for i in range(n)])]
    unnamed x29 -> x25, local copies, waits for them, and re-layouts: 2.4 us -> 5.96 us
    concatenate x4 -> x2, other arithmetic: 0.07 us -> 2.17 us  [gather_rows(): x = jnp.concatenate([x, swap(x, axis, step)], axis=0)]
    ppermute x0 -> x3, starting transfers between devices: none -> 1.98 us  [gather_by_odd(): x = jnp.concatenate([x, lax.ppermute(x, ('req', 'tp'), pairs)], axis=0)]
    dot_general x1, matrix products: 0.41 us -> 2.31 us  [per_device(): lax.dot_general(spread_q, keys, (((1,), (1,)), ((), ())), preferred_eleme...]
    select_n x1, local copies, waits for them, and re-layouts: 0.01 us -> 1.33 us  [per_device(): jnp.where(head_mask[:, None, :], query_own[None], 0)]
    select_n x0 -> x1, other arithmetic: none -> 1.31 us  [per_device(): jnp.where(me_tp % 2 == 0, v, w)]
  transfers between devices with their start and end apart: 13 -> 16, of which waited for: 12 -> 9; matrix products, arithmetic and copies ran while one was open for 11% -> 23% of each run, Pallas kernels for 0% -> 0%
where the time goes in v5:
time: 87.8 us; the launch traced here: 86.6 us
  starting transfers between devices  27.3 us (31%)
  other arithmetic  18 us (21%)
  waiting for transfers between devices  17.4 us (20%)
  local copies, waits for them, and re-layouts  15.4 us (18%)
  matrix products  8.22 us (9%)
    ppermute x13, starting transfers between devices, swap(): return lax.ppermute(x, axis, [(i, i ^ step) for i in range(n)])  25.3 us
    ppermute x13, waiting for transfers between devices, swap(): return lax.ppermute(x, axis, [(i, i ^ step) for i in range(n)])  17.4 us
    unnamed x25, local copies, waits for them, and re-layouts  5.96 us
    dot_general x1, matrix products, per_device(): lax.dot_general(spread_q, keys, (((1,), (1,)), ((), ())), preferred_eleme...  2.31 us
    concatenate x2, other arithmetic, gather_rows(): x = jnp.concatenate([x, swap(x, axis, step)], axis=0)  2.17 us
    ppermute x3, starting transfers between devices, gather_by_odd(): x = jnp.concatenate([x, lax.ppermute(x, ('req', 'tp'), pairs)], axis=0)  1.98 us
  transfers between devices with their start and end apart: 16, of which 9 were waited for; matrix products, arithmetic and copies ran while one was open for 23% of the time, Pallas kernels for 0%

profile of v5, /device:TPU:0, one launch (start us, length us, event | category | flops | bytes accessed | tf_op | source)
XLA Modules:
  0.0 86.6 jit_solution(2387842265408858419)
XLA Ops:
  0.0 1.4 %constant_dynamic-update-slice_fusion.3 = bf16[4,2048]{1,0:T(4,128)(2,1)} fusion(bf16[4,512]{1,0:T(4,128)(2,1)} %param.18), kind=kLoop, calls=%fused_computation.110 | loop fusion | bytes 8192
  1.4 1.3 %constant_dynamic-update-slice_fusion.2 = bf16[4,2048]{1,0:T(4,128)(2,1)} fusion(bf16[4,2048]{1,0:T(4,128)(2,1)} %constant_dynamic-update-slice_fusion.3, bf16[4,512]{1,0:T(4,128)(2,1)} %param.19), kind=kLoop, calls=%fused_computation.109 | loop fusion | bytes 8192
  2.7 1.3 %constant_dynamic-update-slice_fusion.1 = bf16[4,2048]{1,0:T(4,128)(2,1)} fusion(bf16[4,2048]{1,0:T(4,128)(2,1)} %constant_dynamic-update-slice_fusion.2, bf16[4,512]{1,0:T(4,128)(2,1)} %param.20), kind=kLoop, calls=%fused_computation.108 | loop fusion | bytes 8192
  4.0 1.3 %constant_dynamic-update-slice_fusion = bf16[4,2048]{1,0:T(4,128)(2,1)} fusion(bf16[4,2048]{1,0:T(4,128)(2,1)} %constant_dynamic-update-slice_fusion.1, bf16[4,512]{1,0:T(4,128)(2,1)} %param.21), kind=kLoop, calls=%fused_computation.107 | loop fusion | bytes 8192 | tf_op jit(solution)/shard_map/concatenate | solution.py:110
  5.3 4.0 %collective-permute-start = (bf16[4,2048]{1,0:T(4,128)(2,1)}, bf16[4,2048]{1,0:T(4,128)(2,1)}, u32[]{:S(2)}, u32[]{:S(2)}) collective-permute-start(bf16[4,2048]{1,0:T(4,128)(2,1)} %constant_dynamic-update-slice_fusion), channel_id=1, source_target_pairs={{0,16},{4,20},{8,24},{12,28},{16,0},{20,4},{24,8},{28,12},{1,17},{... | collective-permute-start | bytes 49160 | tf_op jit(solution)/shard_map/ppermute | solution.py:15
  10.3 0.9 %convert_reduce_fusion.1 = s32[32]{0:T(128)S(1)} fusion(s32[32]{0:T(128)} %param.23), kind=kLoop, calls=%fused_computation.98 | loop fusion | flops 5088 | bytes 256 | tf_op jit(solution)/shard_map/reduce_sum | solution.py:115
  12.6 1.3 %select_reduce_fusion.1 = (s32[4]{0:T(128)}, s32[4]{0:T(128)}) fusion(s32[32]{0:T(128)} %param.22, s32[32]{0:T(128)S(1)} %convert_reduce_fusion.1, pred[32]{0:T(512)(128)(4,1)S(1)} %broadcast_compare_fusion), kind=kLoop, calls=%fused_computation.150 | loop fusion | flops 760 | bytes 320 | tf_op jit(solution)/shard_map/reduce_sum | solution.py:119
  15.2 1.4 %fusion.128 = (bf16[1,22,32,512]{3,2,1,0:T(8,128)(2,1)S(1)}, bf16[1,22,32,512]{3,2,1,0:T(8,128)(2,1)S(1)}) fusion(bf16[2,22,32,512]{3,2,1,0:T(8,128)(2,1)} %param.25), kind=kLoop, calls=%fused_computation.206 | loop fusion | bytes 2883584 | tf_op jit(solution)/shard_map/slice | solution.py:137
  18.9 1.4 %pad_maximum_fusion.2 = bf16[8,2048]{1,0:T(8,128)(2,1)} fusion(bf16[4,2048]{1,0:T(4,128)(2,1)} %collective-permute-done, bf16[4,2048]{1,0:T(4,128)(2,1)} %constant_dynamic-update-slice_fusion), kind=kLoop, calls=%fused_computation.88 | loop fusion | flops 65536 | bytes 65536 | tf_op jit(solution)/shard_map/concatenate | solution.py:36
  20.3 1.6 %collective-permute-start.1 = (bf16[8,2048]{1,0:T(8,128)(2,1)}, bf16[8,2048]{1,0:T(8,128)(2,1)}, u32[]{:S(2)}, u32[]{:S(2)}) collective-permute-start(bf16[8,2048]{1,0:T(8,128)(2,1)} %pad_maximum_fusion.2), channel_id=1, source_target_pairs={{0,8},{4,12},{8,0},{12,4},{16,24},{20,28},{24,16},{28,20},{1,9},{5... | collective-permute-start | bytes 98312 | tf_op jit(solution)/shard_map/ppermute | solution.py:15
  21.9 1.3 %and_reduce_fusion = pred[4,704]{1,0:T(4,128)(4,1)} fusion(s32[16,704]{1,0:T(8,128)S(1)} %broadcast_add_fusion, s32[704]{0:T(1024)S(1)} %add_select_fusion, s32[4,16]{1,0:T(4,128)S(1)} %multiply_reduce_fusion, s32[4]{0:T(128)} %get-tuple-element.5), kind=kLoop, calls=%fused_computation.14 | loop fusion | flops 177408 | bytes 50960 | tf_op jit(solution)/shard_map/reduce_or | solution.py:134
  27.9 1.6 %collective-permute-start.2 = (bf16[16,2048]{1,0:T(8,128)(2,1)S(1)}, bf16[16,2048]{1,0:T(8,128)(2,1)S(1)}, u32[]{:S(2)}, u32[]{:S(2)}) collective-permute-start(bf16[16,2048]{1,0:T(8,128)(2,1)S(1)} %pad_maximum_fusion), channel_id=1, source_target_pairs={{0,4},{4,0},{8,12},{12,8},{16,20},{20,16},{24,28},{28,24},{1,5},{5... | collective-permute-start | bytes 196616 | tf_op jit(solution)/shard_map/ppermute | solution.py:15
  29.5 1.3 %broadcast_select_fusion.2 = (bf16[512]{0:T(512)(128)(2,1)}, bf16[512]{0:T(512)(128)(2,1)}, bf16[512]{0:T(512)(128)(2,1)}, bf16[512]{0:T(512)(128)(2,1)}) fusion(bf16[512]{0:T(512)(128)(2,1)} %param.29, bf16[512]{0:T(512)(128)(2,1)} %collective-permute-done.6, pred[]{:T(512)S(6)} %eq.161, bf16[512]{0:T(512)(128)(2,1)} %collective-permute-done.5, ...), kind=kLoop, calls=%fused_computation.158 | loop fusion | flops 2048 | bytes 8193 | tf_op jit(solution)/shard_map/jit(_where)/select_n | solution.py:177
  30.8 1.4 %collective-permute-done.2 = bf16[16,2048]{1,0:T(8,128)(2,1)S(1)} collective-permute-done((bf16[16,2048]{1,0:T(8,128)(2,1)S(1)}, bf16[16,2048]{1,0:T(8,128)(2,1)S(1)}, u32[]{:S(2)}, u32[]{:S(2)}) %collective-permute-start.2) | collective-permute-done | bytes 65568 | tf_op jit(solution)/shard_map/ppermute | solution.py:15
  32.2 1.0 %convolution_convert_fusion = bf16[4,2048]{1,0:T(4,128)(2,1)S(1)} fusion(bf16[16,2048]{1,0:T(8,128)(2,1)S(1)} %collective-permute-done.2, bf16[8,2048]{1,0:T(8,128)(2,1)} %collective-permute-done.1, bf16[4,2048]{1,0:T(4,128)(2,1)} %collective-permute-done, bf16[4,2048]{1,0:T(4,128)(2,1)} %constant_dynamic-update-slice_fusion, s32[32]{0:T(128)} %add.198, ...), kind=kOutput, calls=%fused_computation.3 | convolution fusion | flops 1056896 | bytes 147600 | tf_op jit(solution)/shard_map/dot_general | solution.py:124
  34.4 1.3 %broadcast_select_fusion = bf16[4,4,512]{2,1,0:T(4,128)(2,1)} fusion(pred[4,512]{1,0:T(4,128)(4,1)} %iota_compare_fusion.1, bf16[4,512]{1,0:T(4,128)(2,1)S(1)} %get-tuple-element.14), kind=kLoop, calls=%fused_computation.102 | loop fusion | flops 8192 | bytes 22528 | tf_op jit(solution)/shard_map/jit(_where)/select_n | solution.py:140
  35.7 1.3 %select_n.141 = bf16[16,512]{1,0:T(8,128)(2,1)} reshape(bf16[4,4,512]{2,1,0:T(4,128)(2,1)} %broadcast_select_fusion) | data formatting | bytes 32768 | tf_op jit(solution)/shard_map/jit(_where)/select_n | solution.py:140
  37.0 2.3 %fusion.129 = (f32[16]{0:T(128)}, f32[16,704]{1,0:T(8,128)}) fusion(pred[16,704]{1,0:T(8,128)(4,1)} %broadcast_in_dim.67, bf16[16,512]{1,0:T(8,128)(2,1)} %select_n.141, bf16[704,512]{1,0:T(8,128)(2,1)S(1)} %bitcast.37), kind=kOutput, calls=%fused_computation.207 | convolution fusion | flops 11568112 | bytes 793664 | tf_op jit(solution)/shard_map/dot_general | solution.py:142
  41.2 1.0 %fusion.57 = (f32[16]{0:T(128)S(1)}, bf16[16,704]{1,0:T(8,128)(2,1)S(1)}) fusion(f32[16,704]{1,0:T(8,128)} %get-tuple-element.24, f32[16]{0:T(128)S(1)} %sub.51), kind=kLoop, calls=%fused_computation.80 | loop fusion | flops 33776 | bytes 67712 | tf_op jit(solution)/shard_map/reduce_sum | solution.py:154
  42.6 0.9 %fusion.3 = bf16[4,512]{1,0:T(4,128)(2,1)S(1)} fusion(bf16[4,4,704]{2,1,0:T(4,128)(2,1)S(1)} %dot_general.28, bf16[704,512,1]{1,0,2:T(8,128)(2,1)S(1)} %bitcast.38, f32[4,4]{1,0:T(4,128)S(1)} %copy.31, f32[4,512]{1,0:T(4,128)} %get-tuple-element.13, f32[4,4]{1,0:T(4,128)S(1)} %copy.29, pred[4,512]{1,0:T(4,128)(4,1)} %iota_compare_fusion.1), kind=kOutput, calls=%fused_computation.12 | convolution fusion | flops 11573248 | bytes 757888 | tf_op jit(solution)/shard_map/dot_general | solution.py:155
  45.2 1.3 %collective-permute-start.4 = (f32[4,2048]{1,0:T(4,128)S(1)}, f32[4,2048]{1,0:T(4,128)S(1)}, u32[]{:S(2)}, u32[]{:S(2)}) collective-permute-start(f32[4,2048]{1,0:T(4,128)S(1)} %add.209), channel_id=1, source_target_pairs={{0,3},{1,2},{2,1},{3,0},{4,7},{5,6},{6,5},{7,4},{8,11},{9,10},{10,... | collective-permute-start | bytes 98312 | tf_op jit(solution)/shard_map/ppermute | solution.py:15
  46.5 2.1 %collective-permute-done.4 = f32[4,2048]{1,0:T(4,128)S(1)} collective-permute-done((f32[4,2048]{1,0:T(4,128)S(1)}, f32[4,2048]{1,0:T(4,128)S(1)}, u32[]{:S(2)}, u32[]{:S(2)}) %collective-permute-start.4) | collective-permute-done | bytes 32800 | tf_op jit(solution)/shard_map/ppermute | solution.py:15
  51.9 11.9 %collective-permute-start.10 = (bf16[32,512]{1,0:T(8,128)(2,1)S(1)}, bf16[32,512]{1,0:T(8,128)(2,1)S(1)}, u32[]{:S(2)}, u32[]{:S(2)}) collective-permute-start(bf16[32,512]{1,0:T(8,128)(2,1)S(1)} %slice.65), channel_id=1, source_target_pairs={{0,1},{1,0},{2,3},{3,2},{4,5},{5,4},{6,7},{7,6},{8,9},{9,8},{10,11... | collective-permute-start | bytes 98312 | tf_op jit(solution)/shard_map/ppermute | solution.py:15
  64.6 1.7 %convolution_convert_fusion.1 = bf16[32,1024]{1,0:T(8,128)(2,1)S(1)} fusion(bf16[1024,512]{1,0:T(8,128)(2,1)} %param.30, bf16[32,512]{1,0:T(8,128)(2,1)S(1)} %collective-permute-done.10, bf16[32,1024]{1,0:T(8,128)(2,1)S(1)} %pad_maximum_fusion.1, pred[]{:T(512)S(6)} %eq.144, s32[32]{0:T(128)S(1)} %copy-done.5, s32[32]{0:T(128)S(1)} %gather_fusion.1), kind=kOutput, calls=%fused_computation.4 | convolution fusion | flops 34669568 | bytes 1180673 | tf_op jit(solution)/shard_map/dot_general | solution.py:195
  66.8 0.9 %collective-permute-done.11 = bf16[32,1024]{1,0:T(8,128)(2,1)S(1)} collective-permute-done((bf16[32,1024]{1,0:T(8,128)(2,1)S(1)}, bf16[32,1024]{1,0:T(8,128)(2,1)S(1)}, u32[]{:S(2)}, u32[]{:S(2)}) %collective-permute-start.11) | collective-permute-done | bytes 65568 | tf_op jit(solution)/shard_map/ppermute | solution.py:15
  67.7 1.5 %collective-permute-start.12 = (bf16[32,1024]{1,0:T(8,128)(2,1)S(1)}, bf16[32,1024]{1,0:T(8,128)(2,1)S(1)}, u32[]{:S(2)}, u32[]{:S(2)}) collective-permute-start(bf16[32,1024]{1,0:T(8,128)(2,1)S(1)} %add_convert_fusion.1), channel_id=1, source_target_pairs={{0,3},{1,2},{2,1},{3,0},{4,7},{5,6},{6,5},{7,4},{8,11},{9,10},{10,... | collective-permute-start | bytes 196616 | tf_op jit(solution)/shard_map/ppermute | solution.py:15
  69.2 2.5 %collective-permute-done.12 = bf16[32,1024]{1,0:T(8,128)(2,1)S(1)} collective-permute-done((bf16[32,1024]{1,0:T(8,128)(2,1)S(1)}, bf16[32,1024]{1,0:T(8,128)(2,1)S(1)}, u32[]{:S(2)}, u32[]{:S(2)}) %collective-permute-start.12) | collective-permute-done | bytes 65568 | tf_op jit(solution)/shard_map/ppermute | solution.py:15
  71.7 1.7 %fusion.24 = f32[32,512]{1,0:T(8,128)S(1)} fusion(bf16[1024,512]{1,0:T(8,128)(2,1)} %param.32, bf16[32,1024]{1,0:T(8,128)(2,1)S(1)} %collective-permute-done.12, bf16[32,1024]{1,0:T(8,128)(2,1)S(1)} %add_convert_fusion.1, f32[1024]{0:T(1024)S(1)} %convert_element_type.138), kind=kOutput, calls=%fused_computation.45 | convolution fusion | flops 35880960 | bytes 1249280 | tf_op jit(solution)/shard_map/dot_general | solution.py:200
  73.6 1.6 %collective-permute-start.13 = (f32[16,512]{1,0:T(8,128)S(1)}, f32[16,512]{1,0:T(8,128)S(1)}, u32[]{:S(2)}, u32[]{:S(2)}) collective-permute-start(f32[16,512]{1,0:T(8,128)S(1)} %slice.67), channel_id=1, source_target_pairs={{0,4},{4,0},{8,12},{12,8},{16,20},{20,16},{24,28},{28,24},{1,5},{5... | collective-permute-start | bytes 98312 | tf_op jit(solution)/shard_map/ppermute | solution.py:15
  75.2 2.4 %collective-permute-done.13 = f32[16,512]{1,0:T(8,128)S(1)} collective-permute-done((f32[16,512]{1,0:T(8,128)S(1)}, f32[16,512]{1,0:T(8,128)S(1)}, u32[]{:S(2)}, u32[]{:S(2)}) %collective-permute-start.13) | collective-permute-done | bytes 32800 | tf_op jit(solution)/shard_map/ppermute | solution.py:15
  78.1 3.3 %collective-permute-done.14 = f32[8,512]{1,0:T(8,128)S(1)} collective-permute-done((f32[8,512]{1,0:T(8,128)S(1)}, f32[8,512]{1,0:T(8,128)S(1)}, u32[]{:S(2)}, u32[]{:S(2)}) %collective-permute-start.14) | collective-permute-done | bytes 16416 | tf_op jit(solution)/shard_map/ppermute | solution.py:15
  81.8 4.2 %collective-permute-done.15 = f32[4,512]{1,0:T(4,128)S(1)} collective-permute-done((f32[4,512]{1,0:T(4,128)S(1)}, f32[4,512]{1,0:T(4,128)S(1)}, u32[]{:S(2)}, u32[]{:S(2)}) %collective-permute-start.15) | collective-permute-done | bytes 8224 | tf_op jit(solution)/shard_map/ppermute | solution.py:15
  (104 shorter events, 21.9 us)
Async XLA Ops:
  0.0 43.6 %copy-start = (bf16[512,2048]{1,0:T(8,128)(2,1)S(1)}, bf16[512,2048]{1,0:T(8,128)(2,1)}, u32[]{:S(2)}) copy-start(bf16[512,2048]{1,0:T(8,128)(2,1)} %param.26) | copy-start | bytes 6291460
  5.3 13.7 %collective-permute-start = (bf16[4,2048]{1,0:T(4,128)(2,1)}, bf16[4,2048]{1,0:T(4,128)(2,1)}, u32[]{:S(2)}, u32[]{:S(2)}) collective-permute-start(bf16[4,2048]{1,0:T(4,128)(2,1)} %constant_dynamic-update-slice_fusion), channel_id=1, source_target_pairs={{0,16},{4,20},{8,24},{12,28},{16,0},{20,4},{24,8},{28,12},{1,17},{... | collective-permute-start | bytes 49160 | tf_op jit(solution)/shard_map/ppermute | solution.py:15
  9.3 20.2 %collective-permute-start.5 = (bf16[512]{0:T(512)(128)(2,1)}, bf16[512]{0:T(512)(128)(2,1)}, u32[]{:S(2)}, u32[]{:S(2)}) collective-permute-start(bf16[512]{0:T(512)(128)(2,1)} %param.28), channel_id=1, source_target_pairs={{0,1},{1,0},{2,3},{3,2},{4,5},{5,4},{6,7},{7,6},{8,9},{9,8},{10,11... | collective-permute-start | bytes 3080 | tf_op jit(solution)/shard_map/ppermute | solution.py:15
  9.3 20.2 %collective-permute-start.6 = (bf16[512]{0:T(512)(128)(2,1)}, bf16[512]{0:T(512)(128)(2,1)}, u32[]{:S(2)}, u32[]{:S(2)}) collective-permute-start(bf16[512]{0:T(512)(128)(2,1)} %param.29), channel_id=1, source_target_pairs={{0,1},{1,0},{2,3},{3,2},{4,5},{5,4},{6,7},{7,6},{8,9},{9,8},{10,11... | collective-permute-start | bytes 3080 | tf_op jit(solution)/shard_map/ppermute | solution.py:15
  20.3 6.8 %collective-permute-start.1 = (bf16[8,2048]{1,0:T(8,128)(2,1)}, bf16[8,2048]{1,0:T(8,128)(2,1)}, u32[]{:S(2)}, u32[]{:S(2)}) collective-permute-start(bf16[8,2048]{1,0:T(8,128)(2,1)} %pad_maximum_fusion.2), channel_id=1, source_target_pairs={{0,8},{4,12},{8,0},{12,4},{16,24},{20,28},{24,16},{28,20},{1,9},{5... | collective-permute-start | bytes 98312 | tf_op jit(solution)/shard_map/ppermute | solution.py:15
  27.9 4.3 %collective-permute-start.2 = (bf16[16,2048]{1,0:T(8,128)(2,1)S(1)}, bf16[16,2048]{1,0:T(8,128)(2,1)S(1)}, u32[]{:S(2)}, u32[]{:S(2)}) collective-permute-start(bf16[16,2048]{1,0:T(8,128)(2,1)S(1)} %pad_maximum_fusion), channel_id=1, source_target_pairs={{0,4},{4,0},{8,12},{12,8},{16,20},{20,16},{24,28},{28,24},{1,5},{5... | collective-permute-start | bytes 196616 | tf_op jit(solution)/shard_map/ppermute | solution.py:15
  33.2 0.6 copy-start.2
  37.0 13.4 %copy-start.1 = (s32[32]{0:T(128)S(1)}, s32[32]{0:T(128)}, u32[]{:S(2)}) copy-start(s32[32]{0:T(128)} %param.34) | copy-start | bytes 388
  39.4 7.2 %copy-start.3 = (bf16[512]{0:T(512)(128)(2,1)S(1)}, bf16[512]{0:T(512)(128)(2,1)}, u32[]{:S(2)}) copy-start(bf16[512]{0:T(512)(128)(2,1)} %get-tuple-element.21) | copy-start | bytes 3076
  39.4 7.2 %copy-start.4 = (bf16[512]{0:T(512)(128)(2,1)S(1)}, bf16[512]{0:T(512)(128)(2,1)}, u32[]{:S(2)}) copy-start(bf16[512]{0:T(512)(128)(2,1)} %get-tuple-element.22) | copy-start | bytes 3076
  39.4 10.4 %copy-start.8 = (s32[32,1]{0,1:T(1,128)S(1)}, s32[32,1]{0,1:T(1,128)}, u32[]{:S(2)}) copy-start(s32[32,1]{0,1:T(1,128)} %add.195) | copy-start | bytes 388
  42.6 22.0 %copy-start.5 = (s32[32]{0:T(128)S(1)}, s32[32]{0:T(128)}, u32[]{:S(2)}) copy-start(s32[32]{0:T(128)} %add.198) | copy-start | bytes 388
  43.6 23.2 %copy-start.6 = (bf16[1024]{0:T(1024)(128)(2,1)S(1)}, bf16[1024]{0:T(1024)(128)(2,1)}, u32[]{:S(2)}) copy-start(bf16[1024]{0:T(1024)(128)(2,1)} %param.31) | copy-start | bytes 6148
  44.0 1.2 %collective-permute-start.3 = (f32[4,2048]{1,0:T(4,128)S(1)}, f32[4,2048]{1,0:T(4,128)S(1)}, u32[]{:S(2)}, u32[]{:S(2)}) collective-permute-start(f32[4,2048]{1,0:T(4,128)S(1)} %convolution_add_fusion), channel_id=1, source_target_pairs={{0,1},{1,0},{2,3},{3,2},{4,5},{5,4},{6,7},{7,6},{8,9},{9,8},{10,11... | collective-permute-start | bytes 98312 | tf_op jit(solution)/shard_map/ppermute | solution.py:15
  45.2 3.4 %collective-permute-start.4 = (f32[4,2048]{1,0:T(4,128)S(1)}, f32[4,2048]{1,0:T(4,128)S(1)}, u32[]{:S(2)}, u32[]{:S(2)}) collective-permute-start(f32[4,2048]{1,0:T(4,128)S(1)} %add.209), channel_id=1, source_target_pairs={{0,3},{1,2},{2,1},{3,0},{4,7},{5,6},{6,5},{7,4},{8,11},{9,10},{10,... | collective-permute-start | bytes 98312 | tf_op jit(solution)/shard_map/ppermute | solution.py:15
  49.0 0.7 collective-permute-start.7
  49.8 1.4 %collective-permute-start.8 = (bf16[8,1024]{1,0:T(8,128)(2,1)S(1)}, bf16[8,1024]{1,0:T(8,128)(2,1)S(1)}, u32[]{:S(2)}, u32[]{:S(2)}) collective-permute-start(bf16[8,1024]{1,0:T(8,128)(2,1)S(1)} %pad_maximum_fusion.4), channel_id=1, source_target_pairs={{0,0},{1,9},{2,2},{3,11},{4,4},{5,13},{6,6},{7,15},{8,8},{9,1},{10... | collective-permute-start | bytes 49160 | tf_op jit(solution)/shard_map/ppermute | solution.py:72
  51.2 0.7 collective-permute-start.9
  51.9 12.7 %collective-permute-start.10 = (bf16[32,512]{1,0:T(8,128)(2,1)S(1)}, bf16[32,512]{1,0:T(8,128)(2,1)S(1)}, u32[]{:S(2)}, u32[]{:S(2)}) collective-permute-start(bf16[32,512]{1,0:T(8,128)(2,1)S(1)} %slice.65), channel_id=1, source_target_pairs={{0,1},{1,0},{2,3},{3,2},{4,5},{5,4},{6,7},{7,6},{8,9},{9,8},{10,11... | collective-permute-start | bytes 98312 | tf_op jit(solution)/shard_map/ppermute | solution.py:15
  66.4 1.3 %collective-permute-start.11 = (bf16[32,1024]{1,0:T(8,128)(2,1)S(1)}, bf16[32,1024]{1,0:T(8,128)(2,1)S(1)}, u32[]{:S(2)}, u32[]{:S(2)}) collective-permute-start(bf16[32,1024]{1,0:T(8,128)(2,1)S(1)} %convolution_convert_fusion.1), channel_id=1, source_target_pairs={{0,1},{1,0},{2,3},{3,2},{4,5},{5,4},{6,7},{7,6},{8,9},{9,8},{10,11... | collective-permute-start | bytes 196616 | tf_op jit(solution)/shard_map/ppermute | solution.py:15
  66.8 15.0 %copy-start.7 = (bf16[512]{0:T(512)(128)(2,1)S(1)}, bf16[512]{0:T(512)(128)(2,1)}, u32[]{:S(2)}) copy-start(bf16[512]{0:T(512)(128)(2,1)} %param.33) | copy-start | bytes 3076
  67.7 4.0 %collective-permute-start.12 = (bf16[32,1024]{1,0:T(8,128)(2,1)S(1)}, bf16[32,1024]{1,0:T(8,128)(2,1)S(1)}, u32[]{:S(2)}, u32[]{:S(2)}) collective-permute-start(bf16[32,1024]{1,0:T(8,128)(2,1)S(1)} %add_convert_fusion.1), channel_id=1, source_target_pairs={{0,3},{1,2},{2,1},{3,0},{4,7},{5,6},{6,5},{7,4},{8,11},{9,10},{10,... | collective-permute-start | bytes 196616 | tf_op jit(solution)/shard_map/ppermute | solution.py:15
  73.6 4.0 %collective-permute-start.13 = (f32[16,512]{1,0:T(8,128)S(1)}, f32[16,512]{1,0:T(8,128)S(1)}, u32[]{:S(2)}, u32[]{:S(2)}) collective-permute-start(f32[16,512]{1,0:T(8,128)S(1)} %slice.67), channel_id=1, source_target_pairs={{0,4},{4,0},{8,12},{12,8},{16,20},{20,16},{24,28},{28,24},{1,5},{5... | collective-permute-start | bytes 98312 | tf_op jit(solution)/shard_map/ppermute | solution.py:15
  77.6 3.8 %collective-permute-start.14 = (f32[8,512]{1,0:T(8,128)S(1)}, f32[8,512]{1,0:T(8,128)S(1)}, u32[]{:S(2)}, u32[]{:S(2)}) collective-permute-start(f32[8,512]{1,0:T(8,128)S(1)} %slice.69), channel_id=1, source_target_pairs={{0,8},{4,12},{8,0},{12,4},{16,24},{20,28},{24,16},{28,20},{1,9},{5... | collective-permute-start | bytes 49160 | tf_op jit(solution)/shard_map/ppermute | solution.py:15
  81.4 4.6 %collective-permute-start.15 = (f32[4,512]{1,0:T(4,128)S(1)}, f32[4,512]{1,0:T(4,128)S(1)}, u32[]{:S(2)}, u32[]{:S(2)}) collective-permute-start(f32[4,512]{1,0:T(4,128)S(1)} %slice.71), channel_id=1, source_target_pairs={{0,16},{4,20},{8,24},{12,28},{16,0},{20,4},{24,8},{28,12},{1,17},{... | collective-permute-start | bytes 24584 | tf_op jit(solution)/shard_map/ppermute | solution.py:15

commit v6 on v3

--- a/solution.py
+++ b/solution.py
@@ -1,13 +1,306 @@
+import functools
 import math
 
 import jax
 import jax.numpy as jnp
 from jax import lax
+from jax.experimental import pallas as pl
+from jax.experimental.pallas import tpu as pltpu
 from jax.sharding import PartitionSpec as P
 
 HEAD_DIM = 128
 NORM_EPS = 1e-05
 PAIRWISE = 16
+REQ, TP = 8, 4
+F32, BF16, I32 = jnp.float32, jnp.bfloat16, jnp.int32
+VMEM = pl.BlockSpec(memory_space=pltpu.VMEM)
+SMEM = pl.BlockSpec(memory_space=pltpu.SMEM)
+HBM = pl.BlockSpec(memory_space=pltpu.HBM)
+
+
+def iota(shape, dim):
+    return lax.broadcasted_iota(I32, shape, dim)
+
+
+def onto_mxu(a, b):
+    return jnp.dot(a, b, preferred_element_type=F32)
+
+
+def nt_dot(a, b):
+    return lax.dot_general(a, b, (((1,), (1,)), ((), ())), preferred_element_type=F32)
+
+
+def hot(condition):
+    return jnp.where(condition, 1.0, 0.0).astype(BF16)
+
+
+def pile(parts):
+    height = sum(p.shape[0] for p in parts)
+    at, piled = 0, 0
+    for p in parts:
+        around = ((at, height - at - p.shape[0]),) + ((0, 0),) * (p.ndim - 1)
+        piled += jnp.pad(p, around)
+        at += p.shape[0]
+    return piled
+
+
+def row(vectors, i, cols):
+    return vectors[i * cols : (i + 1) * cols][None, :]
+
+
+def pack_kernel(place, numbers, fields_in, out):
+    count = numbers.shape[1]
+    rows = count // REQ
+    fields = 4
+    cols = fields_in.shape[1]
+    shape = (REQ * fields, fields * rows)
+    down, across = iota(shape, 0), iota(shape, 1)
+    here = (count, fields * rows)
+    of_mine = hot(iota(here, 0) == place[0] * rows + iota(here, 1) % rows)
+    owner_of = onto_mxu(numbers[0:1, :].astype(F32).astype(BF16), of_mine).astype(I32)
+    pick = hot((down % fields == across // rows) & (owner_of == down // fields))
+    blocks = onto_mxu(pick, fields_in[...].astype(BF16)).astype(BF16)
+    for d in range(REQ):
+        block = blocks[d * fields : (d + 1) * fields]
+        out[d, :fields, :] = block[:, : cols // 2]
+        out[d, fields:, :] = block[:, cols // 2 :]
+
+
+def index_kernel(
+    place, numbers, pool, pick, valid, arrange, arrange_own, *, page_len
+):
+    del pool
+    owner, order, lengths = (numbers[i : i + 1, :] for i in range(3))
+    table = numbers[8:, :]
+    me = place[0]
+    count = owner.shape[1]
+    rows = count // REQ
+    square = (count, count)
+    down, across = iota(square, 0), iota(square, 1)
+    owner_row = owner
+    same_place = down == across
+    owner_col = jnp.sum(jnp.where(same_place, owner_row, 0), axis=1, keepdims=True)
+    order_col = jnp.sum(jnp.where(same_place, order, 0), axis=1, keepdims=True)
+    same_owner = owner_col == owner_row
+    rank_row = jnp.sum(jnp.where(same_owner & (down < across), 1, 0), axis=0, keepdims=True)
+    rank_col = jnp.sum(jnp.where(same_owner & (across < down), 1, 0), axis=1, keepdims=True)
+
+    shape = pick.shape
+    down_p, across_p = iota(shape, 0), iota(shape, 1)
+    down_i = iota((shape[0], count), 0)
+    mine = hot((owner_row == me) & (rank_row == down_i % rows))
+    came = hot(iota((count, shape[1]), 0) // rows == iota((count, shape[1]), 1) // (2 * rows))
+    from_there = onto_mxu(mine, came)
+    pick[...] = hot((from_there > 0.5) & (down_p // rows == across_p % rows))
+
+    shape = valid.shape
+    slot = iota((shape[0], count), 0) % rows
+    mine_v = hot((owner_row == me) & (rank_row == slot))
+    table_v = nt_dot(mine_v, table.astype(F32).astype(BF16)).astype(I32)
+    length_v = jnp.sum(jnp.where(mine_v > 0.5, lengths, 0), axis=1, keepdims=True)
+    position = iota(shape, 1)
+    page, within = position // page_len, position % page_len
+    seen = jnp.zeros(shape, F32)
+    for j in range(table.shape[0]):
+        inside = (table_v[:, j : j + 1] == page) & (within + j * page_len < length_v)
+        seen = jnp.where(inside, 1.0, seen)
+    valid[...] = seen
+
+    ordered = hot(order_col == across)
+    shape = arrange.shape
+    across_a = iota(shape, 1)
+    holds = hot((owner_col == across_a // (2 * rows)) & (rank_col == across_a % rows))
+    arrange[...] = onto_mxu(ordered, holds).astype(BF16)
+    here = hot((owner_col == me) & (rank_col == iota(arrange_own.shape, 1)))
+    arrange_own[...] = onto_mxu(ordered, here).astype(BF16)
+
+
+def attention_kernel(place, arrived, pick, valid, vectors, pool, weight, partial, *, rows):
+    half = arrived.shape[2]
+    cols = 2 * half
+    heads = cols // HEAD_DIM
+    scale = 1.0 / math.sqrt(HEAD_DIM)
+    came = arrived[...].reshape(-1, half)
+    which = (iota(pick.shape, 1) // rows) % 2
+    chosen = pick[...].astype(F32)
+    own = jnp.concatenate(
+        [onto_mxu(jnp.where(which == i, chosen, 0.0).astype(BF16), came) for i in range(2)], axis=1
+    )
+    query, key, value, resid = (own[i * rows : (i + 1) * rows] for i in range(4))
+
+    def tile(x):
+        return jnp.concatenate([x] * heads, axis=0)
+
+    shape = (heads * rows, cols)
+    in_head = iota(shape, 0) // rows == iota(shape, 1) // HEAD_DIM
+    wide = jnp.where(in_head, tile(query), 0.0)
+    positions = valid.shape[1]
+    self_score = jnp.sum(wide * tile(key), axis=1, keepdims=True) * scale
+    scores = nt_dot(wide.astype(BF16), pool[0].reshape(positions, cols)) * scale
+    scores = jnp.where(valid[...] > 0.5, scores, -jnp.inf)
+    top = jnp.maximum(jnp.max(scores, axis=1, keepdims=True), self_score)
+    weights = jnp.exp(scores - top)
+    self_weight = jnp.exp(self_score - top)
+    total = jnp.sum(weights, axis=1, keepdims=True) + self_weight
+    numer = onto_mxu(weights.astype(BF16), pool[1].reshape(positions, cols))
+    numer = numer + self_weight.astype(BF16).astype(F32) * tile(value)
+    numer = jnp.where(in_head, numer / total, 0.0)
+    attn = sum(numer[i * rows : (i + 1) * rows] for i in range(heads))
+    attn = jnp.concatenate([attn, jnp.zeros_like(attn)], axis=0).astype(BF16)
+    partial[...] = onto_mxu(attn, weight[...])[:rows]
+    mine = pl.ds(pl.multiple_of(place[1] * cols, cols), cols)
+    partial[:, mine] += resid + row(vectors, 0, cols)
+
+
+def norm_kernel(place, near, far, vectors, other, blocks, stream_own):
+    stream = (near[...] + far[...]).astype(BF16).astype(F32)
+    rows, width = stream.shape
+    cols = width // TP
+    mean = jnp.sum(stream, axis=1, keepdims=True) / width
+    var = jnp.sum((stream - mean) ** 2, axis=1, keepdims=True) / width
+    inverse = lax.rsqrt(var + NORM_EPS)
+    core, chip = place[1] % 2, place[1] // 2
+    parts = []
+    for x in range(2):
+        even, odd = (stream[:, (2 * x + c) * cols : (2 * x + c + 1) * cols] for c in range(2))
+        part = jnp.where(core == 0, even, odd)
+        gain, bias = (jnp.where(chip == x, row(vectors, i, cols), row(other, i, cols)) for i in (1, 2))
+        parts.append((part, (part - mean) * inverse * gain + bias))
+    stream_own[...] = jnp.where(chip == 0, parts[0][0], parts[1][0]).astype(BF16)
+    block = jnp.concatenate([parts[0][1], parts[1][1]], axis=0).astype(BF16)
+    for d in range(REQ):
+        blocks[d] = block
+
+
+def up_kernel(place, rows_in, arrange, weight, moved, out, *, rows):
+    came = rows_in[...].reshape(-1, rows_in.shape[2])
+    which = (iota(arrange.shape, 1) // rows) % 2
+    chosen = arrange[...].astype(F32)
+    chip = place[1] // 2
+
+    def ordered(x):
+        return onto_mxu(jnp.where(which == x, chosen, 0.0).astype(BF16), came).astype(BF16)
+
+    hidden = nt_dot(ordered(chip), weight[...]) + nt_dot(ordered(1 - chip), moved[...])
+    out[...] = hidden.astype(BF16)
+
+
+def down_kernel(near, far, vectors, weight, arrange_own, stream_own, out):
+    hidden = near[...].astype(F32) + far[...].astype(F32)
+    hidden = hidden + vectors[vectors.shape[0] - hidden.shape[1] :][None, :]
+    activated = (0.5 * hidden * (1.0 + lax.erf(hidden * math.sqrt(0.5)))).astype(BF16)
+    feed = onto_mxu(activated, weight[...]) + onto_mxu(arrange_own[...], stream_own[...])
+    rows = out.shape[1]
+    for d in range(REQ):
+        out[d] = feed[d * rows : (d + 1) * rows]
+
+
+def call(kernel, shapes, specs, args, scratch=(), room=16, **fixed):
+    moved = sum(a.size * a.dtype.itemsize for a in args)
+    return pl.pallas_call(
+        functools.partial(kernel, **fixed) if fixed else kernel,
+        out_shape=shapes,
+        in_specs=specs,
+        out_specs=[VMEM] * len(shapes),
+        scratch_shapes=scratch,
+        compiler_params=pltpu.CompilerParams(vmem_limit_bytes=room * 2**20),
+        cost_estimate=pl.CostEstimate(flops=0, bytes_accessed=moved, transcendentals=0),
+    )(*args)
+
+
+def trade(blocks):
+    return lax.all_to_all(blocks, "req", 0, 0, tiled=True)
+
+
+def on_pairs(
+    query,
+    key_new,
+    value_new,
+    resid,
+    lengths,
+    owner,
+    page_table,
+    kv_pool,
+    out_weight,
+    out_bias,
+    norm_gain,
+    norm_bias,
+    up_weight_t,
+    up_bias,
+    down_weight,
+    down_bias,
+    order,
+):
+    rows, cols = query.shape
+    width = cols * TP
+    pool_pages, page_len = kv_pool.shape[1], kv_pool.shape[2]
+    positions = pool_pages * page_len
+    heads = cols // HEAD_DIM
+    count = owner.shape[0]
+    hidden = up_bias.shape[0]
+
+    def arr(shape, dtype=BF16):
+        return jax.ShapeDtypeStruct(shape, dtype)
+
+    me, me_tp = lax.axis_index("req").astype(I32), lax.axis_index("tp").astype(I32)
+    place = jnp.stack([me, me_tp])
+
+    numbers = pile(
+        [owner[None, :], order[None, :], lengths[None, :], jnp.zeros((5, count), I32), page_table.T]
+    )
+    fields = pile([x.astype(F32) for x in (query, key_new, value_new, resid)])
+    (packed,) = call(
+        pack_kernel,
+        [arr((REQ, 8, cols // 2))],
+        [SMEM, VMEM, VMEM],
+        [place, numbers, fields],
+    )
+    up_moved = swap(up_weight_t, "tp", 2)
+    arrived = trade(packed)
+    vectors = pile([x.astype(F32) for x in (out_bias, norm_gain, norm_bias, down_bias, up_bias)])
+    pick, valid, arrange, arrange_own = call(
+        index_kernel,
+        [
+            arr((4 * rows, 2 * count)),
+            arr((heads * rows, positions), F32),
+            arr((count, 2 * count)),
+            arr((count, rows)),
+        ],
+        [SMEM, VMEM, HBM],
+        [place, numbers, kv_pool],
+        page_len=page_len,
+    )
+    other = swap(vectors, "tp", 2)
+
+    (partial,) = call(
+        attention_kernel,
+        [arr((rows, width), F32)],
+        [SMEM] + [VMEM] * 6,
+        [place, arrived, pick, valid, vectors, kv_pool, out_weight],
+        rows=rows,
+    )
+    pair = partial + swap(partial, "tp", 1)
+    blocks, stream_own = call(
+        norm_kernel,
+        [arr((REQ, 2 * rows, cols)), arr((rows, cols))],
+        [SMEM] + [VMEM] * 4,
+        [place, pair, swap(pair, "tp", 3), vectors, other],
+    )
+
+    (part,) = call(
+        up_kernel,
+        [arr((count, hidden))],
+        [SMEM] + [VMEM] * 4,
+        [place, trade(blocks), arrange, up_weight_t, up_moved],
+        rows=rows,
+    )
+    (feed,) = call(
+        down_kernel,
+        [arr((REQ, rows, cols), F32)],
+        [VMEM] * 6,
+        [part, swap(part, "tp", 1), vectors, down_weight, arrange_own, stream_own],
+    )
+    return (jnp.sum(trade(feed), axis=0) + down_bias.astype(F32)[None, :]).astype(BF16)
 
 
 def swap(x, axis, step):
@@ -59,7 +352,7 @@
     return x
 
 
-def per_device(
+def on_any_mesh(
     query,
     key_new,
     value_new,
@@ -179,6 +472,8 @@
 
 
 def solution(mesh):
+    pairs = mesh.shape["req"] == REQ and mesh.shape["tp"] == TP
+    per_device = on_pairs if pairs else on_any_mesh
     in_specs = (
         P("req", "tp"),
         P("req", "tp"),

time: 63.3 us -> 54.1 us (0.85)
  blocking collectives: 0 us -> 22.1 us
  waiting for transfers between devices: 28.7 us -> 7.67 us
  Pallas kernels: 0 us -> 6.43 us
  starting transfers between devices: 17 us -> 10.7 us
  matrix products: 4.81 us -> 0 us
  local copies, waits for them, and re-layouts: 7.77 us -> 3.04 us
  other arithmetic: 4.36 us -> 3.67 us
    ppermute x13 -> x5, waiting for transfers between devices: 28.7 us -> 4.77 us  [swap(): return lax.ppermute(x, axis, [(i, i ^ step) for i in range(n)])]
    all_to_all x0 -> x2, blocking collectives: none -> 22.1 us  [trade(): return lax.all_to_all(blocks, 'req', 0, 0, tiled=True)]
    ppermute x13 -> x5, starting transfers between devices: 17 us -> 4.87 us  [swap(): return lax.ppermute(x, axis, [(i, i ^ step) for i in range(n)])]
    pallas_call x0 -> x6, Pallas kernels: none -> 6.43 us  [call(): pl.pallas_call(functools.partial(kernel, **fixed) if fixed else kernel, o...]
    all_to_all x0 -> x1, starting transfers between devices: none -> 5.83 us  [trade(): return lax.all_to_all(blocks, 'req', 0, 0, tiled=True)]
    dot_general x7 -> x0, matrix products: 4.81 us -> none  [the longest x1 1.69 us: per_device(): feed = jnp.dot(activated, down_weight, preferred_element_type=f32)]
    all_to_all x0 -> x1, waiting for transfers between devices: none -> 2.9 us  [trade(): return lax.all_to_all(blocks, 'req', 0, 0, tiled=True)]
    slice x4 -> x0, local copies, waits for them, and re-layouts: 2.32 us -> none  [the longest x1 2.3 us: per_device(): values = kv_pool[1].reshape(positions, cols)]
  transfers between devices with their start and end apart: 13 -> 6, of which waited for: 12 -> 4; matrix products, arithmetic and copies ran while one was open for 11% -> 6% of each run, Pallas kernels for 0% -> 9%
where the time goes in v6:
time: 54.1 us; the launch traced here: 53.6 us
  blocking collectives  22.1 us (41%)
  starting transfers between devices  10.7 us (20%)
  waiting for transfers between devices  7.67 us (14%)
  Pallas kernels  6.43 us (12%)
  other arithmetic  3.67 us (7%)
  local copies, waits for them, and re-layouts  3.04 us (6%)
    all_to_all x2, blocking collectives, trade(): return lax.all_to_all(blocks, 'req', 0, 0, tiled=True)  22.1 us
    pallas_call x6, Pallas kernels, call(): pl.pallas_call(functools.partial(kernel, **fixed) if fixed else kernel, o...  6.43 us
    all_to_all x1, starting transfers between devices, trade(): return lax.all_to_all(blocks, 'req', 0, 0, tiled=True)  5.83 us
    ppermute x5, starting transfers between devices, swap(): return lax.ppermute(x, axis, [(i, i ^ step) for i in range(n)])  4.87 us
    ppermute x5, waiting for transfers between devices, swap(): return lax.ppermute(x, axis, [(i, i ^ step) for i in range(n)])  4.77 us
    unnamed x10, local copies, waits for them, and re-layouts  2.96 us
    all_to_all x1, waiting for transfers between devices, trade(): return lax.all_to_all(blocks, 'req', 0, 0, tiled=True)  2.9 us
    add x3, other arithmetic, pile(): piled += jnp.pad(p, around)  2.28 us
  transfers between devices with their start and end apart: 6, of which 4 were waited for; matrix products, arithmetic and copies ran while one was open for 6% of the time, Pallas kernels for 9%

profile of v6, /device:TPU:0, one launch (start us, length us, event | category | flops | bytes accessed | tf_op | source)
XLA Modules:
  0.0 53.6 jit_solution(5036519857912537738)
XLA Ops:
  0.0 2.9 %collective-permute-start.3 = (bf16[1024,512]{1,0:T(8,128)(2,1)}, bf16[1024,512]{1,0:T(8,128)(2,1)S(1)}, u32[]{:S(2)}, u32[]{:S(2)}) collective-permute-start(bf16[1024,512]{1,0:T(8,128)(2,1)} %weight.4), channel_id=1, source_target_pairs={{0,2},{1,3},{2,0},{3,1},{4,6},{5,7},{6,4},{7,5},{8,10},{9,11},{10,... | collective-permute-start | bytes 3145736 | tf_op jit(solution)/shard_map/ppermute | solution.py:308
  2.9 0.1 pad.85
  3.0 0.1 pad_add_fusion.1.place
  3.1 0.8 %convert_add_fusion.fields_in = f32[16,512]{1,0:T(8,128)S(1)} fusion(bf16[4,512]{1,0:T(4,128)(2,1)} %param.20, bf16[4,512]{1,0:T(4,128)(2,1)} %param.19, bf16[4,512]{1,0:T(4,128)(2,1)} %param.18, bf16[4,512]{1,0:T(4,128)(2,1)} %param.17), kind=kLoop, calls=%fused_computation | loop fusion | flops 57344 | bytes 49152 | tf_op jit(solution)/shard_map/add | solution.py:42
  3.8 0.8 %pad_add_fusion.numbers = s32[24,32]{1,0:T(8,128)S(1)} fusion(s32[16,32]{1,0:T(8,128)} %bitcast.6, s32[1,32]{1,0:T(1,128)} %bitcast.7, s32[1,32]{1,0:T(1,128)} %bitcast.8, s32[1,32]{1,0:T(1,128)} %bitcast.9, s32[24]{0:T(128)S(1)} %pad.85), kind=kLoop, calls=%fused_computation.2 | loop fusion | flops 3072 | bytes 5600 | tf_op jit(solution)/shard_map/add | solution.py:42
  4.6 1.4 %shard_map.163 = bf16[8,8,256]{2,1,0:T(8,128)(2,1)} custom-call(s32[2]{0:T(128)S(1)} %pad_add_fusion.1.place, s32[24,32]{1,0:T(8,128)S(1)} %pad_add_fusion.numbers, f32[16,512]{1,0:T(8,128)S(1)} %convert_add_fusion.fields_in), custom_call_target="tpu_custom_call" | custom-call | bytes 35848 | tf_op jit(solution)/shard_map/pallas_call | solution.py:200
  6.0 5.8 %all-to-all-start = ((bf16[8,8,256]{2,1,0:T(8,128)(2,1)}), bf16[8,8,256]{2,1,0:T(8,128)(2,1)S(1)}, u32[]{:S(2)}, u32[]{:S(2)}) async-start(bf16[8,8,256]{2,1,0:T(8,128)(2,1)} %shard_map.163), calls=%async_computation | async-start | bytes 65536 | tf_op jit(solution)/shard_map/all_to_all | solution.py:212
  11.9 0.7 %convert_element_type.17 = f32[512]{0:T(512)S(1)} convert(bf16[512]{0:T(512)(128)(2,1)} %param.32) | non-fusion elementwise | flops 512 | bytes 3072 | tf_op jit(solution)/shard_map/convert_element_type | solution.py:260
  12.6 1.4 %copy-done = bf16[2,22,32,512]{3,2,1,0:T(8,128)(2,1)S(1)} copy-done((bf16[2,22,32,512]{3,2,1,0:T(8,128)(2,1)S(1)}, bf16[2,22,32,512]{3,2,1,0:T(8,128)(2,1)}, u32[]{:S(2)}) %copy-start) | copy-done | bytes 1441816
  13.9 1.0 %shard_map.164 = (bf16[16,64]{1,0:T(8,128)(2,1)S(1)}, f32[16,704]{1,0:T(8,128)S(1)}, bf16[32,64]{1,0:T(8,128)(2,1)S(1)}, bf16[32,4]{1,0:T(8,128)(2,1)S(1)}) custom-call(s32[2]{0:T(128)S(1)} %pad_add_fusion.1.place, s32[24,32]{1,0:T(8,128)S(1)} %pad_add_fusion.numbers, bf16[2,22,32,512]{3,2,1,0:T(8,128)(2,1)S(1)} %copy-done), custom_call_target="tpu_custom_call" | custom-call | bytes 1444872 | tf_op jit(solution)/shard_map/pallas_call | solution.py:200
  14.9 0.7 %convert_add_fusion.1.vectors = f32[3072]{0:T(1024)S(1)} fusion(f32[512]{0:T(512)S(1)} %convert_element_type.17, bf16[1024]{0:T(1024)(128)(2,1)} %param.30, bf16[512]{0:T(512)(128)(2,1)} %param.28, bf16[512]{0:T(512)(128)(2,1)} %param.27, bf16[512]{0:T(512)(128)(2,1)} %param.26), kind=kLoop, calls=%fused_computation.1 | loop fusion | flops 24576 | bytes 19456 | tf_op jit(solution)/shard_map/add | solution.py:42
  15.7 2.9 %all-to-all-done.arrived = bf16[8,8,256]{2,1,0:T(8,128)(2,1)S(1)} async-done(((bf16[8,8,256]{2,1,0:T(8,128)(2,1)}), bf16[8,8,256]{2,1,0:T(8,128)(2,1)S(1)}, u32[]{:S(2)}, u32[]{:S(2)}) %all-to-all-start) | async-done | bytes 32800 | tf_op jit(solution)/shard_map/all_to_all | solution.py:212
  18.6 0.0 copy-done.1
  18.6 1.6 %copy-done.2 = bf16[512,2048]{1,0:T(8,128)(2,1)S(1)} copy-done((bf16[512,2048]{1,0:T(8,128)(2,1)S(1)}, bf16[512,2048]{1,0:T(8,128)(2,1)}, u32[]{:S(2)}) %copy-start.2) | copy-done | bytes 2097176
  20.2 1.7 %shard_map.165 = f32[4,2048]{1,0:T(4,128)S(1)} custom-call(s32[2]{0:T(128)S(1)} %pad_add_fusion.1.place, bf16[8,8,256]{2,1,0:T(8,128)(2,1)S(1)} %all-to-all-done.arrived, bf16[16,64]{1,0:T(8,128)(2,1)S(1)} %get-tuple-element.11.pick, f32[16,704]{1,0:T(8,128)S(1)} %get-tuple-element.12.valid, f32[3072]{0:T(1024)S(1)} %convert_add_fusion.1.vectors, ...), custom_call_target="tpu_custom_call" | custom-call | bytes 3631112 | tf_op jit(solution)/shard_map/pallas_call | solution.py:200
  21.8 0.0 collective-permute-start
  21.9 1.2 %collective-permute-done = f32[4,2048]{1,0:T(4,128)S(1)} collective-permute-done((f32[4,2048]{1,0:T(4,128)S(1)}, f32[4,2048]{1,0:T(4,128)S(1)}, u32[]{:S(2)}, u32[]{:S(2)}) %collective-permute-start) | collective-permute-done | bytes 32800 | tf_op jit(solution)/shard_map/ppermute | solution.py:308
  23.1 0.4 collective-permute-start.1
  23.5 1.5 %collective-permute-start.2 = (f32[3072]{0:T(1024)S(1)}, f32[3072]{0:T(1024)S(1)}, u32[]{:S(2)}, u32[]{:S(2)}) collective-permute-start(f32[3072]{0:T(1024)S(1)} %convert_add_fusion.1.vectors), channel_id=1, source_target_pairs={{0,2},{1,3},{2,0},{3,1},{4,6},{5,7},{6,4},{7,5},{8,10},{9,11},{10,... | collective-permute-start | bytes 36872 | tf_op jit(solution)/shard_map/ppermute | solution.py:308
  24.9 2.3 %collective-permute-done.2.other = f32[3072]{0:T(1024)S(1)} collective-permute-done((f32[3072]{0:T(1024)S(1)}, f32[3072]{0:T(1024)S(1)}, u32[]{:S(2)}, u32[]{:S(2)}) %collective-permute-start.2) | collective-permute-done | bytes 12320 | tf_op jit(solution)/shard_map/ppermute | solution.py:308
  27.3 0.0 collective-permute-done.1.far
  27.3 0.7 %shard_map.166 = (bf16[8,8,512]{2,1,0:T(8,128)(2,1)S(1)}, bf16[4,512]{1,0:T(4,128)(2,1)S(1)}) custom-call(s32[2]{0:T(128)S(1)} %pad_add_fusion.1.place, f32[4,2048]{1,0:T(4,128)S(1)} %add.83.near, f32[4,2048]{1,0:T(4,128)S(1)} %collective-permute-done.1.far, f32[3072]{0:T(1024)S(1)} %convert_add_fusion.1.vectors, f32[3072]{0:T(1024)S(1)} %collective-permute-done.2.other), custom_call_target="tpu_custom_call" | custom-call | bytes 90120 | tf_op jit(solution)/shard_map/pallas_call | solution.py:200
  28.0 12.8 %all_to_all.15.rows_in = bf16[8,8,512]{2,1,0:T(8,128)(2,1)S(1)} all-to-all(bf16[8,8,512]{2,1,0:T(8,128)(2,1)S(1)} %get-tuple-element.13), channel_id=1, replica_groups=mesh['req'=8,'tp'=4] {'req'}, dimensions={0} | all-to-all | bytes 131072 | tf_op jit(solution)/shard_map/all_to_all | solution.py:212
  40.8 0.0 collective-permute-done.3.moved
  40.8 0.0 copy-done.3
  40.8 1.3 %shard_map.167.near = bf16[32,1024]{1,0:T(8,128)(2,1)S(1)} custom-call(s32[2]{0:T(128)S(1)} %pad_add_fusion.1.place, bf16[8,8,512]{2,1,0:T(8,128)(2,1)S(1)} %all_to_all.15.rows_in, bf16[32,64]{1,0:T(8,128)(2,1)S(1)} %get-tuple-element.14.arrange, bf16[1024,512]{1,0:T(8,128)(2,1)S(1)} %copy-done.3, bf16[1024,512]{1,0:T(8,128)(2,1)S(1)} %collective-permute-done.3.moved), custom_call_target="tpu_custom_call" | custom-call | bytes 2166792 | tf_op jit(solution)/shard_map/pallas_call | solution.py:200
  42.1 0.1 collective-permute-start.4
  42.2 1.2 %collective-permute-done.4.far = bf16[32,1024]{1,0:T(8,128)(2,1)S(1)} collective-permute-done((bf16[32,1024]{1,0:T(8,128)(2,1)S(1)}, bf16[32,1024]{1,0:T(8,128)(2,1)S(1)}, u32[]{:S(2)}, u32[]{:S(2)}) %collective-permute-start.4) | collective-permute-done | bytes 65568 | tf_op jit(solution)/shard_map/ppermute | solution.py:308
  43.4 0.0 copy-done.4
  43.4 0.3 shard_map.168
  43.7 9.3 %all_to_all.16 = f32[8,4,512]{2,1,0:T(4,128)S(1)} all-to-all(f32[8,4,512]{2,1,0:T(4,128)S(1)} %shard_map.168), channel_id=1, replica_groups=mesh['req'=8,'tp'=4] {'req'}, dimensions={0} | all-to-all | bytes 131072 | tf_op jit(solution)/shard_map/all_to_all | solution.py:212
  53.0 0.6 %add_convert_fusion = bf16[4,512]{1,0:T(4,128)(2,1)} fusion(f32[4,512]{1,0:T(4,128)S(1)} %reduce_sum.9, f32[512]{0:T(512)S(1)} %convert_element_type.17), kind=kLoop, calls=%fused_computation.3 | loop fusion | flops 4096 | bytes 14336 | tf_op jit(solution)/shard_map/convert_element_type | solution.py:303
  (8 shorter events, 0.0 us)
Async XLA Ops:
  0.0 40.8 %collective-permute-start.3 = (bf16[1024,512]{1,0:T(8,128)(2,1)}, bf16[1024,512]{1,0:T(8,128)(2,1)S(1)}, u32[]{:S(2)}, u32[]{:S(2)}) collective-permute-start(bf16[1024,512]{1,0:T(8,128)(2,1)} %weight.4), channel_id=1, source_target_pairs={{0,2},{1,3},{2,0},{3,1},{4,6},{5,7},{6,4},{7,5},{8,10},{9,11},{10,... | collective-permute-start | bytes 3145736 | tf_op jit(solution)/shard_map/ppermute | solution.py:308
  6.0 12.5 %all-to-all-start = ((bf16[8,8,256]{2,1,0:T(8,128)(2,1)}), bf16[8,8,256]{2,1,0:T(8,128)(2,1)S(1)}, u32[]{:S(2)}, u32[]{:S(2)}) async-start(bf16[8,8,256]{2,1,0:T(8,128)(2,1)} %shard_map.163), calls=%async_computation | async-start | bytes 65536 | tf_op jit(solution)/shard_map/all_to_all | solution.py:212
  12.5 1.4 %copy-start = (bf16[2,22,32,512]{3,2,1,0:T(8,128)(2,1)S(1)}, bf16[2,22,32,512]{3,2,1,0:T(8,128)(2,1)}, u32[]{:S(2)}) copy-start(bf16[2,22,32,512]{3,2,1,0:T(8,128)(2,1)} %pool.3) | copy-start | bytes 4325380
  13.9 4.6 %copy-start.1 = (bf16[2,22,32,512]{3,2,1,0:T(8,128)(2,1)S(1)}, bf16[2,22,32,512]{3,2,1,0:T(8,128)(2,1)}, u32[]{:S(2)}) copy-start(bf16[2,22,32,512]{3,2,1,0:T(8,128)(2,1)} %pool.3) | copy-start | bytes 4325380
  18.6 1.6 %copy-start.2 = (bf16[512,2048]{1,0:T(8,128)(2,1)S(1)}, bf16[512,2048]{1,0:T(8,128)(2,1)}, u32[]{:S(2)}) copy-start(bf16[512,2048]{1,0:T(8,128)(2,1)} %weight.3) | copy-start | bytes 6291460
  20.1 20.7 %copy-start.3 = (bf16[1024,512]{1,0:T(8,128)(2,1)S(1)}, bf16[1024,512]{1,0:T(8,128)(2,1)}, u32[]{:S(2)}) copy-start(bf16[1024,512]{1,0:T(8,128)(2,1)} %weight.4) | copy-start | bytes 3145732
  21.8 21.6 %copy-start.4 = (bf16[1024,512]{1,0:T(8,128)(2,1)S(1)}, bf16[1024,512]{1,0:T(8,128)(2,1)}, u32[]{:S(2)}) copy-start(bf16[1024,512]{1,0:T(8,128)(2,1)} %weight.5) | copy-start | bytes 3145732
  21.8 1.2 %collective-permute-start = (f32[4,2048]{1,0:T(4,128)S(1)}, f32[4,2048]{1,0:T(4,128)S(1)}, u32[]{:S(2)}, u32[]{:S(2)}) collective-permute-start(f32[4,2048]{1,0:T(4,128)S(1)} %shard_map.165), channel_id=1, source_target_pairs={{0,1},{1,0},{2,3},{3,2},{4,5},{5,4},{6,7},{7,6},{8,9},{9,8},{10,11... | collective-permute-start | bytes 98312 | tf_op jit(solution)/shard_map/ppermute | solution.py:308
  23.1 4.2 %collective-permute-start.1 = (f32[4,2048]{1,0:T(4,128)S(1)}, f32[4,2048]{1,0:T(4,128)S(1)}, u32[]{:S(2)}, u32[]{:S(2)}) collective-permute-start(f32[4,2048]{1,0:T(4,128)S(1)} %add.83.near), channel_id=1, source_target_pairs={{0,3},{1,2},{2,1},{3,0},{4,7},{5,6},{6,5},{7,4},{8,11},{9,10},{10,... | collective-permute-start | bytes 98312 | tf_op jit(solution)/shard_map/ppermute | solution.py:308
  23.5 3.8 %collective-permute-start.2 = (f32[3072]{0:T(1024)S(1)}, f32[3072]{0:T(1024)S(1)}, u32[]{:S(2)}, u32[]{:S(2)}) collective-permute-start(f32[3072]{0:T(1024)S(1)} %convert_add_fusion.1.vectors), channel_id=1, source_target_pairs={{0,2},{1,3},{2,0},{3,1},{4,6},{5,7},{6,4},{7,5},{8,10},{9,11},{10,... | collective-permute-start | bytes 36872 | tf_op jit(solution)/shard_map/ppermute | solution.py:308
  42.1 1.3 %collective-permute-start.4 = (bf16[32,1024]{1,0:T(8,128)(2,1)S(1)}, bf16[32,1024]{1,0:T(8,128)(2,1)S(1)}, u32[]{:S(2)}, u32[]{:S(2)}) collective-permute-start(bf16[32,1024]{1,0:T(8,128)(2,1)S(1)} %shard_map.167.near), channel_id=1, source_target_pairs={{0,1},{1,0},{2,3},{3,2},{4,5},{5,4},{6,7},{7,6},{8,9},{9,8},{10,11... | collective-permute-start | bytes 196616 | tf_op jit(solution)/shard_map/ppermute | solution.py:308

commit v7 on v6

--- a/solution.py
+++ b/solution.py
@@ -14,7 +14,6 @@
 REQ, TP = 8, 4
 F32, BF16, I32 = jnp.float32, jnp.bfloat16, jnp.int32
 VMEM = pl.BlockSpec(memory_space=pltpu.VMEM)
-SMEM = pl.BlockSpec(memory_space=pltpu.SMEM)
 HBM = pl.BlockSpec(memory_space=pltpu.HBM)
 
 
@@ -48,18 +47,20 @@
     return vectors[i * cols : (i + 1) * cols][None, :]
 
 
-def pack_kernel(place, numbers, fields_in, out):
-    count = numbers.shape[1]
-    rows = count // REQ
+def pack_kernel(place, fields_in, out):
     fields = 4
+    used = fields_in.shape[0] - 1
+    rows = used // fields
+    count = REQ * rows
     cols = fields_in.shape[1]
-    shape = (REQ * fields, fields * rows)
+    shape = (REQ * fields, used)
     down, across = iota(shape, 0), iota(shape, 1)
-    here = (count, fields * rows)
-    of_mine = hot(iota(here, 0) == place[0] * rows + iota(here, 1) % rows)
-    owner_of = onto_mxu(numbers[0:1, :].astype(F32).astype(BF16), of_mine).astype(I32)
+    here = (count, used)
+    of_mine = hot(iota(here, 0) == place[0:1, 0:1] * rows + iota(here, 1) % rows)
+    owner = fields_in[used : used + 1, :count].astype(BF16)
+    owner_of = onto_mxu(owner, of_mine).astype(I32)
     pick = hot((down % fields == across // rows) & (owner_of == down // fields))
-    blocks = onto_mxu(pick, fields_in[...].astype(BF16)).astype(BF16)
+    blocks = onto_mxu(pick, fields_in[:used, :].astype(BF16)).astype(BF16)
     for d in range(REQ):
         block = blocks[d * fields : (d + 1) * fields]
         out[d, :fields, :] = block[:, : cols // 2]
@@ -67,12 +68,12 @@
 
 
 def index_kernel(
-    place, numbers, pool, pick, valid, arrange, arrange_own, *, page_len
+    place, numbers, pool, out_weight, pick, valid, arrange, arrange_own, *, page_len
 ):
-    del pool
+    del pool, out_weight
     owner, order, lengths = (numbers[i : i + 1, :] for i in range(3))
     table = numbers[8:, :]
-    me = place[0]
+    me = place[0:1, 0:1]
     count = owner.shape[1]
     rows = count // REQ
     square = (count, count)
@@ -107,9 +108,7 @@
     valid[...] = seen
 
     ordered = hot(order_col == across)
-    shape = arrange.shape
-    across_a = iota(shape, 1)
-    holds = hot((owner_col == across_a // (2 * rows)) & (rank_col == across_a % rows))
+    holds = hot((owner_col == across // rows) & (rank_col == across % rows))
     arrange[...] = onto_mxu(ordered, holds).astype(BF16)
     here = hot((owner_col == me) & (rank_col == iota(arrange_own.shape, 1)))
     arrange_own[...] = onto_mxu(ordered, here).astype(BF16)
@@ -147,42 +146,33 @@
     numer = jnp.where(in_head, numer / total, 0.0)
     attn = sum(numer[i * rows : (i + 1) * rows] for i in range(heads))
     attn = jnp.concatenate([attn, jnp.zeros_like(attn)], axis=0).astype(BF16)
-    partial[...] = onto_mxu(attn, weight[...])[:rows]
-    mine = pl.ds(pl.multiple_of(place[1] * cols, cols), cols)
-    partial[:, mine] += resid + row(vectors, 0, cols)
-
-
-def norm_kernel(place, near, far, vectors, other, blocks, stream_own):
+    projected = onto_mxu(attn, weight[...])[:rows]
+    extra = resid + row(vectors, 0, cols)
+    for t in range(TP):
+        mine = jnp.where(place[1:2, 0:1] == t, extra, 0.0)
+        partial[:, t * cols : (t + 1) * cols] = projected[:, t * cols : (t + 1) * cols] + mine
+
+
+def norm_kernel(place, near, far, vectors, blocks, stream_own):
     stream = (near[...] + far[...]).astype(BF16).astype(F32)
-    rows, width = stream.shape
+    width = stream.shape[1]
     cols = width // TP
     mean = jnp.sum(stream, axis=1, keepdims=True) / width
     var = jnp.sum((stream - mean) ** 2, axis=1, keepdims=True) / width
-    inverse = lax.rsqrt(var + NORM_EPS)
-    core, chip = place[1] % 2, place[1] // 2
-    parts = []
-    for x in range(2):
-        even, odd = (stream[:, (2 * x + c) * cols : (2 * x + c + 1) * cols] for c in range(2))
-        part = jnp.where(core == 0, even, odd)
-        gain, bias = (jnp.where(chip == x, row(vectors, i, cols), row(other, i, cols)) for i in (1, 2))
-        parts.append((part, (part - mean) * inverse * gain + bias))
-    stream_own[...] = jnp.where(chip == 0, parts[0][0], parts[1][0]).astype(BF16)
-    block = jnp.concatenate([parts[0][1], parts[1][1]], axis=0).astype(BF16)
+    own = stream[:, :cols]
+    for t in range(1, TP):
+        own = jnp.where(place[1:2, 0:1] == t, stream[:, t * cols : (t + 1) * cols], own)
+    stream_own[...] = own.astype(BF16)
+    gain, bias = row(vectors, 1, cols), row(vectors, 2, cols)
+    block = ((own - mean) * lax.rsqrt(var + NORM_EPS) * gain + bias).astype(BF16)
     for d in range(REQ):
         blocks[d] = block
 
 
-def up_kernel(place, rows_in, arrange, weight, moved, out, *, rows):
+def up_kernel(rows_in, arrange, weight, out):
     came = rows_in[...].reshape(-1, rows_in.shape[2])
-    which = (iota(arrange.shape, 1) // rows) % 2
-    chosen = arrange[...].astype(F32)
-    chip = place[1] // 2
-
-    def ordered(x):
-        return onto_mxu(jnp.where(which == x, chosen, 0.0).astype(BF16), came).astype(BF16)
-
-    hidden = nt_dot(ordered(chip), weight[...]) + nt_dot(ordered(1 - chip), moved[...])
-    out[...] = hidden.astype(BF16)
+    ordered = onto_mxu(arrange[...], came).astype(BF16)
+    out[...] = nt_dot(ordered, weight[...]).astype(BF16)
 
 
 def down_kernel(near, far, vectors, weight, arrange_own, stream_own, out):
@@ -242,65 +232,59 @@
     def arr(shape, dtype=BF16):
         return jax.ShapeDtypeStruct(shape, dtype)
 
-    me, me_tp = lax.axis_index("req").astype(I32), lax.axis_index("tp").astype(I32)
-    place = jnp.stack([me, me_tp])
-
+    position = jnp.stack([lax.axis_index("req"), lax.axis_index("tp")]).astype(I32)
+    place = jnp.broadcast_to(position[:, None], (2, HEAD_DIM))
+
+    owner_f = jnp.pad(owner.astype(F32)[None, :], ((0, 0), (0, cols - count)))
+    fields = pile([x.astype(F32) for x in (query, key_new, value_new, resid)] + [owner_f])
+    (packed,) = call(pack_kernel, [arr((REQ, 8, cols // 2))], [VMEM] * 2, [place, fields])
+    arrived = trade(packed)
     numbers = pile(
         [owner[None, :], order[None, :], lengths[None, :], jnp.zeros((5, count), I32), page_table.T]
     )
-    fields = pile([x.astype(F32) for x in (query, key_new, value_new, resid)])
-    (packed,) = call(
-        pack_kernel,
-        [arr((REQ, 8, cols // 2))],
-        [SMEM, VMEM, VMEM],
-        [place, numbers, fields],
-    )
-    up_moved = swap(up_weight_t, "tp", 2)
-    arrived = trade(packed)
     vectors = pile([x.astype(F32) for x in (out_bias, norm_gain, norm_bias, down_bias, up_bias)])
     pick, valid, arrange, arrange_own = call(
         index_kernel,
         [
             arr((4 * rows, 2 * count)),
             arr((heads * rows, positions), F32),
-            arr((count, 2 * count)),
+            arr((count, count)),
             arr((count, rows)),
         ],
-        [SMEM, VMEM, HBM],
-        [place, numbers, kv_pool],
+        [VMEM, VMEM, HBM, HBM],
+        [place, numbers, kv_pool, out_weight],
         page_len=page_len,
     )
-    other = swap(vectors, "tp", 2)
 
     (partial,) = call(
         attention_kernel,
         [arr((rows, width), F32)],
-        [SMEM] + [VMEM] * 6,
+        [VMEM] * 7,
         [place, arrived, pick, valid, vectors, kv_pool, out_weight],
         rows=rows,
     )
     pair = partial + swap(partial, "tp", 1)
     blocks, stream_own = call(
         norm_kernel,
-        [arr((REQ, 2 * rows, cols)), arr((rows, cols))],
-        [SMEM] + [VMEM] * 4,
-        [place, pair, swap(pair, "tp", 3), vectors, other],
+        [arr((REQ, rows, cols)), arr((rows, cols))],
+        [VMEM] * 4,
+        [place, pair, swap(pair, "tp", 3), vectors],
     )
 
     (part,) = call(
         up_kernel,
         [arr((count, hidden))],
-        [SMEM] + [VMEM] * 4,
-        [place, trade(blocks), arrange, up_weight_t, up_moved],
-        rows=rows,
-    )
+        [VMEM] * 3,
+        [trade(blocks), arrange, up_weight_t],
+    )
+    part = (part.astype(F32) + swap(part, "tp", 1).astype(F32)).astype(BF16)
     (feed,) = call(
         down_kernel,
         [arr((REQ, rows, cols), F32)],
         [VMEM] * 6,
-        [part, swap(part, "tp", 1), vectors, down_weight, arrange_own, stream_own],
-    )
-    return (jnp.sum(trade(feed), axis=0) + down_bias.astype(F32)[None, :]).astype(BF16)
+        [part, swap(part, "tp", 3), vectors, down_weight, arrange_own, stream_own],
+    )
+    return (jnp.sum(trade(feed), axis=0) + row(vectors, 3, cols)).astype(BF16)
 
 
 def swap(x, axis, step):

time: 54.1 us -> 55.5 us (1.026)
  blocking collectives: 22.1 us -> 12.4 us
  waiting for transfers between devices: 7.67 us -> 14.2 us
  local copies, waits for them, and re-layouts: 3.04 us -> 7.11 us
  starting transfers between devices: 10.7 us -> 13.3 us
  Pallas kernels: 6.43 us -> 4.87 us
  other arithmetic: 3.67 us -> 2.93 us
    all_to_all x2 -> x1, blocking collectives: 22.1 us -> 12.4 us  [trade(): return lax.all_to_all(blocks, 'req', 0, 0, tiled=True)]
    all_to_all x1 -> x2, starting transfers between devices: 5.83 us -> 10.6 us  [trade(): return lax.all_to_all(blocks, 'req', 0, 0, tiled=True)]
    unnamed x10 -> x38, local copies, waits for them, and re-layouts: 2.96 us -> 6.95 us
    all_to_all x1 -> x2, waiting for transfers between devices: 2.9 us -> 6.87 us  [trade(): return lax.all_to_all(blocks, 'req', 0, 0, tiled=True)]
    ppermute x5 -> x4, waiting for transfers between devices: 4.77 us -> 7.32 us  [swap(): return lax.ppermute(x, axis, [(i, i ^ step) for i in range(n)])]
    ppermute x5 -> x4, starting transfers between devices: 4.87 us -> 2.71 us  [swap(): return lax.ppermute(x, axis, [(i, i ^ step) for i in range(n)])]
    pallas_call x6, Pallas kernels: 6.43 us -> 4.87 us  [call(): pl.pallas_call(functools.partial(kernel, **fixed) if fixed else kernel, o...]
    add x3, other arithmetic: 2.28 us -> 1.55 us  [pile(): piled += jnp.pad(p, around)]
  transfers between devices with their start and end apart: 6 -> 6, of which waited for: 4 -> 5; matrix products, arithmetic and copies ran while one was open for 6% -> 2% of each run, Pallas kernels for 9% -> 1%
where the time goes in v7:
time: 55.5 us; the launch traced here: 55 us
  waiting for transfers between devices  14.2 us (26%)
  starting transfers between devices  13.3 us (24%)
  blocking collectives  12.4 us (22%)
  local copies, waits for them, and re-layouts  7.11 us (13%)
  Pallas kernels  4.87 us (9%)
  other arithmetic  2.93 us (5%)
    all_to_all x1, blocking collectives, trade(): return lax.all_to_all(blocks, 'req', 0, 0, tiled=True)  12.4 us
    all_to_all x2, starting transfers between devices, trade(): return lax.all_to_all(blocks, 'req', 0, 0, tiled=True)  10.6 us
    ppermute x4, waiting for transfers between devices, swap(): return lax.ppermute(x, axis, [(i, i ^ step) for i in range(n)])  7.32 us
    unnamed x38, local copies, waits for them, and re-layouts  6.95 us
    all_to_all x2, waiting for transfers between devices, trade(): return lax.all_to_all(blocks, 'req', 0, 0, tiled=True)  6.87 us
    pallas_call x6, Pallas kernels, call(): pl.pallas_call(functools.partial(kernel, **fixed) if fixed else kernel, o...  4.87 us
    ppermute x4, starting transfers between devices, swap(): return lax.ppermute(x, axis, [(i, i ^ step) for i in range(n)])  2.71 us
    add x3, other arithmetic, pile(): piled += jnp.pad(p, around)  1.55 us
  transfers between devices with their start and end apart: 6, of which 5 were waited for; matrix products, arithmetic and copies ran while one was open for 2% of the time, Pallas kernels for 1%

profile of v7, /device:TPU:0, one launch (start us, length us, event | category | flops | bytes accessed | tf_op | source)
XLA Modules:
  0.0 55.0 jit_solution(13484121378027839981)
XLA Ops:
  0.0 0.7 %convert_bitcast_fusion = f32[1,32]{1,0:T(1,128)S(1)} fusion(s32[32]{0:T(128)} %param.22), kind=kLoop, calls=%fused_computation.6 | loop fusion | flops 32 | bytes 256 | tf_op jit(solution)/shard_map/broadcast_in_dim | solution.py:238
  0.7 0.1 pad_add_fusion.2
  0.7 0.8 %pad_add_fusion.fields_in = f32[17,512]{1,0:T(8,128)S(1)} fusion(f32[1,32]{1,0:T(1,128)S(1)} %convert_bitcast_fusion, bf16[4,512]{1,0:T(4,128)(2,1)} %param.20, bf16[4,512]{1,0:T(4,128)(2,1)} %param.19, bf16[4,512]{1,0:T(4,128)(2,1)} %param.18, bf16[4,512]{1,0:T(4,128)(2,1)} %param.17), kind=kLoop, calls=%fused_computation.1 | loop fusion | flops 69632 | bytes 51328 | tf_op jit(solution)/shard_map/add | solution.py:41
  1.5 0.1 broadcast_in_dim.22.place
  1.6 0.9 %shard_map.163 = bf16[8,8,256]{2,1,0:T(8,128)(2,1)} custom-call(s32[2,128]{1,0:T(2,128)S(1)} %broadcast_in_dim.22.place, f32[17,512]{1,0:T(8,128)S(1)} %pad_add_fusion.fields_in), custom_call_target="tpu_custom_call" | custom-call | bytes 35840 | tf_op jit(solution)/shard_map/pallas_call | solution.py:190
  2.4 7.3 %all-to-all-start = ((bf16[8,8,256]{2,1,0:T(8,128)(2,1)}), bf16[8,8,256]{2,1,0:T(8,128)(2,1)}, u32[]{:S(2)}, u32[]{:S(2)}) async-start(bf16[8,8,256]{2,1,0:T(8,128)(2,1)} %shard_map.163), calls=%async_computation | async-start | bytes 65536 | tf_op jit(solution)/shard_map/all_to_all | solution.py:202
  9.8 0.1 pad.106
  9.9 0.8 %pad_add_fusion.1.numbers = s32[24,32]{1,0:T(8,128)S(1)} fusion(s32[16,32]{1,0:T(8,128)} %bitcast.8, s32[1,32]{1,0:T(1,128)} %bitcast.10, s32[1,32]{1,0:T(1,128)} %bitcast.11, s32[1,32]{1,0:T(1,128)} %bitcast.9, s32[24]{0:T(128)S(1)} %pad.106), kind=kLoop, calls=%fused_computation.3 | loop fusion | flops 3072 | bytes 5600 | tf_op jit(solution)/shard_map/add | solution.py:41
  10.7 1.6 %copy-done = bf16[512,2048]{1,0:T(8,128)(2,1)S(1)} copy-done((bf16[512,2048]{1,0:T(8,128)(2,1)S(1)}, bf16[512,2048]{1,0:T(8,128)(2,1)}, u32[]{:S(2)}) %copy-start) | copy-done | bytes 2097176
  12.3 1.4 %copy-done.2 = bf16[2,22,32,512]{3,2,1,0:T(8,128)(2,1)S(1)} copy-done((bf16[2,22,32,512]{3,2,1,0:T(8,128)(2,1)S(1)}, bf16[2,22,32,512]{3,2,1,0:T(8,128)(2,1)}, u32[]{:S(2)}) %copy-start.2) | copy-done | bytes 1441816
  13.6 0.4 shard_map.164
  14.1 0.6 %copy-done.6 = f32[16,704]{1,0:T(8,128)} copy-done((f32[16,704]{1,0:T(8,128)}, f32[16,704]{1,0:T(8,128)S(1)}, u32[]{:S(2)}) %copy-start.6) | copy-done | bytes 45080
  14.7 0.6 %copy-done.8 = bf16[32,4]{1,0:T(8,128)(2,1)} copy-done((bf16[32,4]{1,0:T(8,128)(2,1)}, bf16[32,4]{1,0:T(8,128)(2,1)S(1)}, u32[]{:S(2)}) %copy-start.8) | copy-done | bytes 280
  15.3 0.6 %copy-done.10 = bf16[32,32]{1,0:T(8,128)(2,1)} copy-done((bf16[32,32]{1,0:T(8,128)(2,1)}, bf16[32,32]{1,0:T(8,128)(2,1)S(1)}, u32[]{:S(2)}) %copy-start.10) | copy-done | bytes 2072
  15.8 0.6 %copy-done.12 = bf16[16,64]{1,0:T(8,128)(2,1)} copy-done((bf16[16,64]{1,0:T(8,128)(2,1)}, bf16[16,64]{1,0:T(8,128)(2,1)S(1)}, u32[]{:S(2)}) %copy-start.12) | copy-done | bytes 2072
  16.5 0.0 all-to-all-done.arrived
  16.5 0.9 %copy-done.7 = f32[16,704]{1,0:T(8,128)S(1)} copy-done((f32[16,704]{1,0:T(8,128)S(1)}, f32[16,704]{1,0:T(8,128)}, u32[]{:S(2)}) %copy-start.7) | copy-done | bytes 45080
  17.4 0.7 %copy-done.13 = bf16[16,64]{1,0:T(8,128)(2,1)S(1)} copy-done((bf16[16,64]{1,0:T(8,128)(2,1)S(1)}, bf16[16,64]{1,0:T(8,128)(2,1)}, u32[]{:S(2)}) %copy-start.13) | copy-done | bytes 2072
  18.1 2.0 %shard_map.165 = f32[4,2048]{1,0:T(4,128)S(1)} custom-call(s32[2,128]{1,0:T(2,128)S(1)} %broadcast_in_dim.22.place, bf16[8,8,256]{2,1,0:T(8,128)(2,1)} %all-to-all-done.arrived, bf16[16,64]{1,0:T(8,128)(2,1)S(1)} %copy-done.13, f32[16,704]{1,0:T(8,128)S(1)} %copy-done.7, f32[3072]{0:T(1024)S(1)} %convert_add_fusion.vectors, ...), custom_call_target="tpu_custom_call" | custom-call | bytes 3632128 | tf_op jit(solution)/shard_map/pallas_call | solution.py:190
  20.1 1.2 %collective-permute-done = f32[4,2048]{1,0:T(4,128)S(1)} collective-permute-done((f32[4,2048]{1,0:T(4,128)S(1)}, f32[4,2048]{1,0:T(4,128)S(1)}, u32[]{:S(2)}, u32[]{:S(2)}) %collective-permute-start) | collective-permute-done | bytes 32800 | tf_op jit(solution)/shard_map/ppermute | solution.py:292
  21.3 1.3 %collective-permute-start.1 = (f32[4,2048]{1,0:T(4,128)S(1)}, f32[4,2048]{1,0:T(4,128)S(1)}, u32[]{:S(2)}, u32[]{:S(2)}) collective-permute-start(f32[4,2048]{1,0:T(4,128)S(1)} %add.94.near), channel_id=1, source_target_pairs={{0,3},{1,2},{2,1},{3,0},{4,7},{5,6},{6,5},{7,4},{8,11},{9,10},{10,... | collective-permute-start | bytes 98312 | tf_op jit(solution)/shard_map/ppermute | solution.py:292
  22.7 2.1 %collective-permute-done.1.far = f32[4,2048]{1,0:T(4,128)S(1)} collective-permute-done((f32[4,2048]{1,0:T(4,128)S(1)}, f32[4,2048]{1,0:T(4,128)S(1)}, u32[]{:S(2)}, u32[]{:S(2)}) %collective-permute-start.1) | collective-permute-done | bytes 32800 | tf_op jit(solution)/shard_map/ppermute | solution.py:292
  24.7 0.2 shard_map.166
  24.9 12.4 %all_to_all.15.rows_in = bf16[8,4,512]{2,1,0:T(4,128)(2,1)S(1)} all-to-all(bf16[8,4,512]{2,1,0:T(4,128)(2,1)S(1)} %get-tuple-element.13), channel_id=1, replica_groups=mesh['req'=8,'tp'=4] {'req'}, dimensions={0} | all-to-all | bytes 65536 | tf_op jit(solution)/shard_map/all_to_all | solution.py:202
  37.4 0.5 shard_map.167
  37.9 1.2 %collective-permute-done.2 = bf16[32,1024]{1,0:T(8,128)(2,1)S(1)} collective-permute-done((bf16[32,1024]{1,0:T(8,128)(2,1)S(1)}, bf16[32,1024]{1,0:T(8,128)(2,1)S(1)}, u32[]{:S(2)}, u32[]{:S(2)}) %collective-permute-start.2) | collective-permute-done | bytes 65568 | tf_op jit(solution)/shard_map/ppermute | solution.py:292
  39.2 1.3 %collective-permute-start.3 = (bf16[32,1024]{1,0:T(8,128)(2,1)S(1)}, bf16[32,1024]{1,0:T(8,128)(2,1)S(1)}, u32[]{:S(2)}, u32[]{:S(2)}) collective-permute-start(bf16[32,1024]{1,0:T(8,128)(2,1)S(1)} %add_convert_fusion.near), channel_id=1, source_target_pairs={{0,3},{1,2},{2,1},{3,0},{4,7},{5,6},{6,5},{7,4},{8,11},{9,10},{10,... | collective-permute-start | bytes 196616 | tf_op jit(solution)/shard_map/ppermute | solution.py:292
  40.5 2.8 %collective-permute-done.3.far = bf16[32,1024]{1,0:T(8,128)(2,1)S(1)} collective-permute-done((bf16[32,1024]{1,0:T(8,128)(2,1)S(1)}, bf16[32,1024]{1,0:T(8,128)(2,1)S(1)}, u32[]{:S(2)}, u32[]{:S(2)}) %collective-permute-start.3) | collective-permute-done | bytes 65568 | tf_op jit(solution)/shard_map/ppermute | solution.py:292
  43.3 0.9 %shard_map.168 = f32[8,4,512]{2,1,0:T(4,128)} custom-call(bf16[32,1024]{1,0:T(8,128)(2,1)S(1)} %add_convert_fusion.near, bf16[32,1024]{1,0:T(8,128)(2,1)S(1)} %collective-permute-done.3.far, f32[3072]{0:T(1024)S(1)} %convert_add_fusion.vectors, bf16[1024,512]{1,0:T(8,128)(2,1)S(1)} %copy-done.4, bf16[32,4]{1,0:T(8,128)(2,1)S(1)} %copy-done.9, ...), custom_call_target="tpu_custom_call" | custom-call | bytes 1196288 | tf_op jit(solution)/shard_map/pallas_call | solution.py:190
  44.2 3.3 %all-to-all-start.2 = ((f32[8,4,512]{2,1,0:T(4,128)}), f32[8,4,512]{2,1,0:T(4,128)S(1)}, u32[]{:S(2)}, u32[]{:S(2)}) async-start(f32[8,4,512]{2,1,0:T(4,128)} %shard_map.168), calls=%async_computation.2 | async-start | bytes 131072 | tf_op jit(solution)/shard_map/all_to_all | solution.py:202
  47.6 6.8 %all-to-all-done.2 = f32[8,4,512]{2,1,0:T(4,128)S(1)} async-done(((f32[8,4,512]{2,1,0:T(4,128)}), f32[8,4,512]{2,1,0:T(4,128)S(1)}, u32[]{:S(2)}, u32[]{:S(2)}) %all-to-all-start.2) | async-done | bytes 65568 | tf_op jit(solution)/shard_map/all_to_all | solution.py:202
  54.4 0.6 %add_convert_fusion.1 = bf16[4,512]{1,0:T(4,128)(2,1)} fusion(f32[4,512]{1,0:T(4,128)S(1)} %reduce_sum.9, f32[512]{0:T(512)S(1)} %slice.4), kind=kLoop, calls=%fused_computation.4 | loop fusion | flops 4096 | bytes 14336 | tf_op jit(solution)/shard_map/convert_element_type | solution.py:287
  (38 shorter events, 0.2 us)
Async XLA Ops:
  2.4 14.1 %all-to-all-start = ((bf16[8,8,256]{2,1,0:T(8,128)(2,1)}), bf16[8,8,256]{2,1,0:T(8,128)(2,1)}, u32[]{:S(2)}, u32[]{:S(2)}) async-start(bf16[8,8,256]{2,1,0:T(8,128)(2,1)} %shard_map.163), calls=%async_computation | async-start | bytes 65536 | tf_op jit(solution)/shard_map/all_to_all | solution.py:202
  9.7 6.7 %copy-start.14 = (bf16[1024]{0:T(1024)(128)(2,1)S(1)}, bf16[1024]{0:T(1024)(128)(2,1)}, u32[]{:S(2)}) copy-start(bf16[1024]{0:T(1024)(128)(2,1)} %param.30) | copy-start | bytes 6148
  9.7 6.7 %copy-start.15 = (bf16[512]{0:T(512)(128)(2,1)S(1)}, bf16[512]{0:T(512)(128)(2,1)}, u32[]{:S(2)}) copy-start(bf16[512]{0:T(512)(128)(2,1)} %param.32) | copy-start | bytes 3076
  9.7 6.7 %copy-start.16 = (bf16[512]{0:T(512)(128)(2,1)S(1)}, bf16[512]{0:T(512)(128)(2,1)}, u32[]{:S(2)}) copy-start(bf16[512]{0:T(512)(128)(2,1)} %param.28) | copy-start | bytes 3076
  9.8 6.7 %copy-start.17 = (bf16[512]{0:T(512)(128)(2,1)S(1)}, bf16[512]{0:T(512)(128)(2,1)}, u32[]{:S(2)}) copy-start(bf16[512]{0:T(512)(128)(2,1)} %param.27) | copy-start | bytes 3076
  9.8 6.7 %copy-start.18 = (bf16[512]{0:T(512)(128)(2,1)S(1)}, bf16[512]{0:T(512)(128)(2,1)}, u32[]{:S(2)}) copy-start(bf16[512]{0:T(512)(128)(2,1)} %param.26) | copy-start | bytes 3076
  10.7 1.6 %copy-start = (bf16[512,2048]{1,0:T(8,128)(2,1)S(1)}, bf16[512,2048]{1,0:T(8,128)(2,1)}, u32[]{:S(2)}) copy-start(bf16[512,2048]{1,0:T(8,128)(2,1)} %weight.3) | copy-start | bytes 6291460
  12.3 1.4 %copy-start.2 = (bf16[2,22,32,512]{3,2,1,0:T(8,128)(2,1)S(1)}, bf16[2,22,32,512]{3,2,1,0:T(8,128)(2,1)}, u32[]{:S(2)}) copy-start(bf16[2,22,32,512]{3,2,1,0:T(8,128)(2,1)} %pool.3) | copy-start | bytes 4325380
  13.6 2.9 %copy-start.1 = (bf16[512,2048]{1,0:T(8,128)(2,1)S(1)}, bf16[512,2048]{1,0:T(8,128)(2,1)}, u32[]{:S(2)}) copy-start(bf16[512,2048]{1,0:T(8,128)(2,1)} %weight.3) | copy-start | bytes 6291460
  13.6 2.9 %copy-start.3 = (bf16[2,22,32,512]{3,2,1,0:T(8,128)(2,1)S(1)}, bf16[2,22,32,512]{3,2,1,0:T(8,128)(2,1)}, u32[]{:S(2)}) copy-start(bf16[2,22,32,512]{3,2,1,0:T(8,128)(2,1)} %pool.3) | copy-start | bytes 4325380
  14.0 0.6 %copy-start.6 = (f32[16,704]{1,0:T(8,128)}, f32[16,704]{1,0:T(8,128)S(1)}, u32[]{:S(2)}) copy-start(f32[16,704]{1,0:T(8,128)S(1)} %get-tuple-element.12.valid) | copy-start | bytes 135172
  14.7 0.6 %copy-start.8 = (bf16[32,4]{1,0:T(8,128)(2,1)}, bf16[32,4]{1,0:T(8,128)(2,1)S(1)}, u32[]{:S(2)}) copy-start(bf16[32,4]{1,0:T(8,128)(2,1)S(1)} %get-tuple-element.15.arrange_own) | copy-start | bytes 772
  15.3 0.6 %copy-start.10 = (bf16[32,32]{1,0:T(8,128)(2,1)}, bf16[32,32]{1,0:T(8,128)(2,1)S(1)}, u32[]{:S(2)}) copy-start(bf16[32,32]{1,0:T(8,128)(2,1)S(1)} %get-tuple-element.14.arrange) | copy-start | bytes 6148
  15.8 0.6 %copy-start.12 = (bf16[16,64]{1,0:T(8,128)(2,1)}, bf16[16,64]{1,0:T(8,128)(2,1)S(1)}, u32[]{:S(2)}) copy-start(bf16[16,64]{1,0:T(8,128)(2,1)S(1)} %get-tuple-element.11.pick) | copy-start | bytes 6148
  16.5 20.9 %copy-start.5 = (bf16[1024,512]{1,0:T(8,128)(2,1)S(1)}, bf16[1024,512]{1,0:T(8,128)(2,1)}, u32[]{:S(2)}) copy-start(bf16[1024,512]{1,0:T(8,128)(2,1)} %weight.4) | copy-start | bytes 3145732
  16.5 0.9 %copy-start.7 = (f32[16,704]{1,0:T(8,128)S(1)}, f32[16,704]{1,0:T(8,128)}, u32[]{:S(2)}) copy-start(f32[16,704]{1,0:T(8,128)} %copy-done.6) | copy-start | bytes 135172
  17.4 0.7 %copy-start.13 = (bf16[16,64]{1,0:T(8,128)(2,1)S(1)}, bf16[16,64]{1,0:T(8,128)(2,1)}, u32[]{:S(2)}) copy-start(bf16[16,64]{1,0:T(8,128)(2,1)} %copy-done.12) | copy-start | bytes 6148
  18.1 19.3 %copy-start.11 = (bf16[32,32]{1,0:T(8,128)(2,1)S(1)}, bf16[32,32]{1,0:T(8,128)(2,1)}, u32[]{:S(2)}) copy-start(bf16[32,32]{1,0:T(8,128)(2,1)} %copy-done.10) | copy-start | bytes 6148
  18.1 25.2 %copy-start.4 = (bf16[1024,512]{1,0:T(8,128)(2,1)S(1)}, bf16[1024,512]{1,0:T(8,128)(2,1)}, u32[]{:S(2)}) copy-start(bf16[1024,512]{1,0:T(8,128)(2,1)} %weight.5) | copy-start | bytes 3145732
  18.1 25.2 %copy-start.9 = (bf16[32,4]{1,0:T(8,128)(2,1)S(1)}, bf16[32,4]{1,0:T(8,128)(2,1)}, u32[]{:S(2)}) copy-start(bf16[32,4]{1,0:T(8,128)(2,1)} %copy-done.8) | copy-start | bytes 772
  20.1 1.2 %collective-permute-start = (f32[4,2048]{1,0:T(4,128)S(1)}, f32[4,2048]{1,0:T(4,128)S(1)}, u32[]{:S(2)}, u32[]{:S(2)}) collective-permute-start(f32[4,2048]{1,0:T(4,128)S(1)} %shard_map.165), channel_id=1, source_target_pairs={{0,1},{1,0},{2,3},{3,2},{4,5},{5,4},{6,7},{7,6},{8,9},{9,8},{10,11... | collective-permute-start | bytes 98312 | tf_op jit(solution)/shard_map/ppermute | solution.py:292
  21.3 3.4 %collective-permute-start.1 = (f32[4,2048]{1,0:T(4,128)S(1)}, f32[4,2048]{1,0:T(4,128)S(1)}, u32[]{:S(2)}, u32[]{:S(2)}) collective-permute-start(f32[4,2048]{1,0:T(4,128)S(1)} %add.94.near), channel_id=1, source_target_pairs={{0,3},{1,2},{2,1},{3,0},{4,7},{5,6},{6,5},{7,4},{8,11},{9,10},{10,... | collective-permute-start | bytes 98312 | tf_op jit(solution)/shard_map/ppermute | solution.py:292
  37.9 1.3 %collective-permute-start.2 = (bf16[32,1024]{1,0:T(8,128)(2,1)S(1)}, bf16[32,1024]{1,0:T(8,128)(2,1)S(1)}, u32[]{:S(2)}, u32[]{:S(2)}) collective-permute-start(bf16[32,1024]{1,0:T(8,128)(2,1)S(1)} %shard_map.167), channel_id=1, source_target_pairs={{0,1},{1,0},{2,3},{3,2},{4,5},{5,4},{6,7},{7,6},{8,9},{9,8},{10,11... | collective-permute-start | bytes 196616 | tf_op jit(solution)/shard_map/ppermute | solution.py:292
  39.2 4.1 %collective-permute-start.3 = (bf16[32,1024]{1,0:T(8,128)(2,1)S(1)}, bf16[32,1024]{1,0:T(8,128)(2,1)S(1)}, u32[]{:S(2)}, u32[]{:S(2)}) collective-permute-start(bf16[32,1024]{1,0:T(8,128)(2,1)S(1)} %add_convert_fusion.near), channel_id=1, source_target_pairs={{0,3},{1,2},{2,1},{3,0},{4,7},{5,6},{6,5},{7,4},{8,11},{9,10},{10,... | collective-permute-start | bytes 196616 | tf_op jit(solution)/shard_map/ppermute | solution.py:292
  44.2 10.2 %all-to-all-start.2 = ((f32[8,4,512]{2,1,0:T(4,128)}), f32[8,4,512]{2,1,0:T(4,128)S(1)}, u32[]{:S(2)}, u32[]{:S(2)}) async-start(f32[8,4,512]{2,1,0:T(4,128)} %shard_map.168), calls=%async_computation.2 | async-start | bytes 131072 | tf_op jit(solution)/shard_map/all_to_all | solution.py:202

commit v8 on v7

--- a/solution.py
+++ b/solution.py
@@ -12,6 +12,8 @@
 NORM_EPS = 1e-05
 PAIRWISE = 16
 REQ, TP = 8, 4
+WEIGHT_PARTS = 4
+ATTENTION_ROOM = 63.3
 F32, BF16, I32 = jnp.float32, jnp.bfloat16, jnp.int32
 VMEM = pl.BlockSpec(memory_space=pltpu.VMEM)
 HBM = pl.BlockSpec(memory_space=pltpu.HBM)
@@ -67,10 +69,7 @@
         out[d, fields:, :] = block[:, cols // 2 :]
 
 
-def index_kernel(
-    place, numbers, pool, out_weight, pick, valid, arrange, arrange_own, *, page_len
-):
-    del pool, out_weight
+def index_kernel(place, numbers, pick, valid, arrange, arrange_own, *, page_len):
     owner, order, lengths = (numbers[i : i + 1, :] for i in range(3))
     table = numbers[8:, :]
     me = place[0:1, 0:1]
@@ -114,7 +113,18 @@
     arrange_own[...] = onto_mxu(ordered, here).astype(BF16)
 
 
-def attention_kernel(place, arrived, pick, valid, vectors, pool, weight, partial, *, rows):
+def attention_kernel(
+    place, arrived, pick, valid, vectors, pool_in, weight_in, partial, pool, weight, sems, *, rows
+):
+    deep = weight.shape[0] // WEIGHT_PARTS
+    copies = [pltpu.make_async_copy(pool_in.at[i], pool.at[i], sems.at[i]) for i in range(2)]
+    for i in range(WEIGHT_PARTS):
+        part = pl.ds(i * deep, deep)
+        copies.append(
+            pltpu.make_async_copy(weight_in.at[part], weight.at[part], sems.at[2 + i])
+        )
+    for copy in copies:
+        copy.start()
     half = arrived.shape[2]
     cols = 2 * half
     heads = cols // HEAD_DIM
@@ -135,17 +145,21 @@
     wide = jnp.where(in_head, tile(query), 0.0)
     positions = valid.shape[1]
     self_score = jnp.sum(wide * tile(key), axis=1, keepdims=True) * scale
+    copies[0].wait()
     scores = nt_dot(wide.astype(BF16), pool[0].reshape(positions, cols)) * scale
     scores = jnp.where(valid[...] > 0.5, scores, -jnp.inf)
     top = jnp.maximum(jnp.max(scores, axis=1, keepdims=True), self_score)
     weights = jnp.exp(scores - top)
     self_weight = jnp.exp(self_score - top)
     total = jnp.sum(weights, axis=1, keepdims=True) + self_weight
+    copies[1].wait()
     numer = onto_mxu(weights.astype(BF16), pool[1].reshape(positions, cols))
     numer = numer + self_weight.astype(BF16).astype(F32) * tile(value)
     numer = jnp.where(in_head, numer / total, 0.0)
     attn = sum(numer[i * rows : (i + 1) * rows] for i in range(heads))
     attn = jnp.concatenate([attn, jnp.zeros_like(attn)], axis=0).astype(BF16)
+    for copy in copies[2:]:
+        copy.wait()
     projected = onto_mxu(attn, weight[...])[:rows]
     extra = resid + row(vectors, 0, cols)
     for t in range(TP):
@@ -185,6 +199,11 @@
         out[d] = feed[d * rows : (d + 1) * rows]
 
 
+def finish_kernel(pieces, vectors, out):
+    cols = out.shape[1]
+    out[...] = (jnp.sum(pieces[...], axis=0) + row(vectors, 3, cols)).astype(BF16)
+
+
 def call(kernel, shapes, specs, args, scratch=(), room=16, **fixed):
     moved = sum(a.size * a.dtype.itemsize for a in args)
     return pl.pallas_call(
@@ -193,7 +212,7 @@
         in_specs=specs,
         out_specs=[VMEM] * len(shapes),
         scratch_shapes=scratch,
-        compiler_params=pltpu.CompilerParams(vmem_limit_bytes=room * 2**20),
+        compiler_params=pltpu.CompilerParams(vmem_limit_bytes=int(room * 2**20)),
         cost_estimate=pl.CostEstimate(flops=0, bytes_accessed=moved, transcendentals=0),
     )(*args)
 
@@ -251,16 +270,22 @@
             arr((count, count)),
             arr((count, rows)),
         ],
-        [VMEM, VMEM, HBM, HBM],
-        [place, numbers, kv_pool, out_weight],
+        [VMEM, VMEM],
+        [place, numbers],
         page_len=page_len,
     )
 
     (partial,) = call(
         attention_kernel,
         [arr((rows, width), F32)],
-        [VMEM] * 7,
+        [VMEM] * 5 + [HBM] * 2,
         [place, arrived, pick, valid, vectors, kv_pool, out_weight],
+        [
+            pltpu.VMEM(kv_pool.shape, BF16),
+            pltpu.VMEM(out_weight.shape, BF16),
+            pltpu.SemaphoreType.DMA((2 + WEIGHT_PARTS,)),
+        ],
+        room=ATTENTION_ROOM,
         rows=rows,
     )
     pair = partial + swap(partial, "tp", 1)
@@ -284,7 +309,8 @@
         [VMEM] * 6,
         [part, swap(part, "tp", 3), vectors, down_weight, arrange_own, stream_own],
     )
-    return (jnp.sum(trade(feed), axis=0) + row(vectors, 3, cols)).astype(BF16)
+    (out,) = call(finish_kernel, [arr((rows, cols))], [VMEM] * 2, [trade(feed), vectors])
+    return out
 
 
 def swap(x, axis, step):

time: 55.5 us -> 55 us (level)
  blocking collectives: 12.4 us -> 18.9 us
  waiting for transfers between devices: 14.2 us -> 10.4 us
  starting transfers between devices: 13.3 us -> 10 us
  local copies, waits for them, and re-layouts: 7.11 us -> 3.86 us
  Pallas kernels: 4.87 us -> 6.75 us
  other arithmetic: 2.93 us -> 4.41 us
    all_to_all x1 -> x2, blocking collectives: 12.4 us -> 18.9 us  [trade(): return lax.all_to_all(blocks, 'req', 0, 0, tiled=True)]
    all_to_all x2 -> x1, waiting for transfers between devices: 6.87 us -> 2.83 us  [trade(): return lax.all_to_all(blocks, 'req', 0, 0, tiled=True)]
    all_to_all x2 -> x1, starting transfers between devices: 10.6 us -> 7.28 us  [trade(): return lax.all_to_all(blocks, 'req', 0, 0, tiled=True)]
    unnamed x38 -> x16, local copies, waits for them, and re-layouts: 6.95 us -> 3.72 us
    pallas_call x6 -> x7, Pallas kernels: 4.87 us -> 6.75 us  [call(): pl.pallas_call(functools.partial(kernel, **fixed) if fixed else kernel, o...]
    add x3, other arithmetic: 1.55 us -> 2.89 us  [pile(): piled += jnp.pad(p, around)]
    add x1, other arithmetic: 0.01 us -> 0.77 us  [on_pairs(): pair = partial + swap(partial, 'tp', 1)]
    convert_element_type x1 -> x0, other arithmetic: 0.6 us -> none  [on_pairs(): return (jnp.sum(trade(feed), axis=0) + row(vectors, 3, cols)).astype(BF16)]
  transfers between devices with their start and end apart: 6 -> 5, of which waited for: 5 -> 5; matrix products, arithmetic and copies ran while one was open for 2% -> 4% of each run, Pallas kernels for 1% -> 1%
where the time goes in v8:
time: 55 us; the launch traced here: 54.4 us
  blocking collectives  18.9 us (34%)
  waiting for transfers between devices  10.4 us (19%)
  starting transfers between devices  10 us (18%)
  Pallas kernels  6.75 us (12%)
  other arithmetic  4.41 us (8%)
  local copies, waits for them, and re-layouts  3.86 us (7%)
    all_to_all x2, blocking collectives, trade(): return lax.all_to_all(blocks, 'req', 0, 0, tiled=True)  18.9 us
    ppermute x4, waiting for transfers between devices, swap(): return lax.ppermute(x, axis, [(i, i ^ step) for i in range(n)])  7.53 us
    all_to_all x1, starting transfers between devices, trade(): return lax.all_to_all(blocks, 'req', 0, 0, tiled=True)  7.28 us
    pallas_call x7, Pallas kernels, call(): pl.pallas_call(functools.partial(kernel, **fixed) if fixed else kernel, o...  6.75 us
    unnamed x16, local copies, waits for them, and re-layouts  3.72 us
    add x3, other arithmetic, pile(): piled += jnp.pad(p, around)  2.89 us
    all_to_all x1, waiting for transfers between devices, trade(): return lax.all_to_all(blocks, 'req', 0, 0, tiled=True)  2.83 us
    ppermute x4, starting transfers between devices, swap(): return lax.ppermute(x, axis, [(i, i ^ step) for i in range(n)])  2.74 us
  transfers between devices with their start and end apart: 5, of which 5 were waited for; matrix products, arithmetic and copies ran while one was open for 4% of the time, Pallas kernels for 1%

profile of v8, /device:TPU:0, one launch (start us, length us, event | category | flops | bytes accessed | tf_op | source)
XLA Modules:
  0.0 54.4 jit_solution(10352252772542443056)
XLA Ops:
  0.0 0.7 %convert_bitcast_fusion = f32[1,32]{1,0:T(1,128)S(1)} fusion(s32[32]{0:T(128)} %param.22), kind=kLoop, calls=%fused_computation.5 | loop fusion | flops 32 | bytes 256 | tf_op jit(solution)/shard_map/broadcast_in_dim | solution.py:257
  0.7 0.1 pad_add_fusion.2
  0.7 0.8 %pad_add_fusion.fields_in = f32[17,512]{1,0:T(8,128)S(1)} fusion(f32[1,32]{1,0:T(1,128)S(1)} %convert_bitcast_fusion, bf16[4,512]{1,0:T(4,128)(2,1)} %param.20, bf16[4,512]{1,0:T(4,128)(2,1)} %param.19, bf16[4,512]{1,0:T(4,128)(2,1)} %param.18, bf16[4,512]{1,0:T(4,128)(2,1)} %param.17), kind=kLoop, calls=%fused_computation.1 | loop fusion | flops 69632 | bytes 51328 | tf_op jit(solution)/shard_map/add | solution.py:43
  1.5 0.1 broadcast_in_dim.21.place
  1.6 0.9 %shard_map.163 = bf16[8,8,256]{2,1,0:T(8,128)(2,1)} custom-call(s32[2,128]{1,0:T(2,128)S(1)} %broadcast_in_dim.21.place, f32[17,512]{1,0:T(8,128)S(1)} %pad_add_fusion.fields_in), custom_call_target="tpu_custom_call" | custom-call | bytes 35840 | tf_op jit(solution)/shard_map/pallas_call | solution.py:209
  2.5 7.3 %all-to-all-start = ((bf16[8,8,256]{2,1,0:T(8,128)(2,1)}), bf16[8,8,256]{2,1,0:T(8,128)(2,1)S(1)}, u32[]{:S(2)}, u32[]{:S(2)}) async-start(bf16[8,8,256]{2,1,0:T(8,128)(2,1)} %shard_map.163), calls=%async_computation | async-start | bytes 65536 | tf_op jit(solution)/shard_map/all_to_all | solution.py:221
  9.7 0.1 pad.106
  9.8 0.8 %pad_add_fusion.1.numbers = s32[24,32]{1,0:T(8,128)S(1)} fusion(s32[16,32]{1,0:T(8,128)} %bitcast.8, s32[1,32]{1,0:T(1,128)} %bitcast.10, s32[1,32]{1,0:T(1,128)} %bitcast.11, s32[1,32]{1,0:T(1,128)} %bitcast.9, s32[24]{0:T(128)S(1)} %pad.106), kind=kLoop, calls=%fused_computation.3 | loop fusion | flops 3072 | bytes 5600 | tf_op jit(solution)/shard_map/add | solution.py:43
  10.6 0.4 shard_map.164
  11.1 0.6 %copy-done.3 = f32[16,704]{1,0:T(8,128)} copy-done((f32[16,704]{1,0:T(8,128)}, f32[16,704]{1,0:T(8,128)S(1)}, u32[]{:S(2)}) %copy-start.3) | copy-done | bytes 45080
  11.7 0.6 %copy-done.6 = bf16[16,64]{1,0:T(8,128)(2,1)} copy-done((bf16[16,64]{1,0:T(8,128)(2,1)}, bf16[16,64]{1,0:T(8,128)(2,1)S(1)}, u32[]{:S(2)}) %copy-start.6) | copy-done | bytes 2072
  12.3 1.3 %convert_add_fusion.vectors = f32[3072]{0:T(1024)} fusion(bf16[1024]{0:T(1024)(128)(2,1)} %param.30, bf16[512]{0:T(512)(128)(2,1)} %param.32, bf16[512]{0:T(512)(128)(2,1)} %param.28, bf16[512]{0:T(512)(128)(2,1)} %param.27, bf16[512]{0:T(512)(128)(2,1)} %param.26), kind=kLoop, calls=%fused_computation.2 | loop fusion | flops 27648 | bytes 18432 | tf_op jit(solution)/shard_map/add | solution.py:43
  13.6 2.8 %all-to-all-done.arrived = bf16[8,8,256]{2,1,0:T(8,128)(2,1)S(1)} async-done(((bf16[8,8,256]{2,1,0:T(8,128)(2,1)}), bf16[8,8,256]{2,1,0:T(8,128)(2,1)S(1)}, u32[]{:S(2)}, u32[]{:S(2)}) %all-to-all-start) | async-done | bytes 32800 | tf_op jit(solution)/shard_map/all_to_all | solution.py:221
  16.4 0.6 %copy-done.7 = bf16[8,8,256]{2,1,0:T(8,128)(2,1)} copy-done((bf16[8,8,256]{2,1,0:T(8,128)(2,1)}, bf16[8,8,256]{2,1,0:T(8,128)(2,1)S(1)}, u32[]{:S(2)}) %copy-start.7) | copy-done | bytes 32792
  17.0 3.9 %shard_map.165 = f32[4,2048]{1,0:T(4,128)} custom-call(s32[2,128]{1,0:T(2,128)} %copy-done.4, bf16[8,8,256]{2,1,0:T(8,128)(2,1)} %copy-done.7, bf16[16,64]{1,0:T(8,128)(2,1)} %copy-done.6, f32[16,704]{1,0:T(8,128)} %copy-done.3, f32[3072]{0:T(1024)} %convert_add_fusion.vectors, bf16[2,22,32,512]{3,2,1,0:T(8,128)(2,1)} %pool_in.1, bf16[512,2048]{1,0:T(8,128)(2,1)} %weight_in.1), custom_call_target="tpu_custom_call" | custom-call | bytes 3632128 | tf_op jit(solution)/shard_map/pallas_call | solution.py:209
  20.9 0.1 collective-permute-start
  21.0 1.4 %collective-permute-done = f32[4,2048]{1,0:T(4,128)S(1)} collective-permute-done((f32[4,2048]{1,0:T(4,128)}, f32[4,2048]{1,0:T(4,128)S(1)}, u32[]{:S(2)}, u32[]{:S(2)}) %collective-permute-start) | collective-permute-done | bytes 32800 | tf_op jit(solution)/shard_map/ppermute | solution.py:318
  22.4 0.8 %add.86.near = f32[4,2048]{1,0:T(4,128)S(1)} add(f32[4,2048]{1,0:T(4,128)} %shard_map.165, f32[4,2048]{1,0:T(4,128)S(1)} %collective-permute-done) | non-fusion elementwise | flops 8192 | bytes 98304 | tf_op jit(solution)/shard_map/add | solution.py:291
  23.2 1.3 %collective-permute-start.1 = (f32[4,2048]{1,0:T(4,128)S(1)}, f32[4,2048]{1,0:T(4,128)S(1)}, u32[]{:S(2)}, u32[]{:S(2)}) collective-permute-start(f32[4,2048]{1,0:T(4,128)S(1)} %add.86.near), channel_id=1, source_target_pairs={{0,3},{1,2},{2,1},{3,0},{4,7},{5,6},{6,5},{7,4},{8,11},{9,10},{10,... | collective-permute-start | bytes 98312 | tf_op jit(solution)/shard_map/ppermute | solution.py:318
  24.5 2.1 %collective-permute-done.1.far = f32[4,2048]{1,0:T(4,128)S(1)} collective-permute-done((f32[4,2048]{1,0:T(4,128)S(1)}, f32[4,2048]{1,0:T(4,128)S(1)}, u32[]{:S(2)}, u32[]{:S(2)}) %collective-permute-start.1) | collective-permute-done | bytes 32800 | tf_op jit(solution)/shard_map/ppermute | solution.py:318
  26.6 0.7 %copy-done.5 = s32[2,128]{1,0:T(2,128)S(1)} copy-done((s32[2,128]{1,0:T(2,128)S(1)}, s32[2,128]{1,0:T(2,128)}, u32[]{:S(2)}) %copy-start.5) | copy-done | bytes 1048
  27.3 0.2 shard_map.166
  27.5 9.6 %all_to_all.15.rows_in = bf16[8,4,512]{2,1,0:T(4,128)(2,1)S(1)} all-to-all(bf16[8,4,512]{2,1,0:T(4,128)(2,1)S(1)} %get-tuple-element.13), channel_id=1, replica_groups=mesh['req'=8,'tp'=4] {'req'}, dimensions={0} | all-to-all | bytes 65536 | tf_op jit(solution)/shard_map/all_to_all | solution.py:221
  37.1 1.2 %copy-done.1 = bf16[1024,512]{1,0:T(8,128)(2,1)S(1)} copy-done((bf16[1024,512]{1,0:T(8,128)(2,1)S(1)}, bf16[1024,512]{1,0:T(8,128)(2,1)}, u32[]{:S(2)}) %copy-start.1) | copy-done | bytes 1048600
  38.4 0.5 shard_map.167
  38.8 0.0 collective-permute-start.2
  38.9 1.2 %collective-permute-done.2 = bf16[32,1024]{1,0:T(8,128)(2,1)S(1)} collective-permute-done((bf16[32,1024]{1,0:T(8,128)(2,1)S(1)}, bf16[32,1024]{1,0:T(8,128)(2,1)S(1)}, u32[]{:S(2)}, u32[]{:S(2)}) %collective-permute-start.2) | collective-permute-done | bytes 65568 | tf_op jit(solution)/shard_map/ppermute | solution.py:318
  40.1 1.3 %collective-permute-start.3 = (bf16[32,1024]{1,0:T(8,128)(2,1)S(1)}, bf16[32,1024]{1,0:T(8,128)(2,1)S(1)}, u32[]{:S(2)}, u32[]{:S(2)}) collective-permute-start(bf16[32,1024]{1,0:T(8,128)(2,1)S(1)} %add_convert_fusion.near), channel_id=1, source_target_pairs={{0,3},{1,2},{2,1},{3,0},{4,7},{5,6},{6,5},{7,4},{8,11},{9,10},{10,... | collective-permute-start | bytes 196616 | tf_op jit(solution)/shard_map/ppermute | solution.py:318
  41.4 2.8 %collective-permute-done.3.far = bf16[32,1024]{1,0:T(8,128)(2,1)S(1)} collective-permute-done((bf16[32,1024]{1,0:T(8,128)(2,1)S(1)}, bf16[32,1024]{1,0:T(8,128)(2,1)S(1)}, u32[]{:S(2)}, u32[]{:S(2)}) %collective-permute-start.3) | collective-permute-done | bytes 65568 | tf_op jit(solution)/shard_map/ppermute | solution.py:318
  44.2 0.3 shard_map.168
  44.5 9.3 %all_to_all.16.pieces = f32[8,4,512]{2,1,0:T(4,128)S(1)} all-to-all(f32[8,4,512]{2,1,0:T(4,128)S(1)} %shard_map.168), channel_id=1, replica_groups=mesh['req'=8,'tp'=4] {'req'}, dimensions={0} | all-to-all | bytes 131072 | tf_op jit(solution)/shard_map/all_to_all | solution.py:221
  53.8 0.6 %shard_map.169 = bf16[4,512]{1,0:T(4,128)(2,1)} custom-call(f32[8,4,512]{2,1,0:T(4,128)S(1)} %all_to_all.16.pieces, f32[3072]{0:T(1024)S(1)} %copy-done.2), custom_call_target="tpu_custom_call" | custom-call | bytes 77824 | tf_op jit(solution)/shard_map/pallas_call | solution.py:209
  (13 shorter events, 0.0 us)
Async XLA Ops:
  1.6 14.9 %copy-start.4 = (s32[2,128]{1,0:T(2,128)}, s32[2,128]{1,0:T(2,128)S(1)}, u32[]{:S(2)}) copy-start(s32[2,128]{1,0:T(2,128)S(1)} %broadcast_in_dim.21.place) | copy-start | bytes 3076
  2.5 14.0 %all-to-all-start = ((bf16[8,8,256]{2,1,0:T(8,128)(2,1)}), bf16[8,8,256]{2,1,0:T(8,128)(2,1)S(1)}, u32[]{:S(2)}, u32[]{:S(2)}) async-start(bf16[8,8,256]{2,1,0:T(8,128)(2,1)} %shard_map.163), calls=%async_computation | async-start | bytes 65536 | tf_op jit(solution)/shard_map/all_to_all | solution.py:221
  11.0 0.6 %copy-start.3 = (f32[16,704]{1,0:T(8,128)}, f32[16,704]{1,0:T(8,128)S(1)}, u32[]{:S(2)}) copy-start(f32[16,704]{1,0:T(8,128)S(1)} %get-tuple-element.12.valid) | copy-start | bytes 135172
  11.7 0.6 %copy-start.6 = (bf16[16,64]{1,0:T(8,128)(2,1)}, bf16[16,64]{1,0:T(8,128)(2,1)S(1)}, u32[]{:S(2)}) copy-start(bf16[16,64]{1,0:T(8,128)(2,1)S(1)} %get-tuple-element.11.pick) | copy-start | bytes 6148
  13.6 13.0 %copy-start.2 = (f32[3072]{0:T(1024)S(1)}, f32[3072]{0:T(1024)}, u32[]{:S(2)}) copy-start(f32[3072]{0:T(1024)} %convert_add_fusion.vectors) | copy-start | bytes 36868
  16.4 0.6 %copy-start.7 = (bf16[8,8,256]{2,1,0:T(8,128)(2,1)}, bf16[8,8,256]{2,1,0:T(8,128)(2,1)S(1)}, u32[]{:S(2)}) copy-start(bf16[8,8,256]{2,1,0:T(8,128)(2,1)S(1)} %all-to-all-done.arrived) | copy-start | bytes 98308
  20.9 23.3 %copy-start = (bf16[1024,512]{1,0:T(8,128)(2,1)S(1)}, bf16[1024,512]{1,0:T(8,128)(2,1)}, u32[]{:S(2)}) copy-start(bf16[1024,512]{1,0:T(8,128)(2,1)} %weight.3) | copy-start | bytes 3145732
  20.9 1.5 %collective-permute-start = (f32[4,2048]{1,0:T(4,128)}, f32[4,2048]{1,0:T(4,128)S(1)}, u32[]{:S(2)}, u32[]{:S(2)}) collective-permute-start(f32[4,2048]{1,0:T(4,128)} %shard_map.165), channel_id=1, source_target_pairs={{0,1},{1,0},{2,3},{3,2},{4,5},{5,4},{6,7},{7,6},{8,9},{9,8},{10,11... | collective-permute-start | bytes 98312 | tf_op jit(solution)/shard_map/ppermute | solution.py:318
  23.2 3.4 %collective-permute-start.1 = (f32[4,2048]{1,0:T(4,128)S(1)}, f32[4,2048]{1,0:T(4,128)S(1)}, u32[]{:S(2)}, u32[]{:S(2)}) collective-permute-start(f32[4,2048]{1,0:T(4,128)S(1)} %add.86.near), channel_id=1, source_target_pairs={{0,3},{1,2},{2,1},{3,0},{4,7},{5,6},{6,5},{7,4},{8,11},{9,10},{10,... | collective-permute-start | bytes 98312 | tf_op jit(solution)/shard_map/ppermute | solution.py:318
  26.6 0.7 %copy-start.5 = (s32[2,128]{1,0:T(2,128)S(1)}, s32[2,128]{1,0:T(2,128)}, u32[]{:S(2)}) copy-start(s32[2,128]{1,0:T(2,128)} %copy-done.4) | copy-start | bytes 3076
  37.1 1.2 %copy-start.1 = (bf16[1024,512]{1,0:T(8,128)(2,1)S(1)}, bf16[1024,512]{1,0:T(8,128)(2,1)}, u32[]{:S(2)}) copy-start(bf16[1024,512]{1,0:T(8,128)(2,1)} %weight.2) | copy-start | bytes 3145732
  38.8 1.3 %collective-permute-start.2 = (bf16[32,1024]{1,0:T(8,128)(2,1)S(1)}, bf16[32,1024]{1,0:T(8,128)(2,1)S(1)}, u32[]{:S(2)}, u32[]{:S(2)}) collective-permute-start(bf16[32,1024]{1,0:T(8,128)(2,1)S(1)} %shard_map.167), channel_id=1, source_target_pairs={{0,1},{1,0},{2,3},{3,2},{4,5},{5,4},{6,7},{7,6},{8,9},{9,8},{10,11... | collective-permute-start | bytes 196616 | tf_op jit(solution)/shard_map/ppermute | solution.py:318
  40.1 4.1 %collective-permute-start.3 = (bf16[32,1024]{1,0:T(8,128)(2,1)S(1)}, bf16[32,1024]{1,0:T(8,128)(2,1)S(1)}, u32[]{:S(2)}, u32[]{:S(2)}) collective-permute-start(bf16[32,1024]{1,0:T(8,128)(2,1)S(1)} %add_convert_fusion.near), channel_id=1, source_target_pairs={{0,3},{1,2},{2,1},{3,0},{4,7},{5,6},{6,5},{7,4},{8,11},{9,10},{10,... | collective-permute-start | bytes 196616 | tf_op jit(solution)/shard_map/ppermute | solution.py:318

commit v9 on v8

--- a/solution.py
+++ b/solution.py
@@ -13,7 +13,8 @@
 PAIRWISE = 16
 REQ, TP = 8, 4
 WEIGHT_PARTS = 4
-ATTENTION_ROOM = 63.3
+ATTENTION_ROOM = 53.2
+ALL_ROOM = 58
 F32, BF16, I32 = jnp.float32, jnp.bfloat16, jnp.int32
 VMEM = pl.BlockSpec(memory_space=pltpu.VMEM)
 HBM = pl.BlockSpec(memory_space=pltpu.HBM)
@@ -49,20 +50,25 @@
     return vectors[i * cols : (i + 1) * cols][None, :]
 
 
-def pack_kernel(place, fields_in, out):
+def pack_kernel(owner_in, query, key, value, resid, out, owner, q, k, v, r, sems):
+    parts = ((owner_in, owner), (query, q), (key, k), (value, v), (resid, r))
+    copies = [pltpu.make_async_copy(x, y, sems.at[i]) for i, (x, y) in enumerate(parts)]
+    for copy in copies:
+        copy.start()
+    rows, cols = q.shape
     fields = 4
-    used = fields_in.shape[0] - 1
-    rows = used // fields
     count = REQ * rows
-    cols = fields_in.shape[1]
-    shape = (REQ * fields, used)
+    shape = (REQ * fields, fields * rows)
     down, across = iota(shape, 0), iota(shape, 1)
-    here = (count, used)
-    of_mine = hot(iota(here, 0) == place[0:1, 0:1] * rows + iota(here, 1) % rows)
-    owner = fields_in[used : used + 1, :count].astype(BF16)
-    owner_of = onto_mxu(owner, of_mine).astype(I32)
+    here = (count, fields * rows)
+    of_mine = hot(iota(here, 0) == lax.axis_index("req") * rows + iota(here, 1) % rows)
+    copies[0].wait()
+    owner_of = onto_mxu(owner[...].astype(F32).astype(BF16), of_mine).astype(I32)
     pick = hot((down % fields == across // rows) & (owner_of == down // fields))
-    blocks = onto_mxu(pick, fields_in[:used, :].astype(BF16)).astype(BF16)
+    for copy in copies[1:]:
+        copy.wait()
+    all_rows = jnp.concatenate([q[...], k[...], v[...], r[...]], axis=0)
+    blocks = onto_mxu(pick, all_rows).astype(BF16)
     for d in range(REQ):
         block = blocks[d * fields : (d + 1) * fields]
         out[d, :fields, :] = block[:, : cols // 2]
@@ -254,9 +260,16 @@
     position = jnp.stack([lax.axis_index("req"), lax.axis_index("tp")]).astype(I32)
     place = jnp.broadcast_to(position[:, None], (2, HEAD_DIM))
 
-    owner_f = jnp.pad(owner.astype(F32)[None, :], ((0, 0), (0, cols - count)))
-    fields = pile([x.astype(F32) for x in (query, key_new, value_new, resid)] + [owner_f])
-    (packed,) = call(pack_kernel, [arr((REQ, 8, cols // 2))], [VMEM] * 2, [place, fields])
+    (packed,) = call(
+        pack_kernel,
+        [arr((REQ, 8, cols // 2))],
+        [HBM] * 5,
+        [owner[None, :], query, key_new, value_new, resid],
+        [pltpu.VMEM((1, count), I32)]
+        + [pltpu.VMEM((rows, cols), BF16)] * 4
+        + [pltpu.SemaphoreType.DMA((5,))],
+        room=ALL_ROOM,
+    )
     arrived = trade(packed)
     numbers = pile(
         [owner[None, :], order[None, :], lengths[None, :], jnp.zeros((5, count), I32), page_table.T]

time: 55 us -> 48.6 us (0.88)
  local copies, waits for them, and re-layouts: 3.86 us -> 0.15 us
  other arithmetic: 4.41 us -> 1.65 us
  waiting for transfers between devices: 10.4 us -> 11.8 us
  blocking collectives: 18.9 us -> 18.3 us
  Pallas kernels: 6.75 us -> 6.18 us
    unnamed x16 -> x4, local copies, waits for them, and re-layouts: 3.72 us -> 0.01 us
    all_to_all x1, waiting for transfers between devices: 2.83 us -> 4.49 us  [trade(): return lax.all_to_all(blocks, 'req', 0, 0, tiled=True)]
    add x3 -> x2, other arithmetic: 2.89 us -> 1.54 us  [pile(): piled += jnp.pad(p, around)]
    add x1, other arithmetic: 0.77 us -> 0.01 us  [on_pairs(): pair = partial + swap(partial, 'tp', 1)]
    broadcast_in_dim x1 -> x0, other arithmetic: 0.66 us -> none  [on_pairs(): owner_f = jnp.pad(owner.astype(F32)[None, :], ((0, 0), (0, cols - count)))]
    all_to_all x2, blocking collectives: 18.9 us -> 18.3 us  [trade(): return lax.all_to_all(blocks, 'req', 0, 0, tiled=True)]
    pallas_call x7, Pallas kernels: 6.75 us -> 6.18 us  [call(): pl.pallas_call(functools.partial(kernel, **fixed) if fixed else kernel, o...]
where the time goes in v9:
time: 48.6 us; the launch traced here: 48.2 us
  blocking collectives  18.3 us (38%)
  waiting for transfers between devices  11.8 us (24%)
  starting transfers between devices  10 us (21%)
  Pallas kernels  6.18 us (13%)
  other arithmetic  1.65 us (3%)
    all_to_all x2, blocking collectives, trade(): return lax.all_to_all(blocks, 'req', 0, 0, tiled=True)  18.3 us
    ppermute x4, waiting for transfers between devices, swap(): return lax.ppermute(x, axis, [(i, i ^ step) for i in range(n)])  7.32 us
    all_to_all x1, starting transfers between devices, trade(): return lax.all_to_all(blocks, 'req', 0, 0, tiled=True)  7.29 us
    pallas_call x7, Pallas kernels, call(): pl.pallas_call(functools.partial(kernel, **fixed) if fixed else kernel, o...  6.18 us
    all_to_all x1, waiting for transfers between devices, trade(): return lax.all_to_all(blocks, 'req', 0, 0, tiled=True)  4.49 us
    ppermute x4, starting transfers between devices, swap(): return lax.ppermute(x, axis, [(i, i ^ step) for i in range(n)])  2.74 us
    add x2, other arithmetic, pile(): piled += jnp.pad(p, around)  1.54 us
  transfers between devices with their start and end apart: 5, of which 5 were waited for; matrix products, arithmetic and copies ran while one was open for 4% of the time, Pallas kernels for 1%

profile of v9, /device:TPU:0, one launch (start us, length us, event | category | flops | bytes accessed | tf_op | source)
XLA Modules:
  0.0 48.2 jit_solution(17661159899265858164)
XLA Ops:
  0.0 0.0 copy-start.1
  0.0 1.7 %shard_map.163 = bf16[8,8,256]{2,1,0:T(8,128)(2,1)} custom-call(s32[1,32]{1,0:T(1,128)} %bitcast.7, bf16[4,512]{1,0:T(4,128)(2,1)} %query.1, bf16[4,512]{1,0:T(4,128)(2,1)} %key.1, bf16[4,512]{1,0:T(4,128)(2,1)} %value.1, bf16[4,512]{1,0:T(4,128)(2,1)} %resid.1), custom_call_target="tpu_custom_call" | custom-call | bytes 16512 | tf_op jit(solution)/shard_map/pallas_call | solution.py:215
  1.7 7.3 %all-to-all-start = ((bf16[8,8,256]{2,1,0:T(8,128)(2,1)}), bf16[8,8,256]{2,1,0:T(8,128)(2,1)S(1)}, u32[]{:S(2)}, u32[]{:S(2)}) async-start(bf16[8,8,256]{2,1,0:T(8,128)(2,1)} %shard_map.163), calls=%async_computation | async-start | bytes 65536 | tf_op jit(solution)/shard_map/all_to_all | solution.py:227
  9.0 0.1 pad.60
  9.0 0.1 pad_add_fusion.1
  9.1 0.8 %pad_add_fusion.numbers = s32[24,32]{1,0:T(8,128)S(1)} fusion(s32[16,32]{1,0:T(8,128)} %bitcast.6, s32[1,32]{1,0:T(1,128)} %bitcast.9, s32[1,32]{1,0:T(1,128)} %bitcast.10, s32[1,32]{1,0:T(1,128)} %bitcast.8, s32[24]{0:T(128)S(1)} %pad.60), kind=kLoop, calls=%fused_computation.2 | loop fusion | flops 3072 | bytes 5600 | tf_op jit(solution)/shard_map/add | solution.py:44
  9.9 0.1 broadcast_in_dim.19.place
  10.0 0.4 shard_map.164
  10.4 0.8 %convert_add_fusion.vectors = f32[3072]{0:T(1024)S(1)} fusion(bf16[1024]{0:T(1024)(128)(2,1)} %param.30, bf16[512]{0:T(512)(128)(2,1)} %param.32, bf16[512]{0:T(512)(128)(2,1)} %param.28, bf16[512]{0:T(512)(128)(2,1)} %param.27, bf16[512]{0:T(512)(128)(2,1)} %param.26), kind=kLoop, calls=%fused_computation.1 | loop fusion | flops 27648 | bytes 18432 | tf_op jit(solution)/shard_map/add | solution.py:44
  11.2 4.5 %all-to-all-done.arrived = bf16[8,8,256]{2,1,0:T(8,128)(2,1)S(1)} async-done(((bf16[8,8,256]{2,1,0:T(8,128)(2,1)}), bf16[8,8,256]{2,1,0:T(8,128)(2,1)S(1)}, u32[]{:S(2)}, u32[]{:S(2)}) %all-to-all-start) | async-done | bytes 32800 | tf_op jit(solution)/shard_map/all_to_all | solution.py:227
  15.7 0.0 copy-start
  15.7 2.5 %shard_map.165 = f32[4,2048]{1,0:T(4,128)S(1)} custom-call(s32[2,128]{1,0:T(2,128)S(1)} %broadcast_in_dim.19.place, bf16[8,8,256]{2,1,0:T(8,128)(2,1)S(1)} %all-to-all-done.arrived, bf16[16,64]{1,0:T(8,128)(2,1)S(1)} %get-tuple-element.11.pick, f32[16,704]{1,0:T(8,128)S(1)} %get-tuple-element.12.valid, f32[3072]{0:T(1024)S(1)} %convert_add_fusion.vectors, ...), custom_call_target="tpu_custom_call" | custom-call | bytes 3632128 | tf_op jit(solution)/shard_map/pallas_call | solution.py:215
  18.2 0.1 collective-permute-start
  18.3 1.2 %collective-permute-done = f32[4,2048]{1,0:T(4,128)S(1)} collective-permute-done((f32[4,2048]{1,0:T(4,128)S(1)}, f32[4,2048]{1,0:T(4,128)S(1)}, u32[]{:S(2)}, u32[]{:S(2)}) %collective-permute-start) | collective-permute-done | bytes 32800 | tf_op jit(solution)/shard_map/ppermute | solution.py:331
  19.5 1.3 %collective-permute-start.1 = (f32[4,2048]{1,0:T(4,128)S(1)}, f32[4,2048]{1,0:T(4,128)S(1)}, u32[]{:S(2)}, u32[]{:S(2)}) collective-permute-start(f32[4,2048]{1,0:T(4,128)S(1)} %add.58.near), channel_id=1, source_target_pairs={{0,3},{1,2},{2,1},{3,0},{4,7},{5,6},{6,5},{7,4},{8,11},{9,10},{10,... | collective-permute-start | bytes 98312 | tf_op jit(solution)/shard_map/ppermute | solution.py:331
  20.8 2.1 %collective-permute-done.1.far = f32[4,2048]{1,0:T(4,128)S(1)} collective-permute-done((f32[4,2048]{1,0:T(4,128)S(1)}, f32[4,2048]{1,0:T(4,128)S(1)}, u32[]{:S(2)}, u32[]{:S(2)}) %collective-permute-start.1) | collective-permute-done | bytes 32800 | tf_op jit(solution)/shard_map/ppermute | solution.py:331
  22.9 0.2 shard_map.166
  23.1 9.1 %all_to_all.15.rows_in = bf16[8,4,512]{2,1,0:T(4,128)(2,1)S(1)} all-to-all(bf16[8,4,512]{2,1,0:T(4,128)(2,1)S(1)} %get-tuple-element.13), channel_id=1, replica_groups=mesh['req'=8,'tp'=4] {'req'}, dimensions={0} | all-to-all | bytes 65536 | tf_op jit(solution)/shard_map/all_to_all | solution.py:227
  32.2 0.0 copy-done.1
  32.2 0.5 shard_map.167
  32.6 0.0 collective-permute-start.2
  32.7 1.2 %collective-permute-done.2 = bf16[32,1024]{1,0:T(8,128)(2,1)S(1)} collective-permute-done((bf16[32,1024]{1,0:T(8,128)(2,1)S(1)}, bf16[32,1024]{1,0:T(8,128)(2,1)S(1)}, u32[]{:S(2)}, u32[]{:S(2)}) %collective-permute-start.2) | collective-permute-done | bytes 65568 | tf_op jit(solution)/shard_map/ppermute | solution.py:331
  33.9 1.3 %collective-permute-start.3 = (bf16[32,1024]{1,0:T(8,128)(2,1)S(1)}, bf16[32,1024]{1,0:T(8,128)(2,1)S(1)}, u32[]{:S(2)}, u32[]{:S(2)}) collective-permute-start(bf16[32,1024]{1,0:T(8,128)(2,1)S(1)} %add_convert_fusion.near), channel_id=1, source_target_pairs={{0,3},{1,2},{2,1},{3,0},{4,7},{5,6},{6,5},{7,4},{8,11},{9,10},{10,... | collective-permute-start | bytes 196616 | tf_op jit(solution)/shard_map/ppermute | solution.py:331
  35.2 2.8 %collective-permute-done.3.far = bf16[32,1024]{1,0:T(8,128)(2,1)S(1)} collective-permute-done((bf16[32,1024]{1,0:T(8,128)(2,1)S(1)}, bf16[32,1024]{1,0:T(8,128)(2,1)S(1)}, u32[]{:S(2)}, u32[]{:S(2)}) %collective-permute-start.3) | collective-permute-done | bytes 65568 | tf_op jit(solution)/shard_map/ppermute | solution.py:331
  38.0 0.0 copy-done
  38.0 0.3 shard_map.168
  38.3 9.3 %all_to_all.16.pieces = f32[8,4,512]{2,1,0:T(4,128)S(1)} all-to-all(f32[8,4,512]{2,1,0:T(4,128)S(1)} %shard_map.168), channel_id=1, replica_groups=mesh['req'=8,'tp'=4] {'req'}, dimensions={0} | all-to-all | bytes 131072 | tf_op jit(solution)/shard_map/all_to_all | solution.py:227
  47.6 0.6 %shard_map.169 = bf16[4,512]{1,0:T(4,128)(2,1)} custom-call(f32[8,4,512]{2,1,0:T(4,128)S(1)} %all_to_all.16.pieces, f32[3072]{0:T(1024)S(1)} %convert_add_fusion.vectors), custom_call_target="tpu_custom_call" | custom-call | bytes 77824 | tf_op jit(solution)/shard_map/pallas_call | solution.py:215
  (3 shorter events, 0.0 us)
Async XLA Ops:
  0.0 32.2 %copy-start.1 = (bf16[1024,512]{1,0:T(8,128)(2,1)S(1)}, bf16[1024,512]{1,0:T(8,128)(2,1)}, u32[]{:S(2)}) copy-start(bf16[1024,512]{1,0:T(8,128)(2,1)} %weight.2) | copy-start | bytes 3145732
  1.7 14.0 %all-to-all-start = ((bf16[8,8,256]{2,1,0:T(8,128)(2,1)}), bf16[8,8,256]{2,1,0:T(8,128)(2,1)S(1)}, u32[]{:S(2)}, u32[]{:S(2)}) async-start(bf16[8,8,256]{2,1,0:T(8,128)(2,1)} %shard_map.163), calls=%async_computation | async-start | bytes 65536 | tf_op jit(solution)/shard_map/all_to_all | solution.py:227
  15.7 22.4 %copy-start = (bf16[1024,512]{1,0:T(8,128)(2,1)S(1)}, bf16[1024,512]{1,0:T(8,128)(2,1)}, u32[]{:S(2)}) copy-start(bf16[1024,512]{1,0:T(8,128)(2,1)} %weight.3) | copy-start | bytes 3145732
  18.2 1.3 %collective-permute-start = (f32[4,2048]{1,0:T(4,128)S(1)}, f32[4,2048]{1,0:T(4,128)S(1)}, u32[]{:S(2)}, u32[]{:S(2)}) collective-permute-start(f32[4,2048]{1,0:T(4,128)S(1)} %shard_map.165), channel_id=1, source_target_pairs={{0,1},{1,0},{2,3},{3,2},{4,5},{5,4},{6,7},{7,6},{8,9},{9,8},{10,11... | collective-permute-start | bytes 98312 | tf_op jit(solution)/shard_map/ppermute | solution.py:331
  19.5 3.4 %collective-permute-start.1 = (f32[4,2048]{1,0:T(4,128)S(1)}, f32[4,2048]{1,0:T(4,128)S(1)}, u32[]{:S(2)}, u32[]{:S(2)}) collective-permute-start(f32[4,2048]{1,0:T(4,128)S(1)} %add.58.near), channel_id=1, source_target_pairs={{0,3},{1,2},{2,1},{3,0},{4,7},{5,6},{6,5},{7,4},{8,11},{9,10},{10,... | collective-permute-start | bytes 98312 | tf_op jit(solution)/shard_map/ppermute | solution.py:331
  32.6 1.3 %collective-permute-start.2 = (bf16[32,1024]{1,0:T(8,128)(2,1)S(1)}, bf16[32,1024]{1,0:T(8,128)(2,1)S(1)}, u32[]{:S(2)}, u32[]{:S(2)}) collective-permute-start(bf16[32,1024]{1,0:T(8,128)(2,1)S(1)} %shard_map.167), channel_id=1, source_target_pairs={{0,1},{1,0},{2,3},{3,2},{4,5},{5,4},{6,7},{7,6},{8,9},{9,8},{10,11... | collective-permute-start | bytes 196616 | tf_op jit(solution)/shard_map/ppermute | solution.py:331
  33.9 4.1 %collective-permute-start.3 = (bf16[32,1024]{1,0:T(8,128)(2,1)S(1)}, bf16[32,1024]{1,0:T(8,128)(2,1)S(1)}, u32[]{:S(2)}, u32[]{:S(2)}) collective-permute-start(bf16[32,1024]{1,0:T(8,128)(2,1)S(1)} %add_convert_fusion.near), channel_id=1, source_target_pairs={{0,3},{1,2},{2,1},{3,0},{4,7},{5,6},{6,5},{7,4},{8,11},{9,10},{10,... | collective-permute-start | bytes 196616 | tf_op jit(solution)/shard_map/ppermute | solution.py:331

commit v10 on v9

--- a/solution.py
+++ b/solution.py
@@ -12,8 +12,6 @@
 NORM_EPS = 1e-05
 PAIRWISE = 16
 REQ, TP = 8, 4
-WEIGHT_PARTS = 4
-ATTENTION_ROOM = 53.2
 ALL_ROOM = 58
 F32, BF16, I32 = jnp.float32, jnp.bfloat16, jnp.int32
 VMEM = pl.BlockSpec(memory_space=pltpu.VMEM)
@@ -119,18 +117,7 @@
     arrange_own[...] = onto_mxu(ordered, here).astype(BF16)
 
 
-def attention_kernel(
-    place, arrived, pick, valid, vectors, pool_in, weight_in, partial, pool, weight, sems, *, rows
-):
-    deep = weight.shape[0] // WEIGHT_PARTS
-    copies = [pltpu.make_async_copy(pool_in.at[i], pool.at[i], sems.at[i]) for i in range(2)]
-    for i in range(WEIGHT_PARTS):
-        part = pl.ds(i * deep, deep)
-        copies.append(
-            pltpu.make_async_copy(weight_in.at[part], weight.at[part], sems.at[2 + i])
-        )
-    for copy in copies:
-        copy.start()
+def attention_kernel(place, arrived, pick, valid, vectors, pool, weight, partial, *, rows):
     half = arrived.shape[2]
     cols = 2 * half
     heads = cols // HEAD_DIM
@@ -151,21 +138,17 @@
     wide = jnp.where(in_head, tile(query), 0.0)
     positions = valid.shape[1]
     self_score = jnp.sum(wide * tile(key), axis=1, keepdims=True) * scale
-    copies[0].wait()
     scores = nt_dot(wide.astype(BF16), pool[0].reshape(positions, cols)) * scale
     scores = jnp.where(valid[...] > 0.5, scores, -jnp.inf)
     top = jnp.maximum(jnp.max(scores, axis=1, keepdims=True), self_score)
     weights = jnp.exp(scores - top)
     self_weight = jnp.exp(self_score - top)
     total = jnp.sum(weights, axis=1, keepdims=True) + self_weight
-    copies[1].wait()
     numer = onto_mxu(weights.astype(BF16), pool[1].reshape(positions, cols))
     numer = numer + self_weight.astype(BF16).astype(F32) * tile(value)
     numer = jnp.where(in_head, numer / total, 0.0)
     attn = sum(numer[i * rows : (i + 1) * rows] for i in range(heads))
     attn = jnp.concatenate([attn, jnp.zeros_like(attn)], axis=0).astype(BF16)
-    for copy in copies[2:]:
-        copy.wait()
     projected = onto_mxu(attn, weight[...])[:rows]
     extra = resid + row(vectors, 0, cols)
     for t in range(TP):
@@ -174,7 +157,8 @@
 
 
 def norm_kernel(place, near, far, vectors, blocks, stream_own):
-    stream = (near[...] + far[...]).astype(BF16).astype(F32)
+    mine = near[...].astype(BF16).astype(F32)
+    stream = (mine + far[...].astype(F32)).astype(BF16).astype(F32)
     width = stream.shape[1]
     cols = width // TP
     mean = jnp.sum(stream, axis=1, keepdims=True) / width
@@ -288,17 +272,15 @@
         page_len=page_len,
     )
 
+    here = position[0] >= 0
+    pool = jnp.where(here, kv_pool, jnp.zeros_like(kv_pool))
+    weight = jnp.where(here, out_weight, jnp.zeros_like(out_weight))
+
     (partial,) = call(
         attention_kernel,
         [arr((rows, width), F32)],
-        [VMEM] * 5 + [HBM] * 2,
-        [place, arrived, pick, valid, vectors, kv_pool, out_weight],
-        [
-            pltpu.VMEM(kv_pool.shape, BF16),
-            pltpu.VMEM(out_weight.shape, BF16),
-            pltpu.SemaphoreType.DMA((2 + WEIGHT_PARTS,)),
-        ],
-        room=ATTENTION_ROOM,
+        [VMEM] * 7,
+        [place, arrived, pick, valid, vectors, pool, weight],
         rows=rows,
     )
     pair = partial + swap(partial, "tp", 1)
@@ -306,7 +288,7 @@
         norm_kernel,
         [arr((REQ, rows, cols)), arr((rows, cols))],
         [VMEM] * 4,
-        [place, pair, swap(pair, "tp", 3), vectors],
+        [place, pair, swap(pair.astype(BF16), "tp", 3), vectors],
     )
 
     (part,) = call(

time: 48.6 us -> 51.8 us (1.066)
  local copies, waits for them, and re-layouts: 0.15 us -> 4.9 us
  waiting for transfers between devices: 11.8 us -> 8.19 us
  blocking collectives: 18.3 us -> 20.7 us
  Pallas kernels: 6.18 us -> 5.52 us
    unnamed x4 -> x40, local copies, waits for them, and re-layouts: 0.01 us -> 4.75 us
    all_to_all x1, waiting for transfers between devices: 4.49 us -> 1.05 us  [trade(): return lax.all_to_all(blocks, 'req', 0, 0, tiled=True)]
    all_to_all x2, blocking collectives: 18.3 us -> 20.7 us  [trade(): return lax.all_to_all(blocks, 'req', 0, 0, tiled=True)]
    select_n x0 -> x2, other arithmetic: none -> 1.73 us  [the longest x1 1.59 us: on_pairs(): pool = jnp.where(here, kv_pool, jnp.zeros_like(kv_pool))]
    add x2, other arithmetic: 1.54 us -> 0.08 us  [pile(): piled += jnp.pad(p, around)]
    pallas_call x7, Pallas kernels: 6.18 us -> 5.52 us  [call(): pl.pallas_call(functools.partial(kernel, **fixed) if fixed else kernel, o...]
where the time goes in v10:
time: 51.8 us; the launch traced here: 51.4 us
  blocking collectives  20.7 us (40%)
  starting transfers between devices  10 us (19%)
  waiting for transfers between devices  8.19 us (16%)
  Pallas kernels  5.52 us (11%)
  local copies, waits for them, and re-layouts  4.9 us (9%)
  other arithmetic  1.93 us (4%)
    all_to_all x2, blocking collectives, trade(): return lax.all_to_all(blocks, 'req', 0, 0, tiled=True)  20.7 us
    all_to_all x1, starting transfers between devices, trade(): return lax.all_to_all(blocks, 'req', 0, 0, tiled=True)  7.29 us
    ppermute x4, waiting for transfers between devices, swap(): return lax.ppermute(x, axis, [(i, i ^ step) for i in range(n)])  7.14 us
    pallas_call x7, Pallas kernels, call(): pl.pallas_call(functools.partial(kernel, **fixed) if fixed else kernel, o...  5.52 us
    unnamed x40, local copies, waits for them, and re-layouts  4.75 us
    ppermute x4, starting transfers between devices, swap(): return lax.ppermute(x, axis, [(i, i ^ step) for i in range(n)])  2.71 us
    select_n x1, other arithmetic, on_pairs(): pool = jnp.where(here, kv_pool, jnp.zeros_like(kv_pool))  1.59 us
    all_to_all x1, waiting for transfers between devices, trade(): return lax.all_to_all(blocks, 'req', 0, 0, tiled=True)  1.05 us
  transfers between devices with their start and end apart: 5, of which 5 were waited for; matrix products, arithmetic and copies ran while one was open for 4% of the time, Pallas kernels for 1%

profile of v10, /device:TPU:0, one launch (start us, length us, event | category | flops | bytes accessed | tf_op | source)
XLA Modules:
  0.0 51.4 jit_solution(17651935442787107026)
XLA Ops:
  0.0 1.6 %shard_map.163 = bf16[8,8,256]{2,1,0:T(8,128)(2,1)} custom-call(s32[1,32]{1,0:T(1,128)} %bitcast.7, bf16[4,512]{1,0:T(4,128)(2,1)} %query.1, bf16[4,512]{1,0:T(4,128)(2,1)} %key.1, bf16[4,512]{1,0:T(4,128)(2,1)} %value.1, bf16[4,512]{1,0:T(4,128)(2,1)} %resid.1), custom_call_target="tpu_custom_call" | custom-call | bytes 16512 | tf_op jit(solution)/shard_map/pallas_call | solution.py:199
  1.6 7.3 %all-to-all-start = ((bf16[8,8,256]{2,1,0:T(8,128)(2,1)}), bf16[8,8,256]{2,1,0:T(8,128)(2,1)}, u32[]{:S(2)}, u32[]{:S(2)}) async-start(bf16[8,8,256]{2,1,0:T(8,128)(2,1)} %shard_map.163), calls=%async_computation | async-start | bytes 65536 | tf_op jit(solution)/shard_map/all_to_all | solution.py:211
  8.9 0.1 pad.60
  9.0 1.6 %broadcast_select_fusion.1.pool = bf16[2,22,32,512]{3,2,1,0:T(8,128)(2,1)S(1)} fusion(bf16[2,22,32,512]{3,2,1,0:T(8,128)(2,1)} %param.24, pred[]{:T(512)S(6)} %ge.3), kind=kLoop, calls=%fused_computation.1 | loop fusion | flops 720896 | bytes 2883585 | tf_op jit(solution)/shard_map/jit(_where)/select_n | solution.py:276
  10.6 0.3 copy-done.10
  11.0 0.1 broadcast_select_fusion.weight
  11.1 0.1 pad_add_fusion.1
  11.2 0.4 copy-done.11
  11.6 0.1 pad_add_fusion.numbers
  11.7 0.1 broadcast_in_dim.25.place
  11.7 0.4 shard_map.164
  12.2 0.6 %copy-done.2 = f32[16,704]{1,0:T(8,128)} copy-done((f32[16,704]{1,0:T(8,128)}, f32[16,704]{1,0:T(8,128)S(1)}, u32[]{:S(2)}) %copy-start.2) | copy-done | bytes 45080
  12.8 0.6 %copy-done.4 = bf16[32,4]{1,0:T(8,128)(2,1)} copy-done((bf16[32,4]{1,0:T(8,128)(2,1)}, bf16[32,4]{1,0:T(8,128)(2,1)S(1)}, u32[]{:S(2)}) %copy-start.4) | copy-done | bytes 280
  13.4 0.6 %copy-done.6 = bf16[32,32]{1,0:T(8,128)(2,1)} copy-done((bf16[32,32]{1,0:T(8,128)(2,1)}, bf16[32,32]{1,0:T(8,128)(2,1)S(1)}, u32[]{:S(2)}) %copy-start.6) | copy-done | bytes 2072
  14.0 0.6 %copy-done.8 = bf16[16,64]{1,0:T(8,128)(2,1)} copy-done((bf16[16,64]{1,0:T(8,128)(2,1)}, bf16[16,64]{1,0:T(8,128)(2,1)S(1)}, u32[]{:S(2)}) %copy-start.8) | copy-done | bytes 2072
  14.6 1.1 %all-to-all-done.arrived = bf16[8,8,256]{2,1,0:T(8,128)(2,1)} async-done(((bf16[8,8,256]{2,1,0:T(8,128)(2,1)}), bf16[8,8,256]{2,1,0:T(8,128)(2,1)}, u32[]{:S(2)}, u32[]{:S(2)}) %all-to-all-start) | async-done | bytes 32800 | tf_op jit(solution)/shard_map/all_to_all | solution.py:211
  15.7 0.9 %copy-done.3 = f32[16,704]{1,0:T(8,128)S(1)} copy-done((f32[16,704]{1,0:T(8,128)S(1)}, f32[16,704]{1,0:T(8,128)}, u32[]{:S(2)}) %copy-start.3) | copy-done | bytes 45080
  16.6 0.7 %copy-done.9 = bf16[16,64]{1,0:T(8,128)(2,1)S(1)} copy-done((bf16[16,64]{1,0:T(8,128)(2,1)S(1)}, bf16[16,64]{1,0:T(8,128)(2,1)}, u32[]{:S(2)}) %copy-start.9) | copy-done | bytes 2072
  17.2 2.0 %shard_map.165 = f32[4,2048]{1,0:T(4,128)S(1)} custom-call(s32[2,128]{1,0:T(2,128)S(1)} %broadcast_in_dim.25.place, bf16[8,8,256]{2,1,0:T(8,128)(2,1)} %all-to-all-done.arrived, bf16[16,64]{1,0:T(8,128)(2,1)S(1)} %copy-done.9, f32[16,704]{1,0:T(8,128)S(1)} %copy-done.3, f32[3072]{0:T(1024)S(1)} %convert_add_fusion.vectors, ...), custom_call_target="tpu_custom_call" | custom-call | bytes 3632128 | tf_op jit(solution)/shard_map/pallas_call | solution.py:199
  19.2 0.0 collective-permute-start
  19.3 1.2 %collective-permute-done = f32[4,2048]{1,0:T(4,128)S(1)} collective-permute-done((f32[4,2048]{1,0:T(4,128)S(1)}, f32[4,2048]{1,0:T(4,128)S(1)}, u32[]{:S(2)}, u32[]{:S(2)}) %collective-permute-start) | collective-permute-done | bytes 32800 | tf_op jit(solution)/shard_map/ppermute | solution.py:313
  20.5 1.3 %collective-permute-start.1 = (bf16[4,2048]{1,0:T(4,128)(2,1)S(1)}, bf16[4,2048]{1,0:T(4,128)(2,1)S(1)}, u32[]{:S(2)}, u32[]{:S(2)}) collective-permute-start(bf16[4,2048]{1,0:T(4,128)(2,1)S(1)} %get-tuple-element.17), channel_id=1, source_target_pairs={{0,3},{1,2},{2,1},{3,0},{4,7},{5,6},{6,5},{7,4},{8,11},{9,10},{10,... | collective-permute-start | bytes 49160 | tf_op jit(solution)/shard_map/ppermute | solution.py:313
  21.8 1.9 %collective-permute-done.1.far = bf16[4,2048]{1,0:T(4,128)(2,1)S(1)} collective-permute-done((bf16[4,2048]{1,0:T(4,128)(2,1)S(1)}, bf16[4,2048]{1,0:T(4,128)(2,1)S(1)}, u32[]{:S(2)}, u32[]{:S(2)}) %collective-permute-start.1) | collective-permute-done | bytes 16416 | tf_op jit(solution)/shard_map/ppermute | solution.py:313
  23.7 0.2 shard_map.166
  23.9 11.4 %all_to_all.15.rows_in = bf16[8,4,512]{2,1,0:T(4,128)(2,1)S(1)} all-to-all(bf16[8,4,512]{2,1,0:T(4,128)(2,1)S(1)} %get-tuple-element.13), channel_id=1, replica_groups=mesh['req'=8,'tp'=4] {'req'}, dimensions={0} | all-to-all | bytes 65536 | tf_op jit(solution)/shard_map/all_to_all | solution.py:211
  35.3 0.5 shard_map.167
  35.8 1.2 %collective-permute-done.2 = bf16[32,1024]{1,0:T(8,128)(2,1)S(1)} collective-permute-done((bf16[32,1024]{1,0:T(8,128)(2,1)S(1)}, bf16[32,1024]{1,0:T(8,128)(2,1)S(1)}, u32[]{:S(2)}, u32[]{:S(2)}) %collective-permute-start.2) | collective-permute-done | bytes 65568 | tf_op jit(solution)/shard_map/ppermute | solution.py:313
  37.1 1.3 %collective-permute-start.3 = (bf16[32,1024]{1,0:T(8,128)(2,1)S(1)}, bf16[32,1024]{1,0:T(8,128)(2,1)S(1)}, u32[]{:S(2)}, u32[]{:S(2)}) collective-permute-start(bf16[32,1024]{1,0:T(8,128)(2,1)S(1)} %add_convert_fusion.near), channel_id=1, source_target_pairs={{0,3},{1,2},{2,1},{3,0},{4,7},{5,6},{6,5},{7,4},{8,11},{9,10},{10,... | collective-permute-start | bytes 196616 | tf_op jit(solution)/shard_map/ppermute | solution.py:313
  38.4 2.8 %collective-permute-done.3.far = bf16[32,1024]{1,0:T(8,128)(2,1)S(1)} collective-permute-done((bf16[32,1024]{1,0:T(8,128)(2,1)S(1)}, bf16[32,1024]{1,0:T(8,128)(2,1)S(1)}, u32[]{:S(2)}, u32[]{:S(2)}) %collective-permute-start.3) | collective-permute-done | bytes 65568 | tf_op jit(solution)/shard_map/ppermute | solution.py:313
  41.2 0.3 shard_map.168
  41.5 9.3 %all_to_all.16.pieces = f32[8,4,512]{2,1,0:T(4,128)S(1)} all-to-all(f32[8,4,512]{2,1,0:T(4,128)S(1)} %shard_map.168), channel_id=1, replica_groups=mesh['req'=8,'tp'=4] {'req'}, dimensions={0} | all-to-all | bytes 131072 | tf_op jit(solution)/shard_map/all_to_all | solution.py:211
  50.8 0.6 %shard_map.169 = bf16[4,512]{1,0:T(4,128)(2,1)} custom-call(f32[8,4,512]{2,1,0:T(4,128)S(1)} %all_to_all.16.pieces, f32[3072]{0:T(1024)S(1)} %convert_add_fusion.vectors), custom_call_target="tpu_custom_call" | custom-call | bytes 77824 | tf_op jit(solution)/shard_map/pallas_call | solution.py:199
  (37 shorter events, 0.1 us)
Async XLA Ops:
  1.6 14.1 %all-to-all-start = ((bf16[8,8,256]{2,1,0:T(8,128)(2,1)}), bf16[8,8,256]{2,1,0:T(8,128)(2,1)}, u32[]{:S(2)}, u32[]{:S(2)}) async-start(bf16[8,8,256]{2,1,0:T(8,128)(2,1)} %shard_map.163), calls=%async_computation | async-start | bytes 65536 | tf_op jit(solution)/shard_map/all_to_all | solution.py:211
  8.9 2.0 %copy-start.10 = (bf16[512,2048]{1,0:T(8,128)(2,1)S(1)}, bf16[512,2048]{1,0:T(8,128)(2,1)}, u32[]{:S(2)}) copy-start(bf16[512,2048]{1,0:T(8,128)(2,1)} %param.25) | copy-start | bytes 6291460
  10.9 0.7 %copy-start.11 = (s32[32,16]{0,1:T(8,128)S(1)}, s32[32,16]{0,1:T(8,128)}, u32[]{:S(2)}) copy-start(s32[32,16]{0,1:T(8,128)} %param.23) | copy-start | bytes 6148
  10.9 0.7 %copy-start.12 = (s32[32]{0:T(128)S(1)}, s32[32]{0:T(128)}, u32[]{:S(2)}) copy-start(s32[32]{0:T(128)} %param.22) | copy-start | bytes 388
  10.9 0.7 %copy-start.18 = (s32[32]{0:T(128)S(1)}, s32[32]{0:T(128)}, u32[]{:S(2)}) copy-start(s32[32]{0:T(128)} %param.21) | copy-start | bytes 388
  10.9 0.7 %copy-start.19 = (s32[32]{0:T(128)S(1)}, s32[32]{0:T(128)}, u32[]{:S(2)}) copy-start(s32[32]{0:T(128)} %param.33) | copy-start | bytes 388
  10.9 3.7 %copy-start.13 = (bf16[1024]{0:T(1024)(128)(2,1)S(1)}, bf16[1024]{0:T(1024)(128)(2,1)}, u32[]{:S(2)}) copy-start(bf16[1024]{0:T(1024)(128)(2,1)} %param.30) | copy-start | bytes 6148
  10.9 3.7 %copy-start.14 = (bf16[512]{0:T(512)(128)(2,1)S(1)}, bf16[512]{0:T(512)(128)(2,1)}, u32[]{:S(2)}) copy-start(bf16[512]{0:T(512)(128)(2,1)} %param.32) | copy-start | bytes 3076
  10.9 3.6 %copy-start.15 = (bf16[512]{0:T(512)(128)(2,1)S(1)}, bf16[512]{0:T(512)(128)(2,1)}, u32[]{:S(2)}) copy-start(bf16[512]{0:T(512)(128)(2,1)} %param.28) | copy-start | bytes 3076
  10.9 3.6 %copy-start.16 = (bf16[512]{0:T(512)(128)(2,1)S(1)}, bf16[512]{0:T(512)(128)(2,1)}, u32[]{:S(2)}) copy-start(bf16[512]{0:T(512)(128)(2,1)} %param.27) | copy-start | bytes 3076
  11.0 3.6 %copy-start.17 = (bf16[512]{0:T(512)(128)(2,1)S(1)}, bf16[512]{0:T(512)(128)(2,1)}, u32[]{:S(2)}) copy-start(bf16[512]{0:T(512)(128)(2,1)} %param.26) | copy-start | bytes 3076
  12.2 0.6 %copy-start.2 = (f32[16,704]{1,0:T(8,128)}, f32[16,704]{1,0:T(8,128)S(1)}, u32[]{:S(2)}) copy-start(f32[16,704]{1,0:T(8,128)S(1)} %get-tuple-element.12.valid) | copy-start | bytes 135172
  12.8 0.6 %copy-start.4 = (bf16[32,4]{1,0:T(8,128)(2,1)}, bf16[32,4]{1,0:T(8,128)(2,1)S(1)}, u32[]{:S(2)}) copy-start(bf16[32,4]{1,0:T(8,128)(2,1)S(1)} %get-tuple-element.15.arrange_own) | copy-start | bytes 772
  13.4 0.6 %copy-start.6 = (bf16[32,32]{1,0:T(8,128)(2,1)}, bf16[32,32]{1,0:T(8,128)(2,1)S(1)}, u32[]{:S(2)}) copy-start(bf16[32,32]{1,0:T(8,128)(2,1)S(1)} %get-tuple-element.14.arrange) | copy-start | bytes 6148
  14.0 0.6 %copy-start.8 = (bf16[16,64]{1,0:T(8,128)(2,1)}, bf16[16,64]{1,0:T(8,128)(2,1)S(1)}, u32[]{:S(2)}) copy-start(bf16[16,64]{1,0:T(8,128)(2,1)S(1)} %get-tuple-element.11.pick) | copy-start | bytes 6148
  15.7 19.7 %copy-start.1 = (bf16[1024,512]{1,0:T(8,128)(2,1)S(1)}, bf16[1024,512]{1,0:T(8,128)(2,1)}, u32[]{:S(2)}) copy-start(bf16[1024,512]{1,0:T(8,128)(2,1)} %weight.2) | copy-start | bytes 3145732
  15.7 0.9 %copy-start.3 = (f32[16,704]{1,0:T(8,128)S(1)}, f32[16,704]{1,0:T(8,128)}, u32[]{:S(2)}) copy-start(f32[16,704]{1,0:T(8,128)} %copy-done.2) | copy-start | bytes 135172
  16.6 0.7 %copy-start.9 = (bf16[16,64]{1,0:T(8,128)(2,1)S(1)}, bf16[16,64]{1,0:T(8,128)(2,1)}, u32[]{:S(2)}) copy-start(bf16[16,64]{1,0:T(8,128)(2,1)} %copy-done.8) | copy-start | bytes 6148
  17.2 18.1 %copy-start.7 = (bf16[32,32]{1,0:T(8,128)(2,1)S(1)}, bf16[32,32]{1,0:T(8,128)(2,1)}, u32[]{:S(2)}) copy-start(bf16[32,32]{1,0:T(8,128)(2,1)} %copy-done.6) | copy-start | bytes 6148
  17.2 24.0 %copy-start = (bf16[1024,512]{1,0:T(8,128)(2,1)S(1)}, bf16[1024,512]{1,0:T(8,128)(2,1)}, u32[]{:S(2)}) copy-start(bf16[1024,512]{1,0:T(8,128)(2,1)} %weight.3) | copy-start | bytes 3145732
  17.2 24.0 %copy-start.5 = (bf16[32,4]{1,0:T(8,128)(2,1)S(1)}, bf16[32,4]{1,0:T(8,128)(2,1)}, u32[]{:S(2)}) copy-start(bf16[32,4]{1,0:T(8,128)(2,1)} %copy-done.4) | copy-start | bytes 772
  19.2 1.2 %collective-permute-start = (f32[4,2048]{1,0:T(4,128)S(1)}, f32[4,2048]{1,0:T(4,128)S(1)}, u32[]{:S(2)}, u32[]{:S(2)}) collective-permute-start(f32[4,2048]{1,0:T(4,128)S(1)} %shard_map.165), channel_id=1, source_target_pairs={{0,1},{1,0},{2,3},{3,2},{4,5},{5,4},{6,7},{7,6},{8,9},{9,8},{10,11... | collective-permute-start | bytes 98312 | tf_op jit(solution)/shard_map/ppermute | solution.py:313
  20.5 3.2 %collective-permute-start.1 = (bf16[4,2048]{1,0:T(4,128)(2,1)S(1)}, bf16[4,2048]{1,0:T(4,128)(2,1)S(1)}, u32[]{:S(2)}, u32[]{:S(2)}) collective-permute-start(bf16[4,2048]{1,0:T(4,128)(2,1)S(1)} %get-tuple-element.17), channel_id=1, source_target_pairs={{0,3},{1,2},{2,1},{3,0},{4,7},{5,6},{6,5},{7,4},{8,11},{9,10},{10,... | collective-permute-start | bytes 49160 | tf_op jit(solution)/shard_map/ppermute | solution.py:313
  35.8 1.3 %collective-permute-start.2 = (bf16[32,1024]{1,0:T(8,128)(2,1)S(1)}, bf16[32,1024]{1,0:T(8,128)(2,1)S(1)}, u32[]{:S(2)}, u32[]{:S(2)}) collective-permute-start(bf16[32,1024]{1,0:T(8,128)(2,1)S(1)} %shard_map.167), channel_id=1, source_target_pairs={{0,1},{1,0},{2,3},{3,2},{4,5},{5,4},{6,7},{7,6},{8,9},{9,8},{10,11... | collective-permute-start | bytes 196616 | tf_op jit(solution)/shard_map/ppermute | solution.py:313
  37.1 4.1 %collective-permute-start.3 = (bf16[32,1024]{1,0:T(8,128)(2,1)S(1)}, bf16[32,1024]{1,0:T(8,128)(2,1)S(1)}, u32[]{:S(2)}, u32[]{:S(2)}) collective-permute-start(bf16[32,1024]{1,0:T(8,128)(2,1)S(1)} %add_convert_fusion.near), channel_id=1, source_target_pairs={{0,3},{1,2},{2,1},{3,0},{4,7},{5,6},{6,5},{7,4},{8,11},{9,10},{10,... | collective-permute-start | bytes 196616 | tf_op jit(solution)/shard_map/ppermute | solution.py:313

commit v11 on v9

--- a/solution.py
+++ b/solution.py
@@ -174,7 +174,8 @@
 
 
 def norm_kernel(place, near, far, vectors, blocks, stream_own):
-    stream = (near[...] + far[...]).astype(BF16).astype(F32)
+    mine = near[...].astype(BF16).astype(F32)
+    stream = (mine + far[...].astype(F32)).astype(BF16).astype(F32)
     width = stream.shape[1]
     cols = width // TP
     mean = jnp.sum(stream, axis=1, keepdims=True) / width
@@ -202,7 +203,7 @@
     feed = onto_mxu(activated, weight[...]) + onto_mxu(arrange_own[...], stream_own[...])
     rows = out.shape[1]
     for d in range(REQ):
-        out[d] = feed[d * rows : (d + 1) * rows]
+        out[REQ - 1 - d] = feed[d * rows : (d + 1) * rows]
 
 
 def finish_kernel(pieces, vectors, out):
@@ -225,6 +226,11 @@
 
 def trade(blocks):
     return lax.all_to_all(blocks, "req", 0, 0, tiled=True)
+
+
+def trade_back(blocks):
+    group = [list(reversed(range(REQ)))]
+    return lax.all_to_all(blocks, "req", 0, 0, tiled=True, axis_index_groups=group)
 
 
 def on_pairs(
@@ -306,7 +312,7 @@
         norm_kernel,
         [arr((REQ, rows, cols)), arr((rows, cols))],
         [VMEM] * 4,
-        [place, pair, swap(pair, "tp", 3), vectors],
+        [place, pair, swap(pair.astype(BF16), "tp", 3), vectors],
     )
 
     (part,) = call(
@@ -322,7 +328,7 @@
         [VMEM] * 6,
         [part, swap(part, "tp", 3), vectors, down_weight, arrange_own, stream_own],
     )
-    (out,) = call(finish_kernel, [arr((rows, cols))], [VMEM] * 2, [trade(feed), vectors])
+    (out,) = call(finish_kernel, [arr((rows, cols))], [VMEM] * 2, [trade_back(feed), vectors])
     return out
 
 

time: 48.6 us -> 47.9 us (0.986)
    all_to_all x2 -> x1, blocking collectives: 18.3 us -> 9.05 us  [trade(): return lax.all_to_all(blocks, 'req', 0, 0, tiled=True)]
    all_to_all x0 -> x1, blocking collectives: none -> 8.81 us  [trade_back(): lax.all_to_all(blocks, 'req', 0, 0, tiled=True, axis_index_groups=group)]
where the time goes in v11:
time: 47.9 us; the launch traced here: 47.6 us
  blocking collectives  17.9 us (37%)
  waiting for transfers between devices  11.6 us (24%)
  starting transfers between devices  10 us (21%)
  Pallas kernels  6.19 us (13%)
  other arithmetic  1.65 us (3%)
    all_to_all x1, blocking collectives, trade(): return lax.all_to_all(blocks, 'req', 0, 0, tiled=True)  9.05 us
    all_to_all x1, blocking collectives, trade_back(): lax.all_to_all(blocks, 'req', 0, 0, tiled=True, axis_index_groups=group)  8.81 us
    all_to_all x1, starting transfers between devices, trade(): return lax.all_to_all(blocks, 'req', 0, 0, tiled=True)  7.29 us
    ppermute x4, waiting for transfers between devices, swap(): return lax.ppermute(x, axis, [(i, i ^ step) for i in range(n)])  7.14 us
    pallas_call x7, Pallas kernels, call(): pl.pallas_call(functools.partial(kernel, **fixed) if fixed else kernel, o...  6.19 us
    all_to_all x1, waiting for transfers between devices, trade(): return lax.all_to_all(blocks, 'req', 0, 0, tiled=True)  4.49 us
    ppermute x4, starting transfers between devices, swap(): return lax.ppermute(x, axis, [(i, i ^ step) for i in range(n)])  2.75 us
    add x2, other arithmetic, pile(): piled += jnp.pad(p, around)  1.54 us
  transfers between devices with their start and end apart: 5, of which 5 were waited for; matrix products, arithmetic and copies ran while one was open for 4% of the time, Pallas kernels for 1%

profile of v11, /device:TPU:0, one launch (start us, length us, event | category | flops | bytes accessed | tf_op | source)
XLA Modules:
  0.0 47.6 jit_solution(9770162915545424422)
XLA Ops:
  0.0 0.0 copy-start.1
  0.0 1.7 %shard_map.163 = bf16[8,8,256]{2,1,0:T(8,128)(2,1)} custom-call(s32[1,32]{1,0:T(1,128)} %bitcast.7, bf16[4,512]{1,0:T(4,128)(2,1)} %query.1, bf16[4,512]{1,0:T(4,128)(2,1)} %key.1, bf16[4,512]{1,0:T(4,128)(2,1)} %value.1, bf16[4,512]{1,0:T(4,128)(2,1)} %resid.1), custom_call_target="tpu_custom_call" | custom-call | bytes 16512 | tf_op jit(solution)/shard_map/pallas_call | solution.py:216
  1.7 7.3 %all-to-all-start = ((bf16[8,8,256]{2,1,0:T(8,128)(2,1)}), bf16[8,8,256]{2,1,0:T(8,128)(2,1)S(1)}, u32[]{:S(2)}, u32[]{:S(2)}) async-start(bf16[8,8,256]{2,1,0:T(8,128)(2,1)} %shard_map.163), calls=%async_computation | async-start | bytes 65536 | tf_op jit(solution)/shard_map/all_to_all | solution.py:228
  9.0 0.1 pad.60
  9.1 0.1 pad_add_fusion.1
  9.1 0.8 %pad_add_fusion.numbers = s32[24,32]{1,0:T(8,128)S(1)} fusion(s32[16,32]{1,0:T(8,128)} %bitcast.6, s32[1,32]{1,0:T(1,128)} %bitcast.9, s32[1,32]{1,0:T(1,128)} %bitcast.10, s32[1,32]{1,0:T(1,128)} %bitcast.8, s32[24]{0:T(128)S(1)} %pad.60), kind=kLoop, calls=%fused_computation.2 | loop fusion | flops 3072 | bytes 5600 | tf_op jit(solution)/shard_map/add | solution.py:44
  9.9 0.1 broadcast_in_dim.19.place
  10.0 0.4 shard_map.164
  10.4 0.8 %convert_add_fusion.vectors = f32[3072]{0:T(1024)S(1)} fusion(bf16[1024]{0:T(1024)(128)(2,1)} %param.30, bf16[512]{0:T(512)(128)(2,1)} %param.32, bf16[512]{0:T(512)(128)(2,1)} %param.28, bf16[512]{0:T(512)(128)(2,1)} %param.27, bf16[512]{0:T(512)(128)(2,1)} %param.26), kind=kLoop, calls=%fused_computation.1 | loop fusion | flops 27648 | bytes 18432 | tf_op jit(solution)/shard_map/add | solution.py:44
  11.2 4.5 %all-to-all-done.arrived = bf16[8,8,256]{2,1,0:T(8,128)(2,1)S(1)} async-done(((bf16[8,8,256]{2,1,0:T(8,128)(2,1)}), bf16[8,8,256]{2,1,0:T(8,128)(2,1)S(1)}, u32[]{:S(2)}, u32[]{:S(2)}) %all-to-all-start) | async-done | bytes 32800 | tf_op jit(solution)/shard_map/all_to_all | solution.py:228
  15.7 0.0 copy-start
  15.7 2.5 %shard_map.165 = f32[4,2048]{1,0:T(4,128)S(1)} custom-call(s32[2,128]{1,0:T(2,128)S(1)} %broadcast_in_dim.19.place, bf16[8,8,256]{2,1,0:T(8,128)(2,1)S(1)} %all-to-all-done.arrived, bf16[16,64]{1,0:T(8,128)(2,1)S(1)} %get-tuple-element.11.pick, f32[16,704]{1,0:T(8,128)S(1)} %get-tuple-element.12.valid, f32[3072]{0:T(1024)S(1)} %convert_add_fusion.vectors, ...), custom_call_target="tpu_custom_call" | custom-call | bytes 3632128 | tf_op jit(solution)/shard_map/pallas_call | solution.py:216
  18.2 0.1 collective-permute-start
  18.3 1.2 %collective-permute-done = f32[4,2048]{1,0:T(4,128)S(1)} collective-permute-done((f32[4,2048]{1,0:T(4,128)S(1)}, f32[4,2048]{1,0:T(4,128)S(1)}, u32[]{:S(2)}, u32[]{:S(2)}) %collective-permute-start) | collective-permute-done | bytes 32800 | tf_op jit(solution)/shard_map/ppermute | solution.py:337
  19.5 1.3 %collective-permute-start.1 = (bf16[4,2048]{1,0:T(4,128)(2,1)S(1)}, bf16[4,2048]{1,0:T(4,128)(2,1)S(1)}, u32[]{:S(2)}, u32[]{:S(2)}) collective-permute-start(bf16[4,2048]{1,0:T(4,128)(2,1)S(1)} %get-tuple-element.17), channel_id=1, source_target_pairs={{0,3},{1,2},{2,1},{3,0},{4,7},{5,6},{6,5},{7,4},{8,11},{9,10},{10,... | collective-permute-start | bytes 49160 | tf_op jit(solution)/shard_map/ppermute | solution.py:337
  20.8 1.9 %collective-permute-done.1.far = bf16[4,2048]{1,0:T(4,128)(2,1)S(1)} collective-permute-done((bf16[4,2048]{1,0:T(4,128)(2,1)S(1)}, bf16[4,2048]{1,0:T(4,128)(2,1)S(1)}, u32[]{:S(2)}, u32[]{:S(2)}) %collective-permute-start.1) | collective-permute-done | bytes 16416 | tf_op jit(solution)/shard_map/ppermute | solution.py:337
  22.7 0.2 shard_map.166
  22.9 9.1 %all_to_all.15.rows_in = bf16[8,4,512]{2,1,0:T(4,128)(2,1)S(1)} all-to-all(bf16[8,4,512]{2,1,0:T(4,128)(2,1)S(1)} %get-tuple-element.13), channel_id=1, replica_groups=mesh['req'=8,'tp'=4] {'req'}, dimensions={0} | all-to-all | bytes 65536 | tf_op jit(solution)/shard_map/all_to_all | solution.py:228
  32.0 0.0 copy-done.1
  32.0 0.5 shard_map.167
  32.4 0.0 collective-permute-start.2
  32.5 1.2 %collective-permute-done.2 = bf16[32,1024]{1,0:T(8,128)(2,1)S(1)} collective-permute-done((bf16[32,1024]{1,0:T(8,128)(2,1)S(1)}, bf16[32,1024]{1,0:T(8,128)(2,1)S(1)}, u32[]{:S(2)}, u32[]{:S(2)}) %collective-permute-start.2) | collective-permute-done | bytes 65568 | tf_op jit(solution)/shard_map/ppermute | solution.py:337
  33.7 1.3 %collective-permute-start.3 = (bf16[32,1024]{1,0:T(8,128)(2,1)S(1)}, bf16[32,1024]{1,0:T(8,128)(2,1)S(1)}, u32[]{:S(2)}, u32[]{:S(2)}) collective-permute-start(bf16[32,1024]{1,0:T(8,128)(2,1)S(1)} %add_convert_fusion.near), channel_id=1, source_target_pairs={{0,3},{1,2},{2,1},{3,0},{4,7},{5,6},{6,5},{7,4},{8,11},{9,10},{10,... | collective-permute-start | bytes 196616 | tf_op jit(solution)/shard_map/ppermute | solution.py:337
  35.1 2.8 %collective-permute-done.3.far = bf16[32,1024]{1,0:T(8,128)(2,1)S(1)} collective-permute-done((bf16[32,1024]{1,0:T(8,128)(2,1)S(1)}, bf16[32,1024]{1,0:T(8,128)(2,1)S(1)}, u32[]{:S(2)}, u32[]{:S(2)}) %collective-permute-start.3) | collective-permute-done | bytes 65568 | tf_op jit(solution)/shard_map/ppermute | solution.py:337
  37.9 0.0 copy-done
  37.9 0.3 shard_map.168
  38.2 8.8 %all_to_all.16.pieces = f32[8,4,512]{2,1,0:T(4,128)S(1)} all-to-all(f32[8,4,512]{2,1,0:T(4,128)S(1)} %shard_map.168), channel_id=1, replica_groups={{28,24,20,16,12,8,4,0},{29,25,21,17,13,9,5,1},{30,26,22,18,14,10,6,2},{..., dimensions={0} | all-to-all | bytes 131072 | tf_op jit(solution)/shard_map/all_to_all | solution.py:233
  47.0 0.6 %shard_map.169 = bf16[4,512]{1,0:T(4,128)(2,1)} custom-call(f32[8,4,512]{2,1,0:T(4,128)S(1)} %all_to_all.16.pieces, f32[3072]{0:T(1024)S(1)} %convert_add_fusion.vectors), custom_call_target="tpu_custom_call" | custom-call | bytes 77824 | tf_op jit(solution)/shard_map/pallas_call | solution.py:216
  (3 shorter events, 0.0 us)
Async XLA Ops:
  0.0 32.0 %copy-start.1 = (bf16[1024,512]{1,0:T(8,128)(2,1)S(1)}, bf16[1024,512]{1,0:T(8,128)(2,1)}, u32[]{:S(2)}) copy-start(bf16[1024,512]{1,0:T(8,128)(2,1)} %weight.2) | copy-start | bytes 3145732
  1.7 14.0 %all-to-all-start = ((bf16[8,8,256]{2,1,0:T(8,128)(2,1)}), bf16[8,8,256]{2,1,0:T(8,128)(2,1)S(1)}, u32[]{:S(2)}, u32[]{:S(2)}) async-start(bf16[8,8,256]{2,1,0:T(8,128)(2,1)} %shard_map.163), calls=%async_computation | async-start | bytes 65536 | tf_op jit(solution)/shard_map/all_to_all | solution.py:228
  15.7 22.2 %copy-start = (bf16[1024,512]{1,0:T(8,128)(2,1)S(1)}, bf16[1024,512]{1,0:T(8,128)(2,1)}, u32[]{:S(2)}) copy-start(bf16[1024,512]{1,0:T(8,128)(2,1)} %weight.3) | copy-start | bytes 3145732
  18.2 1.3 %collective-permute-start = (f32[4,2048]{1,0:T(4,128)S(1)}, f32[4,2048]{1,0:T(4,128)S(1)}, u32[]{:S(2)}, u32[]{:S(2)}) collective-permute-start(f32[4,2048]{1,0:T(4,128)S(1)} %shard_map.165), channel_id=1, source_target_pairs={{0,1},{1,0},{2,3},{3,2},{4,5},{5,4},{6,7},{7,6},{8,9},{9,8},{10,11... | collective-permute-start | bytes 98312 | tf_op jit(solution)/shard_map/ppermute | solution.py:337
  19.5 3.2 %collective-permute-start.1 = (bf16[4,2048]{1,0:T(4,128)(2,1)S(1)}, bf16[4,2048]{1,0:T(4,128)(2,1)S(1)}, u32[]{:S(2)}, u32[]{:S(2)}) collective-permute-start(bf16[4,2048]{1,0:T(4,128)(2,1)S(1)} %get-tuple-element.17), channel_id=1, source_target_pairs={{0,3},{1,2},{2,1},{3,0},{4,7},{5,6},{6,5},{7,4},{8,11},{9,10},{10,... | collective-permute-start | bytes 49160 | tf_op jit(solution)/shard_map/ppermute | solution.py:337
  32.4 1.3 %collective-permute-start.2 = (bf16[32,1024]{1,0:T(8,128)(2,1)S(1)}, bf16[32,1024]{1,0:T(8,128)(2,1)S(1)}, u32[]{:S(2)}, u32[]{:S(2)}) collective-permute-start(bf16[32,1024]{1,0:T(8,128)(2,1)S(1)} %shard_map.167), channel_id=1, source_target_pairs={{0,1},{1,0},{2,3},{3,2},{4,5},{5,4},{6,7},{7,6},{8,9},{9,8},{10,11... | collective-permute-start | bytes 196616 | tf_op jit(solution)/shard_map/ppermute | solution.py:337
  33.7 4.1 %collective-permute-start.3 = (bf16[32,1024]{1,0:T(8,128)(2,1)S(1)}, bf16[32,1024]{1,0:T(8,128)(2,1)S(1)}, u32[]{:S(2)}, u32[]{:S(2)}) collective-permute-start(bf16[32,1024]{1,0:T(8,128)(2,1)S(1)} %add_convert_fusion.near), channel_id=1, source_target_pairs={{0,3},{1,2},{2,1},{3,0},{4,7},{5,6},{6,5},{7,4},{8,11},{9,10},{10,... | collective-permute-start | bytes 196616 | tf_op jit(solution)/shard_map/ppermute | solution.py:337

commit v12 on v11

--- a/solution.py
+++ b/solution.py
@@ -71,8 +71,8 @@
     blocks = onto_mxu(pick, all_rows).astype(BF16)
     for d in range(REQ):
         block = blocks[d * fields : (d + 1) * fields]
-        out[d, :fields, :] = block[:, : cols // 2]
-        out[d, fields:, :] = block[:, cols // 2 :]
+        out[REQ - 1 - d, :fields, :] = block[:, : cols // 2]
+        out[REQ - 1 - d, fields:, :] = block[:, cols // 2 :]
 
 
 def index_kernel(place, numbers, pick, valid, arrange, arrange_own, *, page_len):
@@ -95,7 +95,8 @@
     down_p, across_p = iota(shape, 0), iota(shape, 1)
     down_i = iota((shape[0], count), 0)
     mine = hot((owner_row == me) & (rank_row == down_i % rows))
-    came = hot(iota((count, shape[1]), 0) // rows == iota((count, shape[1]), 1) // (2 * rows))
+    source = REQ - 1 - iota((count, shape[1]), 1) // (2 * rows)
+    came = hot(iota((count, shape[1]), 0) // rows == source)
     from_there = onto_mxu(mine, came)
     pick[...] = hot((from_there > 0.5) & (down_p // rows == across_p % rows))
 
@@ -113,7 +114,7 @@
     valid[...] = seen
 
     ordered = hot(order_col == across)
-    holds = hot((owner_col == across // rows) & (rank_col == across % rows))
+    holds = hot((owner_col == REQ - 1 - across // rows) & (rank_col == across % rows))
     arrange[...] = onto_mxu(ordered, holds).astype(BF16)
     here = hot((owner_col == me) & (rank_col == iota(arrange_own.shape, 1)))
     arrange_own[...] = onto_mxu(ordered, here).astype(BF16)
@@ -225,10 +226,6 @@
 
 
 def trade(blocks):
-    return lax.all_to_all(blocks, "req", 0, 0, tiled=True)
-
-
-def trade_back(blocks):
     group = [list(reversed(range(REQ)))]
     return lax.all_to_all(blocks, "req", 0, 0, tiled=True, axis_index_groups=group)
 
@@ -328,7 +325,7 @@
         [VMEM] * 6,
         [part, swap(part, "tp", 3), vectors, down_weight, arrange_own, stream_own],
     )
-    (out,) = call(finish_kernel, [arr((rows, cols))], [VMEM] * 2, [trade_back(feed), vectors])
+    (out,) = call(finish_kernel, [arr((rows, cols))], [VMEM] * 2, [trade(feed), vectors])
     return out
 
 

time: 47.9 us -> 46.5 us (0.971)
  waiting for transfers between devices: 11.6 us -> 7.56 us
  starting transfers between devices: 10 us -> 12 us
  blocking collectives: 17.9 us -> 18.5 us
    all_to_all x1, waiting for transfers between devices: 4.49 us -> 0.42 us  [trade(): lax.all_to_all(blocks, 'req', 0, 0, tiled=True, axis_index_groups=group)]
    all_to_all x1, starting transfers between devices: 7.29 us -> 9.29 us  [trade(): lax.all_to_all(blocks, 'req', 0, 0, tiled=True, axis_index_groups=group)]
    all_to_all x2, blocking collectives: 17.9 us -> 18.5 us  [trade(): lax.all_to_all(blocks, 'req', 0, 0, tiled=True, axis_index_groups=group)]
where the time goes in v12:
time: 46.5 us; the launch traced here: 46.1 us
  blocking collectives  18.5 us (40%)
  starting transfers between devices  12 us (26%)
  waiting for transfers between devices  7.56 us (16%)
  Pallas kernels  6.19 us (13%)
  other arithmetic  1.65 us (4%)
    all_to_all x2, blocking collectives, trade(): lax.all_to_all(blocks, 'req', 0, 0, tiled=True, axis_index_groups=group)  18.5 us
    all_to_all x1, starting transfers between devices, trade(): lax.all_to_all(blocks, 'req', 0, 0, tiled=True, axis_index_groups=group)  9.29 us
    ppermute x4, waiting for transfers between devices, swap(): return lax.ppermute(x, axis, [(i, i ^ step) for i in range(n)])  7.14 us
    pallas_call x7, Pallas kernels, call(): pl.pallas_call(functools.partial(kernel, **fixed) if fixed else kernel, o...  6.19 us
    ppermute x4, starting transfers between devices, swap(): return lax.ppermute(x, axis, [(i, i ^ step) for i in range(n)])  2.75 us
    add x2, other arithmetic, pile(): piled += jnp.pad(p, around)  1.54 us
  transfers between devices with their start and end apart: 5, of which 5 were waited for; matrix products, arithmetic and copies ran while one was open for 4% of the time, Pallas kernels for 1%

profile of v12, /device:TPU:0, one launch (start us, length us, event | category | flops | bytes accessed | tf_op | source)
XLA Modules:
  0.0 46.1 jit_solution(14264974585432505168)
XLA Ops:
  0.0 0.0 copy-start.1
  0.0 1.7 %shard_map.163 = bf16[8,8,256]{2,1,0:T(8,128)(2,1)} custom-call(s32[1,32]{1,0:T(1,128)} %bitcast.7, bf16[4,512]{1,0:T(4,128)(2,1)} %query.1, bf16[4,512]{1,0:T(4,128)(2,1)} %key.1, bf16[4,512]{1,0:T(4,128)(2,1)} %value.1, bf16[4,512]{1,0:T(4,128)(2,1)} %resid.1), custom_call_target="tpu_custom_call" | custom-call | bytes 16512 | tf_op jit(solution)/shard_map/pallas_call | solution.py:217
  1.7 9.3 %all-to-all-start = ((bf16[8,8,256]{2,1,0:T(8,128)(2,1)}), bf16[8,8,256]{2,1,0:T(8,128)(2,1)S(1)}, u32[]{:S(2)}, u32[]{:S(2)}) async-start(bf16[8,8,256]{2,1,0:T(8,128)(2,1)} %shard_map.163), calls=%async_computation | async-start | bytes 65536 | tf_op jit(solution)/shard_map/all_to_all | solution.py:230
  11.0 0.1 pad.60
  11.0 0.1 pad_add_fusion.1
  11.1 0.8 %pad_add_fusion.numbers = s32[24,32]{1,0:T(8,128)S(1)} fusion(s32[16,32]{1,0:T(8,128)} %bitcast.6, s32[1,32]{1,0:T(1,128)} %bitcast.9, s32[1,32]{1,0:T(1,128)} %bitcast.10, s32[1,32]{1,0:T(1,128)} %bitcast.8, s32[24]{0:T(128)S(1)} %pad.60), kind=kLoop, calls=%fused_computation.2 | loop fusion | flops 3072 | bytes 5600 | tf_op jit(solution)/shard_map/add | solution.py:44
  11.9 0.1 broadcast_in_dim.19.place
  12.0 0.4 shard_map.164
  12.4 0.8 %convert_add_fusion.vectors = f32[3072]{0:T(1024)S(1)} fusion(bf16[1024]{0:T(1024)(128)(2,1)} %param.30, bf16[512]{0:T(512)(128)(2,1)} %param.32, bf16[512]{0:T(512)(128)(2,1)} %param.28, bf16[512]{0:T(512)(128)(2,1)} %param.27, bf16[512]{0:T(512)(128)(2,1)} %param.26), kind=kLoop, calls=%fused_computation.1 | loop fusion | flops 27648 | bytes 18432 | tf_op jit(solution)/shard_map/add | solution.py:44
  13.2 0.4 all-to-all-done.arrived
  13.6 0.0 copy-start
  13.6 2.5 %shard_map.165 = f32[4,2048]{1,0:T(4,128)S(1)} custom-call(s32[2,128]{1,0:T(2,128)S(1)} %broadcast_in_dim.19.place, bf16[8,8,256]{2,1,0:T(8,128)(2,1)S(1)} %all-to-all-done.arrived, bf16[16,64]{1,0:T(8,128)(2,1)S(1)} %get-tuple-element.11.pick, f32[16,704]{1,0:T(8,128)S(1)} %get-tuple-element.12.valid, f32[3072]{0:T(1024)S(1)} %convert_add_fusion.vectors, ...), custom_call_target="tpu_custom_call" | custom-call | bytes 3632128 | tf_op jit(solution)/shard_map/pallas_call | solution.py:217
  16.1 0.1 collective-permute-start
  16.2 1.2 %collective-permute-done = f32[4,2048]{1,0:T(4,128)S(1)} collective-permute-done((f32[4,2048]{1,0:T(4,128)S(1)}, f32[4,2048]{1,0:T(4,128)S(1)}, u32[]{:S(2)}, u32[]{:S(2)}) %collective-permute-start) | collective-permute-done | bytes 32800 | tf_op jit(solution)/shard_map/ppermute | solution.py:334
  17.4 1.3 %collective-permute-start.1 = (bf16[4,2048]{1,0:T(4,128)(2,1)S(1)}, bf16[4,2048]{1,0:T(4,128)(2,1)S(1)}, u32[]{:S(2)}, u32[]{:S(2)}) collective-permute-start(bf16[4,2048]{1,0:T(4,128)(2,1)S(1)} %get-tuple-element.17), channel_id=1, source_target_pairs={{0,3},{1,2},{2,1},{3,0},{4,7},{5,6},{6,5},{7,4},{8,11},{9,10},{10,... | collective-permute-start | bytes 49160 | tf_op jit(solution)/shard_map/ppermute | solution.py:334
  18.7 1.9 %collective-permute-done.1.far = bf16[4,2048]{1,0:T(4,128)(2,1)S(1)} collective-permute-done((bf16[4,2048]{1,0:T(4,128)(2,1)S(1)}, bf16[4,2048]{1,0:T(4,128)(2,1)S(1)}, u32[]{:S(2)}, u32[]{:S(2)}) %collective-permute-start.1) | collective-permute-done | bytes 16416 | tf_op jit(solution)/shard_map/ppermute | solution.py:334
  20.7 0.2 shard_map.166
  20.9 9.1 %all_to_all.15.rows_in = bf16[8,4,512]{2,1,0:T(4,128)(2,1)S(1)} all-to-all(bf16[8,4,512]{2,1,0:T(4,128)(2,1)S(1)} %get-tuple-element.13), channel_id=1, replica_groups={{28,24,20,16,12,8,4,0},{29,25,21,17,13,9,5,1},{30,26,22,18,14,10,6,2},{..., dimensions={0} | all-to-all | bytes 65536 | tf_op jit(solution)/shard_map/all_to_all | solution.py:230
  29.9 0.0 copy-done.1
  29.9 0.5 shard_map.167
  30.4 0.0 collective-permute-start.2
  30.4 1.2 %collective-permute-done.2 = bf16[32,1024]{1,0:T(8,128)(2,1)S(1)} collective-permute-done((bf16[32,1024]{1,0:T(8,128)(2,1)S(1)}, bf16[32,1024]{1,0:T(8,128)(2,1)S(1)}, u32[]{:S(2)}, u32[]{:S(2)}) %collective-permute-start.2) | collective-permute-done | bytes 65568 | tf_op jit(solution)/shard_map/ppermute | solution.py:334
  31.7 1.3 %collective-permute-start.3 = (bf16[32,1024]{1,0:T(8,128)(2,1)S(1)}, bf16[32,1024]{1,0:T(8,128)(2,1)S(1)}, u32[]{:S(2)}, u32[]{:S(2)}) collective-permute-start(bf16[32,1024]{1,0:T(8,128)(2,1)S(1)} %add_convert_fusion.near), channel_id=1, source_target_pairs={{0,3},{1,2},{2,1},{3,0},{4,7},{5,6},{6,5},{7,4},{8,11},{9,10},{10,... | collective-permute-start | bytes 196616 | tf_op jit(solution)/shard_map/ppermute | solution.py:334
  33.0 2.8 %collective-permute-done.3.far = bf16[32,1024]{1,0:T(8,128)(2,1)S(1)} collective-permute-done((bf16[32,1024]{1,0:T(8,128)(2,1)S(1)}, bf16[32,1024]{1,0:T(8,128)(2,1)S(1)}, u32[]{:S(2)}, u32[]{:S(2)}) %collective-permute-start.3) | collective-permute-done | bytes 65568 | tf_op jit(solution)/shard_map/ppermute | solution.py:334
  35.8 0.0 copy-done
  35.8 0.3 shard_map.168
  36.1 9.4 %all_to_all.16.pieces = f32[8,4,512]{2,1,0:T(4,128)S(1)} all-to-all(f32[8,4,512]{2,1,0:T(4,128)S(1)} %shard_map.168), channel_id=1, replica_groups={{28,24,20,16,12,8,4,0},{29,25,21,17,13,9,5,1},{30,26,22,18,14,10,6,2},{..., dimensions={0} | all-to-all | bytes 131072 | tf_op jit(solution)/shard_map/all_to_all | solution.py:230
  45.5 0.6 %shard_map.169 = bf16[4,512]{1,0:T(4,128)(2,1)} custom-call(f32[8,4,512]{2,1,0:T(4,128)S(1)} %all_to_all.16.pieces, f32[3072]{0:T(1024)S(1)} %convert_add_fusion.vectors), custom_call_target="tpu_custom_call" | custom-call | bytes 77824 | tf_op jit(solution)/shard_map/pallas_call | solution.py:217
  (3 shorter events, 0.0 us)
Async XLA Ops:
  0.0 29.9 %copy-start.1 = (bf16[1024,512]{1,0:T(8,128)(2,1)S(1)}, bf16[1024,512]{1,0:T(8,128)(2,1)}, u32[]{:S(2)}) copy-start(bf16[1024,512]{1,0:T(8,128)(2,1)} %weight.2) | copy-start | bytes 3145732
  1.7 11.9 %all-to-all-start = ((bf16[8,8,256]{2,1,0:T(8,128)(2,1)}), bf16[8,8,256]{2,1,0:T(8,128)(2,1)S(1)}, u32[]{:S(2)}, u32[]{:S(2)}) async-start(bf16[8,8,256]{2,1,0:T(8,128)(2,1)} %shard_map.163), calls=%async_computation | async-start | bytes 65536 | tf_op jit(solution)/shard_map/all_to_all | solution.py:230
  13.6 22.2 %copy-start = (bf16[1024,512]{1,0:T(8,128)(2,1)S(1)}, bf16[1024,512]{1,0:T(8,128)(2,1)}, u32[]{:S(2)}) copy-start(bf16[1024,512]{1,0:T(8,128)(2,1)} %weight.3) | copy-start | bytes 3145732
  16.1 1.3 %collective-permute-start = (f32[4,2048]{1,0:T(4,128)S(1)}, f32[4,2048]{1,0:T(4,128)S(1)}, u32[]{:S(2)}, u32[]{:S(2)}) collective-permute-start(f32[4,2048]{1,0:T(4,128)S(1)} %shard_map.165), channel_id=1, source_target_pairs={{0,1},{1,0},{2,3},{3,2},{4,5},{5,4},{6,7},{7,6},{8,9},{9,8},{10,11... | collective-permute-start | bytes 98312 | tf_op jit(solution)/shard_map/ppermute | solution.py:334
  17.4 3.2 %collective-permute-start.1 = (bf16[4,2048]{1,0:T(4,128)(2,1)S(1)}, bf16[4,2048]{1,0:T(4,128)(2,1)S(1)}, u32[]{:S(2)}, u32[]{:S(2)}) collective-permute-start(bf16[4,2048]{1,0:T(4,128)(2,1)S(1)} %get-tuple-element.17), channel_id=1, source_target_pairs={{0,3},{1,2},{2,1},{3,0},{4,7},{5,6},{6,5},{7,4},{8,11},{9,10},{10,... | collective-permute-start | bytes 49160 | tf_op jit(solution)/shard_map/ppermute | solution.py:334
  30.4 1.3 %collective-permute-start.2 = (bf16[32,1024]{1,0:T(8,128)(2,1)S(1)}, bf16[32,1024]{1,0:T(8,128)(2,1)S(1)}, u32[]{:S(2)}, u32[]{:S(2)}) collective-permute-start(bf16[32,1024]{1,0:T(8,128)(2,1)S(1)} %shard_map.167), channel_id=1, source_target_pairs={{0,1},{1,0},{2,3},{3,2},{4,5},{5,4},{6,7},{7,6},{8,9},{9,8},{10,11... | collective-permute-start | bytes 196616 | tf_op jit(solution)/shard_map/ppermute | solution.py:334
  31.7 4.1 %collective-permute-start.3 = (bf16[32,1024]{1,0:T(8,128)(2,1)S(1)}, bf16[32,1024]{1,0:T(8,128)(2,1)S(1)}, u32[]{:S(2)}, u32[]{:S(2)}) collective-permute-start(bf16[32,1024]{1,0:T(8,128)(2,1)S(1)} %add_convert_fusion.near), channel_id=1, source_target_pairs={{0,3},{1,2},{2,1},{3,0},{4,7},{5,6},{6,5},{7,4},{8,11},{9,10},{10,... | collective-permute-start | bytes 196616 | tf_op jit(solution)/shard_map/ppermute | solution.py:334

commit v13 on v12

--- a/solution.py
+++ b/solution.py
@@ -13,7 +13,7 @@
 PAIRWISE = 16
 REQ, TP = 8, 4
 WEIGHT_PARTS = 4
-ATTENTION_ROOM = 53.2
+ATTENTION_ROOM = 52.2
 ALL_ROOM = 58
 F32, BF16, I32 = jnp.float32, jnp.bfloat16, jnp.int32
 VMEM = pl.BlockSpec(memory_space=pltpu.VMEM)
@@ -121,15 +121,13 @@
 
 
 def attention_kernel(
-    place, arrived, pick, valid, vectors, pool_in, weight_in, partial, pool, weight, sems, *, rows
+    place, arrived, pick, valid, vectors, pool, weight_in, partial, weight, sems, *, rows
 ):
     deep = weight.shape[0] // WEIGHT_PARTS
-    copies = [pltpu.make_async_copy(pool_in.at[i], pool.at[i], sems.at[i]) for i in range(2)]
+    copies = []
     for i in range(WEIGHT_PARTS):
         part = pl.ds(i * deep, deep)
-        copies.append(
-            pltpu.make_async_copy(weight_in.at[part], weight.at[part], sems.at[2 + i])
-        )
+        copies.append(pltpu.make_async_copy(weight_in.at[part], weight.at[part], sems.at[i]))
     for copy in copies:
         copy.start()
     half = arrived.shape[2]
@@ -152,20 +150,18 @@
     wide = jnp.where(in_head, tile(query), 0.0)
     positions = valid.shape[1]
     self_score = jnp.sum(wide * tile(key), axis=1, keepdims=True) * scale
-    copies[0].wait()
     scores = nt_dot(wide.astype(BF16), pool[0].reshape(positions, cols)) * scale
     scores = jnp.where(valid[...] > 0.5, scores, -jnp.inf)
     top = jnp.maximum(jnp.max(scores, axis=1, keepdims=True), self_score)
     weights = jnp.exp(scores - top)
     self_weight = jnp.exp(self_score - top)
     total = jnp.sum(weights, axis=1, keepdims=True) + self_weight
-    copies[1].wait()
     numer = onto_mxu(weights.astype(BF16), pool[1].reshape(positions, cols))
     numer = numer + self_weight.astype(BF16).astype(F32) * tile(value)
     numer = jnp.where(in_head, numer / total, 0.0)
     attn = sum(numer[i * rows : (i + 1) * rows] for i in range(heads))
     attn = jnp.concatenate([attn, jnp.zeros_like(attn)], axis=0).astype(BF16)
-    for copy in copies[2:]:
+    for copy in copies:
         copy.wait()
     projected = onto_mxu(attn, weight[...])[:rows]
     extra = resid + row(vectors, 0, cols)
@@ -204,12 +200,12 @@
     feed = onto_mxu(activated, weight[...]) + onto_mxu(arrange_own[...], stream_own[...])
     rows = out.shape[1]
     for d in range(REQ):
-        out[REQ - 1 - d] = feed[d * rows : (d + 1) * rows]
+        out[REQ - 1 - d] = feed[d * rows : (d + 1) * rows].astype(BF16)
 
 
 def finish_kernel(pieces, vectors, out):
     cols = out.shape[1]
-    out[...] = (jnp.sum(pieces[...], axis=0) + row(vectors, 3, cols)).astype(BF16)
+    out[...] = (jnp.sum(pieces[...].astype(F32), axis=0) + row(vectors, 3, cols)).astype(BF16)
 
 
 def call(kernel, shapes, specs, args, scratch=(), room=16, **fixed):
@@ -291,15 +287,16 @@
         page_len=page_len,
     )
 
+    pool = jnp.where(position[0] >= 0, kv_pool, jnp.zeros_like(kv_pool))
+
     (partial,) = call(
         attention_kernel,
         [arr((rows, width), F32)],
-        [VMEM] * 5 + [HBM] * 2,
-        [place, arrived, pick, valid, vectors, kv_pool, out_weight],
+        [VMEM] * 6 + [HBM],
+        [place, arrived, pick, valid, vectors, pool, out_weight],
         [
-            pltpu.VMEM(kv_pool.shape, BF16),
             pltpu.VMEM(out_weight.shape, BF16),
-            pltpu.SemaphoreType.DMA((2 + WEIGHT_PARTS,)),
+            pltpu.SemaphoreType.DMA((WEIGHT_PARTS,)),
         ],
         room=ATTENTION_ROOM,
         rows=rows,
@@ -321,7 +318,7 @@
     part = (part.astype(F32) + swap(part, "tp", 1).astype(F32)).astype(BF16)
     (feed,) = call(
         down_kernel,
-        [arr((REQ, rows, cols), F32)],
+        [arr((REQ, rows, cols))],
         [VMEM] * 6,
         [part, swap(part, "tp", 3), vectors, down_weight, arrange_own, stream_own],
     )

time: 46.5 us -> 46.2 us (level)
  blocking collectives: 18.5 us -> 17.7 us
  other arithmetic: 1.65 us -> 2.38 us
    select_n x0 -> x1, other arithmetic: none -> 1.48 us  [on_pairs(): pool = jnp.where(position[0] >= 0, kv_pool, jnp.zeros_like(kv_pool))]
    all_to_all x2, blocking collectives: 18.5 us -> 17.7 us  [trade(): lax.all_to_all(blocks, 'req', 0, 0, tiled=True, axis_index_groups=group)]
    add x2, other arithmetic: 1.54 us -> 0.8 us  [pile(): piled += jnp.pad(p, around)]
  transfers between devices with their start and end apart: 5 -> 5, of which waited for: 5 -> 4; matrix products, arithmetic and copies ran while one was open for 4% -> 5% of each run, Pallas kernels for 1% -> 1%
where the time goes in v13:
time: 46.2 us; the launch traced here: 45.8 us
  blocking collectives  17.7 us (38%)
  starting transfers between devices  12 us (26%)
  waiting for transfers between devices  7.14 us (15%)
  Pallas kernels  6.17 us (13%)
  other arithmetic  2.38 us (5%)
    all_to_all x2, blocking collectives, trade(): lax.all_to_all(blocks, 'req', 0, 0, tiled=True, axis_index_groups=group)  17.7 us
    all_to_all x1, starting transfers between devices, trade(): lax.all_to_all(blocks, 'req', 0, 0, tiled=True, axis_index_groups=group)  9.29 us
    ppermute x4, waiting for transfers between devices, swap(): return lax.ppermute(x, axis, [(i, i ^ step) for i in range(n)])  7.14 us
    pallas_call x7, Pallas kernels, call(): pl.pallas_call(functools.partial(kernel, **fixed) if fixed else kernel, o...  6.17 us
    ppermute x4, starting transfers between devices, swap(): return lax.ppermute(x, axis, [(i, i ^ step) for i in range(n)])  2.74 us
    select_n x1, other arithmetic, on_pairs(): pool = jnp.where(position[0] >= 0, kv_pool, jnp.zeros_like(kv_pool))  1.48 us
  transfers between devices with their start and end apart: 5, of which 4 were waited for; matrix products, arithmetic and copies ran while one was open for 5% of the time, Pallas kernels for 1%

profile of v13, /device:TPU:0, one launch (start us, length us, event | category | flops | bytes accessed | tf_op | source)
XLA Modules:
  0.0 45.8 jit_solution(9422898164310130219)
XLA Ops:
  0.0 1.6 %shard_map.163 = bf16[8,8,256]{2,1,0:T(8,128)(2,1)} custom-call(s32[1,32]{1,0:T(1,128)} %bitcast.7, bf16[4,512]{1,0:T(4,128)(2,1)} %query.1, bf16[4,512]{1,0:T(4,128)(2,1)} %key.1, bf16[4,512]{1,0:T(4,128)(2,1)} %value.1, bf16[4,512]{1,0:T(4,128)(2,1)} %resid.1), custom_call_target="tpu_custom_call" | custom-call | bytes 16512 | tf_op jit(solution)/shard_map/pallas_call | solution.py:213
  1.6 9.3 %all-to-all-start = ((bf16[8,8,256]{2,1,0:T(8,128)(2,1)}), bf16[8,8,256]{2,1,0:T(8,128)(2,1)S(1)}, u32[]{:S(2)}, u32[]{:S(2)}) async-start(bf16[8,8,256]{2,1,0:T(8,128)(2,1)} %shard_map.163), calls=%async_computation | async-start | bytes 65536 | tf_op jit(solution)/shard_map/all_to_all | solution.py:226
  10.9 0.1 pad.60
  10.9 0.1 pad_add_fusion.1
  11.0 0.8 %pad_add_fusion.numbers = s32[24,32]{1,0:T(8,128)S(1)} fusion(s32[16,32]{1,0:T(8,128)} %bitcast.6, s32[1,32]{1,0:T(1,128)} %bitcast.9, s32[1,32]{1,0:T(1,128)} %bitcast.10, s32[1,32]{1,0:T(1,128)} %bitcast.8, s32[24]{0:T(128)S(1)} %pad.60), kind=kLoop, calls=%fused_computation.3 | loop fusion | flops 3072 | bytes 5600 | tf_op jit(solution)/shard_map/add | solution.py:44
  11.8 0.1 broadcast_in_dim.22.place
  11.9 0.4 shard_map.164
  12.3 0.0 copy-start.2
  12.3 0.0 copy-start.3
  12.3 0.0 copy-start.4
  12.3 0.0 copy-start.5
  12.3 0.0 copy-start.6
  12.4 1.5 %broadcast_select_fusion.pool = bf16[2,22,32,512]{3,2,1,0:T(8,128)(2,1)S(1)} fusion(bf16[2,22,32,512]{3,2,1,0:T(8,128)(2,1)} %param.24, pred[]{:T(512)S(6)} %ge.3), kind=kLoop, calls=%fused_computation | loop fusion | flops 720896 | bytes 2883585 | tf_op jit(solution)/shard_map/jit(_where)/select_n | solution.py:290
  13.9 0.0 all-to-all-done.arrived
  13.9 0.0 copy-start.1
  13.9 2.6 %shard_map.165 = f32[4,2048]{1,0:T(4,128)S(1)} custom-call(s32[2,128]{1,0:T(2,128)S(1)} %broadcast_in_dim.22.place, bf16[8,8,256]{2,1,0:T(8,128)(2,1)S(1)} %all-to-all-done.arrived, bf16[16,64]{1,0:T(8,128)(2,1)S(1)} %get-tuple-element.11.pick, f32[16,704]{1,0:T(8,128)S(1)} %get-tuple-element.12.valid, f32[3072]{0:T(1024)S(1)} %convert_add_fusion.vectors, ...), custom_call_target="tpu_custom_call" | custom-call | bytes 3632128 | tf_op jit(solution)/shard_map/pallas_call | solution.py:213
  16.6 0.0 copy-start
  16.6 0.1 collective-permute-start
  16.7 1.2 %collective-permute-done = f32[4,2048]{1,0:T(4,128)S(1)} collective-permute-done((f32[4,2048]{1,0:T(4,128)S(1)}, f32[4,2048]{1,0:T(4,128)S(1)}, u32[]{:S(2)}, u32[]{:S(2)}) %collective-permute-start) | collective-permute-done | bytes 32800 | tf_op jit(solution)/shard_map/ppermute | solution.py:331
  17.9 1.3 %collective-permute-start.1 = (bf16[4,2048]{1,0:T(4,128)(2,1)S(1)}, bf16[4,2048]{1,0:T(4,128)(2,1)S(1)}, u32[]{:S(2)}, u32[]{:S(2)}) collective-permute-start(bf16[4,2048]{1,0:T(4,128)(2,1)S(1)} %get-tuple-element.17), channel_id=1, source_target_pairs={{0,3},{1,2},{2,1},{3,0},{4,7},{5,6},{6,5},{7,4},{8,11},{9,10},{10,... | collective-permute-start | bytes 49160 | tf_op jit(solution)/shard_map/ppermute | solution.py:331
  19.2 1.9 %collective-permute-done.1.far = bf16[4,2048]{1,0:T(4,128)(2,1)S(1)} collective-permute-done((bf16[4,2048]{1,0:T(4,128)(2,1)S(1)}, bf16[4,2048]{1,0:T(4,128)(2,1)S(1)}, u32[]{:S(2)}, u32[]{:S(2)}) %collective-permute-start.1) | collective-permute-done | bytes 16416 | tf_op jit(solution)/shard_map/ppermute | solution.py:331
  21.1 0.2 shard_map.166
  21.3 8.6 %all_to_all.15.rows_in = bf16[8,4,512]{2,1,0:T(4,128)(2,1)S(1)} all-to-all(bf16[8,4,512]{2,1,0:T(4,128)(2,1)S(1)} %get-tuple-element.13), channel_id=1, replica_groups={{28,24,20,16,12,8,4,0},{29,25,21,17,13,9,5,1},{30,26,22,18,14,10,6,2},{..., dimensions={0} | all-to-all | bytes 65536 | tf_op jit(solution)/shard_map/all_to_all | solution.py:226
  29.9 0.5 shard_map.167
  30.4 0.0 collective-permute-start.2
  30.4 1.2 %collective-permute-done.2 = bf16[32,1024]{1,0:T(8,128)(2,1)S(1)} collective-permute-done((bf16[32,1024]{1,0:T(8,128)(2,1)S(1)}, bf16[32,1024]{1,0:T(8,128)(2,1)S(1)}, u32[]{:S(2)}, u32[]{:S(2)}) %collective-permute-start.2) | collective-permute-done | bytes 65568 | tf_op jit(solution)/shard_map/ppermute | solution.py:331
  31.7 1.3 %collective-permute-start.3 = (bf16[32,1024]{1,0:T(8,128)(2,1)S(1)}, bf16[32,1024]{1,0:T(8,128)(2,1)S(1)}, u32[]{:S(2)}, u32[]{:S(2)}) collective-permute-start(bf16[32,1024]{1,0:T(8,128)(2,1)S(1)} %add_convert_fusion.near), channel_id=1, source_target_pairs={{0,3},{1,2},{2,1},{3,0},{4,7},{5,6},{6,5},{7,4},{8,11},{9,10},{10,... | collective-permute-start | bytes 196616 | tf_op jit(solution)/shard_map/ppermute | solution.py:331
  33.0 2.8 %collective-permute-done.3.far = bf16[32,1024]{1,0:T(8,128)(2,1)S(1)} collective-permute-done((bf16[32,1024]{1,0:T(8,128)(2,1)S(1)}, bf16[32,1024]{1,0:T(8,128)(2,1)S(1)}, u32[]{:S(2)}, u32[]{:S(2)}) %collective-permute-start.3) | collective-permute-done | bytes 65568 | tf_op jit(solution)/shard_map/ppermute | solution.py:331
  35.8 0.0 copy-done
  35.8 0.3 shard_map.168
  36.1 9.1 %all_to_all.16.pieces = bf16[8,4,512]{2,1,0:T(4,128)(2,1)S(1)} all-to-all(bf16[8,4,512]{2,1,0:T(4,128)(2,1)S(1)} %shard_map.168), channel_id=1, replica_groups={{28,24,20,16,12,8,4,0},{29,25,21,17,13,9,5,1},{30,26,22,18,14,10,6,2},{..., dimensions={0} | all-to-all | bytes 65536 | tf_op jit(solution)/shard_map/all_to_all | solution.py:226
  45.2 0.6 %shard_map.169 = bf16[4,512]{1,0:T(4,128)(2,1)} custom-call(bf16[8,4,512]{2,1,0:T(4,128)(2,1)S(1)} %all_to_all.16.pieces, f32[3072]{0:T(1024)S(1)} %convert_add_fusion.vectors), custom_call_target="tpu_custom_call" | custom-call | bytes 45056 | tf_op jit(solution)/shard_map/pallas_call | solution.py:213
  (10 shorter events, 0.1 us)
Async XLA Ops:
  1.6 12.3 %all-to-all-start = ((bf16[8,8,256]{2,1,0:T(8,128)(2,1)}), bf16[8,8,256]{2,1,0:T(8,128)(2,1)S(1)}, u32[]{:S(2)}, u32[]{:S(2)}) async-start(bf16[8,8,256]{2,1,0:T(8,128)(2,1)} %shard_map.163), calls=%async_computation | async-start | bytes 65536 | tf_op jit(solution)/shard_map/all_to_all | solution.py:226
  12.3 1.5 %copy-start.2 = (bf16[1024]{0:T(1024)(128)(2,1)S(1)}, bf16[1024]{0:T(1024)(128)(2,1)}, u32[]{:S(2)}) copy-start(bf16[1024]{0:T(1024)(128)(2,1)} %param.30) | copy-start | bytes 6148
  12.3 1.5 %copy-start.3 = (bf16[512]{0:T(512)(128)(2,1)S(1)}, bf16[512]{0:T(512)(128)(2,1)}, u32[]{:S(2)}) copy-start(bf16[512]{0:T(512)(128)(2,1)} %param.32) | copy-start | bytes 3076
  12.3 1.5 %copy-start.4 = (bf16[512]{0:T(512)(128)(2,1)S(1)}, bf16[512]{0:T(512)(128)(2,1)}, u32[]{:S(2)}) copy-start(bf16[512]{0:T(512)(128)(2,1)} %param.28) | copy-start | bytes 3076
  12.3 1.5 %copy-start.5 = (bf16[512]{0:T(512)(128)(2,1)S(1)}, bf16[512]{0:T(512)(128)(2,1)}, u32[]{:S(2)}) copy-start(bf16[512]{0:T(512)(128)(2,1)} %param.27) | copy-start | bytes 3076
  12.3 1.5 %copy-start.6 = (bf16[512]{0:T(512)(128)(2,1)S(1)}, bf16[512]{0:T(512)(128)(2,1)}, u32[]{:S(2)}) copy-start(bf16[512]{0:T(512)(128)(2,1)} %param.26) | copy-start | bytes 3076
  13.9 16.0 %copy-start.1 = (bf16[1024,512]{1,0:T(8,128)(2,1)S(1)}, bf16[1024,512]{1,0:T(8,128)(2,1)}, u32[]{:S(2)}) copy-start(bf16[1024,512]{1,0:T(8,128)(2,1)} %weight.2) | copy-start | bytes 3145732
  16.6 19.2 %copy-start = (bf16[1024,512]{1,0:T(8,128)(2,1)S(1)}, bf16[1024,512]{1,0:T(8,128)(2,1)}, u32[]{:S(2)}) copy-start(bf16[1024,512]{1,0:T(8,128)(2,1)} %weight.3) | copy-start | bytes 3145732
  16.6 1.3 %collective-permute-start = (f32[4,2048]{1,0:T(4,128)S(1)}, f32[4,2048]{1,0:T(4,128)S(1)}, u32[]{:S(2)}, u32[]{:S(2)}) collective-permute-start(f32[4,2048]{1,0:T(4,128)S(1)} %shard_map.165), channel_id=1, source_target_pairs={{0,1},{1,0},{2,3},{3,2},{4,5},{5,4},{6,7},{7,6},{8,9},{9,8},{10,11... | collective-permute-start | bytes 98312 | tf_op jit(solution)/shard_map/ppermute | solution.py:331
  17.9 3.2 %collective-permute-start.1 = (bf16[4,2048]{1,0:T(4,128)(2,1)S(1)}, bf16[4,2048]{1,0:T(4,128)(2,1)S(1)}, u32[]{:S(2)}, u32[]{:S(2)}) collective-permute-start(bf16[4,2048]{1,0:T(4,128)(2,1)S(1)} %get-tuple-element.17), channel_id=1, source_target_pairs={{0,3},{1,2},{2,1},{3,0},{4,7},{5,6},{6,5},{7,4},{8,11},{9,10},{10,... | collective-permute-start | bytes 49160 | tf_op jit(solution)/shard_map/ppermute | solution.py:331
  30.4 1.3 %collective-permute-start.2 = (bf16[32,1024]{1,0:T(8,128)(2,1)S(1)}, bf16[32,1024]{1,0:T(8,128)(2,1)S(1)}, u32[]{:S(2)}, u32[]{:S(2)}) collective-permute-start(bf16[32,1024]{1,0:T(8,128)(2,1)S(1)} %shard_map.167), channel_id=1, source_target_pairs={{0,1},{1,0},{2,3},{3,2},{4,5},{5,4},{6,7},{7,6},{8,9},{9,8},{10,11... | collective-permute-start | bytes 196616 | tf_op jit(solution)/shard_map/ppermute | solution.py:331
  31.7 4.1 %collective-permute-start.3 = (bf16[32,1024]{1,0:T(8,128)(2,1)S(1)}, bf16[32,1024]{1,0:T(8,128)(2,1)S(1)}, u32[]{:S(2)}, u32[]{:S(2)}) collective-permute-start(bf16[32,1024]{1,0:T(8,128)(2,1)S(1)} %add_convert_fusion.near), channel_id=1, source_target_pairs={{0,3},{1,2},{2,1},{3,0},{4,7},{5,6},{6,5},{7,4},{8,11},{9,10},{10,... | collective-permute-start | bytes 196616 | tf_op jit(solution)/shard_map/ppermute | solution.py:331

commit v14 on v13

--- a/solution.py
+++ b/solution.py
@@ -12,8 +12,7 @@
 NORM_EPS = 1e-05
 PAIRWISE = 16
 REQ, TP = 8, 4
-WEIGHT_PARTS = 4
-ATTENTION_ROOM = 52.2
+ATTENTION_ROOM = 51.2
 ALL_ROOM = 58
 F32, BF16, I32 = jnp.float32, jnp.bfloat16, jnp.int32
 VMEM = pl.BlockSpec(memory_space=pltpu.VMEM)
@@ -121,15 +120,11 @@
 
 
 def attention_kernel(
-    place, arrived, pick, valid, vectors, pool, weight_in, partial, weight, sems, *, rows
+    place, arrived, pick, valid, vectors, pool, upper, weight, partial, rounded, lower, sem, *, rows
 ):
-    deep = weight.shape[0] // WEIGHT_PARTS
-    copies = []
-    for i in range(WEIGHT_PARTS):
-        part = pl.ds(i * deep, deep)
-        copies.append(pltpu.make_async_copy(weight_in.at[part], weight.at[part], sems.at[i]))
-    for copy in copies:
-        copy.start()
+    deep = upper.shape[0]
+    copy = pltpu.make_async_copy(weight.at[pl.ds(deep, deep)], lower, sem)
+    copy.start()
     half = arrived.shape[2]
     cols = 2 * half
     heads = cols // HEAD_DIM
@@ -161,28 +156,30 @@
     numer = jnp.where(in_head, numer / total, 0.0)
     attn = sum(numer[i * rows : (i + 1) * rows] for i in range(heads))
     attn = jnp.concatenate([attn, jnp.zeros_like(attn)], axis=0).astype(BF16)
-    for copy in copies:
-        copy.wait()
-    projected = onto_mxu(attn, weight[...])[:rows]
+    projected = onto_mxu(attn[:, :deep], upper[...])
+    copy.wait()
+    projected = (projected + onto_mxu(attn[:, deep:], lower[...]))[:rows]
     extra = resid + row(vectors, 0, cols)
     for t in range(TP):
         mine = jnp.where(place[1:2, 0:1] == t, extra, 0.0)
-        partial[:, t * cols : (t + 1) * cols] = projected[:, t * cols : (t + 1) * cols] + mine
-
-
-def norm_kernel(place, near, far, vectors, blocks, stream_own):
-    mine = near[...].astype(BF16).astype(F32)
-    stream = (mine + far[...].astype(F32)).astype(BF16).astype(F32)
+        whole = projected[:, t * cols : (t + 1) * cols] + mine
+        partial[:, t * cols : (t + 1) * cols] = whole
+        rounded[:, t * cols : (t + 1) * cols] = whole.astype(BF16)
+
+
+def norm_kernel(place, own, sibling, far, far_sibling, vectors, blocks, stream_own):
+    others = sibling[...].astype(F32) + far[...].astype(F32) + far_sibling[...].astype(F32)
+    stream = (own[...] + others).astype(BF16).astype(F32)
     width = stream.shape[1]
     cols = width // TP
     mean = jnp.sum(stream, axis=1, keepdims=True) / width
     var = jnp.sum((stream - mean) ** 2, axis=1, keepdims=True) / width
-    own = stream[:, :cols]
+    mine = stream[:, :cols]
     for t in range(1, TP):
-        own = jnp.where(place[1:2, 0:1] == t, stream[:, t * cols : (t + 1) * cols], own)
-    stream_own[...] = own.astype(BF16)
+        mine = jnp.where(place[1:2, 0:1] == t, stream[:, t * cols : (t + 1) * cols], mine)
+    stream_own[...] = mine.astype(BF16)
     gain, bias = row(vectors, 1, cols), row(vectors, 2, cols)
-    block = ((own - mean) * lax.rsqrt(var + NORM_EPS) * gain + bias).astype(BF16)
+    block = ((mine - mean) * lax.rsqrt(var + NORM_EPS) * gain + bias).astype(BF16)
     for d in range(REQ):
         blocks[d] = block
 
@@ -287,26 +284,25 @@
         page_len=page_len,
     )
 
-    pool = jnp.where(position[0] >= 0, kv_pool, jnp.zeros_like(kv_pool))
-
-    (partial,) = call(
+    here = position[0] >= 0
+    pool = jnp.where(here, kv_pool, jnp.zeros_like(kv_pool))
+    upper = out_weight[: cols // 2]
+    upper = jnp.where(here, upper, jnp.zeros_like(upper))
+
+    partial, rounded = call(
         attention_kernel,
-        [arr((rows, width), F32)],
-        [VMEM] * 6 + [HBM],
-        [place, arrived, pick, valid, vectors, pool, out_weight],
-        [
-            pltpu.VMEM(out_weight.shape, BF16),
-            pltpu.SemaphoreType.DMA((WEIGHT_PARTS,)),
-        ],
+        [arr((rows, width), F32), arr((rows, width))],
+        [VMEM] * 7 + [HBM],
+        [place, arrived, pick, valid, vectors, pool, upper, out_weight],
+        [pltpu.VMEM(upper.shape, BF16), pltpu.SemaphoreType.DMA],
         room=ATTENTION_ROOM,
         rows=rows,
     )
-    pair = partial + swap(partial, "tp", 1)
     blocks, stream_own = call(
         norm_kernel,
         [arr((REQ, rows, cols)), arr((rows, cols))],
-        [VMEM] * 4,
-        [place, pair, swap(pair.astype(BF16), "tp", 3), vectors],
+        [VMEM] * 6,
+        [place, partial] + [swap(rounded, "tp", step) for step in (1, 2, 3)] + [vectors],
     )
 
     (part,) = call(

time: 46.2 us -> 45.2 us (0.978)
  Pallas kernels: 6.17 us -> 5.32 us
  other arithmetic: 2.38 us -> 1.67 us
  local copies, waits for them, and re-layouts: 0.19 us -> 0.85 us
    pallas_call x7, Pallas kernels: 6.17 us -> 5.32 us  [call(): pl.pallas_call(functools.partial(kernel, **fixed) if fixed else kernel, o...]
    add x2, other arithmetic: 0.8 us -> 0.08 us  [pile(): piled += jnp.pad(p, around)]
    unnamed x14 -> x24, local copies, waits for them, and re-layouts: 0.04 us -> 0.7 us
    ppermute x4 -> x5, waiting for transfers between devices: 7.14 us -> 7.26 us  [swap(): return lax.ppermute(x, axis, [(i, i ^ step) for i in range(n)])]
    select_n x1 -> x2, other arithmetic: 1.48 us -> 1.49 us  [the longest x1 1.39 us: on_pairs(): upper = jnp.where(here, upper, jnp.zeros_like(upper))]
    ppermute x4 -> x5, starting transfers between devices: 2.74 us -> 2.75 us  [swap(): return lax.ppermute(x, axis, [(i, i ^ step) for i in range(n)])]
  transfers between devices with their start and end apart: 5 -> 6, of which waited for: 4 -> 4; matrix products, arithmetic and copies ran while one was open for 5% -> 4% of each run, Pallas kernels for 1% -> 1%
where the time goes in v14:
time: 45.2 us; the launch traced here: 44.8 us
  blocking collectives  17.5 us (39%)
  starting transfers between devices  12 us (27%)
  waiting for transfers between devices  7.26 us (16%)
  Pallas kernels  5.32 us (12%)
  other arithmetic  1.67 us (4%)
  local copies, waits for them, and re-layouts  0.85 us (2%)
    all_to_all x2, blocking collectives, trade(): lax.all_to_all(blocks, 'req', 0, 0, tiled=True, axis_index_groups=group)  17.5 us
    all_to_all x1, starting transfers between devices, trade(): lax.all_to_all(blocks, 'req', 0, 0, tiled=True, axis_index_groups=group)  9.28 us
    ppermute x5, waiting for transfers between devices, swap(): return lax.ppermute(x, axis, [(i, i ^ step) for i in range(n)])  7.26 us
    pallas_call x7, Pallas kernels, call(): pl.pallas_call(functools.partial(kernel, **fixed) if fixed else kernel, o...  5.32 us
    ppermute x5, starting transfers between devices, swap(): return lax.ppermute(x, axis, [(i, i ^ step) for i in range(n)])  2.75 us
    select_n x1, other arithmetic, on_pairs(): upper = jnp.where(here, upper, jnp.zeros_like(upper))  1.39 us
  transfers between devices with their start and end apart: 6, of which 4 were waited for; matrix products, arithmetic and copies ran while one was open for 4% of the time, Pallas kernels for 1%

profile of v14, /device:TPU:0, one launch (start us, length us, event | category | flops | bytes accessed | tf_op | source)
XLA Modules:
  0.0 44.8 jit_solution(17223384123702649785)
XLA Ops:
  0.0 1.6 %shard_map.163 = bf16[8,8,256]{2,1,0:T(8,128)(2,1)} custom-call(s32[1,32]{1,0:T(1,128)} %bitcast.7, bf16[4,512]{1,0:T(4,128)(2,1)} %query.1, bf16[4,512]{1,0:T(4,128)(2,1)} %key.1, bf16[4,512]{1,0:T(4,128)(2,1)} %value.1, bf16[4,512]{1,0:T(4,128)(2,1)} %resid.1), custom_call_target="tpu_custom_call" | custom-call | bytes 16512 | tf_op jit(solution)/shard_map/pallas_call | solution.py:210
  1.6 9.3 %all-to-all-start = ((bf16[8,8,256]{2,1,0:T(8,128)(2,1)}), bf16[8,8,256]{2,1,0:T(8,128)(2,1)S(1)}, u32[]{:S(2)}, u32[]{:S(2)}) async-start(bf16[8,8,256]{2,1,0:T(8,128)(2,1)} %shard_map.163), calls=%async_computation | async-start | bytes 65536 | tf_op jit(solution)/shard_map/all_to_all | solution.py:223
  10.9 0.1 pad.60
  10.9 1.4 %slice_select_fusion.upper = bf16[256,2048]{1,0:T(8,128)(2,1)S(1)} fusion(bf16[512,2048]{1,0:T(8,128)(2,1)} %weight.3, pred[]{:T(512)S(6)} %ge.3), kind=kLoop, calls=%fused_computation.1 | loop fusion | flops 524288 | bytes 2097153 | tf_op jit(solution)/shard_map/jit(_where)/select_n | solution.py:290
  12.3 0.2 copy-done.2
  12.5 0.0 copy-start.5
  12.6 0.0 copy-start.6
  12.6 0.0 copy-start.7
  12.6 0.0 copy-start.8
  12.6 0.1 broadcast_select_fusion.pool
  12.7 0.1 pad_add_fusion.1
  12.8 0.4 copy-done.3
  13.2 0.1 pad_add_fusion.numbers
  13.3 0.1 broadcast_in_dim.25.place
  13.4 0.4 shard_map.164
  13.9 0.0 copy-start.1
  13.9 1.8 %shard_map.165 = (f32[4,2048]{1,0:T(4,128)S(1)}, bf16[4,2048]{1,0:T(4,128)(2,1)S(1)}) custom-call(s32[2,128]{1,0:T(2,128)S(1)} %broadcast_in_dim.25.place, bf16[8,8,256]{2,1,0:T(8,128)(2,1)S(1)} %all-to-all-done.arrived, bf16[16,64]{1,0:T(8,128)(2,1)S(1)} %get-tuple-element.13.pick, f32[16,704]{1,0:T(8,128)S(1)} %get-tuple-element.14.valid, ...), custom_call_target="tpu_custom_call" | custom-call | bytes 4680704 | tf_op jit(solution)/shard_map/pallas_call | solution.py:210
  15.7 0.7 %collective-permute-start.2 = (bf16[4,2048]{1,0:T(4,128)(2,1)S(1)}, bf16[4,2048]{1,0:T(4,128)(2,1)S(1)}, u32[]{:S(2)}, u32[]{:S(2)}) collective-permute-start(bf16[4,2048]{1,0:T(4,128)(2,1)S(1)} %get-tuple-element.16), channel_id=1, source_target_pairs={{0,3},{1,2},{2,1},{3,0},{4,7},{5,6},{6,5},{7,4},{8,11},{9,10},{10,... | collective-permute-start | bytes 49160 | tf_op jit(solution)/shard_map/ppermute | solution.py:327
  16.4 0.9 %collective-permute-start.1 = (bf16[4,2048]{1,0:T(4,128)(2,1)S(1)}, bf16[4,2048]{1,0:T(4,128)(2,1)S(1)}, u32[]{:S(2)}, u32[]{:S(2)}) collective-permute-start(bf16[4,2048]{1,0:T(4,128)(2,1)S(1)} %get-tuple-element.16), channel_id=1, source_target_pairs={{0,2},{1,3},{2,0},{3,1},{4,6},{5,7},{6,4},{7,5},{8,10},{9,11},{10,... | collective-permute-start | bytes 49160 | tf_op jit(solution)/shard_map/ppermute | solution.py:327
  17.3 0.3 collective-permute-start
  17.6 1.4 %collective-permute-done.2.far_sibling = bf16[4,2048]{1,0:T(4,128)(2,1)S(1)} collective-permute-done((bf16[4,2048]{1,0:T(4,128)(2,1)S(1)}, bf16[4,2048]{1,0:T(4,128)(2,1)S(1)}, u32[]{:S(2)}, u32[]{:S(2)}) %collective-permute-start.2) | collective-permute-done | bytes 16416 | tf_op jit(solution)/shard_map/ppermute | solution.py:327
  19.1 1.3 %collective-permute-done.1.far = bf16[4,2048]{1,0:T(4,128)(2,1)S(1)} collective-permute-done((bf16[4,2048]{1,0:T(4,128)(2,1)S(1)}, bf16[4,2048]{1,0:T(4,128)(2,1)S(1)}, u32[]{:S(2)}, u32[]{:S(2)}) %collective-permute-start.1) | collective-permute-done | bytes 16416 | tf_op jit(solution)/shard_map/ppermute | solution.py:327
  20.3 0.2 shard_map.166
  20.5 8.4 %all_to_all.15.rows_in = bf16[8,4,512]{2,1,0:T(4,128)(2,1)S(1)} all-to-all(bf16[8,4,512]{2,1,0:T(4,128)(2,1)S(1)} %get-tuple-element.17), channel_id=1, replica_groups={{28,24,20,16,12,8,4,0},{29,25,21,17,13,9,5,1},{30,26,22,18,14,10,6,2},{..., dimensions={0} | all-to-all | bytes 65536 | tf_op jit(solution)/shard_map/all_to_all | solution.py:223
  29.0 0.5 %shard_map.167 = bf16[32,1024]{1,0:T(8,128)(2,1)S(1)} custom-call(bf16[8,4,512]{2,1,0:T(4,128)(2,1)S(1)} %all_to_all.15.rows_in, bf16[32,32]{1,0:T(8,128)(2,1)S(1)} %get-tuple-element.18.arrange, bf16[1024,512]{1,0:T(8,128)(2,1)S(1)} %copy-done.1), custom_call_target="tpu_custom_call" | custom-call | bytes 1083392 | tf_op jit(solution)/shard_map/pallas_call | solution.py:210
  29.4 0.0 collective-permute-start.3
  29.5 1.2 %collective-permute-done.3 = bf16[32,1024]{1,0:T(8,128)(2,1)S(1)} collective-permute-done((bf16[32,1024]{1,0:T(8,128)(2,1)S(1)}, bf16[32,1024]{1,0:T(8,128)(2,1)S(1)}, u32[]{:S(2)}, u32[]{:S(2)}) %collective-permute-start.3) | collective-permute-done | bytes 65568 | tf_op jit(solution)/shard_map/ppermute | solution.py:327
  30.7 0.8 %collective-permute-start.4 = (bf16[32,1024]{1,0:T(8,128)(2,1)S(1)}, bf16[32,1024]{1,0:T(8,128)(2,1)S(1)}, u32[]{:S(2)}, u32[]{:S(2)}) collective-permute-start(bf16[32,1024]{1,0:T(8,128)(2,1)S(1)} %add_convert_fusion.near), channel_id=1, source_target_pairs={{0,3},{1,2},{2,1},{3,0},{4,7},{5,6},{6,5},{7,4},{8,11},{9,10},{10,... | collective-permute-start | bytes 196616 | tf_op jit(solution)/shard_map/ppermute | solution.py:327
  31.5 3.3 %collective-permute-done.4.far = bf16[32,1024]{1,0:T(8,128)(2,1)S(1)} collective-permute-done((bf16[32,1024]{1,0:T(8,128)(2,1)S(1)}, bf16[32,1024]{1,0:T(8,128)(2,1)S(1)}, u32[]{:S(2)}, u32[]{:S(2)}) %collective-permute-start.4) | collective-permute-done | bytes 65568 | tf_op jit(solution)/shard_map/ppermute | solution.py:327
  34.9 0.3 shard_map.168
  35.1 9.1 %all_to_all.16.pieces = bf16[8,4,512]{2,1,0:T(4,128)(2,1)S(1)} all-to-all(bf16[8,4,512]{2,1,0:T(4,128)(2,1)S(1)} %shard_map.168), channel_id=1, replica_groups={{28,24,20,16,12,8,4,0},{29,25,21,17,13,9,5,1},{30,26,22,18,14,10,6,2},{..., dimensions={0} | all-to-all | bytes 65536 | tf_op jit(solution)/shard_map/all_to_all | solution.py:223
  44.2 0.6 %shard_map.169 = bf16[4,512]{1,0:T(4,128)(2,1)} custom-call(bf16[8,4,512]{2,1,0:T(4,128)(2,1)S(1)} %all_to_all.16.pieces, f32[3072]{0:T(1024)S(1)} %convert_add_fusion.vectors), custom_call_target="tpu_custom_call" | custom-call | bytes 45056 | tf_op jit(solution)/shard_map/pallas_call | solution.py:210
  (22 shorter events, 0.1 us)
Async XLA Ops:
  1.6 12.3 %all-to-all-start = ((bf16[8,8,256]{2,1,0:T(8,128)(2,1)}), bf16[8,8,256]{2,1,0:T(8,128)(2,1)S(1)}, u32[]{:S(2)}, u32[]{:S(2)}) async-start(bf16[8,8,256]{2,1,0:T(8,128)(2,1)} %shard_map.163), calls=%async_computation | async-start | bytes 65536 | tf_op jit(solution)/shard_map/all_to_all | solution.py:223
  10.9 1.7 %copy-start.2 = (bf16[2,22,32,512]{3,2,1,0:T(8,128)(2,1)S(1)}, bf16[2,22,32,512]{3,2,1,0:T(8,128)(2,1)}, u32[]{:S(2)}) copy-start(bf16[2,22,32,512]{3,2,1,0:T(8,128)(2,1)} %param.24) | copy-start | bytes 4325380
  12.5 0.7 %copy-start.3 = (s32[32,16]{0,1:T(8,128)S(1)}, s32[32,16]{0,1:T(8,128)}, u32[]{:S(2)}) copy-start(s32[32,16]{0,1:T(8,128)} %param.23) | copy-start | bytes 6148
  12.5 0.7 %copy-start.4 = (s32[32]{0:T(128)S(1)}, s32[32]{0:T(128)}, u32[]{:S(2)}) copy-start(s32[32]{0:T(128)} %param.22) | copy-start | bytes 388
  12.5 0.7 %copy-start.10 = (s32[32]{0:T(128)S(1)}, s32[32]{0:T(128)}, u32[]{:S(2)}) copy-start(s32[32]{0:T(128)} %param.21) | copy-start | bytes 388
  12.5 0.7 %copy-start.11 = (s32[32]{0:T(128)S(1)}, s32[32]{0:T(128)}, u32[]{:S(2)}) copy-start(s32[32]{0:T(128)} %param.33) | copy-start | bytes 388
  12.5 1.3 %copy-start.5 = (bf16[1024]{0:T(1024)(128)(2,1)S(1)}, bf16[1024]{0:T(1024)(128)(2,1)}, u32[]{:S(2)}) copy-start(bf16[1024]{0:T(1024)(128)(2,1)} %param.30) | copy-start | bytes 6148
  12.6 1.3 %copy-start.6 = (bf16[512]{0:T(512)(128)(2,1)S(1)}, bf16[512]{0:T(512)(128)(2,1)}, u32[]{:S(2)}) copy-start(bf16[512]{0:T(512)(128)(2,1)} %param.32) | copy-start | bytes 3076
  12.6 1.3 %copy-start.7 = (bf16[512]{0:T(512)(128)(2,1)S(1)}, bf16[512]{0:T(512)(128)(2,1)}, u32[]{:S(2)}) copy-start(bf16[512]{0:T(512)(128)(2,1)} %param.28) | copy-start | bytes 3076
  12.6 1.3 %copy-start.8 = (bf16[512]{0:T(512)(128)(2,1)S(1)}, bf16[512]{0:T(512)(128)(2,1)}, u32[]{:S(2)}) copy-start(bf16[512]{0:T(512)(128)(2,1)} %param.27) | copy-start | bytes 3076
  12.6 1.3 %copy-start.9 = (bf16[512]{0:T(512)(128)(2,1)S(1)}, bf16[512]{0:T(512)(128)(2,1)}, u32[]{:S(2)}) copy-start(bf16[512]{0:T(512)(128)(2,1)} %param.26) | copy-start | bytes 3076
  13.9 15.1 %copy-start.1 = (bf16[1024,512]{1,0:T(8,128)(2,1)S(1)}, bf16[1024,512]{1,0:T(8,128)(2,1)}, u32[]{:S(2)}) copy-start(bf16[1024,512]{1,0:T(8,128)(2,1)} %weight.4) | copy-start | bytes 3145732
  15.7 19.2 %copy-start = (bf16[1024,512]{1,0:T(8,128)(2,1)S(1)}, bf16[1024,512]{1,0:T(8,128)(2,1)}, u32[]{:S(2)}) copy-start(bf16[1024,512]{1,0:T(8,128)(2,1)} %weight.5) | copy-start | bytes 3145732
  15.7 3.4 %collective-permute-start.2 = (bf16[4,2048]{1,0:T(4,128)(2,1)S(1)}, bf16[4,2048]{1,0:T(4,128)(2,1)S(1)}, u32[]{:S(2)}, u32[]{:S(2)}) collective-permute-start(bf16[4,2048]{1,0:T(4,128)(2,1)S(1)} %get-tuple-element.16), channel_id=1, source_target_pairs={{0,3},{1,2},{2,1},{3,0},{4,7},{5,6},{6,5},{7,4},{8,11},{9,10},{10,... | collective-permute-start | bytes 49160 | tf_op jit(solution)/shard_map/ppermute | solution.py:327
  16.4 3.9 %collective-permute-start.1 = (bf16[4,2048]{1,0:T(4,128)(2,1)S(1)}, bf16[4,2048]{1,0:T(4,128)(2,1)S(1)}, u32[]{:S(2)}, u32[]{:S(2)}) collective-permute-start(bf16[4,2048]{1,0:T(4,128)(2,1)S(1)} %get-tuple-element.16), channel_id=1, source_target_pairs={{0,2},{1,3},{2,0},{3,1},{4,6},{5,7},{6,4},{7,5},{8,10},{9,11},{10,... | collective-permute-start | bytes 49160 | tf_op jit(solution)/shard_map/ppermute | solution.py:327
  17.3 3.0 %collective-permute-start = (bf16[4,2048]{1,0:T(4,128)(2,1)S(1)}, bf16[4,2048]{1,0:T(4,128)(2,1)S(1)}, u32[]{:S(2)}, u32[]{:S(2)}) collective-permute-start(bf16[4,2048]{1,0:T(4,128)(2,1)S(1)} %get-tuple-element.16), channel_id=1, source_target_pairs={{0,1},{1,0},{2,3},{3,2},{4,5},{5,4},{6,7},{7,6},{8,9},{9,8},{10,11... | collective-permute-start | bytes 49160 | tf_op jit(solution)/shard_map/ppermute | solution.py:327
  29.4 1.3 %collective-permute-start.3 = (bf16[32,1024]{1,0:T(8,128)(2,1)S(1)}, bf16[32,1024]{1,0:T(8,128)(2,1)S(1)}, u32[]{:S(2)}, u32[]{:S(2)}) collective-permute-start(bf16[32,1024]{1,0:T(8,128)(2,1)S(1)} %shard_map.167), channel_id=1, source_target_pairs={{0,1},{1,0},{2,3},{3,2},{4,5},{5,4},{6,7},{7,6},{8,9},{9,8},{10,11... | collective-permute-start | bytes 196616 | tf_op jit(solution)/shard_map/ppermute | solution.py:327
  30.7 4.1 %collective-permute-start.4 = (bf16[32,1024]{1,0:T(8,128)(2,1)S(1)}, bf16[32,1024]{1,0:T(8,128)(2,1)S(1)}, u32[]{:S(2)}, u32[]{:S(2)}) collective-permute-start(bf16[32,1024]{1,0:T(8,128)(2,1)S(1)} %add_convert_fusion.near), channel_id=1, source_target_pairs={{0,3},{1,2},{2,1},{3,0},{4,7},{5,6},{6,5},{7,4},{8,11},{9,10},{10,... | collective-permute-start | bytes 196616 | tf_op jit(solution)/shard_map/ppermute | solution.py:327

commit v15 on v14

--- a/solution.py
+++ b/solution.py
@@ -17,6 +17,13 @@
 F32, BF16, I32 = jnp.float32, jnp.bfloat16, jnp.int32
 VMEM = pl.BlockSpec(memory_space=pltpu.VMEM)
 HBM = pl.BlockSpec(memory_space=pltpu.HBM)
+
+ENDS_FIRST = [3, 4, 2, 5, 1, 6, 0, 7]
+LOW_FIRST = [7, 6, 5, 4, 3, 2, 1, 0]
+
+
+def ends_first(place):
+    return jnp.where(place % 2 == 0, 3 - place // 2, 4 + place // 2)
 
 
 def iota(shape, dim):
@@ -70,8 +77,9 @@
     blocks = onto_mxu(pick, all_rows).astype(BF16)
     for d in range(REQ):
         block = blocks[d * fields : (d + 1) * fields]
-        out[REQ - 1 - d, :fields, :] = block[:, : cols // 2]
-        out[REQ - 1 - d, fields:, :] = block[:, cols // 2 :]
+        at = ENDS_FIRST.index(d)
+        out[at, :fields, :] = block[:, : cols // 2]
+        out[at, fields:, :] = block[:, cols // 2 :]
 
 
 def index_kernel(place, numbers, pick, valid, arrange, arrange_own, *, page_len):
@@ -94,7 +102,7 @@
     down_p, across_p = iota(shape, 0), iota(shape, 1)
     down_i = iota((shape[0], count), 0)
     mine = hot((owner_row == me) & (rank_row == down_i % rows))
-    source = REQ - 1 - iota((count, shape[1]), 1) // (2 * rows)
+    source = ends_first(iota((count, shape[1]), 1) // (2 * rows))
     came = hot(iota((count, shape[1]), 0) // rows == source)
     from_there = onto_mxu(mine, came)
     pick[...] = hot((from_there > 0.5) & (down_p // rows == across_p % rows))
@@ -113,7 +121,7 @@
     valid[...] = seen
 
     ordered = hot(order_col == across)
-    holds = hot((owner_col == REQ - 1 - across // rows) & (rank_col == across % rows))
+    holds = hot((owner_col == ends_first(across // rows)) & (rank_col == across % rows))
     arrange[...] = onto_mxu(ordered, holds).astype(BF16)
     here = hot((owner_col == me) & (rank_col == iota(arrange_own.shape, 1)))
     arrange_own[...] = onto_mxu(ordered, here).astype(BF16)
@@ -197,7 +205,7 @@
     feed = onto_mxu(activated, weight[...]) + onto_mxu(arrange_own[...], stream_own[...])
     rows = out.shape[1]
     for d in range(REQ):
-        out[REQ - 1 - d] = feed[d * rows : (d + 1) * rows].astype(BF16)
+        out[LOW_FIRST.index(d)] = feed[d * rows : (d + 1) * rows].astype(BF16)
 
 
 def finish_kernel(pieces, vectors, out):
@@ -218,9 +226,8 @@
     )(*args)
 
 
-def trade(blocks):
-    group = [list(reversed(range(REQ)))]
-    return lax.all_to_all(blocks, "req", 0, 0, tiled=True, axis_index_groups=group)
+def trade(blocks, group):
+    return lax.all_to_all(blocks, "req", 0, 0, tiled=True, axis_index_groups=[group])
 
 
 def on_pairs(
@@ -266,7 +273,7 @@
         + [pltpu.SemaphoreType.DMA((5,))],
         room=ALL_ROOM,
     )
-    arrived = trade(packed)
+    arrived = trade(packed, ENDS_FIRST)
     numbers = pile(
         [owner[None, :], order[None, :], lengths[None, :], jnp.zeros((5, count), I32), page_table.T]
     )
@@ -309,7 +316,7 @@
         up_kernel,
         [arr((count, hidden))],
         [VMEM] * 3,
-        [trade(blocks), arrange, up_weight_t],
+        [trade(blocks, ENDS_FIRST), arrange, up_weight_t],
     )
     part = (part.astype(F32) + swap(part, "tp", 1).astype(F32)).astype(BF16)
     (feed,) = call(
@@ -318,7 +325,7 @@
         [VMEM] * 6,
         [part, swap(part, "tp", 3), vectors, down_weight, arrange_own, stream_own],
     )
-    (out,) = call(finish_kernel, [arr((rows, cols))], [VMEM] * 2, [trade(feed), vectors])
+    (out,) = call(finish_kernel, [arr((rows, cols))], [VMEM] * 2, [trade(feed, LOW_FIRST), vectors])
     return out
 
 

time: 45.2 us -> 43.6 us (0.965)
  starting transfers between devices: 12 us -> 11.1 us
  blocking collectives: 17.5 us -> 16.8 us
    all_to_all x1, starting transfers between devices: 9.28 us -> 7.85 us  [trade(): lax.all_to_all(blocks, 'req', 0, 0, tiled=True, axis_index_groups=[group])]
    all_to_all x1, waiting for transfers between devices: 0.01 us -> 1.3 us  [trade(): lax.all_to_all(blocks, 'req', 0, 0, tiled=True, axis_index_groups=[group])]
    ppermute x5, waiting for transfers between devices: 7.26 us -> 6.02 us  [swap(): return lax.ppermute(x, axis, [(i, i ^ step) for i in range(n)])]
    all_to_all x2, blocking collectives: 17.5 us -> 16.8 us  [trade(): lax.all_to_all(blocks, 'req', 0, 0, tiled=True, axis_index_groups=[group])]
    ppermute x5, starting transfers between devices: 2.75 us -> 3.25 us  [swap(): return lax.ppermute(x, axis, [(i, i ^ step) for i in range(n)])]
  transfers between devices with their start and end apart: 6 -> 6, of which waited for: 4 -> 5; matrix products, arithmetic and copies ran while one was open for 4% -> 4% of each run, Pallas kernels for 1% -> 1%
where the time goes in v15:
time: 43.6 us; the launch traced here: 43.2 us
  blocking collectives  16.8 us (39%)
  starting transfers between devices  11.1 us (25%)
  waiting for transfers between devices  7.32 us (17%)
  Pallas kernels  5.32 us (12%)
  other arithmetic  1.67 us (4%)
  local copies, waits for them, and re-layouts  0.84 us (2%)
    all_to_all x2, blocking collectives, trade(): lax.all_to_all(blocks, 'req', 0, 0, tiled=True, axis_index_groups=[group])  16.8 us
    all_to_all x1, starting transfers between devices, trade(): lax.all_to_all(blocks, 'req', 0, 0, tiled=True, axis_index_groups=[group])  7.85 us
    ppermute x5, waiting for transfers between devices, swap(): return lax.ppermute(x, axis, [(i, i ^ step) for i in range(n)])  6.02 us
    pallas_call x7, Pallas kernels, call(): pl.pallas_call(functools.partial(kernel, **fixed) if fixed else kernel, o...  5.32 us
    ppermute x5, starting transfers between devices, swap(): return lax.ppermute(x, axis, [(i, i ^ step) for i in range(n)])  3.25 us
    select_n x1, other arithmetic, on_pairs(): upper = jnp.where(here, upper, jnp.zeros_like(upper))  1.39 us
    all_to_all x1, waiting for transfers between devices, trade(): lax.all_to_all(blocks, 'req', 0, 0, tiled=True, axis_index_groups=[group])  1.3 us
  transfers between devices with their start and end apart: 6, of which 5 were waited for; matrix products, arithmetic and copies ran while one was open for 4% of the time, Pallas kernels for 1%

profile of v15, /device:TPU:0, one launch (start us, length us, event | category | flops | bytes accessed | tf_op | source)
XLA Modules:
  0.0 43.2 jit_solution(6001004081088277036)
XLA Ops:
  0.0 1.6 %shard_map.163 = bf16[8,8,256]{2,1,0:T(8,128)(2,1)} custom-call(s32[1,32]{1,0:T(1,128)} %bitcast.7, bf16[4,512]{1,0:T(4,128)(2,1)} %query.1, bf16[4,512]{1,0:T(4,128)(2,1)} %key.1, bf16[4,512]{1,0:T(4,128)(2,1)} %value.1, bf16[4,512]{1,0:T(4,128)(2,1)} %resid.1), custom_call_target="tpu_custom_call" | custom-call | bytes 16512 | tf_op jit(solution)/shard_map/pallas_call | solution.py:218
  1.6 7.9 %all-to-all-start = ((bf16[8,8,256]{2,1,0:T(8,128)(2,1)}), bf16[8,8,256]{2,1,0:T(8,128)(2,1)S(1)}, u32[]{:S(2)}, u32[]{:S(2)}) async-start(bf16[8,8,256]{2,1,0:T(8,128)(2,1)} %shard_map.163), calls=%async_computation | async-start | bytes 65536 | tf_op jit(solution)/shard_map/all_to_all | solution.py:230
  9.4 0.1 pad.60
  9.5 1.4 %slice_select_fusion.upper = bf16[256,2048]{1,0:T(8,128)(2,1)S(1)} fusion(bf16[512,2048]{1,0:T(8,128)(2,1)} %weight.3, pred[]{:T(512)S(6)} %ge.3), kind=kLoop, calls=%fused_computation.1 | loop fusion | flops 524288 | bytes 2097153 | tf_op jit(solution)/shard_map/jit(_where)/select_n | solution.py:297
  10.9 0.2 copy-done.2
  11.1 0.0 copy-start.5
  11.1 0.0 copy-start.6
  11.1 0.0 copy-start.7
  11.2 0.0 copy-start.9
  11.2 0.1 broadcast_select_fusion.pool
  11.3 0.1 pad_add_fusion.1
  11.4 0.4 %copy-done.3 = s32[32,16]{0,1:T(8,128)S(1)} copy-done((s32[32,16]{0,1:T(8,128)S(1)}, s32[32,16]{0,1:T(8,128)}, u32[]{:S(2)}) %copy-start.3) | copy-done | bytes 2072
  11.8 0.1 pad_add_fusion.numbers
  11.9 0.1 broadcast_in_dim.25.place
  12.0 0.4 shard_map.164
  12.5 1.3 %all-to-all-done.arrived = bf16[8,8,256]{2,1,0:T(8,128)(2,1)S(1)} async-done(((bf16[8,8,256]{2,1,0:T(8,128)(2,1)}), bf16[8,8,256]{2,1,0:T(8,128)(2,1)S(1)}, u32[]{:S(2)}, u32[]{:S(2)}) %all-to-all-start) | async-done | bytes 32800 | tf_op jit(solution)/shard_map/all_to_all | solution.py:230
  13.8 1.8 %shard_map.165 = (f32[4,2048]{1,0:T(4,128)S(1)}, bf16[4,2048]{1,0:T(4,128)(2,1)S(1)}) custom-call(s32[2,128]{1,0:T(2,128)S(1)} %broadcast_in_dim.25.place, bf16[8,8,256]{2,1,0:T(8,128)(2,1)S(1)} %all-to-all-done.arrived, bf16[16,64]{1,0:T(8,128)(2,1)S(1)} %get-tuple-element.13.pick, f32[16,704]{1,0:T(8,128)S(1)} %get-tuple-element.14.valid, ...), custom_call_target="tpu_custom_call" | custom-call | bytes 4680704 | tf_op jit(solution)/shard_map/pallas_call | solution.py:218
  15.5 0.1 collective-permute-start.2
  15.6 1.6 %collective-permute-start.1 = (bf16[4,2048]{1,0:T(4,128)(2,1)S(1)}, bf16[4,2048]{1,0:T(4,128)(2,1)S(1)}, u32[]{:S(2)}, u32[]{:S(2)}) collective-permute-start(bf16[4,2048]{1,0:T(4,128)(2,1)S(1)} %get-tuple-element.16), channel_id=1, source_target_pairs={{0,2},{1,3},{2,0},{3,1},{4,6},{5,7},{6,4},{7,5},{8,10},{9,11},{10,... | collective-permute-start | bytes 49160 | tf_op jit(solution)/shard_map/ppermute | solution.py:334
  17.2 0.3 collective-permute-start
  17.5 1.4 %collective-permute-done.2.far_sibling = bf16[4,2048]{1,0:T(4,128)(2,1)S(1)} collective-permute-done((bf16[4,2048]{1,0:T(4,128)(2,1)S(1)}, bf16[4,2048]{1,0:T(4,128)(2,1)S(1)}, u32[]{:S(2)}, u32[]{:S(2)}) %collective-permute-start.2) | collective-permute-done | bytes 16416 | tf_op jit(solution)/shard_map/ppermute | solution.py:334
  18.9 0.5 %collective-permute-done.1.far = bf16[4,2048]{1,0:T(4,128)(2,1)S(1)} collective-permute-done((bf16[4,2048]{1,0:T(4,128)(2,1)S(1)}, bf16[4,2048]{1,0:T(4,128)(2,1)S(1)}, u32[]{:S(2)}, u32[]{:S(2)}) %collective-permute-start.1) | collective-permute-done | bytes 16416 | tf_op jit(solution)/shard_map/ppermute | solution.py:334
  19.4 0.2 shard_map.166
  19.6 8.3 %all_to_all.15.rows_in = bf16[8,4,512]{2,1,0:T(4,128)(2,1)S(1)} all-to-all(bf16[8,4,512]{2,1,0:T(4,128)(2,1)S(1)} %get-tuple-element.17), channel_id=1, replica_groups={{12,16,8,20,4,24,0,28},{13,17,9,21,5,25,1,29},{14,18,10,22,6,26,2,30},{..., dimensions={0} | all-to-all | bytes 65536 | tf_op jit(solution)/shard_map/all_to_all | solution.py:230
  28.0 0.5 %shard_map.167 = bf16[32,1024]{1,0:T(8,128)(2,1)S(1)} custom-call(bf16[8,4,512]{2,1,0:T(4,128)(2,1)S(1)} %all_to_all.15.rows_in, bf16[32,32]{1,0:T(8,128)(2,1)S(1)} %get-tuple-element.18.arrange, bf16[1024,512]{1,0:T(8,128)(2,1)S(1)} %copy-done.1), custom_call_target="tpu_custom_call" | custom-call | bytes 1083392 | tf_op jit(solution)/shard_map/pallas_call | solution.py:218
  28.4 0.0 collective-permute-start.3
  28.5 1.2 %collective-permute-done.3 = bf16[32,1024]{1,0:T(8,128)(2,1)S(1)} collective-permute-done((bf16[32,1024]{1,0:T(8,128)(2,1)S(1)}, bf16[32,1024]{1,0:T(8,128)(2,1)S(1)}, u32[]{:S(2)}, u32[]{:S(2)}) %collective-permute-start.3) | collective-permute-done | bytes 65568 | tf_op jit(solution)/shard_map/ppermute | solution.py:334
  29.7 1.3 %collective-permute-start.4 = (bf16[32,1024]{1,0:T(8,128)(2,1)S(1)}, bf16[32,1024]{1,0:T(8,128)(2,1)S(1)}, u32[]{:S(2)}, u32[]{:S(2)}) collective-permute-start(bf16[32,1024]{1,0:T(8,128)(2,1)S(1)} %add_convert_fusion.near), channel_id=1, source_target_pairs={{0,3},{1,2},{2,1},{3,0},{4,7},{5,6},{6,5},{7,4},{8,11},{9,10},{10,... | collective-permute-start | bytes 196616 | tf_op jit(solution)/shard_map/ppermute | solution.py:334
  31.0 2.8 %collective-permute-done.4.far = bf16[32,1024]{1,0:T(8,128)(2,1)S(1)} collective-permute-done((bf16[32,1024]{1,0:T(8,128)(2,1)S(1)}, bf16[32,1024]{1,0:T(8,128)(2,1)S(1)}, u32[]{:S(2)}, u32[]{:S(2)}) %collective-permute-start.4) | collective-permute-done | bytes 65568 | tf_op jit(solution)/shard_map/ppermute | solution.py:334
  33.9 0.3 shard_map.168
  34.1 8.5 %all_to_all.16.pieces = bf16[8,4,512]{2,1,0:T(4,128)(2,1)S(1)} all-to-all(bf16[8,4,512]{2,1,0:T(4,128)(2,1)S(1)} %shard_map.168), channel_id=1, replica_groups={{28,24,20,16,12,8,4,0},{29,25,21,17,13,9,5,1},{30,26,22,18,14,10,6,2},{..., dimensions={0} | all-to-all | bytes 65536 | tf_op jit(solution)/shard_map/all_to_all | solution.py:230
  42.6 0.6 %shard_map.169 = bf16[4,512]{1,0:T(4,128)(2,1)} custom-call(bf16[8,4,512]{2,1,0:T(4,128)(2,1)S(1)} %all_to_all.16.pieces, f32[3072]{0:T(1024)S(1)} %convert_add_fusion.vectors), custom_call_target="tpu_custom_call" | custom-call | bytes 45056 | tf_op jit(solution)/shard_map/pallas_call | solution.py:218
  (22 shorter events, 0.1 us)
Async XLA Ops:
  1.6 12.2 %all-to-all-start = ((bf16[8,8,256]{2,1,0:T(8,128)(2,1)}), bf16[8,8,256]{2,1,0:T(8,128)(2,1)S(1)}, u32[]{:S(2)}, u32[]{:S(2)}) async-start(bf16[8,8,256]{2,1,0:T(8,128)(2,1)} %shard_map.163), calls=%async_computation | async-start | bytes 65536 | tf_op jit(solution)/shard_map/all_to_all | solution.py:230
  9.4 1.7 %copy-start.2 = (bf16[2,22,32,512]{3,2,1,0:T(8,128)(2,1)S(1)}, bf16[2,22,32,512]{3,2,1,0:T(8,128)(2,1)}, u32[]{:S(2)}) copy-start(bf16[2,22,32,512]{3,2,1,0:T(8,128)(2,1)} %param.24) | copy-start | bytes 4325380
  11.1 0.7 %copy-start.3 = (s32[32,16]{0,1:T(8,128)S(1)}, s32[32,16]{0,1:T(8,128)}, u32[]{:S(2)}) copy-start(s32[32,16]{0,1:T(8,128)} %param.23) | copy-start | bytes 6148
  11.1 0.7 %copy-start.4 = (s32[32]{0:T(128)S(1)}, s32[32]{0:T(128)}, u32[]{:S(2)}) copy-start(s32[32]{0:T(128)} %param.22) | copy-start | bytes 388
  11.1 0.7 %copy-start.10 = (s32[32]{0:T(128)S(1)}, s32[32]{0:T(128)}, u32[]{:S(2)}) copy-start(s32[32]{0:T(128)} %param.21) | copy-start | bytes 388
  11.1 0.7 %copy-start.11 = (s32[32]{0:T(128)S(1)}, s32[32]{0:T(128)}, u32[]{:S(2)}) copy-start(s32[32]{0:T(128)} %param.33) | copy-start | bytes 388
  11.1 1.3 %copy-start.5 = (bf16[1024]{0:T(1024)(128)(2,1)S(1)}, bf16[1024]{0:T(1024)(128)(2,1)}, u32[]{:S(2)}) copy-start(bf16[1024]{0:T(1024)(128)(2,1)} %param.30) | copy-start | bytes 6148
  11.1 1.3 %copy-start.6 = (bf16[512]{0:T(512)(128)(2,1)S(1)}, bf16[512]{0:T(512)(128)(2,1)}, u32[]{:S(2)}) copy-start(bf16[512]{0:T(512)(128)(2,1)} %param.32) | copy-start | bytes 3076
  11.1 1.3 %copy-start.7 = (bf16[512]{0:T(512)(128)(2,1)S(1)}, bf16[512]{0:T(512)(128)(2,1)}, u32[]{:S(2)}) copy-start(bf16[512]{0:T(512)(128)(2,1)} %param.28) | copy-start | bytes 3076
  11.2 1.3 %copy-start.8 = (bf16[512]{0:T(512)(128)(2,1)S(1)}, bf16[512]{0:T(512)(128)(2,1)}, u32[]{:S(2)}) copy-start(bf16[512]{0:T(512)(128)(2,1)} %param.27) | copy-start | bytes 3076
  11.2 1.3 %copy-start.9 = (bf16[512]{0:T(512)(128)(2,1)S(1)}, bf16[512]{0:T(512)(128)(2,1)}, u32[]{:S(2)}) copy-start(bf16[512]{0:T(512)(128)(2,1)} %param.26) | copy-start | bytes 3076
  13.8 14.2 %copy-start.1 = (bf16[1024,512]{1,0:T(8,128)(2,1)S(1)}, bf16[1024,512]{1,0:T(8,128)(2,1)}, u32[]{:S(2)}) copy-start(bf16[1024,512]{1,0:T(8,128)(2,1)} %weight.4) | copy-start | bytes 3145732
  15.5 18.3 %copy-start = (bf16[1024,512]{1,0:T(8,128)(2,1)S(1)}, bf16[1024,512]{1,0:T(8,128)(2,1)}, u32[]{:S(2)}) copy-start(bf16[1024,512]{1,0:T(8,128)(2,1)} %weight.5) | copy-start | bytes 3145732
  15.5 3.4 %collective-permute-start.2 = (bf16[4,2048]{1,0:T(4,128)(2,1)S(1)}, bf16[4,2048]{1,0:T(4,128)(2,1)S(1)}, u32[]{:S(2)}, u32[]{:S(2)}) collective-permute-start(bf16[4,2048]{1,0:T(4,128)(2,1)S(1)} %get-tuple-element.16), channel_id=1, source_target_pairs={{0,3},{1,2},{2,1},{3,0},{4,7},{5,6},{6,5},{7,4},{8,11},{9,10},{10,... | collective-permute-start | bytes 49160 | tf_op jit(solution)/shard_map/ppermute | solution.py:334
  15.6 3.8 %collective-permute-start.1 = (bf16[4,2048]{1,0:T(4,128)(2,1)S(1)}, bf16[4,2048]{1,0:T(4,128)(2,1)S(1)}, u32[]{:S(2)}, u32[]{:S(2)}) collective-permute-start(bf16[4,2048]{1,0:T(4,128)(2,1)S(1)} %get-tuple-element.16), channel_id=1, source_target_pairs={{0,2},{1,3},{2,0},{3,1},{4,6},{5,7},{6,4},{7,5},{8,10},{9,11},{10,... | collective-permute-start | bytes 49160 | tf_op jit(solution)/shard_map/ppermute | solution.py:334
  17.2 2.3 %collective-permute-start = (bf16[4,2048]{1,0:T(4,128)(2,1)S(1)}, bf16[4,2048]{1,0:T(4,128)(2,1)S(1)}, u32[]{:S(2)}, u32[]{:S(2)}) collective-permute-start(bf16[4,2048]{1,0:T(4,128)(2,1)S(1)} %get-tuple-element.16), channel_id=1, source_target_pairs={{0,1},{1,0},{2,3},{3,2},{4,5},{5,4},{6,7},{7,6},{8,9},{9,8},{10,11... | collective-permute-start | bytes 49160 | tf_op jit(solution)/shard_map/ppermute | solution.py:334
  28.4 1.3 %collective-permute-start.3 = (bf16[32,1024]{1,0:T(8,128)(2,1)S(1)}, bf16[32,1024]{1,0:T(8,128)(2,1)S(1)}, u32[]{:S(2)}, u32[]{:S(2)}) collective-permute-start(bf16[32,1024]{1,0:T(8,128)(2,1)S(1)} %shard_map.167), channel_id=1, source_target_pairs={{0,1},{1,0},{2,3},{3,2},{4,5},{5,4},{6,7},{7,6},{8,9},{9,8},{10,11... | collective-permute-start | bytes 196616 | tf_op jit(solution)/shard_map/ppermute | solution.py:334
  29.7 4.1 %collective-permute-start.4 = (bf16[32,1024]{1,0:T(8,128)(2,1)S(1)}, bf16[32,1024]{1,0:T(8,128)(2,1)S(1)}, u32[]{:S(2)}, u32[]{:S(2)}) collective-permute-start(bf16[32,1024]{1,0:T(8,128)(2,1)S(1)} %add_convert_fusion.near), channel_id=1, source_target_pairs={{0,3},{1,2},{2,1},{3,0},{4,7},{5,6},{6,5},{7,4},{8,11},{9,10},{10,... | collective-permute-start | bytes 196616 | tf_op jit(solution)/shard_map/ppermute | solution.py:334

commit v16 on v14

--- a/solution.py
+++ b/solution.py
@@ -17,6 +17,12 @@
 F32, BF16, I32 = jnp.float32, jnp.bfloat16, jnp.int32
 VMEM = pl.BlockSpec(memory_space=pltpu.VMEM)
 HBM = pl.BlockSpec(memory_space=pltpu.HBM)
+
+RING = [0, 1, 3, 5, 7, 6, 4, 2]
+
+
+def on_ring(place):
+    return jnp.where(place < 5, jnp.maximum(2 * place - 1, 0), 16 - 2 * place)
 
 
 def iota(shape, dim):
@@ -70,8 +76,9 @@
     blocks = onto_mxu(pick, all_rows).astype(BF16)
     for d in range(REQ):
         block = blocks[d * fields : (d + 1) * fields]
-        out[REQ - 1 - d, :fields, :] = block[:, : cols // 2]
-        out[REQ - 1 - d, fields:, :] = block[:, cols // 2 :]
+        at = RING.index(d)
+        out[at, :fields, :] = block[:, : cols // 2]
+        out[at, fields:, :] = block[:, cols // 2 :]
 
 
 def index_kernel(place, numbers, pick, valid, arrange, arrange_own, *, page_len):
@@ -94,7 +101,7 @@
     down_p, across_p = iota(shape, 0), iota(shape, 1)
     down_i = iota((shape[0], count), 0)
     mine = hot((owner_row == me) & (rank_row == down_i % rows))
-    source = REQ - 1 - iota((count, shape[1]), 1) // (2 * rows)
+    source = on_ring(iota((count, shape[1]), 1) // (2 * rows))
     came = hot(iota((count, shape[1]), 0) // rows == source)
     from_there = onto_mxu(mine, came)
     pick[...] = hot((from_there > 0.5) & (down_p // rows == across_p % rows))
@@ -113,7 +120,7 @@
     valid[...] = seen
 
     ordered = hot(order_col == across)
-    holds = hot((owner_col == REQ - 1 - across // rows) & (rank_col == across % rows))
+    holds = hot((owner_col == on_ring(across // rows)) & (rank_col == across % rows))
     arrange[...] = onto_mxu(ordered, holds).astype(BF16)
     here = hot((owner_col == me) & (rank_col == iota(arrange_own.shape, 1)))
     arrange_own[...] = onto_mxu(ordered, here).astype(BF16)
@@ -197,7 +204,7 @@
     feed = onto_mxu(activated, weight[...]) + onto_mxu(arrange_own[...], stream_own[...])
     rows = out.shape[1]
     for d in range(REQ):
-        out[REQ - 1 - d] = feed[d * rows : (d + 1) * rows].astype(BF16)
+        out[RING.index(d)] = feed[d * rows : (d + 1) * rows].astype(BF16)
 
 
 def finish_kernel(pieces, vectors, out):
@@ -219,8 +226,7 @@
 
 
 def trade(blocks):
-    group = [list(reversed(range(REQ)))]
-    return lax.all_to_all(blocks, "req", 0, 0, tiled=True, axis_index_groups=group)
+    return lax.all_to_all(blocks, "req", 0, 0, tiled=True, axis_index_groups=[RING])
 
 
 def on_pairs(

time: 45.2 us -> 46.9 us (1.038)
  waiting for transfers between devices: 7.26 us -> 9.74 us
  starting transfers between devices: 12 us -> 10.5 us
  blocking collectives: 17.5 us -> 18.2 us
    all_to_all x1, waiting for transfers between devices: 0.01 us -> 3.7 us  [trade(): lax.all_to_all(blocks, 'req', 0, 0, tiled=True, axis_index_groups=[RING])]
    all_to_all x1, starting transfers between devices: 9.28 us -> 7.29 us  [trade(): lax.all_to_all(blocks, 'req', 0, 0, tiled=True, axis_index_groups=[RING])]
    ppermute x5, waiting for transfers between devices: 7.26 us -> 6.03 us  [swap(): return lax.ppermute(x, axis, [(i, i ^ step) for i in range(n)])]
    all_to_all x2, blocking collectives: 17.5 us -> 18.2 us  [trade(): lax.all_to_all(blocks, 'req', 0, 0, tiled=True, axis_index_groups=[RING])]
    ppermute x5, starting transfers between devices: 2.75 us -> 3.24 us  [swap(): return lax.ppermute(x, axis, [(i, i ^ step) for i in range(n)])]
  transfers between devices with their start and end apart: 6 -> 6, of which waited for: 4 -> 5; matrix products, arithmetic and copies ran while one was open for 4% -> 4% of each run, Pallas kernels for 1% -> 1%
where the time goes in v16:
time: 46.9 us; the launch traced here: 46.5 us
  blocking collectives  18.2 us (39%)
  starting transfers between devices  10.5 us (22%)
  waiting for transfers between devices  9.74 us (21%)
  Pallas kernels  5.32 us (11%)
  other arithmetic  1.67 us (4%)
  local copies, waits for them, and re-layouts  0.83 us (2%)
    all_to_all x2, blocking collectives, trade(): lax.all_to_all(blocks, 'req', 0, 0, tiled=True, axis_index_groups=[RING])  18.2 us
    all_to_all x1, starting transfers between devices, trade(): lax.all_to_all(blocks, 'req', 0, 0, tiled=True, axis_index_groups=[RING])  7.29 us
    ppermute x5, waiting for transfers between devices, swap(): return lax.ppermute(x, axis, [(i, i ^ step) for i in range(n)])  6.03 us
    pallas_call x7, Pallas kernels, call(): pl.pallas_call(functools.partial(kernel, **fixed) if fixed else kernel, o...  5.32 us
    all_to_all x1, waiting for transfers between devices, trade(): lax.all_to_all(blocks, 'req', 0, 0, tiled=True, axis_index_groups=[RING])  3.7 us
    ppermute x5, starting transfers between devices, swap(): return lax.ppermute(x, axis, [(i, i ^ step) for i in range(n)])  3.24 us
    select_n x1, other arithmetic, on_pairs(): upper = jnp.where(here, upper, jnp.zeros_like(upper))  1.39 us
  transfers between devices with their start and end apart: 6, of which 5 were waited for; matrix products, arithmetic and copies ran while one was open for 4% of the time, Pallas kernels for 1%

profile of v16, /device:TPU:0, one launch (start us, length us, event | category | flops | bytes accessed | tf_op | source)
XLA Modules:
  0.0 46.5 jit_solution(4405097897108392300)
XLA Ops:
  0.0 1.6 %shard_map.163 = bf16[8,8,256]{2,1,0:T(8,128)(2,1)} custom-call(s32[1,32]{1,0:T(1,128)} %bitcast.7, bf16[4,512]{1,0:T(4,128)(2,1)} %query.1, bf16[4,512]{1,0:T(4,128)(2,1)} %key.1, bf16[4,512]{1,0:T(4,128)(2,1)} %value.1, bf16[4,512]{1,0:T(4,128)(2,1)} %resid.1), custom_call_target="tpu_custom_call" | custom-call | bytes 16512 | tf_op jit(solution)/shard_map/pallas_call | solution.py:217
  1.6 7.3 %all-to-all-start = ((bf16[8,8,256]{2,1,0:T(8,128)(2,1)}), bf16[8,8,256]{2,1,0:T(8,128)(2,1)S(1)}, u32[]{:S(2)}, u32[]{:S(2)}) async-start(bf16[8,8,256]{2,1,0:T(8,128)(2,1)} %shard_map.163), calls=%async_computation | async-start | bytes 65536 | tf_op jit(solution)/shard_map/all_to_all | solution.py:229
  8.9 0.1 pad.60
  9.0 1.4 %slice_select_fusion.upper = bf16[256,2048]{1,0:T(8,128)(2,1)S(1)} fusion(bf16[512,2048]{1,0:T(8,128)(2,1)} %weight.3, pred[]{:T(512)S(6)} %ge.3), kind=kLoop, calls=%fused_computation.1 | loop fusion | flops 524288 | bytes 2097153 | tf_op jit(solution)/shard_map/jit(_where)/select_n | solution.py:296
  10.4 0.2 copy-done.2
  10.6 0.0 copy-start.5
  10.6 0.0 copy-start.6
  10.6 0.0 copy-start.7
  10.6 0.0 copy-start.9
  10.6 0.1 broadcast_select_fusion.pool
  10.7 0.1 pad_add_fusion.1
  10.8 0.4 copy-done.3
  11.3 0.1 pad_add_fusion.numbers
  11.3 0.1 broadcast_in_dim.25.place
  11.4 0.4 shard_map.164
  11.9 3.7 %all-to-all-done.arrived = bf16[8,8,256]{2,1,0:T(8,128)(2,1)S(1)} async-done(((bf16[8,8,256]{2,1,0:T(8,128)(2,1)}), bf16[8,8,256]{2,1,0:T(8,128)(2,1)S(1)}, u32[]{:S(2)}, u32[]{:S(2)}) %all-to-all-start) | async-done | bytes 32800 | tf_op jit(solution)/shard_map/all_to_all | solution.py:229
  15.6 1.8 %shard_map.165 = (f32[4,2048]{1,0:T(4,128)S(1)}, bf16[4,2048]{1,0:T(4,128)(2,1)S(1)}) custom-call(s32[2,128]{1,0:T(2,128)S(1)} %broadcast_in_dim.25.place, bf16[8,8,256]{2,1,0:T(8,128)(2,1)S(1)} %all-to-all-done.arrived, bf16[16,64]{1,0:T(8,128)(2,1)S(1)} %get-tuple-element.13.pick, f32[16,704]{1,0:T(8,128)S(1)} %get-tuple-element.14.valid, ...), custom_call_target="tpu_custom_call" | custom-call | bytes 4680704 | tf_op jit(solution)/shard_map/pallas_call | solution.py:217
  17.4 0.1 collective-permute-start.2
  17.5 1.6 %collective-permute-start.1 = (bf16[4,2048]{1,0:T(4,128)(2,1)S(1)}, bf16[4,2048]{1,0:T(4,128)(2,1)S(1)}, u32[]{:S(2)}, u32[]{:S(2)}) collective-permute-start(bf16[4,2048]{1,0:T(4,128)(2,1)S(1)} %get-tuple-element.16), channel_id=1, source_target_pairs={{0,2},{1,3},{2,0},{3,1},{4,6},{5,7},{6,4},{7,5},{8,10},{9,11},{10,... | collective-permute-start | bytes 49160 | tf_op jit(solution)/shard_map/ppermute | solution.py:333
  19.0 0.3 collective-permute-start
  19.3 1.4 %collective-permute-done.2.far_sibling = bf16[4,2048]{1,0:T(4,128)(2,1)S(1)} collective-permute-done((bf16[4,2048]{1,0:T(4,128)(2,1)S(1)}, bf16[4,2048]{1,0:T(4,128)(2,1)S(1)}, u32[]{:S(2)}, u32[]{:S(2)}) %collective-permute-start.2) | collective-permute-done | bytes 16416 | tf_op jit(solution)/shard_map/ppermute | solution.py:333
  20.7 0.5 %collective-permute-done.1.far = bf16[4,2048]{1,0:T(4,128)(2,1)S(1)} collective-permute-done((bf16[4,2048]{1,0:T(4,128)(2,1)S(1)}, bf16[4,2048]{1,0:T(4,128)(2,1)S(1)}, u32[]{:S(2)}, u32[]{:S(2)}) %collective-permute-start.1) | collective-permute-done | bytes 16416 | tf_op jit(solution)/shard_map/ppermute | solution.py:333
  21.3 0.2 shard_map.166
  21.5 9.1 %all_to_all.15.rows_in = bf16[8,4,512]{2,1,0:T(4,128)(2,1)S(1)} all-to-all(bf16[8,4,512]{2,1,0:T(4,128)(2,1)S(1)} %get-tuple-element.17), channel_id=1, replica_groups={{0,4,12,20,28,24,16,8},{1,5,13,21,29,25,17,9},{2,6,14,22,30,26,18,10},{..., dimensions={0} | all-to-all | bytes 65536 | tf_op jit(solution)/shard_map/all_to_all | solution.py:229
  30.6 0.5 shard_map.167
  31.1 0.0 collective-permute-start.3
  31.1 1.2 %collective-permute-done.3 = bf16[32,1024]{1,0:T(8,128)(2,1)S(1)} collective-permute-done((bf16[32,1024]{1,0:T(8,128)(2,1)S(1)}, bf16[32,1024]{1,0:T(8,128)(2,1)S(1)}, u32[]{:S(2)}, u32[]{:S(2)}) %collective-permute-start.3) | collective-permute-done | bytes 65568 | tf_op jit(solution)/shard_map/ppermute | solution.py:333
  32.4 1.3 %collective-permute-start.4 = (bf16[32,1024]{1,0:T(8,128)(2,1)S(1)}, bf16[32,1024]{1,0:T(8,128)(2,1)S(1)}, u32[]{:S(2)}, u32[]{:S(2)}) collective-permute-start(bf16[32,1024]{1,0:T(8,128)(2,1)S(1)} %add_convert_fusion.near), channel_id=1, source_target_pairs={{0,3},{1,2},{2,1},{3,0},{4,7},{5,6},{6,5},{7,4},{8,11},{9,10},{10,... | collective-permute-start | bytes 196616 | tf_op jit(solution)/shard_map/ppermute | solution.py:333
  33.7 2.8 %collective-permute-done.4.far = bf16[32,1024]{1,0:T(8,128)(2,1)S(1)} collective-permute-done((bf16[32,1024]{1,0:T(8,128)(2,1)S(1)}, bf16[32,1024]{1,0:T(8,128)(2,1)S(1)}, u32[]{:S(2)}, u32[]{:S(2)}) %collective-permute-start.4) | collective-permute-done | bytes 65568 | tf_op jit(solution)/shard_map/ppermute | solution.py:333
  36.5 0.3 shard_map.168
  36.8 9.1 %all_to_all.16.pieces = bf16[8,4,512]{2,1,0:T(4,128)(2,1)S(1)} all-to-all(bf16[8,4,512]{2,1,0:T(4,128)(2,1)S(1)} %shard_map.168), channel_id=1, replica_groups={{0,4,12,20,28,24,16,8},{1,5,13,21,29,25,17,9},{2,6,14,22,30,26,18,10},{..., dimensions={0} | all-to-all | bytes 65536 | tf_op jit(solution)/shard_map/all_to_all | solution.py:229
  45.9 0.6 %shard_map.169 = bf16[4,512]{1,0:T(4,128)(2,1)} custom-call(bf16[8,4,512]{2,1,0:T(4,128)(2,1)S(1)} %all_to_all.16.pieces, f32[3072]{0:T(1024)S(1)} %convert_add_fusion.vectors), custom_call_target="tpu_custom_call" | custom-call | bytes 45056 | tf_op jit(solution)/shard_map/pallas_call | solution.py:217
  (22 shorter events, 0.1 us)
Async XLA Ops:
  1.6 14.0 %all-to-all-start = ((bf16[8,8,256]{2,1,0:T(8,128)(2,1)}), bf16[8,8,256]{2,1,0:T(8,128)(2,1)S(1)}, u32[]{:S(2)}, u32[]{:S(2)}) async-start(bf16[8,8,256]{2,1,0:T(8,128)(2,1)} %shard_map.163), calls=%async_computation | async-start | bytes 65536 | tf_op jit(solution)/shard_map/all_to_all | solution.py:229
  8.9 1.7 %copy-start.2 = (bf16[2,22,32,512]{3,2,1,0:T(8,128)(2,1)S(1)}, bf16[2,22,32,512]{3,2,1,0:T(8,128)(2,1)}, u32[]{:S(2)}) copy-start(bf16[2,22,32,512]{3,2,1,0:T(8,128)(2,1)} %param.24) | copy-start | bytes 4325380
  10.5 0.7 %copy-start.3 = (s32[32,16]{0,1:T(8,128)S(1)}, s32[32,16]{0,1:T(8,128)}, u32[]{:S(2)}) copy-start(s32[32,16]{0,1:T(8,128)} %param.23) | copy-start | bytes 6148
  10.5 0.7 %copy-start.4 = (s32[32]{0:T(128)S(1)}, s32[32]{0:T(128)}, u32[]{:S(2)}) copy-start(s32[32]{0:T(128)} %param.22) | copy-start | bytes 388
  10.6 0.7 %copy-start.10 = (s32[32]{0:T(128)S(1)}, s32[32]{0:T(128)}, u32[]{:S(2)}) copy-start(s32[32]{0:T(128)} %param.21) | copy-start | bytes 388
  10.6 0.7 %copy-start.11 = (s32[32]{0:T(128)S(1)}, s32[32]{0:T(128)}, u32[]{:S(2)}) copy-start(s32[32]{0:T(128)} %param.33) | copy-start | bytes 388
  10.6 1.3 %copy-start.5 = (bf16[1024]{0:T(1024)(128)(2,1)S(1)}, bf16[1024]{0:T(1024)(128)(2,1)}, u32[]{:S(2)}) copy-start(bf16[1024]{0:T(1024)(128)(2,1)} %param.30) | copy-start | bytes 6148
  10.6 1.3 %copy-start.6 = (bf16[512]{0:T(512)(128)(2,1)S(1)}, bf16[512]{0:T(512)(128)(2,1)}, u32[]{:S(2)}) copy-start(bf16[512]{0:T(512)(128)(2,1)} %param.32) | copy-start | bytes 3076
  10.6 1.3 %copy-start.7 = (bf16[512]{0:T(512)(128)(2,1)S(1)}, bf16[512]{0:T(512)(128)(2,1)}, u32[]{:S(2)}) copy-start(bf16[512]{0:T(512)(128)(2,1)} %param.28) | copy-start | bytes 3076
  10.6 1.3 %copy-start.8 = (bf16[512]{0:T(512)(128)(2,1)S(1)}, bf16[512]{0:T(512)(128)(2,1)}, u32[]{:S(2)}) copy-start(bf16[512]{0:T(512)(128)(2,1)} %param.27) | copy-start | bytes 3076
  10.6 1.3 %copy-start.9 = (bf16[512]{0:T(512)(128)(2,1)S(1)}, bf16[512]{0:T(512)(128)(2,1)}, u32[]{:S(2)}) copy-start(bf16[512]{0:T(512)(128)(2,1)} %param.26) | copy-start | bytes 3076
  15.6 15.0 %copy-start.1 = (bf16[1024,512]{1,0:T(8,128)(2,1)S(1)}, bf16[1024,512]{1,0:T(8,128)(2,1)}, u32[]{:S(2)}) copy-start(bf16[1024,512]{1,0:T(8,128)(2,1)} %weight.4) | copy-start | bytes 3145732
  17.4 19.1 %copy-start = (bf16[1024,512]{1,0:T(8,128)(2,1)S(1)}, bf16[1024,512]{1,0:T(8,128)(2,1)}, u32[]{:S(2)}) copy-start(bf16[1024,512]{1,0:T(8,128)(2,1)} %weight.5) | copy-start | bytes 3145732
  17.4 3.4 %collective-permute-start.2 = (bf16[4,2048]{1,0:T(4,128)(2,1)S(1)}, bf16[4,2048]{1,0:T(4,128)(2,1)S(1)}, u32[]{:S(2)}, u32[]{:S(2)}) collective-permute-start(bf16[4,2048]{1,0:T(4,128)(2,1)S(1)} %get-tuple-element.16), channel_id=1, source_target_pairs={{0,3},{1,2},{2,1},{3,0},{4,7},{5,6},{6,5},{7,4},{8,11},{9,10},{10,... | collective-permute-start | bytes 49160 | tf_op jit(solution)/shard_map/ppermute | solution.py:333
  17.5 3.8 %collective-permute-start.1 = (bf16[4,2048]{1,0:T(4,128)(2,1)S(1)}, bf16[4,2048]{1,0:T(4,128)(2,1)S(1)}, u32[]{:S(2)}, u32[]{:S(2)}) collective-permute-start(bf16[4,2048]{1,0:T(4,128)(2,1)S(1)} %get-tuple-element.16), channel_id=1, source_target_pairs={{0,2},{1,3},{2,0},{3,1},{4,6},{5,7},{6,4},{7,5},{8,10},{9,11},{10,... | collective-permute-start | bytes 49160 | tf_op jit(solution)/shard_map/ppermute | solution.py:333
  19.0 2.3 %collective-permute-start = (bf16[4,2048]{1,0:T(4,128)(2,1)S(1)}, bf16[4,2048]{1,0:T(4,128)(2,1)S(1)}, u32[]{:S(2)}, u32[]{:S(2)}) collective-permute-start(bf16[4,2048]{1,0:T(4,128)(2,1)S(1)} %get-tuple-element.16), channel_id=1, source_target_pairs={{0,1},{1,0},{2,3},{3,2},{4,5},{5,4},{6,7},{7,6},{8,9},{9,8},{10,11... | collective-permute-start | bytes 49160 | tf_op jit(solution)/shard_map/ppermute | solution.py:333
  31.1 1.3 %collective-permute-start.3 = (bf16[32,1024]{1,0:T(8,128)(2,1)S(1)}, bf16[32,1024]{1,0:T(8,128)(2,1)S(1)}, u32[]{:S(2)}, u32[]{:S(2)}) collective-permute-start(bf16[32,1024]{1,0:T(8,128)(2,1)S(1)} %shard_map.167), channel_id=1, source_target_pairs={{0,1},{1,0},{2,3},{3,2},{4,5},{5,4},{6,7},{7,6},{8,9},{9,8},{10,11... | collective-permute-start | bytes 196616 | tf_op jit(solution)/shard_map/ppermute | solution.py:333
  32.4 4.1 %collective-permute-start.4 = (bf16[32,1024]{1,0:T(8,128)(2,1)S(1)}, bf16[32,1024]{1,0:T(8,128)(2,1)S(1)}, u32[]{:S(2)}, u32[]{:S(2)}) collective-permute-start(bf16[32,1024]{1,0:T(8,128)(2,1)S(1)} %add_convert_fusion.near), channel_id=1, source_target_pairs={{0,3},{1,2},{2,1},{3,0},{4,7},{5,6},{6,5},{7,4},{8,11},{9,10},{10,... | collective-permute-start | bytes 196616 | tf_op jit(solution)/shard_map/ppermute | solution.py:333

commit v17 on v15

--- a/solution.py
+++ b/solution.py
@@ -18,12 +18,12 @@
 VMEM = pl.BlockSpec(memory_space=pltpu.VMEM)
 HBM = pl.BlockSpec(memory_space=pltpu.HBM)
 
-ENDS_FIRST = [3, 4, 2, 5, 1, 6, 0, 7]
+ENDS_FIRST = [4, 3, 5, 2, 6, 1, 7, 0]
 LOW_FIRST = [7, 6, 5, 4, 3, 2, 1, 0]
 
 
 def ends_first(place):
-    return jnp.where(place % 2 == 0, 3 - place // 2, 4 + place // 2)
+    return jnp.where(place % 2 == 0, 4 + place // 2, 3 - place // 2)
 
 
 def iota(shape, dim):

time: 43.6 us -> 43.6 us (level)
  no operation moved by 1% of the time
where the time goes in v17:
time: 43.6 us; the launch traced here: 43.2 us
  blocking collectives  16.8 us (39%)
  starting transfers between devices  11.1 us (25%)
  waiting for transfers between devices  7.32 us (17%)
  Pallas kernels  5.32 us (12%)
  other arithmetic  1.67 us (4%)
  local copies, waits for them, and re-layouts  0.84 us (2%)
    all_to_all x2, blocking collectives, trade(): lax.all_to_all(blocks, 'req', 0, 0, tiled=True, axis_index_groups=[group])  16.8 us
    all_to_all x1, starting transfers between devices, trade(): lax.all_to_all(blocks, 'req', 0, 0, tiled=True, axis_index_groups=[group])  7.86 us
    ppermute x5, waiting for transfers between devices, swap(): return lax.ppermute(x, axis, [(i, i ^ step) for i in range(n)])  6.02 us
    pallas_call x7, Pallas kernels, call(): pl.pallas_call(functools.partial(kernel, **fixed) if fixed else kernel, o...  5.32 us
    ppermute x5, starting transfers between devices, swap(): return lax.ppermute(x, axis, [(i, i ^ step) for i in range(n)])  3.25 us
    select_n x1, other arithmetic, on_pairs(): upper = jnp.where(here, upper, jnp.zeros_like(upper))  1.39 us
    all_to_all x1, waiting for transfers between devices, trade(): lax.all_to_all(blocks, 'req', 0, 0, tiled=True, axis_index_groups=[group])  1.3 us
  transfers between devices with their start and end apart: 6, of which 5 were waited for; matrix products, arithmetic and copies ran while one was open for 4% of the time, Pallas kernels for 1%

profile of v17, /device:TPU:0, one launch (start us, length us, event | category | flops | bytes accessed | tf_op | source)
XLA Modules:
  0.0 43.2 jit_solution(12178890645918604877)
XLA Ops:
  0.0 1.6 %shard_map.163 = bf16[8,8,256]{2,1,0:T(8,128)(2,1)} custom-call(s32[1,32]{1,0:T(1,128)} %bitcast.7, bf16[4,512]{1,0:T(4,128)(2,1)} %query.1, bf16[4,512]{1,0:T(4,128)(2,1)} %key.1, bf16[4,512]{1,0:T(4,128)(2,1)} %value.1, bf16[4,512]{1,0:T(4,128)(2,1)} %resid.1), custom_call_target="tpu_custom_call" | custom-call | bytes 16512 | tf_op jit(solution)/shard_map/pallas_call | solution.py:218
  1.6 7.9 %all-to-all-start = ((bf16[8,8,256]{2,1,0:T(8,128)(2,1)}), bf16[8,8,256]{2,1,0:T(8,128)(2,1)S(1)}, u32[]{:S(2)}, u32[]{:S(2)}) async-start(bf16[8,8,256]{2,1,0:T(8,128)(2,1)} %shard_map.163), calls=%async_computation | async-start | bytes 65536 | tf_op jit(solution)/shard_map/all_to_all | solution.py:230
  9.4 0.1 pad.60
  9.5 1.4 %slice_select_fusion.upper = bf16[256,2048]{1,0:T(8,128)(2,1)S(1)} fusion(bf16[512,2048]{1,0:T(8,128)(2,1)} %weight.3, pred[]{:T(512)S(6)} %ge.3), kind=kLoop, calls=%fused_computation.1 | loop fusion | flops 524288 | bytes 2097153 | tf_op jit(solution)/shard_map/jit(_where)/select_n | solution.py:297
  10.9 0.2 copy-done.2
  11.1 0.0 copy-start.5
  11.2 0.0 copy-start.8
  11.2 0.0 copy-start.9
  11.2 0.1 broadcast_select_fusion.pool
  11.3 0.1 pad_add_fusion.1
  11.4 0.4 %copy-done.3 = s32[32,16]{0,1:T(8,128)S(1)} copy-done((s32[32,16]{0,1:T(8,128)S(1)}, s32[32,16]{0,1:T(8,128)}, u32[]{:S(2)}) %copy-start.3) | copy-done | bytes 2072
  11.8 0.1 pad_add_fusion.numbers
  11.9 0.1 broadcast_in_dim.25.place
  12.0 0.4 shard_map.164
  12.5 1.3 %all-to-all-done.arrived = bf16[8,8,256]{2,1,0:T(8,128)(2,1)S(1)} async-done(((bf16[8,8,256]{2,1,0:T(8,128)(2,1)}), bf16[8,8,256]{2,1,0:T(8,128)(2,1)S(1)}, u32[]{:S(2)}, u32[]{:S(2)}) %all-to-all-start) | async-done | bytes 32800 | tf_op jit(solution)/shard_map/all_to_all | solution.py:230
  13.8 1.8 %shard_map.165 = (f32[4,2048]{1,0:T(4,128)S(1)}, bf16[4,2048]{1,0:T(4,128)(2,1)S(1)}) custom-call(s32[2,128]{1,0:T(2,128)S(1)} %broadcast_in_dim.25.place, bf16[8,8,256]{2,1,0:T(8,128)(2,1)S(1)} %all-to-all-done.arrived, bf16[16,64]{1,0:T(8,128)(2,1)S(1)} %get-tuple-element.13.pick, f32[16,704]{1,0:T(8,128)S(1)} %get-tuple-element.14.valid, ...), custom_call_target="tpu_custom_call" | custom-call | bytes 4680704 | tf_op jit(solution)/shard_map/pallas_call | solution.py:218
  15.5 0.0 copy-start
  15.5 0.1 collective-permute-start.2
  15.6 1.6 %collective-permute-start.1 = (bf16[4,2048]{1,0:T(4,128)(2,1)S(1)}, bf16[4,2048]{1,0:T(4,128)(2,1)S(1)}, u32[]{:S(2)}, u32[]{:S(2)}) collective-permute-start(bf16[4,2048]{1,0:T(4,128)(2,1)S(1)} %get-tuple-element.16), channel_id=1, source_target_pairs={{0,2},{1,3},{2,0},{3,1},{4,6},{5,7},{6,4},{7,5},{8,10},{9,11},{10,... | collective-permute-start | bytes 49160 | tf_op jit(solution)/shard_map/ppermute | solution.py:334
  17.2 0.3 collective-permute-start
  17.5 1.4 %collective-permute-done.2.far_sibling = bf16[4,2048]{1,0:T(4,128)(2,1)S(1)} collective-permute-done((bf16[4,2048]{1,0:T(4,128)(2,1)S(1)}, bf16[4,2048]{1,0:T(4,128)(2,1)S(1)}, u32[]{:S(2)}, u32[]{:S(2)}) %collective-permute-start.2) | collective-permute-done | bytes 16416 | tf_op jit(solution)/shard_map/ppermute | solution.py:334
  18.9 0.5 %collective-permute-done.1.far = bf16[4,2048]{1,0:T(4,128)(2,1)S(1)} collective-permute-done((bf16[4,2048]{1,0:T(4,128)(2,1)S(1)}, bf16[4,2048]{1,0:T(4,128)(2,1)S(1)}, u32[]{:S(2)}, u32[]{:S(2)}) %collective-permute-start.1) | collective-permute-done | bytes 16416 | tf_op jit(solution)/shard_map/ppermute | solution.py:334
  19.4 0.2 shard_map.166
  19.6 8.3 %all_to_all.15.rows_in = bf16[8,4,512]{2,1,0:T(4,128)(2,1)S(1)} all-to-all(bf16[8,4,512]{2,1,0:T(4,128)(2,1)S(1)} %get-tuple-element.17), channel_id=1, replica_groups={{16,12,20,8,24,4,28,0},{17,13,21,9,25,5,29,1},{18,14,22,10,26,6,30,2},{..., dimensions={0} | all-to-all | bytes 65536 | tf_op jit(solution)/shard_map/all_to_all | solution.py:230
  28.0 0.5 %shard_map.167 = bf16[32,1024]{1,0:T(8,128)(2,1)S(1)} custom-call(bf16[8,4,512]{2,1,0:T(4,128)(2,1)S(1)} %all_to_all.15.rows_in, bf16[32,32]{1,0:T(8,128)(2,1)S(1)} %get-tuple-element.18.arrange, bf16[1024,512]{1,0:T(8,128)(2,1)S(1)} %copy-done.1), custom_call_target="tpu_custom_call" | custom-call | bytes 1083392 | tf_op jit(solution)/shard_map/pallas_call | solution.py:218
  28.4 0.0 collective-permute-start.3
  28.5 1.2 %collective-permute-done.3 = bf16[32,1024]{1,0:T(8,128)(2,1)S(1)} collective-permute-done((bf16[32,1024]{1,0:T(8,128)(2,1)S(1)}, bf16[32,1024]{1,0:T(8,128)(2,1)S(1)}, u32[]{:S(2)}, u32[]{:S(2)}) %collective-permute-start.3) | collective-permute-done | bytes 65568 | tf_op jit(solution)/shard_map/ppermute | solution.py:334
  29.7 1.3 %collective-permute-start.4 = (bf16[32,1024]{1,0:T(8,128)(2,1)S(1)}, bf16[32,1024]{1,0:T(8,128)(2,1)S(1)}, u32[]{:S(2)}, u32[]{:S(2)}) collective-permute-start(bf16[32,1024]{1,0:T(8,128)(2,1)S(1)} %add_convert_fusion.near), channel_id=1, source_target_pairs={{0,3},{1,2},{2,1},{3,0},{4,7},{5,6},{6,5},{7,4},{8,11},{9,10},{10,... | collective-permute-start | bytes 196616 | tf_op jit(solution)/shard_map/ppermute | solution.py:334
  31.0 2.8 %collective-permute-done.4.far = bf16[32,1024]{1,0:T(8,128)(2,1)S(1)} collective-permute-done((bf16[32,1024]{1,0:T(8,128)(2,1)S(1)}, bf16[32,1024]{1,0:T(8,128)(2,1)S(1)}, u32[]{:S(2)}, u32[]{:S(2)}) %collective-permute-start.4) | collective-permute-done | bytes 65568 | tf_op jit(solution)/shard_map/ppermute | solution.py:334
  33.9 0.3 shard_map.168
  34.1 8.5 %all_to_all.16.pieces = bf16[8,4,512]{2,1,0:T(4,128)(2,1)S(1)} all-to-all(bf16[8,4,512]{2,1,0:T(4,128)(2,1)S(1)} %shard_map.168), channel_id=1, replica_groups={{28,24,20,16,12,8,4,0},{29,25,21,17,13,9,5,1},{30,26,22,18,14,10,6,2},{..., dimensions={0} | all-to-all | bytes 65536 | tf_op jit(solution)/shard_map/all_to_all | solution.py:230
  42.6 0.6 %shard_map.169 = bf16[4,512]{1,0:T(4,128)(2,1)} custom-call(bf16[8,4,512]{2,1,0:T(4,128)(2,1)S(1)} %all_to_all.16.pieces, f32[3072]{0:T(1024)S(1)} %convert_add_fusion.vectors), custom_call_target="tpu_custom_call" | custom-call | bytes 45056 | tf_op jit(solution)/shard_map/pallas_call | solution.py:218
  (22 shorter events, 0.1 us)
Async XLA Ops:
  1.6 12.2 %all-to-all-start = ((bf16[8,8,256]{2,1,0:T(8,128)(2,1)}), bf16[8,8,256]{2,1,0:T(8,128)(2,1)S(1)}, u32[]{:S(2)}, u32[]{:S(2)}) async-start(bf16[8,8,256]{2,1,0:T(8,128)(2,1)} %shard_map.163), calls=%async_computation | async-start | bytes 65536 | tf_op jit(solution)/shard_map/all_to_all | solution.py:230
  9.4 1.7 %copy-start.2 = (bf16[2,22,32,512]{3,2,1,0:T(8,128)(2,1)S(1)}, bf16[2,22,32,512]{3,2,1,0:T(8,128)(2,1)}, u32[]{:S(2)}) copy-start(bf16[2,22,32,512]{3,2,1,0:T(8,128)(2,1)} %param.24) | copy-start | bytes 4325380
  11.1 0.7 %copy-start.3 = (s32[32,16]{0,1:T(8,128)S(1)}, s32[32,16]{0,1:T(8,128)}, u32[]{:S(2)}) copy-start(s32[32,16]{0,1:T(8,128)} %param.23) | copy-start | bytes 6148
  11.1 0.7 %copy-start.4 = (s32[32]{0:T(128)S(1)}, s32[32]{0:T(128)}, u32[]{:S(2)}) copy-start(s32[32]{0:T(128)} %param.22) | copy-start | bytes 388
  11.1 0.7 %copy-start.10 = (s32[32]{0:T(128)S(1)}, s32[32]{0:T(128)}, u32[]{:S(2)}) copy-start(s32[32]{0:T(128)} %param.21) | copy-start | bytes 388
  11.1 0.7 %copy-start.11 = (s32[32]{0:T(128)S(1)}, s32[32]{0:T(128)}, u32[]{:S(2)}) copy-start(s32[32]{0:T(128)} %param.33) | copy-start | bytes 388
  11.1 1.3 %copy-start.5 = (bf16[1024]{0:T(1024)(128)(2,1)S(1)}, bf16[1024]{0:T(1024)(128)(2,1)}, u32[]{:S(2)}) copy-start(bf16[1024]{0:T(1024)(128)(2,1)} %param.30) | copy-start | bytes 6148
  11.1 1.3 %copy-start.6 = (bf16[512]{0:T(512)(128)(2,1)S(1)}, bf16[512]{0:T(512)(128)(2,1)}, u32[]{:S(2)}) copy-start(bf16[512]{0:T(512)(128)(2,1)} %param.32) | copy-start | bytes 3076
  11.1 1.3 %copy-start.7 = (bf16[512]{0:T(512)(128)(2,1)S(1)}, bf16[512]{0:T(512)(128)(2,1)}, u32[]{:S(2)}) copy-start(bf16[512]{0:T(512)(128)(2,1)} %param.28) | copy-start | bytes 3076
  11.2 1.3 %copy-start.8 = (bf16[512]{0:T(512)(128)(2,1)S(1)}, bf16[512]{0:T(512)(128)(2,1)}, u32[]{:S(2)}) copy-start(bf16[512]{0:T(512)(128)(2,1)} %param.27) | copy-start | bytes 3076
  11.2 1.3 %copy-start.9 = (bf16[512]{0:T(512)(128)(2,1)S(1)}, bf16[512]{0:T(512)(128)(2,1)}, u32[]{:S(2)}) copy-start(bf16[512]{0:T(512)(128)(2,1)} %param.26) | copy-start | bytes 3076
  13.8 14.2 %copy-start.1 = (bf16[1024,512]{1,0:T(8,128)(2,1)S(1)}, bf16[1024,512]{1,0:T(8,128)(2,1)}, u32[]{:S(2)}) copy-start(bf16[1024,512]{1,0:T(8,128)(2,1)} %weight.4) | copy-start | bytes 3145732
  15.5 18.3 %copy-start = (bf16[1024,512]{1,0:T(8,128)(2,1)S(1)}, bf16[1024,512]{1,0:T(8,128)(2,1)}, u32[]{:S(2)}) copy-start(bf16[1024,512]{1,0:T(8,128)(2,1)} %weight.5) | copy-start | bytes 3145732
  15.5 3.4 %collective-permute-start.2 = (bf16[4,2048]{1,0:T(4,128)(2,1)S(1)}, bf16[4,2048]{1,0:T(4,128)(2,1)S(1)}, u32[]{:S(2)}, u32[]{:S(2)}) collective-permute-start(bf16[4,2048]{1,0:T(4,128)(2,1)S(1)} %get-tuple-element.16), channel_id=1, source_target_pairs={{0,3},{1,2},{2,1},{3,0},{4,7},{5,6},{6,5},{7,4},{8,11},{9,10},{10,... | collective-permute-start | bytes 49160 | tf_op jit(solution)/shard_map/ppermute | solution.py:334
  15.6 3.8 %collective-permute-start.1 = (bf16[4,2048]{1,0:T(4,128)(2,1)S(1)}, bf16[4,2048]{1,0:T(4,128)(2,1)S(1)}, u32[]{:S(2)}, u32[]{:S(2)}) collective-permute-start(bf16[4,2048]{1,0:T(4,128)(2,1)S(1)} %get-tuple-element.16), channel_id=1, source_target_pairs={{0,2},{1,3},{2,0},{3,1},{4,6},{5,7},{6,4},{7,5},{8,10},{9,11},{10,... | collective-permute-start | bytes 49160 | tf_op jit(solution)/shard_map/ppermute | solution.py:334
  17.2 2.3 %collective-permute-start = (bf16[4,2048]{1,0:T(4,128)(2,1)S(1)}, bf16[4,2048]{1,0:T(4,128)(2,1)S(1)}, u32[]{:S(2)}, u32[]{:S(2)}) collective-permute-start(bf16[4,2048]{1,0:T(4,128)(2,1)S(1)} %get-tuple-element.16), channel_id=1, source_target_pairs={{0,1},{1,0},{2,3},{3,2},{4,5},{5,4},{6,7},{7,6},{8,9},{9,8},{10,11... | collective-permute-start | bytes 49160 | tf_op jit(solution)/shard_map/ppermute | solution.py:334
  28.4 1.3 %collective-permute-start.3 = (bf16[32,1024]{1,0:T(8,128)(2,1)S(1)}, bf16[32,1024]{1,0:T(8,128)(2,1)S(1)}, u32[]{:S(2)}, u32[]{:S(2)}) collective-permute-start(bf16[32,1024]{1,0:T(8,128)(2,1)S(1)} %shard_map.167), channel_id=1, source_target_pairs={{0,1},{1,0},{2,3},{3,2},{4,5},{5,4},{6,7},{7,6},{8,9},{9,8},{10,11... | collective-permute-start | bytes 196616 | tf_op jit(solution)/shard_map/ppermute | solution.py:334
  29.7 4.1 %collective-permute-start.4 = (bf16[32,1024]{1,0:T(8,128)(2,1)S(1)}, bf16[32,1024]{1,0:T(8,128)(2,1)S(1)}, u32[]{:S(2)}, u32[]{:S(2)}) collective-permute-start(bf16[32,1024]{1,0:T(8,128)(2,1)S(1)} %add_convert_fusion.near), channel_id=1, source_target_pairs={{0,3},{1,2},{2,1},{3,0},{4,7},{5,6},{6,5},{7,4},{8,11},{9,10},{10,... | collective-permute-start | bytes 196616 | tf_op jit(solution)/shard_map/ppermute | solution.py:334

commit v18 on v15

--- a/solution.py
+++ b/solution.py
@@ -121,14 +121,17 @@
     valid[...] = seen
 
     ordered = hot(order_col == across)
-    holds = hot((owner_col == ends_first(across // rows)) & (rank_col == across % rows))
+    across_a = iota(arrange.shape, 1)
+    held_by = ends_first(across_a // (2 * rows))
+    holds = hot((owner_col == held_by) & (rank_col == across_a % rows))
     arrange[...] = onto_mxu(ordered, holds).astype(BF16)
     here = hot((owner_col == me) & (rank_col == iota(arrange_own.shape, 1)))
     arrange_own[...] = onto_mxu(ordered, here).astype(BF16)
 
 
 def attention_kernel(
-    place, arrived, pick, valid, vectors, pool, upper, weight, partial, rounded, lower, sem, *, rows
+    place, arrived, pick, valid, vectors, pool, upper, weight,
+    partial, rounded, near, lower, sem, *, rows
 ):
     deep = upper.shape[0]
     copy = pltpu.make_async_copy(weight.at[pl.ds(deep, deep)], lower, sem)
@@ -173,29 +176,54 @@
         whole = projected[:, t * cols : (t + 1) * cols] + mine
         partial[:, t * cols : (t + 1) * cols] = whole
         rounded[:, t * cols : (t + 1) * cols] = whole.astype(BF16)
+        near[:rows, t * cols : (t + 1) * cols] = whole.astype(BF16)
+    for i in (1, 2):
+        near[rows : 2 * rows, (i - 1) * cols : i * cols] = jnp.broadcast_to(
+            row(vectors, i, cols), (rows, cols)
+        ).astype(BF16)
 
 
 def norm_kernel(place, own, sibling, far, far_sibling, vectors, blocks, stream_own):
-    others = sibling[...].astype(F32) + far[...].astype(F32) + far_sibling[...].astype(F32)
+    rows = own.shape[0]
+    others = sibling[:rows, :].astype(F32) + far[...].astype(F32) + far_sibling[...].astype(F32)
     stream = (own[...] + others).astype(BF16).astype(F32)
     width = stream.shape[1]
     cols = width // TP
     mean = jnp.sum(stream, axis=1, keepdims=True) / width
     var = jnp.sum((stream - mean) ** 2, axis=1, keepdims=True) / width
-    mine = stream[:, :cols]
-    for t in range(1, TP):
-        mine = jnp.where(place[1:2, 0:1] == t, stream[:, t * cols : (t + 1) * cols], mine)
-    stream_own[...] = mine.astype(BF16)
-    gain, bias = row(vectors, 1, cols), row(vectors, 2, cols)
-    block = ((mine - mean) * lax.rsqrt(var + NORM_EPS) * gain + bias).astype(BF16)
+    inverse = lax.rsqrt(var + NORM_EPS)
+    me = place[1:2, 0:1]
+    chip = jnp.where(me // 2 == 0, stream[:, : 2 * cols], stream[:, 2 * cols :])
+    core = me % 2
+    halves = []
+    for half in range(2):
+        gain, bias = (
+            jnp.where(
+                core == half,
+                row(vectors, i, cols),
+                sibling[rows : rows + 1, (i - 1) * cols : i * cols].astype(F32),
+            )
+            for i in (1, 2)
+        )
+        part = chip[:, half * cols : (half + 1) * cols]
+        halves.append((part - mean) * inverse * gain + bias)
+    stream_own[...] = jnp.where(core == 0, chip[:, :cols], chip[:, cols:]).astype(BF16)
+    block = jnp.concatenate(halves, axis=0).astype(BF16)
     for d in range(REQ):
         blocks[d] = block
 
 
-def up_kernel(rows_in, arrange, weight, out):
+def up_kernel(place, rows_in, arrange, weight, other, out, *, rows):
     came = rows_in[...].reshape(-1, rows_in.shape[2])
-    ordered = onto_mxu(arrange[...], came).astype(BF16)
-    out[...] = nt_dot(ordered, weight[...]).astype(BF16)
+    which = (iota(arrange.shape, 1) // rows) % 2
+    chosen = arrange[...].astype(F32)
+    core = place[1:2, 0:1] % 2
+
+    def ordered(half):
+        return onto_mxu(jnp.where(which == half, chosen, 0.0).astype(BF16), came).astype(BF16)
+
+    hidden = nt_dot(ordered(core), weight[...]) + nt_dot(ordered(1 - core), other[...])
+    out[...] = hidden.astype(BF16)
 
 
 def down_kernel(near, far, vectors, weight, arrange_own, stream_own, out):
@@ -273,6 +301,7 @@
         + [pltpu.SemaphoreType.DMA((5,))],
         room=ALL_ROOM,
     )
+    up_other = swap(up_weight_t, "tp", 1)
     arrived = trade(packed, ENDS_FIRST)
     numbers = pile(
         [owner[None, :], order[None, :], lengths[None, :], jnp.zeros((5, count), I32), page_table.T]
@@ -283,7 +312,7 @@
         [
             arr((4 * rows, 2 * count)),
             arr((heads * rows, positions), F32),
-            arr((count, count)),
+            arr((count, 2 * count)),
             arr((count, rows)),
         ],
         [VMEM, VMEM],
@@ -296,9 +325,9 @@
     upper = out_weight[: cols // 2]
     upper = jnp.where(here, upper, jnp.zeros_like(upper))
 
-    partial, rounded = call(
+    partial, rounded, near = call(
         attention_kernel,
-        [arr((rows, width), F32), arr((rows, width))],
+        [arr((rows, width), F32), arr((rows, width)), arr((2 * rows, width))],
         [VMEM] * 7 + [HBM],
         [place, arrived, pick, valid, vectors, pool, upper, out_weight],
         [pltpu.VMEM(upper.shape, BF16), pltpu.SemaphoreType.DMA],
@@ -307,18 +336,20 @@
     )
     blocks, stream_own = call(
         norm_kernel,
-        [arr((REQ, rows, cols)), arr((rows, cols))],
+        [arr((REQ, 2 * rows, cols)), arr((rows, cols))],
         [VMEM] * 6,
-        [place, partial] + [swap(rounded, "tp", step) for step in (1, 2, 3)] + [vectors],
+        [place, partial, swap(near, "tp", 1)]
+        + [swap(rounded, "tp", step) for step in (2, 3)]
+        + [vectors],
     )
 
     (part,) = call(
         up_kernel,
         [arr((count, hidden))],
-        [VMEM] * 3,
-        [trade(blocks, ENDS_FIRST), arrange, up_weight_t],
-    )
-    part = (part.astype(F32) + swap(part, "tp", 1).astype(F32)).astype(BF16)
+        [VMEM] * 5,
+        [place, trade(blocks, ENDS_FIRST), arrange, up_weight_t, up_other],
+        rows=rows,
+    )
     (feed,) = call(
         down_kernel,
         [arr((REQ, rows, cols))],

time: 43.6 us -> 49 us (1.12)
  local copies, waits for them, and re-layouts: 0.84 us -> 4.49 us
  Pallas kernels: 5.32 us -> 6.5 us
  starting transfers between devices: 11.1 us -> 9.95 us
  blocking collectives: 16.8 us -> 17.9 us
  other arithmetic: 1.67 us -> 2.55 us
    unnamed x24 -> x32, local copies, waits for them, and re-layouts: 0.7 us -> 4.34 us
    select_n x1, other arithmetic: 0.1 us -> 1.61 us  [on_pairs(): pool = jnp.where(here, kv_pool, jnp.zeros_like(kv_pool))]
    select_n x1, other arithmetic: 1.39 us -> 0.07 us  [on_pairs(): upper = jnp.where(here, upper, jnp.zeros_like(upper))]
    all_to_all x1, waiting for transfers between devices: 1.3 us -> 0.01 us  [trade(): lax.all_to_all(blocks, 'req', 0, 0, tiled=True, axis_index_groups=[group])]
    pallas_call x7, Pallas kernels: 5.32 us -> 6.5 us  [call(): pl.pallas_call(functools.partial(kernel, **fixed) if fixed else kernel, o...]
    ppermute x5, starting transfers between devices: 3.25 us -> 2.1 us  [swap(): return lax.ppermute(x, axis, [(i, i ^ step) for i in range(n)])]
    all_to_all x2, blocking collectives: 16.8 us -> 17.9 us  [trade(): lax.all_to_all(blocks, 'req', 0, 0, tiled=True, axis_index_groups=[group])]
    ppermute x5, waiting for transfers between devices: 6.02 us -> 7 us  [swap(): return lax.ppermute(x, axis, [(i, i ^ step) for i in range(n)])]
  transfers between devices with their start and end apart: 6 -> 6, of which waited for: 5 -> 3; matrix products, arithmetic and copies ran while one was open for 4% -> 6% of each run, Pallas kernels for 1% -> 7%
where the time goes in v18:
time: 49 us; the launch traced here: 48.5 us
  blocking collectives  17.9 us (37%)
  starting transfers between devices  9.95 us (20%)
  waiting for transfers between devices  7 us (14%)
  Pallas kernels  6.5 us (13%)
  local copies, waits for them, and re-layouts  4.49 us (9%)
  other arithmetic  2.55 us (5%)
    all_to_all x2, blocking collectives, trade(): lax.all_to_all(blocks, 'req', 0, 0, tiled=True, axis_index_groups=[group])  17.9 us
    all_to_all x1, starting transfers between devices, trade(): lax.all_to_all(blocks, 'req', 0, 0, tiled=True, axis_index_groups=[group])  7.85 us
    ppermute x5, waiting for transfers between devices, swap(): return lax.ppermute(x, axis, [(i, i ^ step) for i in range(n)])  7 us
    pallas_call x7, Pallas kernels, call(): pl.pallas_call(functools.partial(kernel, **fixed) if fixed else kernel, o...  6.5 us
    unnamed x32, local copies, waits for them, and re-layouts  4.34 us
    ppermute x5, starting transfers between devices, swap(): return lax.ppermute(x, axis, [(i, i ^ step) for i in range(n)])  2.1 us
    select_n x1, other arithmetic, on_pairs(): pool = jnp.where(here, kv_pool, jnp.zeros_like(kv_pool))  1.61 us
  transfers between devices with their start and end apart: 6, of which 3 were waited for; matrix products, arithmetic and copies ran while one was open for 6% of the time, Pallas kernels for 7%

profile of v18, /device:TPU:0, one launch (start us, length us, event | category | flops | bytes accessed | tf_op | source)
XLA Modules:
  0.0 48.5 jit_solution(11667158916285117513)
XLA Ops:
  0.0 1.6 %shard_map.163 = bf16[8,8,256]{2,1,0:T(8,128)(2,1)} custom-call(s32[1,32]{1,0:T(1,128)} %bitcast.7, bf16[4,512]{1,0:T(4,128)(2,1)} %query.1, bf16[4,512]{1,0:T(4,128)(2,1)} %key.1, bf16[4,512]{1,0:T(4,128)(2,1)} %value.1, bf16[4,512]{1,0:T(4,128)(2,1)} %resid.1), custom_call_target="tpu_custom_call" | custom-call | bytes 16512 | tf_op jit(solution)/shard_map/pallas_call | solution.py:246
  1.6 7.9 %all-to-all-start = ((bf16[8,8,256]{2,1,0:T(8,128)(2,1)}), bf16[8,8,256]{2,1,0:T(8,128)(2,1)}, u32[]{:S(2)}, u32[]{:S(2)}) async-start(bf16[8,8,256]{2,1,0:T(8,128)(2,1)} %shard_map.163), calls=%async_computation | async-start | bytes 65536 | tf_op jit(solution)/shard_map/all_to_all | solution.py:258
  9.4 0.1 pad.60
  9.5 0.1 pad_add_fusion.1
  9.6 0.8 %pad_add_fusion.numbers = s32[24,32]{1,0:T(8,128)S(1)} fusion(s32[16,32]{1,0:T(8,128)} %bitcast.6, s32[1,32]{1,0:T(1,128)} %bitcast.9, s32[1,32]{1,0:T(1,128)} %bitcast.10, s32[1,32]{1,0:T(1,128)} %bitcast.8, s32[24]{0:T(128)S(1)} %pad.60), kind=kLoop, calls=%fused_computation.3 | loop fusion | flops 3072 | bytes 5600 | tf_op jit(solution)/shard_map/add | solution.py:50
  10.4 0.1 broadcast_in_dim.25.place
  10.4 0.4 shard_map.164
  10.9 0.6 %copy-done.2 = f32[16,704]{1,0:T(8,128)} copy-done((f32[16,704]{1,0:T(8,128)}, f32[16,704]{1,0:T(8,128)S(1)}, u32[]{:S(2)}) %copy-start.2) | copy-done | bytes 45080
  11.5 0.6 %copy-done.6 = bf16[32,64]{1,0:T(8,128)(2,1)} copy-done((bf16[32,64]{1,0:T(8,128)(2,1)}, bf16[32,64]{1,0:T(8,128)(2,1)S(1)}, u32[]{:S(2)}) %copy-start.6) | copy-done | bytes 4120
  12.1 0.6 %copy-done.8 = bf16[16,64]{1,0:T(8,128)(2,1)} copy-done((bf16[16,64]{1,0:T(8,128)(2,1)}, bf16[16,64]{1,0:T(8,128)(2,1)S(1)}, u32[]{:S(2)}) %copy-start.8) | copy-done | bytes 2072
  12.7 1.6 %broadcast_select_fusion.pool = bf16[2,22,32,512]{3,2,1,0:T(8,128)(2,1)S(1)} fusion(bf16[2,22,32,512]{3,2,1,0:T(8,128)(2,1)} %param.24, pred[]{:T(512)S(6)} %ge.3), kind=kLoop, calls=%fused_computation | loop fusion | flops 720896 | bytes 2883585 | tf_op jit(solution)/shard_map/jit(_where)/select_n | solution.py:324
  14.3 0.4 copy-done.10
  14.7 0.1 slice_select_fusion.upper
  14.8 0.6 %copy-done.11 = bf16[1024]{0:T(1024)(128)(2,1)S(1)} copy-done((bf16[1024]{0:T(1024)(128)(2,1)S(1)}, bf16[1024]{0:T(1024)(128)(2,1)}, u32[]{:S(2)}) %copy-start.11) | copy-done | bytes 2072
  15.4 0.0 copy-done.12
  15.4 0.0 copy-done.14
  15.4 0.0 copy-done.15
  15.5 0.8 %copy-done.3 = f32[16,704]{1,0:T(8,128)S(1)} copy-done((f32[16,704]{1,0:T(8,128)S(1)}, f32[16,704]{1,0:T(8,128)}, u32[]{:S(2)}) %copy-start.3) | copy-done | bytes 45080
  16.3 0.7 %copy-done.9 = bf16[16,64]{1,0:T(8,128)(2,1)S(1)} copy-done((bf16[16,64]{1,0:T(8,128)(2,1)S(1)}, bf16[16,64]{1,0:T(8,128)(2,1)}, u32[]{:S(2)}) %copy-start.9) | copy-done | bytes 2072
  17.0 2.6 %shard_map.165 = (f32[4,2048]{1,0:T(4,128)S(1)}, bf16[4,2048]{1,0:T(4,128)(2,1)S(1)}, bf16[8,2048]{1,0:T(8,128)(2,1)S(1)}) custom-call(s32[2,128]{1,0:T(2,128)S(1)} %broadcast_in_dim.25.place, bf16[8,8,256]{2,1,0:T(8,128)(2,1)} %all-to-all-done.arrived, bf16[16,64]{1,0:T(8,128)(2,1)S(1)} %copy-done.9, f32[16,704]{1,0:T(8,128)S(1)} %copy-done.3, ...), custom_call_target="tpu_custom_call" | custom-call | bytes 4680704 | tf_op jit(solution)/shard_map/pallas_call | solution.py:246
  19.6 0.6 %collective-permute-start = (bf16[8,2048]{1,0:T(8,128)(2,1)S(1)}, bf16[8,2048]{1,0:T(8,128)(2,1)S(1)}, u32[]{:S(2)}, u32[]{:S(2)}) collective-permute-start(bf16[8,2048]{1,0:T(8,128)(2,1)S(1)} %get-tuple-element.17), channel_id=1, source_target_pairs={{0,1},{1,0},{2,3},{3,2},{4,5},{5,4},{6,7},{7,6},{8,9},{9,8},{10,11... | collective-permute-start | bytes 98312 | tf_op jit(solution)/shard_map/ppermute | solution.py:365
  20.2 1.5 %collective-permute-start.1 = (bf16[4,2048]{1,0:T(4,128)(2,1)S(1)}, bf16[4,2048]{1,0:T(4,128)(2,1)S(1)}, u32[]{:S(2)}, u32[]{:S(2)}) collective-permute-start(bf16[4,2048]{1,0:T(4,128)(2,1)S(1)} %get-tuple-element.18), channel_id=1, source_target_pairs={{0,2},{1,3},{2,0},{3,1},{4,6},{5,7},{6,4},{7,5},{8,10},{9,11},{10,... | collective-permute-start | bytes 49160 | tf_op jit(solution)/shard_map/ppermute | solution.py:365
  21.7 2.2 %collective-permute-done.1.far = bf16[4,2048]{1,0:T(4,128)(2,1)S(1)} collective-permute-done((bf16[4,2048]{1,0:T(4,128)(2,1)S(1)}, bf16[4,2048]{1,0:T(4,128)(2,1)S(1)}, u32[]{:S(2)}, u32[]{:S(2)}) %collective-permute-start.1) | collective-permute-done | bytes 16416 | tf_op jit(solution)/shard_map/ppermute | solution.py:365
  23.9 1.1 %collective-permute-done.2.far_sibling = bf16[4,2048]{1,0:T(4,128)(2,1)S(1)} collective-permute-done((bf16[4,2048]{1,0:T(4,128)(2,1)S(1)}, bf16[4,2048]{1,0:T(4,128)(2,1)S(1)}, u32[]{:S(2)}, u32[]{:S(2)}) %collective-permute-start.2) | collective-permute-done | bytes 16416 | tf_op jit(solution)/shard_map/ppermute | solution.py:365
  25.0 0.2 shard_map.166
  25.2 9.4 %all_to_all.15.rows_in = bf16[8,8,512]{2,1,0:T(8,128)(2,1)S(1)} all-to-all(bf16[8,8,512]{2,1,0:T(8,128)(2,1)S(1)} %get-tuple-element.19), channel_id=1, replica_groups={{12,16,8,20,4,24,0,28},{13,17,9,21,5,25,1,29},{14,18,10,22,6,26,2,30},{..., dimensions={0} | all-to-all | bytes 131072 | tf_op jit(solution)/shard_map/all_to_all | solution.py:258
  34.6 0.8 %shard_map.167.near = bf16[32,1024]{1,0:T(8,128)(2,1)S(1)} custom-call(s32[2,128]{1,0:T(2,128)S(1)} %broadcast_in_dim.25.place, bf16[8,8,512]{2,1,0:T(8,128)(2,1)S(1)} %all_to_all.15.rows_in, bf16[32,64]{1,0:T(8,128)(2,1)S(1)} %copy-done.7, bf16[1024,512]{1,0:T(8,128)(2,1)S(1)} %copy-done.1, bf16[1024,512]{1,0:T(8,128)(2,1)S(1)} %collective-permute-done.3.other), custom_call_target="tpu_custom_call" | custom-call | bytes 2167808 | tf_op jit(solution)/shard_map/pallas_call | solution.py:246
  35.4 0.0 collective-permute-start.4
  35.5 3.7 %collective-permute-done.4.far = bf16[32,1024]{1,0:T(8,128)(2,1)S(1)} collective-permute-done((bf16[32,1024]{1,0:T(8,128)(2,1)S(1)}, bf16[32,1024]{1,0:T(8,128)(2,1)S(1)}, u32[]{:S(2)}, u32[]{:S(2)}) %collective-permute-start.4) | collective-permute-done | bytes 65568 | tf_op jit(solution)/shard_map/ppermute | solution.py:365
  39.2 0.3 shard_map.168
  39.5 8.5 %all_to_all.16.pieces = bf16[8,4,512]{2,1,0:T(4,128)(2,1)S(1)} all-to-all(bf16[8,4,512]{2,1,0:T(4,128)(2,1)S(1)} %shard_map.168), channel_id=1, replica_groups={{28,24,20,16,12,8,4,0},{29,25,21,17,13,9,5,1},{30,26,22,18,14,10,6,2},{..., dimensions={0} | all-to-all | bytes 65536 | tf_op jit(solution)/shard_map/all_to_all | solution.py:258
  47.9 0.6 %shard_map.169 = bf16[4,512]{1,0:T(4,128)(2,1)} custom-call(bf16[8,4,512]{2,1,0:T(4,128)(2,1)S(1)} %all_to_all.16.pieces, f32[3072]{0:T(1024)S(1)} %convert_add_fusion.vectors), custom_call_target="tpu_custom_call" | custom-call | bytes 45056 | tf_op jit(solution)/shard_map/pallas_call | solution.py:246
  (29 shorter events, 0.1 us)
Async XLA Ops:
  1.6 13.9 %all-to-all-start = ((bf16[8,8,256]{2,1,0:T(8,128)(2,1)}), bf16[8,8,256]{2,1,0:T(8,128)(2,1)}, u32[]{:S(2)}, u32[]{:S(2)}) async-start(bf16[8,8,256]{2,1,0:T(8,128)(2,1)} %shard_map.163), calls=%async_computation | async-start | bytes 65536 | tf_op jit(solution)/shard_map/all_to_all | solution.py:258
  9.4 25.2 %collective-permute-start.3 = (bf16[1024,512]{1,0:T(8,128)(2,1)}, bf16[1024,512]{1,0:T(8,128)(2,1)S(1)}, u32[]{:S(2)}, u32[]{:S(2)}) collective-permute-start(bf16[1024,512]{1,0:T(8,128)(2,1)} %weight.4), channel_id=1, source_target_pairs={{0,1},{1,0},{2,3},{3,2},{4,5},{5,4},{6,7},{7,6},{8,9},{9,8},{10,11... | collective-permute-start | bytes 3145736 | tf_op jit(solution)/shard_map/ppermute | solution.py:365
  10.9 0.6 %copy-start.2 = (f32[16,704]{1,0:T(8,128)}, f32[16,704]{1,0:T(8,128)S(1)}, u32[]{:S(2)}) copy-start(f32[16,704]{1,0:T(8,128)S(1)} %get-tuple-element.15.valid) | copy-start | bytes 135172
  11.5 0.6 %copy-start.6 = (bf16[32,64]{1,0:T(8,128)(2,1)}, bf16[32,64]{1,0:T(8,128)(2,1)S(1)}, u32[]{:S(2)}) copy-start(bf16[32,64]{1,0:T(8,128)(2,1)S(1)} %get-tuple-element.20.arrange) | copy-start | bytes 12292
  12.1 0.6 %copy-start.8 = (bf16[16,64]{1,0:T(8,128)(2,1)}, bf16[16,64]{1,0:T(8,128)(2,1)S(1)}, u32[]{:S(2)}) copy-start(bf16[16,64]{1,0:T(8,128)(2,1)S(1)} %get-tuple-element.14.pick) | copy-start | bytes 6148
  12.7 1.6 %copy-start.4 = (bf16[32,4]{1,0:T(8,128)(2,1)}, bf16[32,4]{1,0:T(8,128)(2,1)S(1)}, u32[]{:S(2)}) copy-start(bf16[32,4]{1,0:T(8,128)(2,1)S(1)} %get-tuple-element.21.arrange_own) | copy-start | bytes 772
  12.7 2.0 %copy-start.10 = (bf16[512,2048]{1,0:T(8,128)(2,1)S(1)}, bf16[512,2048]{1,0:T(8,128)(2,1)}, u32[]{:S(2)}) copy-start(bf16[512,2048]{1,0:T(8,128)(2,1)} %weight.3) | copy-start | bytes 6291460
  14.7 0.7 %copy-start.11 = (bf16[1024]{0:T(1024)(128)(2,1)S(1)}, bf16[1024]{0:T(1024)(128)(2,1)}, u32[]{:S(2)}) copy-start(bf16[1024]{0:T(1024)(128)(2,1)} %param.30) | copy-start | bytes 6148
  14.7 0.7 %copy-start.12 = (bf16[512]{0:T(512)(128)(2,1)S(1)}, bf16[512]{0:T(512)(128)(2,1)}, u32[]{:S(2)}) copy-start(bf16[512]{0:T(512)(128)(2,1)} %param.32) | copy-start | bytes 3076
  14.7 0.7 %copy-start.13 = (bf16[512]{0:T(512)(128)(2,1)S(1)}, bf16[512]{0:T(512)(128)(2,1)}, u32[]{:S(2)}) copy-start(bf16[512]{0:T(512)(128)(2,1)} %param.28) | copy-start | bytes 3076
  14.7 0.7 %copy-start.14 = (bf16[512]{0:T(512)(128)(2,1)S(1)}, bf16[512]{0:T(512)(128)(2,1)}, u32[]{:S(2)}) copy-start(bf16[512]{0:T(512)(128)(2,1)} %param.27) | copy-start | bytes 3076
  14.7 0.7 %copy-start.15 = (bf16[512]{0:T(512)(128)(2,1)S(1)}, bf16[512]{0:T(512)(128)(2,1)}, u32[]{:S(2)}) copy-start(bf16[512]{0:T(512)(128)(2,1)} %param.26) | copy-start | bytes 3076
  15.5 0.8 %copy-start.3 = (f32[16,704]{1,0:T(8,128)S(1)}, f32[16,704]{1,0:T(8,128)}, u32[]{:S(2)}) copy-start(f32[16,704]{1,0:T(8,128)} %copy-done.2) | copy-start | bytes 135172
  16.3 0.7 %copy-start.9 = (bf16[16,64]{1,0:T(8,128)(2,1)S(1)}, bf16[16,64]{1,0:T(8,128)(2,1)}, u32[]{:S(2)}) copy-start(bf16[16,64]{1,0:T(8,128)(2,1)} %copy-done.8) | copy-start | bytes 6148
  17.0 17.7 %copy-start.1 = (bf16[1024,512]{1,0:T(8,128)(2,1)S(1)}, bf16[1024,512]{1,0:T(8,128)(2,1)}, u32[]{:S(2)}) copy-start(bf16[1024,512]{1,0:T(8,128)(2,1)} %weight.4) | copy-start | bytes 3145732
  17.0 17.7 %copy-start.7 = (bf16[32,64]{1,0:T(8,128)(2,1)S(1)}, bf16[32,64]{1,0:T(8,128)(2,1)}, u32[]{:S(2)}) copy-start(bf16[32,64]{1,0:T(8,128)(2,1)} %copy-done.6) | copy-start | bytes 12292
  19.6 19.6 %copy-start = (bf16[1024,512]{1,0:T(8,128)(2,1)S(1)}, bf16[1024,512]{1,0:T(8,128)(2,1)}, u32[]{:S(2)}) copy-start(bf16[1024,512]{1,0:T(8,128)(2,1)} %weight.5) | copy-start | bytes 3145732
  19.6 19.6 %copy-start.5 = (bf16[32,4]{1,0:T(8,128)(2,1)S(1)}, bf16[32,4]{1,0:T(8,128)(2,1)}, u32[]{:S(2)}) copy-start(bf16[32,4]{1,0:T(8,128)(2,1)} %copy-done.4) | copy-start | bytes 772
  19.6 5.4 %collective-permute-start = (bf16[8,2048]{1,0:T(8,128)(2,1)S(1)}, bf16[8,2048]{1,0:T(8,128)(2,1)S(1)}, u32[]{:S(2)}, u32[]{:S(2)}) collective-permute-start(bf16[8,2048]{1,0:T(8,128)(2,1)S(1)} %get-tuple-element.17), channel_id=1, source_target_pairs={{0,1},{1,0},{2,3},{3,2},{4,5},{5,4},{6,7},{7,6},{8,9},{9,8},{10,11... | collective-permute-start | bytes 98312 | tf_op jit(solution)/shard_map/ppermute | solution.py:365
  20.2 3.7 %collective-permute-start.1 = (bf16[4,2048]{1,0:T(4,128)(2,1)S(1)}, bf16[4,2048]{1,0:T(4,128)(2,1)S(1)}, u32[]{:S(2)}, u32[]{:S(2)}) collective-permute-start(bf16[4,2048]{1,0:T(4,128)(2,1)S(1)} %get-tuple-element.18), channel_id=1, source_target_pairs={{0,2},{1,3},{2,0},{3,1},{4,6},{5,7},{6,4},{7,5},{8,10},{9,11},{10,... | collective-permute-start | bytes 49160 | tf_op jit(solution)/shard_map/ppermute | solution.py:365
  21.6 3.3 %collective-permute-start.2 = (bf16[4,2048]{1,0:T(4,128)(2,1)S(1)}, bf16[4,2048]{1,0:T(4,128)(2,1)S(1)}, u32[]{:S(2)}, u32[]{:S(2)}) collective-permute-start(bf16[4,2048]{1,0:T(4,128)(2,1)S(1)} %get-tuple-element.18), channel_id=1, source_target_pairs={{0,3},{1,2},{2,1},{3,0},{4,7},{5,6},{6,5},{7,4},{8,11},{9,10},{10,... | collective-permute-start | bytes 49160 | tf_op jit(solution)/shard_map/ppermute | solution.py:365
  35.4 3.7 %collective-permute-start.4 = (bf16[32,1024]{1,0:T(8,128)(2,1)S(1)}, bf16[32,1024]{1,0:T(8,128)(2,1)S(1)}, u32[]{:S(2)}, u32[]{:S(2)}) collective-permute-start(bf16[32,1024]{1,0:T(8,128)(2,1)S(1)} %shard_map.167.near), channel_id=1, source_target_pairs={{0,3},{1,2},{2,1},{3,0},{4,7},{5,6},{6,5},{7,4},{8,11},{9,10},{10,... | collective-permute-start | bytes 196616 | tf_op jit(solution)/shard_map/ppermute | solution.py:365

commit v19 on v17

--- a/solution.py
+++ b/solution.py
@@ -18,12 +18,16 @@
 VMEM = pl.BlockSpec(memory_space=pltpu.VMEM)
 HBM = pl.BlockSpec(memory_space=pltpu.HBM)
 
-ENDS_FIRST = [4, 3, 5, 2, 6, 1, 7, 0]
-LOW_FIRST = [7, 6, 5, 4, 3, 2, 1, 0]
-
-
-def ends_first(place):
-    return jnp.where(place % 2 == 0, 4 + place // 2, 3 - place // 2)
+FIRST_ORDER = [3, 5, 2, 4, 1, 7, 0, 6]
+MIDDLE_ORDER = [3, 4, 1, 6, 2, 5, 0, 7]
+LAST_ORDER = [4, 3, 5, 2, 6, 1, 7, 0]
+
+
+def pick_from(order, place):
+    found = jnp.zeros_like(place)
+    for i, index in enumerate(order):
+        found = jnp.where(place == i, index, found)
+    return found
 
 
 def iota(shape, dim):
@@ -77,7 +81,7 @@
     blocks = onto_mxu(pick, all_rows).astype(BF16)
     for d in range(REQ):
         block = blocks[d * fields : (d + 1) * fields]
-        at = ENDS_FIRST.index(d)
+        at = FIRST_ORDER.index(d)
         out[at, :fields, :] = block[:, : cols // 2]
         out[at, fields:, :] = block[:, cols // 2 :]
 
@@ -102,7 +106,7 @@
     down_p, across_p = iota(shape, 0), iota(shape, 1)
     down_i = iota((shape[0], count), 0)
     mine = hot((owner_row == me) & (rank_row == down_i % rows))
-    source = ends_first(iota((count, shape[1]), 1) // (2 * rows))
+    source = pick_from(FIRST_ORDER, iota((count, shape[1]), 1) // (2 * rows))
     came = hot(iota((count, shape[1]), 0) // rows == source)
     from_there = onto_mxu(mine, came)
     pick[...] = hot((from_there > 0.5) & (down_p // rows == across_p % rows))
@@ -121,7 +125,7 @@
     valid[...] = seen
 
     ordered = hot(order_col == across)
-    holds = hot((owner_col == ends_first(across // rows)) & (rank_col == across % rows))
+    holds = hot((owner_col == pick_from(MIDDLE_ORDER, across // rows)) & (rank_col == across % rows))
     arrange[...] = onto_mxu(ordered, holds).astype(BF16)
     here = hot((owner_col == me) & (rank_col == iota(arrange_own.shape, 1)))
     arrange_own[...] = onto_mxu(ordered, here).astype(BF16)
@@ -205,7 +209,7 @@
     feed = onto_mxu(activated, weight[...]) + onto_mxu(arrange_own[...], stream_own[...])
     rows = out.shape[1]
     for d in range(REQ):
-        out[LOW_FIRST.index(d)] = feed[d * rows : (d + 1) * rows].astype(BF16)
+        out[LAST_ORDER.index(d)] = feed[d * rows : (d + 1) * rows].astype(BF16)
 
 
 def finish_kernel(pieces, vectors, out):
@@ -273,7 +277,7 @@
         + [pltpu.SemaphoreType.DMA((5,))],
         room=ALL_ROOM,
     )
-    arrived = trade(packed, ENDS_FIRST)
+    arrived = trade(packed, FIRST_ORDER)
     numbers = pile(
         [owner[None, :], order[None, :], lengths[None, :], jnp.zeros((5, count), I32), page_table.T]
     )
@@ -316,7 +320,7 @@
         up_kernel,
         [arr((count, hidden))],
         [VMEM] * 3,
-        [trade(blocks, ENDS_FIRST), arrange, up_weight_t],
+        [trade(blocks, MIDDLE_ORDER), arrange, up_weight_t],
     )
     part = (part.astype(F32) + swap(part, "tp", 1).astype(F32)).astype(BF16)
     (feed,) = call(
@@ -325,7 +329,7 @@
         [VMEM] * 6,
         [part, swap(part, "tp", 3), vectors, down_weight, arrange_own, stream_own],
     )
-    (out,) = call(finish_kernel, [arr((rows, cols))], [VMEM] * 2, [trade(feed, LOW_FIRST), vectors])
+    (out,) = call(finish_kernel, [arr((rows, cols))], [VMEM] * 2, [trade(feed, LAST_ORDER), vectors])
     return out
 
 

time: 43.6 us -> 44.2 us (1.014)
  blocking collectives: 16.8 us -> 17.4 us
    all_to_all x2, blocking collectives: 16.8 us -> 17.4 us  [trade(): lax.all_to_all(blocks, 'req', 0, 0, tiled=True, axis_index_groups=[group])]
where the time goes in v19:
time: 44.2 us; the launch traced here: 43.8 us
  blocking collectives  17.4 us (39%)
  starting transfers between devices  11.1 us (25%)
  waiting for transfers between devices  7.32 us (17%)
  Pallas kernels  5.32 us (12%)
  other arithmetic  1.67 us (4%)
  local copies, waits for them, and re-layouts  0.84 us (2%)
    all_to_all x2, blocking collectives, trade(): lax.all_to_all(blocks, 'req', 0, 0, tiled=True, axis_index_groups=[group])  17.4 us
    all_to_all x1, starting transfers between devices, trade(): lax.all_to_all(blocks, 'req', 0, 0, tiled=True, axis_index_groups=[group])  7.85 us
    ppermute x5, waiting for transfers between devices, swap(): return lax.ppermute(x, axis, [(i, i ^ step) for i in range(n)])  6.01 us
    pallas_call x7, Pallas kernels, call(): pl.pallas_call(functools.partial(kernel, **fixed) if fixed else kernel, o...  5.32 us
    ppermute x5, starting transfers between devices, swap(): return lax.ppermute(x, axis, [(i, i ^ step) for i in range(n)])  3.25 us
    select_n x1, other arithmetic, on_pairs(): upper = jnp.where(here, upper, jnp.zeros_like(upper))  1.39 us
    all_to_all x1, waiting for transfers between devices, trade(): lax.all_to_all(blocks, 'req', 0, 0, tiled=True, axis_index_groups=[group])  1.3 us
  transfers between devices with their start and end apart: 6, of which 5 were waited for; matrix products, arithmetic and copies ran while one was open for 4% of the time, Pallas kernels for 1%

profile of v19, /device:TPU:0, one launch (start us, length us, event | category | flops | bytes accessed | tf_op | source)
XLA Modules:
  0.0 43.8 jit_solution(10690667278152210057)
XLA Ops:
  0.0 1.6 %shard_map.163 = bf16[8,8,256]{2,1,0:T(8,128)(2,1)} custom-call(s32[1,32]{1,0:T(1,128)} %bitcast.7, bf16[4,512]{1,0:T(4,128)(2,1)} %query.1, bf16[4,512]{1,0:T(4,128)(2,1)} %key.1, bf16[4,512]{1,0:T(4,128)(2,1)} %value.1, bf16[4,512]{1,0:T(4,128)(2,1)} %resid.1), custom_call_target="tpu_custom_call" | custom-call | bytes 16512 | tf_op jit(solution)/shard_map/pallas_call | solution.py:222
  1.6 7.9 %all-to-all-start = ((bf16[8,8,256]{2,1,0:T(8,128)(2,1)}), bf16[8,8,256]{2,1,0:T(8,128)(2,1)S(1)}, u32[]{:S(2)}, u32[]{:S(2)}) async-start(bf16[8,8,256]{2,1,0:T(8,128)(2,1)} %shard_map.163), calls=%async_computation | async-start | bytes 65536 | tf_op jit(solution)/shard_map/all_to_all | solution.py:234
  9.4 0.1 pad.60
  9.5 1.4 %slice_select_fusion.upper = bf16[256,2048]{1,0:T(8,128)(2,1)S(1)} fusion(bf16[512,2048]{1,0:T(8,128)(2,1)} %weight.3, pred[]{:T(512)S(6)} %ge.3), kind=kLoop, calls=%fused_computation.1 | loop fusion | flops 524288 | bytes 2097153 | tf_op jit(solution)/shard_map/jit(_where)/select_n | solution.py:301
  10.9 0.2 copy-done.2
  11.1 0.0 copy-start.5
  11.2 0.0 copy-start.8
  11.2 0.0 copy-start.9
  11.2 0.1 broadcast_select_fusion.pool
  11.3 0.1 pad_add_fusion.1
  11.4 0.4 %copy-done.3 = s32[32,16]{0,1:T(8,128)S(1)} copy-done((s32[32,16]{0,1:T(8,128)S(1)}, s32[32,16]{0,1:T(8,128)}, u32[]{:S(2)}) %copy-start.3) | copy-done | bytes 2072
  11.8 0.1 pad_add_fusion.numbers
  11.9 0.1 broadcast_in_dim.25.place
  12.0 0.4 shard_map.164
  12.5 1.3 %all-to-all-done.arrived = bf16[8,8,256]{2,1,0:T(8,128)(2,1)S(1)} async-done(((bf16[8,8,256]{2,1,0:T(8,128)(2,1)}), bf16[8,8,256]{2,1,0:T(8,128)(2,1)S(1)}, u32[]{:S(2)}, u32[]{:S(2)}) %all-to-all-start) | async-done | bytes 32800 | tf_op jit(solution)/shard_map/all_to_all | solution.py:234
  13.8 1.8 %shard_map.165 = (f32[4,2048]{1,0:T(4,128)S(1)}, bf16[4,2048]{1,0:T(4,128)(2,1)S(1)}) custom-call(s32[2,128]{1,0:T(2,128)S(1)} %broadcast_in_dim.25.place, bf16[8,8,256]{2,1,0:T(8,128)(2,1)S(1)} %all-to-all-done.arrived, bf16[16,64]{1,0:T(8,128)(2,1)S(1)} %get-tuple-element.13.pick, f32[16,704]{1,0:T(8,128)S(1)} %get-tuple-element.14.valid, ...), custom_call_target="tpu_custom_call" | custom-call | bytes 4680704 | tf_op jit(solution)/shard_map/pallas_call | solution.py:222
  15.5 0.0 copy-start
  15.5 0.1 collective-permute-start.2
  15.6 1.6 %collective-permute-start.1 = (bf16[4,2048]{1,0:T(4,128)(2,1)S(1)}, bf16[4,2048]{1,0:T(4,128)(2,1)S(1)}, u32[]{:S(2)}, u32[]{:S(2)}) collective-permute-start(bf16[4,2048]{1,0:T(4,128)(2,1)S(1)} %get-tuple-element.16), channel_id=1, source_target_pairs={{0,2},{1,3},{2,0},{3,1},{4,6},{5,7},{6,4},{7,5},{8,10},{9,11},{10,... | collective-permute-start | bytes 49160 | tf_op jit(solution)/shard_map/ppermute | solution.py:338
  17.2 0.3 collective-permute-start
  17.5 1.4 %collective-permute-done.2.far_sibling = bf16[4,2048]{1,0:T(4,128)(2,1)S(1)} collective-permute-done((bf16[4,2048]{1,0:T(4,128)(2,1)S(1)}, bf16[4,2048]{1,0:T(4,128)(2,1)S(1)}, u32[]{:S(2)}, u32[]{:S(2)}) %collective-permute-start.2) | collective-permute-done | bytes 16416 | tf_op jit(solution)/shard_map/ppermute | solution.py:338
  18.9 0.5 %collective-permute-done.1.far = bf16[4,2048]{1,0:T(4,128)(2,1)S(1)} collective-permute-done((bf16[4,2048]{1,0:T(4,128)(2,1)S(1)}, bf16[4,2048]{1,0:T(4,128)(2,1)S(1)}, u32[]{:S(2)}, u32[]{:S(2)}) %collective-permute-start.1) | collective-permute-done | bytes 16416 | tf_op jit(solution)/shard_map/ppermute | solution.py:338
  19.4 0.2 shard_map.166
  19.6 8.2 %all_to_all.15.rows_in = bf16[8,4,512]{2,1,0:T(4,128)(2,1)S(1)} all-to-all(bf16[8,4,512]{2,1,0:T(4,128)(2,1)S(1)} %get-tuple-element.17), channel_id=1, replica_groups={{12,16,4,24,8,20,0,28},{13,17,5,25,9,21,1,29},{14,18,6,26,10,22,2,30},{..., dimensions={0} | all-to-all | bytes 65536 | tf_op jit(solution)/shard_map/all_to_all | solution.py:234
  27.8 0.5 %shard_map.167 = bf16[32,1024]{1,0:T(8,128)(2,1)S(1)} custom-call(bf16[8,4,512]{2,1,0:T(4,128)(2,1)S(1)} %all_to_all.15.rows_in, bf16[32,32]{1,0:T(8,128)(2,1)S(1)} %get-tuple-element.18.arrange, bf16[1024,512]{1,0:T(8,128)(2,1)S(1)} %copy-done.1), custom_call_target="tpu_custom_call" | custom-call | bytes 1083392 | tf_op jit(solution)/shard_map/pallas_call | solution.py:222
  28.3 0.0 collective-permute-start.3
  28.3 1.2 %collective-permute-done.3 = bf16[32,1024]{1,0:T(8,128)(2,1)S(1)} collective-permute-done((bf16[32,1024]{1,0:T(8,128)(2,1)S(1)}, bf16[32,1024]{1,0:T(8,128)(2,1)S(1)}, u32[]{:S(2)}, u32[]{:S(2)}) %collective-permute-start.3) | collective-permute-done | bytes 65568 | tf_op jit(solution)/shard_map/ppermute | solution.py:338
  29.6 1.3 %collective-permute-start.4 = (bf16[32,1024]{1,0:T(8,128)(2,1)S(1)}, bf16[32,1024]{1,0:T(8,128)(2,1)S(1)}, u32[]{:S(2)}, u32[]{:S(2)}) collective-permute-start(bf16[32,1024]{1,0:T(8,128)(2,1)S(1)} %add_convert_fusion.near), channel_id=1, source_target_pairs={{0,3},{1,2},{2,1},{3,0},{4,7},{5,6},{6,5},{7,4},{8,11},{9,10},{10,... | collective-permute-start | bytes 196616 | tf_op jit(solution)/shard_map/ppermute | solution.py:338
  30.9 2.8 %collective-permute-done.4.far = bf16[32,1024]{1,0:T(8,128)(2,1)S(1)} collective-permute-done((bf16[32,1024]{1,0:T(8,128)(2,1)S(1)}, bf16[32,1024]{1,0:T(8,128)(2,1)S(1)}, u32[]{:S(2)}, u32[]{:S(2)}) %collective-permute-start.4) | collective-permute-done | bytes 65568 | tf_op jit(solution)/shard_map/ppermute | solution.py:338
  33.7 0.3 shard_map.168
  34.0 9.2 %all_to_all.16.pieces = bf16[8,4,512]{2,1,0:T(4,128)(2,1)S(1)} all-to-all(bf16[8,4,512]{2,1,0:T(4,128)(2,1)S(1)} %shard_map.168), channel_id=1, replica_groups={{16,12,20,8,24,4,28,0},{17,13,21,9,25,5,29,1},{18,14,22,10,26,6,30,2},{..., dimensions={0} | all-to-all | bytes 65536 | tf_op jit(solution)/shard_map/all_to_all | solution.py:234
  43.2 0.6 %shard_map.169 = bf16[4,512]{1,0:T(4,128)(2,1)} custom-call(bf16[8,4,512]{2,1,0:T(4,128)(2,1)S(1)} %all_to_all.16.pieces, f32[3072]{0:T(1024)S(1)} %convert_add_fusion.vectors), custom_call_target="tpu_custom_call" | custom-call | bytes 45056 | tf_op jit(solution)/shard_map/pallas_call | solution.py:222
  (22 shorter events, 0.1 us)
Async XLA Ops:
  1.6 12.2 %all-to-all-start = ((bf16[8,8,256]{2,1,0:T(8,128)(2,1)}), bf16[8,8,256]{2,1,0:T(8,128)(2,1)S(1)}, u32[]{:S(2)}, u32[]{:S(2)}) async-start(bf16[8,8,256]{2,1,0:T(8,128)(2,1)} %shard_map.163), calls=%async_computation | async-start | bytes 65536 | tf_op jit(solution)/shard_map/all_to_all | solution.py:234
  9.4 1.7 %copy-start.2 = (bf16[2,22,32,512]{3,2,1,0:T(8,128)(2,1)S(1)}, bf16[2,22,32,512]{3,2,1,0:T(8,128)(2,1)}, u32[]{:S(2)}) copy-start(bf16[2,22,32,512]{3,2,1,0:T(8,128)(2,1)} %param.24) | copy-start | bytes 4325380
  11.1 0.7 %copy-start.3 = (s32[32,16]{0,1:T(8,128)S(1)}, s32[32,16]{0,1:T(8,128)}, u32[]{:S(2)}) copy-start(s32[32,16]{0,1:T(8,128)} %param.23) | copy-start | bytes 6148
  11.1 0.7 %copy-start.4 = (s32[32]{0:T(128)S(1)}, s32[32]{0:T(128)}, u32[]{:S(2)}) copy-start(s32[32]{0:T(128)} %param.22) | copy-start | bytes 388
  11.1 0.7 %copy-start.10 = (s32[32]{0:T(128)S(1)}, s32[32]{0:T(128)}, u32[]{:S(2)}) copy-start(s32[32]{0:T(128)} %param.21) | copy-start | bytes 388
  11.1 0.7 %copy-start.11 = (s32[32]{0:T(128)S(1)}, s32[32]{0:T(128)}, u32[]{:S(2)}) copy-start(s32[32]{0:T(128)} %param.33) | copy-start | bytes 388
  11.1 1.3 %copy-start.5 = (bf16[1024]{0:T(1024)(128)(2,1)S(1)}, bf16[1024]{0:T(1024)(128)(2,1)}, u32[]{:S(2)}) copy-start(bf16[1024]{0:T(1024)(128)(2,1)} %param.30) | copy-start | bytes 6148
  11.1 1.3 %copy-start.6 = (bf16[512]{0:T(512)(128)(2,1)S(1)}, bf16[512]{0:T(512)(128)(2,1)}, u32[]{:S(2)}) copy-start(bf16[512]{0:T(512)(128)(2,1)} %param.32) | copy-start | bytes 3076
  11.1 1.3 %copy-start.7 = (bf16[512]{0:T(512)(128)(2,1)S(1)}, bf16[512]{0:T(512)(128)(2,1)}, u32[]{:S(2)}) copy-start(bf16[512]{0:T(512)(128)(2,1)} %param.28) | copy-start | bytes 3076
  11.2 1.3 %copy-start.8 = (bf16[512]{0:T(512)(128)(2,1)S(1)}, bf16[512]{0:T(512)(128)(2,1)}, u32[]{:S(2)}) copy-start(bf16[512]{0:T(512)(128)(2,1)} %param.27) | copy-start | bytes 3076
  11.2 1.3 %copy-start.9 = (bf16[512]{0:T(512)(128)(2,1)S(1)}, bf16[512]{0:T(512)(128)(2,1)}, u32[]{:S(2)}) copy-start(bf16[512]{0:T(512)(128)(2,1)} %param.26) | copy-start | bytes 3076
  13.8 14.1 %copy-start.1 = (bf16[1024,512]{1,0:T(8,128)(2,1)S(1)}, bf16[1024,512]{1,0:T(8,128)(2,1)}, u32[]{:S(2)}) copy-start(bf16[1024,512]{1,0:T(8,128)(2,1)} %weight.4) | copy-start | bytes 3145732
  15.5 18.2 %copy-start = (bf16[1024,512]{1,0:T(8,128)(2,1)S(1)}, bf16[1024,512]{1,0:T(8,128)(2,1)}, u32[]{:S(2)}) copy-start(bf16[1024,512]{1,0:T(8,128)(2,1)} %weight.5) | copy-start | bytes 3145732
  15.5 3.4 %collective-permute-start.2 = (bf16[4,2048]{1,0:T(4,128)(2,1)S(1)}, bf16[4,2048]{1,0:T(4,128)(2,1)S(1)}, u32[]{:S(2)}, u32[]{:S(2)}) collective-permute-start(bf16[4,2048]{1,0:T(4,128)(2,1)S(1)} %get-tuple-element.16), channel_id=1, source_target_pairs={{0,3},{1,2},{2,1},{3,0},{4,7},{5,6},{6,5},{7,4},{8,11},{9,10},{10,... | collective-permute-start | bytes 49160 | tf_op jit(solution)/shard_map/ppermute | solution.py:338
  15.6 3.8 %collective-permute-start.1 = (bf16[4,2048]{1,0:T(4,128)(2,1)S(1)}, bf16[4,2048]{1,0:T(4,128)(2,1)S(1)}, u32[]{:S(2)}, u32[]{:S(2)}) collective-permute-start(bf16[4,2048]{1,0:T(4,128)(2,1)S(1)} %get-tuple-element.16), channel_id=1, source_target_pairs={{0,2},{1,3},{2,0},{3,1},{4,6},{5,7},{6,4},{7,5},{8,10},{9,11},{10,... | collective-permute-start | bytes 49160 | tf_op jit(solution)/shard_map/ppermute | solution.py:338
  17.2 2.3 %collective-permute-start = (bf16[4,2048]{1,0:T(4,128)(2,1)S(1)}, bf16[4,2048]{1,0:T(4,128)(2,1)S(1)}, u32[]{:S(2)}, u32[]{:S(2)}) collective-permute-start(bf16[4,2048]{1,0:T(4,128)(2,1)S(1)} %get-tuple-element.16), channel_id=1, source_target_pairs={{0,1},{1,0},{2,3},{3,2},{4,5},{5,4},{6,7},{7,6},{8,9},{9,8},{10,11... | collective-permute-start | bytes 49160 | tf_op jit(solution)/shard_map/ppermute | solution.py:338
  28.3 1.3 %collective-permute-start.3 = (bf16[32,1024]{1,0:T(8,128)(2,1)S(1)}, bf16[32,1024]{1,0:T(8,128)(2,1)S(1)}, u32[]{:S(2)}, u32[]{:S(2)}) collective-permute-start(bf16[32,1024]{1,0:T(8,128)(2,1)S(1)} %shard_map.167), channel_id=1, source_target_pairs={{0,1},{1,0},{2,3},{3,2},{4,5},{5,4},{6,7},{7,6},{8,9},{9,8},{10,11... | collective-permute-start | bytes 196616 | tf_op jit(solution)/shard_map/ppermute | solution.py:338
  29.6 4.1 %collective-permute-start.4 = (bf16[32,1024]{1,0:T(8,128)(2,1)S(1)}, bf16[32,1024]{1,0:T(8,128)(2,1)S(1)}, u32[]{:S(2)}, u32[]{:S(2)}) collective-permute-start(bf16[32,1024]{1,0:T(8,128)(2,1)S(1)} %add_convert_fusion.near), channel_id=1, source_target_pairs={{0,3},{1,2},{2,1},{3,0},{4,7},{5,6},{6,5},{7,4},{8,11},{9,10},{10,... | collective-permute-start | bytes 196616 | tf_op jit(solution)/shard_map/ppermute | solution.py:338

commit v20 on v19

--- a/solution.py
+++ b/solution.py
@@ -20,7 +20,7 @@
 
 FIRST_ORDER = [3, 5, 2, 4, 1, 7, 0, 6]
 MIDDLE_ORDER = [3, 4, 1, 6, 2, 5, 0, 7]
-LAST_ORDER = [4, 3, 5, 2, 6, 1, 7, 0]
+LAST_ORDER = [7, 6, 5, 4, 3, 2, 1, 0]
 
 
 def pick_from(order, place):
@@ -86,7 +86,7 @@
         out[at, fields:, :] = block[:, cols // 2 :]
 
 
-def index_kernel(place, numbers, pick, valid, arrange, arrange_own, *, page_len):
+def index_kernel(place, numbers, pick, valid, arrange, arrange_own, *, page_len, heads):
     owner, order, lengths = (numbers[i : i + 1, :] for i in range(3))
     table = numbers[8:, :]
     me = place[0:1, 0:1]
@@ -109,7 +109,8 @@
     source = pick_from(FIRST_ORDER, iota((count, shape[1]), 1) // (2 * rows))
     came = hot(iota((count, shape[1]), 0) // rows == source)
     from_there = onto_mxu(mine, came)
-    pick[...] = hot((from_there > 0.5) & (down_p // rows == across_p % rows))
+    field = jnp.minimum(down_p // (heads * rows), 3)
+    pick[...] = hot((from_there > 0.5) & (field == across_p % rows))
 
     shape = valid.shape
     slot = iota((shape[0], count), 0) % rows
@@ -147,16 +148,14 @@
     own = jnp.concatenate(
         [onto_mxu(jnp.where(which == i, chosen, 0.0).astype(BF16), came) for i in range(2)], axis=1
     )
-    query, key, value, resid = (own[i * rows : (i + 1) * rows] for i in range(4))
-
-    def tile(x):
-        return jnp.concatenate([x] * heads, axis=0)
-
-    shape = (heads * rows, cols)
+    each = heads * rows
+    query, key, value = (own[i * each : (i + 1) * each] for i in range(3))
+    resid = own[3 * each : 3 * each + rows]
+    shape = (each, cols)
     in_head = iota(shape, 0) // rows == iota(shape, 1) // HEAD_DIM
-    wide = jnp.where(in_head, tile(query), 0.0)
+    wide = jnp.where(in_head, query, 0.0)
     positions = valid.shape[1]
-    self_score = jnp.sum(wide * tile(key), axis=1, keepdims=True) * scale
+    self_score = jnp.sum(wide * key, axis=1, keepdims=True) * scale
     scores = nt_dot(wide.astype(BF16), pool[0].reshape(positions, cols)) * scale
     scores = jnp.where(valid[...] > 0.5, scores, -jnp.inf)
     top = jnp.maximum(jnp.max(scores, axis=1, keepdims=True), self_score)
@@ -164,7 +163,7 @@
     self_weight = jnp.exp(self_score - top)
     total = jnp.sum(weights, axis=1, keepdims=True) + self_weight
     numer = onto_mxu(weights.astype(BF16), pool[1].reshape(positions, cols))
-    numer = numer + self_weight.astype(BF16).astype(F32) * tile(value)
+    numer = numer + self_weight.astype(BF16).astype(F32) * value
     numer = jnp.where(in_head, numer / total, 0.0)
     attn = sum(numer[i * rows : (i + 1) * rows] for i in range(heads))
     attn = jnp.concatenate([attn, jnp.zeros_like(attn)], axis=0).astype(BF16)
@@ -285,7 +284,7 @@
     pick, valid, arrange, arrange_own = call(
         index_kernel,
         [
-            arr((4 * rows, 2 * count)),
+            arr((3 * heads * rows + 2 * rows, 2 * count)),
             arr((heads * rows, positions), F32),
             arr((count, count)),
             arr((count, rows)),
@@ -293,6 +292,7 @@
         [VMEM, VMEM],
         [place, numbers],
         page_len=page_len,
+        heads=heads,
     )
 
     here = position[0] >= 0

time: 44.2 us -> 43.5 us (0.984)
  blocking collectives: 17.4 us -> 16.7 us
    all_to_all x2, blocking collectives: 17.4 us -> 16.7 us  [trade(): lax.all_to_all(blocks, 'req', 0, 0, tiled=True, axis_index_groups=[group])]
where the time goes in v20:
time: 43.5 us; the launch traced here: 43.1 us
  blocking collectives  16.7 us (38%)
  starting transfers between devices  11.1 us (26%)
  waiting for transfers between devices  7.32 us (17%)
  Pallas kernels  5.33 us (12%)
  other arithmetic  1.67 us (4%)
  local copies, waits for them, and re-layouts  0.84 us (2%)
    all_to_all x2, blocking collectives, trade(): lax.all_to_all(blocks, 'req', 0, 0, tiled=True, axis_index_groups=[group])  16.7 us
    all_to_all x1, starting transfers between devices, trade(): lax.all_to_all(blocks, 'req', 0, 0, tiled=True, axis_index_groups=[group])  7.85 us
    ppermute x5, waiting for transfers between devices, swap(): return lax.ppermute(x, axis, [(i, i ^ step) for i in range(n)])  6.02 us
    pallas_call x7, Pallas kernels, call(): pl.pallas_call(functools.partial(kernel, **fixed) if fixed else kernel, o...  5.33 us
    ppermute x5, starting transfers between devices, swap(): return lax.ppermute(x, axis, [(i, i ^ step) for i in range(n)])  3.25 us
    select_n x1, other arithmetic, on_pairs(): upper = jnp.where(here, upper, jnp.zeros_like(upper))  1.39 us
    all_to_all x1, waiting for transfers between devices, trade(): lax.all_to_all(blocks, 'req', 0, 0, tiled=True, axis_index_groups=[group])  1.3 us
  transfers between devices with their start and end apart: 6, of which 5 were waited for; matrix products, arithmetic and copies ran while one was open for 4% of the time, Pallas kernels for 1%

profile of v20, /device:TPU:0, one launch (start us, length us, event | category | flops | bytes accessed | tf_op | source)
XLA Modules:
  0.0 43.1 jit_solution(14068387241144084036)
XLA Ops:
  0.0 1.6 %shard_map.163 = bf16[8,8,256]{2,1,0:T(8,128)(2,1)} custom-call(s32[1,32]{1,0:T(1,128)} %bitcast.7, bf16[4,512]{1,0:T(4,128)(2,1)} %query.1, bf16[4,512]{1,0:T(4,128)(2,1)} %key.1, bf16[4,512]{1,0:T(4,128)(2,1)} %value.1, bf16[4,512]{1,0:T(4,128)(2,1)} %resid.1), custom_call_target="tpu_custom_call" | custom-call | bytes 16512 | tf_op jit(solution)/shard_map/pallas_call | solution.py:221
  1.6 7.9 %all-to-all-start = ((bf16[8,8,256]{2,1,0:T(8,128)(2,1)}), bf16[8,8,256]{2,1,0:T(8,128)(2,1)S(1)}, u32[]{:S(2)}, u32[]{:S(2)}) async-start(bf16[8,8,256]{2,1,0:T(8,128)(2,1)} %shard_map.163), calls=%async_computation | async-start | bytes 65536 | tf_op jit(solution)/shard_map/all_to_all | solution.py:233
  9.4 0.1 pad.60
  9.5 1.4 %slice_select_fusion.upper = bf16[256,2048]{1,0:T(8,128)(2,1)S(1)} fusion(bf16[512,2048]{1,0:T(8,128)(2,1)} %weight.3, pred[]{:T(512)S(6)} %ge.3), kind=kLoop, calls=%fused_computation.1 | loop fusion | flops 524288 | bytes 2097153 | tf_op jit(solution)/shard_map/jit(_where)/select_n | solution.py:301
  10.9 0.2 copy-done.2
  11.1 0.0 copy-start.5
  11.1 0.0 copy-start.6
  11.1 0.0 copy-start.7
  11.2 0.0 copy-start.9
  11.2 0.1 broadcast_select_fusion.pool
  11.3 0.1 pad_add_fusion.1
  11.4 0.4 %copy-done.3 = s32[32,16]{0,1:T(8,128)S(1)} copy-done((s32[32,16]{0,1:T(8,128)S(1)}, s32[32,16]{0,1:T(8,128)}, u32[]{:S(2)}) %copy-start.3) | copy-done | bytes 2072
  11.8 0.1 pad_add_fusion.numbers
  11.9 0.1 broadcast_in_dim.25.place
  12.0 0.4 shard_map.164
  12.5 1.3 %all-to-all-done.arrived = bf16[8,8,256]{2,1,0:T(8,128)(2,1)S(1)} async-done(((bf16[8,8,256]{2,1,0:T(8,128)(2,1)}), bf16[8,8,256]{2,1,0:T(8,128)(2,1)S(1)}, u32[]{:S(2)}, u32[]{:S(2)}) %all-to-all-start) | async-done | bytes 32800 | tf_op jit(solution)/shard_map/all_to_all | solution.py:233
  13.8 1.8 %shard_map.165 = (f32[4,2048]{1,0:T(4,128)S(1)}, bf16[4,2048]{1,0:T(4,128)(2,1)S(1)}) custom-call(s32[2,128]{1,0:T(2,128)S(1)} %broadcast_in_dim.25.place, bf16[8,8,256]{2,1,0:T(8,128)(2,1)S(1)} %all-to-all-done.arrived, bf16[56,64]{1,0:T(8,128)(2,1)S(1)} %get-tuple-element.13.pick, f32[16,704]{1,0:T(8,128)S(1)} %get-tuple-element.14.valid, ...), custom_call_target="tpu_custom_call" | custom-call | bytes 4685824 | tf_op jit(solution)/shard_map/pallas_call | solution.py:221
  15.6 0.1 collective-permute-start.2
  15.6 1.6 %collective-permute-start.1 = (bf16[4,2048]{1,0:T(4,128)(2,1)S(1)}, bf16[4,2048]{1,0:T(4,128)(2,1)S(1)}, u32[]{:S(2)}, u32[]{:S(2)}) collective-permute-start(bf16[4,2048]{1,0:T(4,128)(2,1)S(1)} %get-tuple-element.16), channel_id=1, source_target_pairs={{0,2},{1,3},{2,0},{3,1},{4,6},{5,7},{6,4},{7,5},{8,10},{9,11},{10,... | collective-permute-start | bytes 49160 | tf_op jit(solution)/shard_map/ppermute | solution.py:338
  17.2 0.3 collective-permute-start
  17.5 1.4 %collective-permute-done.2.far_sibling = bf16[4,2048]{1,0:T(4,128)(2,1)S(1)} collective-permute-done((bf16[4,2048]{1,0:T(4,128)(2,1)S(1)}, bf16[4,2048]{1,0:T(4,128)(2,1)S(1)}, u32[]{:S(2)}, u32[]{:S(2)}) %collective-permute-start.2) | collective-permute-done | bytes 16416 | tf_op jit(solution)/shard_map/ppermute | solution.py:338
  18.9 0.5 %collective-permute-done.1.far = bf16[4,2048]{1,0:T(4,128)(2,1)S(1)} collective-permute-done((bf16[4,2048]{1,0:T(4,128)(2,1)S(1)}, bf16[4,2048]{1,0:T(4,128)(2,1)S(1)}, u32[]{:S(2)}, u32[]{:S(2)}) %collective-permute-start.1) | collective-permute-done | bytes 16416 | tf_op jit(solution)/shard_map/ppermute | solution.py:338
  19.4 0.2 shard_map.166
  19.6 8.2 %all_to_all.15.rows_in = bf16[8,4,512]{2,1,0:T(4,128)(2,1)S(1)} all-to-all(bf16[8,4,512]{2,1,0:T(4,128)(2,1)S(1)} %get-tuple-element.17), channel_id=1, replica_groups={{12,16,4,24,8,20,0,28},{13,17,5,25,9,21,1,29},{14,18,6,26,10,22,2,30},{..., dimensions={0} | all-to-all | bytes 65536 | tf_op jit(solution)/shard_map/all_to_all | solution.py:233
  27.9 0.5 %shard_map.167 = bf16[32,1024]{1,0:T(8,128)(2,1)S(1)} custom-call(bf16[8,4,512]{2,1,0:T(4,128)(2,1)S(1)} %all_to_all.15.rows_in, bf16[32,32]{1,0:T(8,128)(2,1)S(1)} %get-tuple-element.18.arrange, bf16[1024,512]{1,0:T(8,128)(2,1)S(1)} %copy-done.1), custom_call_target="tpu_custom_call" | custom-call | bytes 1083392 | tf_op jit(solution)/shard_map/pallas_call | solution.py:221
  28.3 0.0 collective-permute-start.3
  28.3 1.2 %collective-permute-done.3 = bf16[32,1024]{1,0:T(8,128)(2,1)S(1)} collective-permute-done((bf16[32,1024]{1,0:T(8,128)(2,1)S(1)}, bf16[32,1024]{1,0:T(8,128)(2,1)S(1)}, u32[]{:S(2)}, u32[]{:S(2)}) %collective-permute-start.3) | collective-permute-done | bytes 65568 | tf_op jit(solution)/shard_map/ppermute | solution.py:338
  29.6 1.3 %collective-permute-start.4 = (bf16[32,1024]{1,0:T(8,128)(2,1)S(1)}, bf16[32,1024]{1,0:T(8,128)(2,1)S(1)}, u32[]{:S(2)}, u32[]{:S(2)}) collective-permute-start(bf16[32,1024]{1,0:T(8,128)(2,1)S(1)} %add_convert_fusion.near), channel_id=1, source_target_pairs={{0,3},{1,2},{2,1},{3,0},{4,7},{5,6},{6,5},{7,4},{8,11},{9,10},{10,... | collective-permute-start | bytes 196616 | tf_op jit(solution)/shard_map/ppermute | solution.py:338
  30.9 2.8 %collective-permute-done.4.far = bf16[32,1024]{1,0:T(8,128)(2,1)S(1)} collective-permute-done((bf16[32,1024]{1,0:T(8,128)(2,1)S(1)}, bf16[32,1024]{1,0:T(8,128)(2,1)S(1)}, u32[]{:S(2)}, u32[]{:S(2)}) %collective-permute-start.4) | collective-permute-done | bytes 65568 | tf_op jit(solution)/shard_map/ppermute | solution.py:338
  33.7 0.3 shard_map.168
  34.0 8.5 %all_to_all.16.pieces = bf16[8,4,512]{2,1,0:T(4,128)(2,1)S(1)} all-to-all(bf16[8,4,512]{2,1,0:T(4,128)(2,1)S(1)} %shard_map.168), channel_id=1, replica_groups={{28,24,20,16,12,8,4,0},{29,25,21,17,13,9,5,1},{30,26,22,18,14,10,6,2},{..., dimensions={0} | all-to-all | bytes 65536 | tf_op jit(solution)/shard_map/all_to_all | solution.py:233
  42.5 0.6 %shard_map.169 = bf16[4,512]{1,0:T(4,128)(2,1)} custom-call(bf16[8,4,512]{2,1,0:T(4,128)(2,1)S(1)} %all_to_all.16.pieces, f32[3072]{0:T(1024)S(1)} %convert_add_fusion.vectors), custom_call_target="tpu_custom_call" | custom-call | bytes 45056 | tf_op jit(solution)/shard_map/pallas_call | solution.py:221
  (22 shorter events, 0.1 us)
Async XLA Ops:
  1.6 12.2 %all-to-all-start = ((bf16[8,8,256]{2,1,0:T(8,128)(2,1)}), bf16[8,8,256]{2,1,0:T(8,128)(2,1)S(1)}, u32[]{:S(2)}, u32[]{:S(2)}) async-start(bf16[8,8,256]{2,1,0:T(8,128)(2,1)} %shard_map.163), calls=%async_computation | async-start | bytes 65536 | tf_op jit(solution)/shard_map/all_to_all | solution.py:233
  9.4 1.7 %copy-start.2 = (bf16[2,22,32,512]{3,2,1,0:T(8,128)(2,1)S(1)}, bf16[2,22,32,512]{3,2,1,0:T(8,128)(2,1)}, u32[]{:S(2)}) copy-start(bf16[2,22,32,512]{3,2,1,0:T(8,128)(2,1)} %param.24) | copy-start | bytes 4325380
  11.1 0.7 %copy-start.3 = (s32[32,16]{0,1:T(8,128)S(1)}, s32[32,16]{0,1:T(8,128)}, u32[]{:S(2)}) copy-start(s32[32,16]{0,1:T(8,128)} %param.23) | copy-start | bytes 6148
  11.1 0.7 %copy-start.4 = (s32[32]{0:T(128)S(1)}, s32[32]{0:T(128)}, u32[]{:S(2)}) copy-start(s32[32]{0:T(128)} %param.22) | copy-start | bytes 388
  11.1 0.7 %copy-start.10 = (s32[32]{0:T(128)S(1)}, s32[32]{0:T(128)}, u32[]{:S(2)}) copy-start(s32[32]{0:T(128)} %param.21) | copy-start | bytes 388
  11.1 0.7 %copy-start.11 = (s32[32]{0:T(128)S(1)}, s32[32]{0:T(128)}, u32[]{:S(2)}) copy-start(s32[32]{0:T(128)} %param.33) | copy-start | bytes 388
  11.1 1.3 %copy-start.5 = (bf16[1024]{0:T(1024)(128)(2,1)S(1)}, bf16[1024]{0:T(1024)(128)(2,1)}, u32[]{:S(2)}) copy-start(bf16[1024]{0:T(1024)(128)(2,1)} %param.30) | copy-start | bytes 6148
  11.1 1.3 %copy-start.6 = (bf16[512]{0:T(512)(128)(2,1)S(1)}, bf16[512]{0:T(512)(128)(2,1)}, u32[]{:S(2)}) copy-start(bf16[512]{0:T(512)(128)(2,1)} %param.32) | copy-start | bytes 3076
  11.1 1.3 %copy-start.7 = (bf16[512]{0:T(512)(128)(2,1)S(1)}, bf16[512]{0:T(512)(128)(2,1)}, u32[]{:S(2)}) copy-start(bf16[512]{0:T(512)(128)(2,1)} %param.28) | copy-start | bytes 3076
  11.2 1.3 %copy-start.8 = (bf16[512]{0:T(512)(128)(2,1)S(1)}, bf16[512]{0:T(512)(128)(2,1)}, u32[]{:S(2)}) copy-start(bf16[512]{0:T(512)(128)(2,1)} %param.27) | copy-start | bytes 3076
  11.2 1.3 %copy-start.9 = (bf16[512]{0:T(512)(128)(2,1)S(1)}, bf16[512]{0:T(512)(128)(2,1)}, u32[]{:S(2)}) copy-start(bf16[512]{0:T(512)(128)(2,1)} %param.26) | copy-start | bytes 3076
  13.8 14.1 %copy-start.1 = (bf16[1024,512]{1,0:T(8,128)(2,1)S(1)}, bf16[1024,512]{1,0:T(8,128)(2,1)}, u32[]{:S(2)}) copy-start(bf16[1024,512]{1,0:T(8,128)(2,1)} %weight.4) | copy-start | bytes 3145732
  15.5 18.2 %copy-start = (bf16[1024,512]{1,0:T(8,128)(2,1)S(1)}, bf16[1024,512]{1,0:T(8,128)(2,1)}, u32[]{:S(2)}) copy-start(bf16[1024,512]{1,0:T(8,128)(2,1)} %weight.5) | copy-start | bytes 3145732
  15.6 3.4 %collective-permute-start.2 = (bf16[4,2048]{1,0:T(4,128)(2,1)S(1)}, bf16[4,2048]{1,0:T(4,128)(2,1)S(1)}, u32[]{:S(2)}, u32[]{:S(2)}) collective-permute-start(bf16[4,2048]{1,0:T(4,128)(2,1)S(1)} %get-tuple-element.16), channel_id=1, source_target_pairs={{0,3},{1,2},{2,1},{3,0},{4,7},{5,6},{6,5},{7,4},{8,11},{9,10},{10,... | collective-permute-start | bytes 49160 | tf_op jit(solution)/shard_map/ppermute | solution.py:338
  15.6 3.8 %collective-permute-start.1 = (bf16[4,2048]{1,0:T(4,128)(2,1)S(1)}, bf16[4,2048]{1,0:T(4,128)(2,1)S(1)}, u32[]{:S(2)}, u32[]{:S(2)}) collective-permute-start(bf16[4,2048]{1,0:T(4,128)(2,1)S(1)} %get-tuple-element.16), channel_id=1, source_target_pairs={{0,2},{1,3},{2,0},{3,1},{4,6},{5,7},{6,4},{7,5},{8,10},{9,11},{10,... | collective-permute-start | bytes 49160 | tf_op jit(solution)/shard_map/ppermute | solution.py:338
  17.2 2.3 %collective-permute-start = (bf16[4,2048]{1,0:T(4,128)(2,1)S(1)}, bf16[4,2048]{1,0:T(4,128)(2,1)S(1)}, u32[]{:S(2)}, u32[]{:S(2)}) collective-permute-start(bf16[4,2048]{1,0:T(4,128)(2,1)S(1)} %get-tuple-element.16), channel_id=1, source_target_pairs={{0,1},{1,0},{2,3},{3,2},{4,5},{5,4},{6,7},{7,6},{8,9},{9,8},{10,11... | collective-permute-start | bytes 49160 | tf_op jit(solution)/shard_map/ppermute | solution.py:338
  28.3 1.3 %collective-permute-start.3 = (bf16[32,1024]{1,0:T(8,128)(2,1)S(1)}, bf16[32,1024]{1,0:T(8,128)(2,1)S(1)}, u32[]{:S(2)}, u32[]{:S(2)}) collective-permute-start(bf16[32,1024]{1,0:T(8,128)(2,1)S(1)} %shard_map.167), channel_id=1, source_target_pairs={{0,1},{1,0},{2,3},{3,2},{4,5},{5,4},{6,7},{7,6},{8,9},{9,8},{10,11... | collective-permute-start | bytes 196616 | tf_op jit(solution)/shard_map/ppermute | solution.py:338
  29.6 4.1 %collective-permute-start.4 = (bf16[32,1024]{1,0:T(8,128)(2,1)S(1)}, bf16[32,1024]{1,0:T(8,128)(2,1)S(1)}, u32[]{:S(2)}, u32[]{:S(2)}) collective-permute-start(bf16[32,1024]{1,0:T(8,128)(2,1)S(1)} %add_convert_fusion.near), channel_id=1, source_target_pairs={{0,3},{1,2},{2,1},{3,0},{4,7},{5,6},{6,5},{7,4},{8,11},{9,10},{10,... | collective-permute-start | bytes 196616 | tf_op jit(solution)/shard_map/ppermute | solution.py:338

commit v21 on v20

--- a/solution.py
+++ b/solution.py
@@ -12,14 +12,14 @@
 NORM_EPS = 1e-05
 PAIRWISE = 16
 REQ, TP = 8, 4
-ATTENTION_ROOM = 51.2
+ATTENTION_ROOM = 50.6
 ALL_ROOM = 58
 F32, BF16, I32 = jnp.float32, jnp.bfloat16, jnp.int32
 VMEM = pl.BlockSpec(memory_space=pltpu.VMEM)
 HBM = pl.BlockSpec(memory_space=pltpu.HBM)
 
-FIRST_ORDER = [3, 5, 2, 4, 1, 7, 0, 6]
-MIDDLE_ORDER = [3, 4, 1, 6, 2, 5, 0, 7]
+FIRST_ORDER = [2, 4, 0, 6, 3, 5, 1, 7]
+MIDDLE_ORDER = [1, 4, 3, 6, 0, 5, 2, 7]
 LAST_ORDER = [7, 6, 5, 4, 3, 2, 1, 0]
 
 
@@ -136,7 +136,7 @@
     place, arrived, pick, valid, vectors, pool, upper, weight, partial, rounded, lower, sem, *, rows
 ):
     deep = upper.shape[0]
-    copy = pltpu.make_async_copy(weight.at[pl.ds(deep, deep)], lower, sem)
+    copy = pltpu.make_async_copy(weight.at[pl.ds(deep, lower.shape[0])], lower, sem)
     copy.start()
     half = arrived.shape[2]
     cols = 2 * half
@@ -297,7 +297,7 @@
 
     here = position[0] >= 0
     pool = jnp.where(here, kv_pool, jnp.zeros_like(kv_pool))
-    upper = out_weight[: cols // 2]
+    upper = out_weight[: 3 * cols // 4]
     upper = jnp.where(here, upper, jnp.zeros_like(upper))
 
     partial, rounded = call(
@@ -305,7 +305,7 @@
         [arr((rows, width), F32), arr((rows, width))],
         [VMEM] * 7 + [HBM],
         [place, arrived, pick, valid, vectors, pool, upper, out_weight],
-        [pltpu.VMEM(upper.shape, BF16), pltpu.SemaphoreType.DMA],
+        [pltpu.VMEM((cols - upper.shape[0], width), BF16), pltpu.SemaphoreType.DMA],
         room=ATTENTION_ROOM,
         rows=rows,
     )

time: 43.5 us -> 45.3 us (1.041)
  blocking collectives: 16.7 us -> 17.9 us
    select_n x1, other arithmetic: 0.1 us -> 1.59 us  [on_pairs(): pool = jnp.where(here, kv_pool, jnp.zeros_like(kv_pool))]
    select_n x1, other arithmetic: 1.39 us -> 0.11 us  [on_pairs(): upper = jnp.where(here, upper, jnp.zeros_like(upper))]
    all_to_all x2, blocking collectives: 16.7 us -> 17.9 us  [trade(): lax.all_to_all(blocks, 'req', 0, 0, tiled=True, axis_index_groups=[group])]
where the time goes in v21:
time: 45.3 us; the launch traced here: 44.9 us
  blocking collectives  17.9 us (40%)
  starting transfers between devices  11.1 us (25%)
  waiting for transfers between devices  7.74 us (17%)
  Pallas kernels  5.17 us (11%)
  other arithmetic  1.88 us (4%)
  local copies, waits for them, and re-layouts  0.98 us (2%)
    all_to_all x2, blocking collectives, trade(): lax.all_to_all(blocks, 'req', 0, 0, tiled=True, axis_index_groups=[group])  17.9 us
    all_to_all x1, starting transfers between devices, trade(): lax.all_to_all(blocks, 'req', 0, 0, tiled=True, axis_index_groups=[group])  7.85 us
    ppermute x5, waiting for transfers between devices, swap(): return lax.ppermute(x, axis, [(i, i ^ step) for i in range(n)])  6.02 us
    pallas_call x7, Pallas kernels, call(): pl.pallas_call(functools.partial(kernel, **fixed) if fixed else kernel, o...  5.17 us
    ppermute x5, starting transfers between devices, swap(): return lax.ppermute(x, axis, [(i, i ^ step) for i in range(n)])  3.25 us
    all_to_all x1, waiting for transfers between devices, trade(): lax.all_to_all(blocks, 'req', 0, 0, tiled=True, axis_index_groups=[group])  1.73 us
    select_n x1, other arithmetic, on_pairs(): pool = jnp.where(here, kv_pool, jnp.zeros_like(kv_pool))  1.59 us
  transfers between devices with their start and end apart: 6, of which 5 were waited for; matrix products, arithmetic and copies ran while one was open for 4% of the time, Pallas kernels for 1%

profile of v21, /device:TPU:0, one launch (start us, length us, event | category | flops | bytes accessed | tf_op | source)
XLA Modules:
  0.0 44.9 jit_solution(14808428847527868952)
XLA Ops:
  0.0 1.6 %shard_map.163 = bf16[8,8,256]{2,1,0:T(8,128)(2,1)} custom-call(s32[1,32]{1,0:T(1,128)} %bitcast.7, bf16[4,512]{1,0:T(4,128)(2,1)} %query.1, bf16[4,512]{1,0:T(4,128)(2,1)} %key.1, bf16[4,512]{1,0:T(4,128)(2,1)} %value.1, bf16[4,512]{1,0:T(4,128)(2,1)} %resid.1), custom_call_target="tpu_custom_call" | custom-call | bytes 16512 | tf_op jit(solution)/shard_map/pallas_call | solution.py:221
  1.6 7.9 %all-to-all-start = ((bf16[8,8,256]{2,1,0:T(8,128)(2,1)}), bf16[8,8,256]{2,1,0:T(8,128)(2,1)S(1)}, u32[]{:S(2)}, u32[]{:S(2)}) async-start(bf16[8,8,256]{2,1,0:T(8,128)(2,1)} %shard_map.163), calls=%async_computation | async-start | bytes 65536 | tf_op jit(solution)/shard_map/all_to_all | solution.py:233
  9.4 0.1 pad.60
  9.5 1.6 %broadcast_select_fusion.pool = bf16[2,22,32,512]{3,2,1,0:T(8,128)(2,1)S(1)} fusion(bf16[2,22,32,512]{3,2,1,0:T(8,128)(2,1)} %param.24, pred[]{:T(512)S(6)} %ge.3), kind=kLoop, calls=%fused_computation.1 | loop fusion | flops 720896 | bytes 2883585 | tf_op jit(solution)/shard_map/jit(_where)/select_n | solution.py:299
  11.1 0.3 copy-done.2
  11.5 0.0 copy-start.5
  11.5 0.0 copy-start.7
  11.5 0.0 copy-start.8
  11.5 0.1 slice_select_fusion.upper
  11.6 0.1 pad_add_fusion.1
  11.7 0.4 copy-done.3
  12.2 0.1 pad_add_fusion.numbers
  12.2 0.1 broadcast_in_dim.25.place
  12.3 0.4 shard_map.164
  12.8 1.7 %all-to-all-done.arrived = bf16[8,8,256]{2,1,0:T(8,128)(2,1)S(1)} async-done(((bf16[8,8,256]{2,1,0:T(8,128)(2,1)}), bf16[8,8,256]{2,1,0:T(8,128)(2,1)S(1)}, u32[]{:S(2)}, u32[]{:S(2)}) %all-to-all-start) | async-done | bytes 32800 | tf_op jit(solution)/shard_map/all_to_all | solution.py:233
  14.5 1.6 %shard_map.165 = (f32[4,2048]{1,0:T(4,128)S(1)}, bf16[4,2048]{1,0:T(4,128)(2,1)S(1)}) custom-call(s32[2,128]{1,0:T(2,128)S(1)} %broadcast_in_dim.25.place, bf16[8,8,256]{2,1,0:T(8,128)(2,1)S(1)} %all-to-all-done.arrived, bf16[56,64]{1,0:T(8,128)(2,1)S(1)} %get-tuple-element.13.pick, f32[16,704]{1,0:T(8,128)S(1)} %get-tuple-element.14.valid, ...), custom_call_target="tpu_custom_call" | custom-call | bytes 5210112 | tf_op jit(solution)/shard_map/pallas_call | solution.py:221
  16.1 0.0 copy-start
  16.2 0.1 collective-permute-start.2
  16.2 1.6 %collective-permute-start.1 = (bf16[4,2048]{1,0:T(4,128)(2,1)S(1)}, bf16[4,2048]{1,0:T(4,128)(2,1)S(1)}, u32[]{:S(2)}, u32[]{:S(2)}) collective-permute-start(bf16[4,2048]{1,0:T(4,128)(2,1)S(1)} %get-tuple-element.16), channel_id=1, source_target_pairs={{0,2},{1,3},{2,0},{3,1},{4,6},{5,7},{6,4},{7,5},{8,10},{9,11},{10,... | collective-permute-start | bytes 49160 | tf_op jit(solution)/shard_map/ppermute | solution.py:338
  17.8 0.3 collective-permute-start
  18.1 1.4 %collective-permute-done.2.far_sibling = bf16[4,2048]{1,0:T(4,128)(2,1)S(1)} collective-permute-done((bf16[4,2048]{1,0:T(4,128)(2,1)S(1)}, bf16[4,2048]{1,0:T(4,128)(2,1)S(1)}, u32[]{:S(2)}, u32[]{:S(2)}) %collective-permute-start.2) | collective-permute-done | bytes 16416 | tf_op jit(solution)/shard_map/ppermute | solution.py:338
  19.5 0.5 %collective-permute-done.1.far = bf16[4,2048]{1,0:T(4,128)(2,1)S(1)} collective-permute-done((bf16[4,2048]{1,0:T(4,128)(2,1)S(1)}, bf16[4,2048]{1,0:T(4,128)(2,1)S(1)}, u32[]{:S(2)}, u32[]{:S(2)}) %collective-permute-start.1) | collective-permute-done | bytes 16416 | tf_op jit(solution)/shard_map/ppermute | solution.py:338
  20.0 0.2 shard_map.166
  20.3 9.4 %all_to_all.15.rows_in = bf16[8,4,512]{2,1,0:T(4,128)(2,1)S(1)} all-to-all(bf16[8,4,512]{2,1,0:T(4,128)(2,1)S(1)} %get-tuple-element.17), channel_id=1, replica_groups={{4,16,12,24,0,20,8,28},{5,17,13,25,1,21,9,29},{6,18,14,26,2,22,10,30},{..., dimensions={0} | all-to-all | bytes 65536 | tf_op jit(solution)/shard_map/all_to_all | solution.py:233
  29.7 0.5 %shard_map.167 = bf16[32,1024]{1,0:T(8,128)(2,1)S(1)} custom-call(bf16[8,4,512]{2,1,0:T(4,128)(2,1)S(1)} %all_to_all.15.rows_in, bf16[32,32]{1,0:T(8,128)(2,1)S(1)} %get-tuple-element.18.arrange, bf16[1024,512]{1,0:T(8,128)(2,1)S(1)} %copy-done.1), custom_call_target="tpu_custom_call" | custom-call | bytes 1083392 | tf_op jit(solution)/shard_map/pallas_call | solution.py:221
  30.1 0.0 collective-permute-start.3
  30.2 1.2 %collective-permute-done.3 = bf16[32,1024]{1,0:T(8,128)(2,1)S(1)} collective-permute-done((bf16[32,1024]{1,0:T(8,128)(2,1)S(1)}, bf16[32,1024]{1,0:T(8,128)(2,1)S(1)}, u32[]{:S(2)}, u32[]{:S(2)}) %collective-permute-start.3) | collective-permute-done | bytes 65568 | tf_op jit(solution)/shard_map/ppermute | solution.py:338
  31.4 1.3 %collective-permute-start.4 = (bf16[32,1024]{1,0:T(8,128)(2,1)S(1)}, bf16[32,1024]{1,0:T(8,128)(2,1)S(1)}, u32[]{:S(2)}, u32[]{:S(2)}) collective-permute-start(bf16[32,1024]{1,0:T(8,128)(2,1)S(1)} %add_convert_fusion.near), channel_id=1, source_target_pairs={{0,3},{1,2},{2,1},{3,0},{4,7},{5,6},{6,5},{7,4},{8,11},{9,10},{10,... | collective-permute-start | bytes 196616 | tf_op jit(solution)/shard_map/ppermute | solution.py:338
  32.7 2.8 %collective-permute-done.4.far = bf16[32,1024]{1,0:T(8,128)(2,1)S(1)} collective-permute-done((bf16[32,1024]{1,0:T(8,128)(2,1)S(1)}, bf16[32,1024]{1,0:T(8,128)(2,1)S(1)}, u32[]{:S(2)}, u32[]{:S(2)}) %collective-permute-start.4) | collective-permute-done | bytes 65568 | tf_op jit(solution)/shard_map/ppermute | solution.py:338
  35.5 0.3 shard_map.168
  35.8 8.5 %all_to_all.16.pieces = bf16[8,4,512]{2,1,0:T(4,128)(2,1)S(1)} all-to-all(bf16[8,4,512]{2,1,0:T(4,128)(2,1)S(1)} %shard_map.168), channel_id=1, replica_groups={{28,24,20,16,12,8,4,0},{29,25,21,17,13,9,5,1},{30,26,22,18,14,10,6,2},{..., dimensions={0} | all-to-all | bytes 65536 | tf_op jit(solution)/shard_map/all_to_all | solution.py:233
  44.3 0.6 %shard_map.169 = bf16[4,512]{1,0:T(4,128)(2,1)} custom-call(bf16[8,4,512]{2,1,0:T(4,128)(2,1)S(1)} %all_to_all.16.pieces, f32[3072]{0:T(1024)S(1)} %convert_add_fusion.vectors), custom_call_target="tpu_custom_call" | custom-call | bytes 45056 | tf_op jit(solution)/shard_map/pallas_call | solution.py:221
  (22 shorter events, 0.1 us)
Async XLA Ops:
  1.6 12.9 %all-to-all-start = ((bf16[8,8,256]{2,1,0:T(8,128)(2,1)}), bf16[8,8,256]{2,1,0:T(8,128)(2,1)S(1)}, u32[]{:S(2)}, u32[]{:S(2)}) async-start(bf16[8,8,256]{2,1,0:T(8,128)(2,1)} %shard_map.163), calls=%async_computation | async-start | bytes 65536 | tf_op jit(solution)/shard_map/all_to_all | solution.py:233
  9.4 2.0 %copy-start.2 = (bf16[512,2048]{1,0:T(8,128)(2,1)S(1)}, bf16[512,2048]{1,0:T(8,128)(2,1)}, u32[]{:S(2)}) copy-start(bf16[512,2048]{1,0:T(8,128)(2,1)} %weight.3) | copy-start | bytes 6291460
  11.5 0.7 %copy-start.3 = (s32[32,16]{0,1:T(8,128)S(1)}, s32[32,16]{0,1:T(8,128)}, u32[]{:S(2)}) copy-start(s32[32,16]{0,1:T(8,128)} %param.23) | copy-start | bytes 6148
  11.5 0.7 %copy-start.4 = (s32[32]{0:T(128)S(1)}, s32[32]{0:T(128)}, u32[]{:S(2)}) copy-start(s32[32]{0:T(128)} %param.22) | copy-start | bytes 388
  11.5 0.7 %copy-start.10 = (s32[32]{0:T(128)S(1)}, s32[32]{0:T(128)}, u32[]{:S(2)}) copy-start(s32[32]{0:T(128)} %param.21) | copy-start | bytes 388
  11.5 0.7 %copy-start.11 = (s32[32]{0:T(128)S(1)}, s32[32]{0:T(128)}, u32[]{:S(2)}) copy-start(s32[32]{0:T(128)} %param.33) | copy-start | bytes 388
  11.5 1.3 %copy-start.5 = (bf16[1024]{0:T(1024)(128)(2,1)S(1)}, bf16[1024]{0:T(1024)(128)(2,1)}, u32[]{:S(2)}) copy-start(bf16[1024]{0:T(1024)(128)(2,1)} %param.30) | copy-start | bytes 6148
  11.5 1.3 %copy-start.6 = (bf16[512]{0:T(512)(128)(2,1)S(1)}, bf16[512]{0:T(512)(128)(2,1)}, u32[]{:S(2)}) copy-start(bf16[512]{0:T(512)(128)(2,1)} %param.32) | copy-start | bytes 3076
  11.5 1.3 %copy-start.7 = (bf16[512]{0:T(512)(128)(2,1)S(1)}, bf16[512]{0:T(512)(128)(2,1)}, u32[]{:S(2)}) copy-start(bf16[512]{0:T(512)(128)(2,1)} %param.28) | copy-start | bytes 3076
  11.5 1.3 %copy-start.8 = (bf16[512]{0:T(512)(128)(2,1)S(1)}, bf16[512]{0:T(512)(128)(2,1)}, u32[]{:S(2)}) copy-start(bf16[512]{0:T(512)(128)(2,1)} %param.27) | copy-start | bytes 3076
  11.5 1.3 %copy-start.9 = (bf16[512]{0:T(512)(128)(2,1)S(1)}, bf16[512]{0:T(512)(128)(2,1)}, u32[]{:S(2)}) copy-start(bf16[512]{0:T(512)(128)(2,1)} %param.26) | copy-start | bytes 3076
  14.5 15.1 %copy-start.1 = (bf16[1024,512]{1,0:T(8,128)(2,1)S(1)}, bf16[1024,512]{1,0:T(8,128)(2,1)}, u32[]{:S(2)}) copy-start(bf16[1024,512]{1,0:T(8,128)(2,1)} %weight.4) | copy-start | bytes 3145732
  16.1 19.4 %copy-start = (bf16[1024,512]{1,0:T(8,128)(2,1)S(1)}, bf16[1024,512]{1,0:T(8,128)(2,1)}, u32[]{:S(2)}) copy-start(bf16[1024,512]{1,0:T(8,128)(2,1)} %weight.5) | copy-start | bytes 3145732
  16.2 3.4 %collective-permute-start.2 = (bf16[4,2048]{1,0:T(4,128)(2,1)S(1)}, bf16[4,2048]{1,0:T(4,128)(2,1)S(1)}, u32[]{:S(2)}, u32[]{:S(2)}) collective-permute-start(bf16[4,2048]{1,0:T(4,128)(2,1)S(1)} %get-tuple-element.16), channel_id=1, source_target_pairs={{0,3},{1,2},{2,1},{3,0},{4,7},{5,6},{6,5},{7,4},{8,11},{9,10},{10,... | collective-permute-start | bytes 49160 | tf_op jit(solution)/shard_map/ppermute | solution.py:338
  16.2 3.8 %collective-permute-start.1 = (bf16[4,2048]{1,0:T(4,128)(2,1)S(1)}, bf16[4,2048]{1,0:T(4,128)(2,1)S(1)}, u32[]{:S(2)}, u32[]{:S(2)}) collective-permute-start(bf16[4,2048]{1,0:T(4,128)(2,1)S(1)} %get-tuple-element.16), channel_id=1, source_target_pairs={{0,2},{1,3},{2,0},{3,1},{4,6},{5,7},{6,4},{7,5},{8,10},{9,11},{10,... | collective-permute-start | bytes 49160 | tf_op jit(solution)/shard_map/ppermute | solution.py:338
  17.8 2.3 %collective-permute-start = (bf16[4,2048]{1,0:T(4,128)(2,1)S(1)}, bf16[4,2048]{1,0:T(4,128)(2,1)S(1)}, u32[]{:S(2)}, u32[]{:S(2)}) collective-permute-start(bf16[4,2048]{1,0:T(4,128)(2,1)S(1)} %get-tuple-element.16), channel_id=1, source_target_pairs={{0,1},{1,0},{2,3},{3,2},{4,5},{5,4},{6,7},{7,6},{8,9},{9,8},{10,11... | collective-permute-start | bytes 49160 | tf_op jit(solution)/shard_map/ppermute | solution.py:338
  30.1 1.3 %collective-permute-start.3 = (bf16[32,1024]{1,0:T(8,128)(2,1)S(1)}, bf16[32,1024]{1,0:T(8,128)(2,1)S(1)}, u32[]{:S(2)}, u32[]{:S(2)}) collective-permute-start(bf16[32,1024]{1,0:T(8,128)(2,1)S(1)} %shard_map.167), channel_id=1, source_target_pairs={{0,1},{1,0},{2,3},{3,2},{4,5},{5,4},{6,7},{7,6},{8,9},{9,8},{10,11... | collective-permute-start | bytes 196616 | tf_op jit(solution)/shard_map/ppermute | solution.py:338
  31.4 4.1 %collective-permute-start.4 = (bf16[32,1024]{1,0:T(8,128)(2,1)S(1)}, bf16[32,1024]{1,0:T(8,128)(2,1)S(1)}, u32[]{:S(2)}, u32[]{:S(2)}) collective-permute-start(bf16[32,1024]{1,0:T(8,128)(2,1)S(1)} %add_convert_fusion.near), channel_id=1, source_target_pairs={{0,3},{1,2},{2,1},{3,0},{4,7},{5,6},{6,5},{7,4},{8,11},{9,10},{10,... | collective-permute-start | bytes 196616 | tf_op jit(solution)/shard_map/ppermute | solution.py:338

commit v22 on v21

--- a/solution.py
+++ b/solution.py
@@ -18,14 +18,12 @@
 VMEM = pl.BlockSpec(memory_space=pltpu.VMEM)
 HBM = pl.BlockSpec(memory_space=pltpu.HBM)
 
-FIRST_ORDER = [2, 4, 0, 6, 3, 5, 1, 7]
-MIDDLE_ORDER = [1, 4, 3, 6, 0, 5, 2, 7]
-LAST_ORDER = [7, 6, 5, 4, 3, 2, 1, 0]
-
-
-def pick_from(order, place):
+ORDER = [3, 4, 1, 6, 2, 5, 0, 7]
+
+
+def index_at(place):
     found = jnp.zeros_like(place)
-    for i, index in enumerate(order):
+    for i, index in enumerate(ORDER):
         found = jnp.where(place == i, index, found)
     return found
 
@@ -81,7 +79,7 @@
     blocks = onto_mxu(pick, all_rows).astype(BF16)
     for d in range(REQ):
         block = blocks[d * fields : (d + 1) * fields]
-        at = FIRST_ORDER.index(d)
+        at = ORDER.index(d)
         out[at, :fields, :] = block[:, : cols // 2]
         out[at, fields:, :] = block[:, cols // 2 :]
 
@@ -106,7 +104,7 @@
     down_p, across_p = iota(shape, 0), iota(shape, 1)
     down_i = iota((shape[0], count), 0)
     mine = hot((owner_row == me) & (rank_row == down_i % rows))
-    source = pick_from(FIRST_ORDER, iota((count, shape[1]), 1) // (2 * rows))
+    source = index_at(iota((count, shape[1]), 1) // (2 * rows))
     came = hot(iota((count, shape[1]), 0) // rows == source)
     from_there = onto_mxu(mine, came)
     field = jnp.minimum(down_p // (heads * rows), 3)
@@ -126,7 +124,7 @@
     valid[...] = seen
 
     ordered = hot(order_col == across)
-    holds = hot((owner_col == pick_from(MIDDLE_ORDER, across // rows)) & (rank_col == across % rows))
+    holds = hot((owner_col == index_at(across // rows)) & (rank_col == across % rows))
     arrange[...] = onto_mxu(ordered, holds).astype(BF16)
     here = hot((owner_col == me) & (rank_col == iota(arrange_own.shape, 1)))
     arrange_own[...] = onto_mxu(ordered, here).astype(BF16)
@@ -208,7 +206,7 @@
     feed = onto_mxu(activated, weight[...]) + onto_mxu(arrange_own[...], stream_own[...])
     rows = out.shape[1]
     for d in range(REQ):
-        out[LAST_ORDER.index(d)] = feed[d * rows : (d + 1) * rows].astype(BF16)
+        out[ORDER.index(d)] = feed[d * rows : (d + 1) * rows].astype(BF16)
 
 
 def finish_kernel(pieces, vectors, out):
@@ -229,8 +227,8 @@
     )(*args)
 
 
-def trade(blocks, group):
-    return lax.all_to_all(blocks, "req", 0, 0, tiled=True, axis_index_groups=[group])
+def trade(blocks):
+    return lax.all_to_all(blocks, "req", 0, 0, tiled=True, axis_index_groups=[ORDER])
 
 
 def on_pairs(
@@ -276,7 +274,7 @@
         + [pltpu.SemaphoreType.DMA((5,))],
         room=ALL_ROOM,
     )
-    arrived = trade(packed, FIRST_ORDER)
+    arrived = trade(packed)
     numbers = pile(
         [owner[None, :], order[None, :], lengths[None, :], jnp.zeros((5, count), I32), page_table.T]
     )
@@ -320,7 +318,7 @@
         up_kernel,
         [arr((count, hidden))],
         [VMEM] * 3,
-        [trade(blocks, MIDDLE_ORDER), arrange, up_weight_t],
+        [trade(blocks), arrange, up_weight_t],
     )
     part = (part.astype(F32) + swap(part, "tp", 1).astype(F32)).astype(BF16)
     (feed,) = call(
@@ -329,7 +327,7 @@
         [VMEM] * 6,
         [part, swap(part, "tp", 3), vectors, down_weight, arrange_own, stream_own],
     )
-    (out,) = call(finish_kernel, [arr((rows, cols))], [VMEM] * 2, [trade(feed, LAST_ORDER), vectors])
+    (out,) = call(finish_kernel, [arr((rows, cols))], [VMEM] * 2, [trade(feed), vectors])
     return out
 
 

time: 45.3 us -> 43.4 us (0.958)
  blocking collectives: 17.9 us -> 16.9 us
  waiting for transfers between devices: 7.74 us -> 7.03 us
    all_to_all x2, blocking collectives: 17.9 us -> 16.9 us  [trade(): lax.all_to_all(blocks, 'req', 0, 0, tiled=True, axis_index_groups=[ORDER])]
    all_to_all x1, waiting for transfers between devices: 1.73 us -> 0.82 us  [trade(): lax.all_to_all(blocks, 'req', 0, 0, tiled=True, axis_index_groups=[ORDER])]
  transfers between devices with their start and end apart: 6 -> 6, of which waited for: 5 -> 5; matrix products, arithmetic and copies ran while one was open for 4% -> 5% of each run, Pallas kernels for 1% -> 1%
where the time goes in v22:
time: 43.4 us; the launch traced here: 43.1 us
  blocking collectives  16.9 us (39%)
  starting transfers between devices  10.9 us (25%)
  waiting for transfers between devices  7.03 us (16%)
  Pallas kernels  5.17 us (12%)
  other arithmetic  1.88 us (4%)
  local copies, waits for them, and re-layouts  0.98 us (2%)
    all_to_all x2, blocking collectives, trade(): lax.all_to_all(blocks, 'req', 0, 0, tiled=True, axis_index_groups=[ORDER])  16.9 us
    all_to_all x1, starting transfers between devices, trade(): lax.all_to_all(blocks, 'req', 0, 0, tiled=True, axis_index_groups=[ORDER])  7.85 us
    ppermute x5, waiting for transfers between devices, swap(): return lax.ppermute(x, axis, [(i, i ^ step) for i in range(n)])  6.21 us
    pallas_call x7, Pallas kernels, call(): pl.pallas_call(functools.partial(kernel, **fixed) if fixed else kernel, o...  5.17 us
    ppermute x5, starting transfers between devices, swap(): return lax.ppermute(x, axis, [(i, i ^ step) for i in range(n)])  3.06 us
    select_n x1, other arithmetic, on_pairs(): pool = jnp.where(here, kv_pool, jnp.zeros_like(kv_pool))  1.59 us
  transfers between devices with their start and end apart: 6, of which 5 were waited for; matrix products, arithmetic and copies ran while one was open for 5% of the time, Pallas kernels for 1%

profile of v22, /device:TPU:0, one launch (start us, length us, event | category | flops | bytes accessed | tf_op | source)
XLA Modules:
  0.0 43.1 jit_solution(9946069954406771869)
XLA Ops:
  0.0 1.6 %shard_map.163 = bf16[8,8,256]{2,1,0:T(8,128)(2,1)} custom-call(s32[1,32]{1,0:T(1,128)} %bitcast.7, bf16[4,512]{1,0:T(4,128)(2,1)} %query.1, bf16[4,512]{1,0:T(4,128)(2,1)} %key.1, bf16[4,512]{1,0:T(4,128)(2,1)} %value.1, bf16[4,512]{1,0:T(4,128)(2,1)} %resid.1), custom_call_target="tpu_custom_call" | custom-call | bytes 16512 | tf_op jit(solution)/shard_map/pallas_call | solution.py:219
  1.6 7.9 %all-to-all-start = ((bf16[8,8,256]{2,1,0:T(8,128)(2,1)}), bf16[8,8,256]{2,1,0:T(8,128)(2,1)S(1)}, u32[]{:S(2)}, u32[]{:S(2)}) async-start(bf16[8,8,256]{2,1,0:T(8,128)(2,1)} %shard_map.163), calls=%async_computation | async-start | bytes 65536 | tf_op jit(solution)/shard_map/all_to_all | solution.py:231
  9.4 0.1 pad.60
  9.5 1.6 %broadcast_select_fusion.pool = bf16[2,22,32,512]{3,2,1,0:T(8,128)(2,1)S(1)} fusion(bf16[2,22,32,512]{3,2,1,0:T(8,128)(2,1)} %param.24, pred[]{:T(512)S(6)} %ge.3), kind=kLoop, calls=%fused_computation.1 | loop fusion | flops 720896 | bytes 2883585 | tf_op jit(solution)/shard_map/jit(_where)/select_n | solution.py:297
  11.1 0.3 copy-done.2
  11.5 0.0 copy-start.5
  11.5 0.0 copy-start.6
  11.5 0.0 copy-start.7
  11.5 0.0 copy-start.9
  11.5 0.1 slice_select_fusion.upper
  11.6 0.1 pad_add_fusion.1
  11.7 0.4 copy-done.3
  12.2 0.1 pad_add_fusion.numbers
  12.2 0.1 broadcast_in_dim.25.place
  12.3 0.4 shard_map.164
  12.8 0.8 %all-to-all-done.arrived = bf16[8,8,256]{2,1,0:T(8,128)(2,1)S(1)} async-done(((bf16[8,8,256]{2,1,0:T(8,128)(2,1)}), bf16[8,8,256]{2,1,0:T(8,128)(2,1)S(1)}, u32[]{:S(2)}, u32[]{:S(2)}) %all-to-all-start) | async-done | bytes 32800 | tf_op jit(solution)/shard_map/all_to_all | solution.py:231
  13.6 1.6 %shard_map.165 = (f32[4,2048]{1,0:T(4,128)S(1)}, bf16[4,2048]{1,0:T(4,128)(2,1)S(1)}) custom-call(s32[2,128]{1,0:T(2,128)S(1)} %broadcast_in_dim.25.place, bf16[8,8,256]{2,1,0:T(8,128)(2,1)S(1)} %all-to-all-done.arrived, bf16[56,64]{1,0:T(8,128)(2,1)S(1)} %get-tuple-element.13.pick, f32[16,704]{1,0:T(8,128)S(1)} %get-tuple-element.14.valid, ...), custom_call_target="tpu_custom_call" | custom-call | bytes 5210112 | tf_op jit(solution)/shard_map/pallas_call | solution.py:219
  15.3 0.1 collective-permute-start.2
  15.3 1.6 %collective-permute-start.1 = (bf16[4,2048]{1,0:T(4,128)(2,1)S(1)}, bf16[4,2048]{1,0:T(4,128)(2,1)S(1)}, u32[]{:S(2)}, u32[]{:S(2)}) collective-permute-start(bf16[4,2048]{1,0:T(4,128)(2,1)S(1)} %get-tuple-element.16), channel_id=1, source_target_pairs={{0,2},{1,3},{2,0},{3,1},{4,6},{5,7},{6,4},{7,5},{8,10},{9,11},{10,... | collective-permute-start | bytes 49160 | tf_op jit(solution)/shard_map/ppermute | solution.py:336
  16.9 0.3 collective-permute-start
  17.2 1.4 %collective-permute-done.2.far_sibling = bf16[4,2048]{1,0:T(4,128)(2,1)S(1)} collective-permute-done((bf16[4,2048]{1,0:T(4,128)(2,1)S(1)}, bf16[4,2048]{1,0:T(4,128)(2,1)S(1)}, u32[]{:S(2)}, u32[]{:S(2)}) %collective-permute-start.2) | collective-permute-done | bytes 16416 | tf_op jit(solution)/shard_map/ppermute | solution.py:336
  18.6 0.5 %collective-permute-done.1.far = bf16[4,2048]{1,0:T(4,128)(2,1)S(1)} collective-permute-done((bf16[4,2048]{1,0:T(4,128)(2,1)S(1)}, bf16[4,2048]{1,0:T(4,128)(2,1)S(1)}, u32[]{:S(2)}, u32[]{:S(2)}) %collective-permute-start.1) | collective-permute-done | bytes 16416 | tf_op jit(solution)/shard_map/ppermute | solution.py:336
  19.1 0.2 shard_map.166
  19.4 8.6 %all_to_all.15.rows_in = bf16[8,4,512]{2,1,0:T(4,128)(2,1)S(1)} all-to-all(bf16[8,4,512]{2,1,0:T(4,128)(2,1)S(1)} %get-tuple-element.17), channel_id=1, replica_groups={{12,16,4,24,8,20,0,28},{13,17,5,25,9,21,1,29},{14,18,6,26,10,22,2,30},{..., dimensions={0} | all-to-all | bytes 65536 | tf_op jit(solution)/shard_map/all_to_all | solution.py:231
  27.9 0.5 %shard_map.167 = bf16[32,1024]{1,0:T(8,128)(2,1)S(1)} custom-call(bf16[8,4,512]{2,1,0:T(4,128)(2,1)S(1)} %all_to_all.15.rows_in, bf16[32,32]{1,0:T(8,128)(2,1)S(1)} %get-tuple-element.18.arrange, bf16[1024,512]{1,0:T(8,128)(2,1)S(1)} %copy-done.1), custom_call_target="tpu_custom_call" | custom-call | bytes 1083392 | tf_op jit(solution)/shard_map/pallas_call | solution.py:219
  28.4 0.0 collective-permute-start.3
  28.4 1.2 %collective-permute-done.3 = bf16[32,1024]{1,0:T(8,128)(2,1)S(1)} collective-permute-done((bf16[32,1024]{1,0:T(8,128)(2,1)S(1)}, bf16[32,1024]{1,0:T(8,128)(2,1)S(1)}, u32[]{:S(2)}, u32[]{:S(2)}) %collective-permute-start.3) | collective-permute-done | bytes 65568 | tf_op jit(solution)/shard_map/ppermute | solution.py:336
  29.7 1.1 %collective-permute-start.4 = (bf16[32,1024]{1,0:T(8,128)(2,1)S(1)}, bf16[32,1024]{1,0:T(8,128)(2,1)S(1)}, u32[]{:S(2)}, u32[]{:S(2)}) collective-permute-start(bf16[32,1024]{1,0:T(8,128)(2,1)S(1)} %add_convert_fusion.near), channel_id=1, source_target_pairs={{0,3},{1,2},{2,1},{3,0},{4,7},{5,6},{6,5},{7,4},{8,11},{9,10},{10,... | collective-permute-start | bytes 196616 | tf_op jit(solution)/shard_map/ppermute | solution.py:336
  30.8 3.0 %collective-permute-done.4.far = bf16[32,1024]{1,0:T(8,128)(2,1)S(1)} collective-permute-done((bf16[32,1024]{1,0:T(8,128)(2,1)S(1)}, bf16[32,1024]{1,0:T(8,128)(2,1)S(1)}, u32[]{:S(2)}, u32[]{:S(2)}) %collective-permute-start.4) | collective-permute-done | bytes 65568 | tf_op jit(solution)/shard_map/ppermute | solution.py:336
  33.8 0.3 shard_map.168
  34.1 8.4 %all_to_all.16.pieces = bf16[8,4,512]{2,1,0:T(4,128)(2,1)S(1)} all-to-all(bf16[8,4,512]{2,1,0:T(4,128)(2,1)S(1)} %shard_map.168), channel_id=1, replica_groups={{12,16,4,24,8,20,0,28},{13,17,5,25,9,21,1,29},{14,18,6,26,10,22,2,30},{..., dimensions={0} | all-to-all | bytes 65536 | tf_op jit(solution)/shard_map/all_to_all | solution.py:231
  42.5 0.6 %shard_map.169 = bf16[4,512]{1,0:T(4,128)(2,1)} custom-call(bf16[8,4,512]{2,1,0:T(4,128)(2,1)S(1)} %all_to_all.16.pieces, f32[3072]{0:T(1024)S(1)} %convert_add_fusion.vectors), custom_call_target="tpu_custom_call" | custom-call | bytes 45056 | tf_op jit(solution)/shard_map/pallas_call | solution.py:219
  (22 shorter events, 0.1 us)
Async XLA Ops:
  1.6 12.0 %all-to-all-start = ((bf16[8,8,256]{2,1,0:T(8,128)(2,1)}), bf16[8,8,256]{2,1,0:T(8,128)(2,1)S(1)}, u32[]{:S(2)}, u32[]{:S(2)}) async-start(bf16[8,8,256]{2,1,0:T(8,128)(2,1)} %shard_map.163), calls=%async_computation | async-start | bytes 65536 | tf_op jit(solution)/shard_map/all_to_all | solution.py:231
  9.4 2.0 %copy-start.2 = (bf16[512,2048]{1,0:T(8,128)(2,1)S(1)}, bf16[512,2048]{1,0:T(8,128)(2,1)}, u32[]{:S(2)}) copy-start(bf16[512,2048]{1,0:T(8,128)(2,1)} %weight.3) | copy-start | bytes 6291460
  11.5 0.7 %copy-start.3 = (s32[32,16]{0,1:T(8,128)S(1)}, s32[32,16]{0,1:T(8,128)}, u32[]{:S(2)}) copy-start(s32[32,16]{0,1:T(8,128)} %param.23) | copy-start | bytes 6148
  11.5 0.7 %copy-start.4 = (s32[32]{0:T(128)S(1)}, s32[32]{0:T(128)}, u32[]{:S(2)}) copy-start(s32[32]{0:T(128)} %param.22) | copy-start | bytes 388
  11.5 0.7 %copy-start.10 = (s32[32]{0:T(128)S(1)}, s32[32]{0:T(128)}, u32[]{:S(2)}) copy-start(s32[32]{0:T(128)} %param.21) | copy-start | bytes 388
  11.5 0.7 %copy-start.11 = (s32[32]{0:T(128)S(1)}, s32[32]{0:T(128)}, u32[]{:S(2)}) copy-start(s32[32]{0:T(128)} %param.33) | copy-start | bytes 388
  11.5 1.3 %copy-start.5 = (bf16[1024]{0:T(1024)(128)(2,1)S(1)}, bf16[1024]{0:T(1024)(128)(2,1)}, u32[]{:S(2)}) copy-start(bf16[1024]{0:T(1024)(128)(2,1)} %param.30) | copy-start | bytes 6148
  11.5 1.3 %copy-start.6 = (bf16[512]{0:T(512)(128)(2,1)S(1)}, bf16[512]{0:T(512)(128)(2,1)}, u32[]{:S(2)}) copy-start(bf16[512]{0:T(512)(128)(2,1)} %param.32) | copy-start | bytes 3076
  11.5 1.3 %copy-start.7 = (bf16[512]{0:T(512)(128)(2,1)S(1)}, bf16[512]{0:T(512)(128)(2,1)}, u32[]{:S(2)}) copy-start(bf16[512]{0:T(512)(128)(2,1)} %param.28) | copy-start | bytes 3076
  11.5 1.3 %copy-start.8 = (bf16[512]{0:T(512)(128)(2,1)S(1)}, bf16[512]{0:T(512)(128)(2,1)}, u32[]{:S(2)}) copy-start(bf16[512]{0:T(512)(128)(2,1)} %param.27) | copy-start | bytes 3076
  11.5 1.3 %copy-start.9 = (bf16[512]{0:T(512)(128)(2,1)S(1)}, bf16[512]{0:T(512)(128)(2,1)}, u32[]{:S(2)}) copy-start(bf16[512]{0:T(512)(128)(2,1)} %param.26) | copy-start | bytes 3076
  13.6 14.3 %copy-start.1 = (bf16[1024,512]{1,0:T(8,128)(2,1)S(1)}, bf16[1024,512]{1,0:T(8,128)(2,1)}, u32[]{:S(2)}) copy-start(bf16[1024,512]{1,0:T(8,128)(2,1)} %weight.4) | copy-start | bytes 3145732
  15.2 18.6 %copy-start = (bf16[1024,512]{1,0:T(8,128)(2,1)S(1)}, bf16[1024,512]{1,0:T(8,128)(2,1)}, u32[]{:S(2)}) copy-start(bf16[1024,512]{1,0:T(8,128)(2,1)} %weight.5) | copy-start | bytes 3145732
  15.3 3.4 %collective-permute-start.2 = (bf16[4,2048]{1,0:T(4,128)(2,1)S(1)}, bf16[4,2048]{1,0:T(4,128)(2,1)S(1)}, u32[]{:S(2)}, u32[]{:S(2)}) collective-permute-start(bf16[4,2048]{1,0:T(4,128)(2,1)S(1)} %get-tuple-element.16), channel_id=1, source_target_pairs={{0,3},{1,2},{2,1},{3,0},{4,7},{5,6},{6,5},{7,4},{8,11},{9,10},{10,... | collective-permute-start | bytes 49160 | tf_op jit(solution)/shard_map/ppermute | solution.py:336
  15.3 3.8 %collective-permute-start.1 = (bf16[4,2048]{1,0:T(4,128)(2,1)S(1)}, bf16[4,2048]{1,0:T(4,128)(2,1)S(1)}, u32[]{:S(2)}, u32[]{:S(2)}) collective-permute-start(bf16[4,2048]{1,0:T(4,128)(2,1)S(1)} %get-tuple-element.16), channel_id=1, source_target_pairs={{0,2},{1,3},{2,0},{3,1},{4,6},{5,7},{6,4},{7,5},{8,10},{9,11},{10,... | collective-permute-start | bytes 49160 | tf_op jit(solution)/shard_map/ppermute | solution.py:336
  16.9 2.3 %collective-permute-start = (bf16[4,2048]{1,0:T(4,128)(2,1)S(1)}, bf16[4,2048]{1,0:T(4,128)(2,1)S(1)}, u32[]{:S(2)}, u32[]{:S(2)}) collective-permute-start(bf16[4,2048]{1,0:T(4,128)(2,1)S(1)} %get-tuple-element.16), channel_id=1, source_target_pairs={{0,1},{1,0},{2,3},{3,2},{4,5},{5,4},{6,7},{7,6},{8,9},{9,8},{10,11... | collective-permute-start | bytes 49160 | tf_op jit(solution)/shard_map/ppermute | solution.py:336
  28.4 1.3 %collective-permute-start.3 = (bf16[32,1024]{1,0:T(8,128)(2,1)S(1)}, bf16[32,1024]{1,0:T(8,128)(2,1)S(1)}, u32[]{:S(2)}, u32[]{:S(2)}) collective-permute-start(bf16[32,1024]{1,0:T(8,128)(2,1)S(1)} %shard_map.167), channel_id=1, source_target_pairs={{0,1},{1,0},{2,3},{3,2},{4,5},{5,4},{6,7},{7,6},{8,9},{9,8},{10,11... | collective-permute-start | bytes 196616 | tf_op jit(solution)/shard_map/ppermute | solution.py:336
  29.7 4.1 %collective-permute-start.4 = (bf16[32,1024]{1,0:T(8,128)(2,1)S(1)}, bf16[32,1024]{1,0:T(8,128)(2,1)S(1)}, u32[]{:S(2)}, u32[]{:S(2)}) collective-permute-start(bf16[32,1024]{1,0:T(8,128)(2,1)S(1)} %add_convert_fusion.near), channel_id=1, source_target_pairs={{0,3},{1,2},{2,1},{3,0},{4,7},{5,6},{6,5},{7,4},{8,11},{9,10},{10,... | collective-permute-start | bytes 196616 | tf_op jit(solution)/shard_map/ppermute | solution.py:336

commit v23 on v21

--- a/solution.py
+++ b/solution.py
@@ -18,8 +18,8 @@
 VMEM = pl.BlockSpec(memory_space=pltpu.VMEM)
 HBM = pl.BlockSpec(memory_space=pltpu.HBM)
 
-FIRST_ORDER = [2, 4, 0, 6, 3, 5, 1, 7]
-MIDDLE_ORDER = [1, 4, 3, 6, 0, 5, 2, 7]
+FIRST_ORDER = [3, 5, 2, 4, 1, 7, 0, 6]
+MIDDLE_ORDER = [3, 4, 1, 6, 2, 5, 0, 7]
 LAST_ORDER = [7, 6, 5, 4, 3, 2, 1, 0]
 
 

time: 45.3 us -> 43.5 us (0.960)
  blocking collectives: 17.9 us -> 16.9 us
  waiting for transfers between devices: 7.74 us -> 7.21 us
    all_to_all x2, blocking collectives: 17.9 us -> 16.9 us  [trade(): lax.all_to_all(blocks, 'req', 0, 0, tiled=True, axis_index_groups=[group])]
    all_to_all x1, waiting for transfers between devices: 1.73 us -> 0.95 us  [trade(): lax.all_to_all(blocks, 'req', 0, 0, tiled=True, axis_index_groups=[group])]
  transfers between devices with their start and end apart: 6 -> 6, of which waited for: 5 -> 5; matrix products, arithmetic and copies ran while one was open for 4% -> 5% of each run, Pallas kernels for 1% -> 1%
where the time goes in v23:
time: 43.5 us; the launch traced here: 43.2 us
  blocking collectives  16.9 us (39%)
  starting transfers between devices  10.9 us (25%)
  waiting for transfers between devices  7.21 us (17%)
  Pallas kernels  5.16 us (12%)
  other arithmetic  1.88 us (4%)
  local copies, waits for them, and re-layouts  0.98 us (2%)
    all_to_all x2, blocking collectives, trade(): lax.all_to_all(blocks, 'req', 0, 0, tiled=True, axis_index_groups=[group])  16.9 us
    all_to_all x1, starting transfers between devices, trade(): lax.all_to_all(blocks, 'req', 0, 0, tiled=True, axis_index_groups=[group])  7.85 us
    ppermute x5, waiting for transfers between devices, swap(): return lax.ppermute(x, axis, [(i, i ^ step) for i in range(n)])  6.25 us
    pallas_call x7, Pallas kernels, call(): pl.pallas_call(functools.partial(kernel, **fixed) if fixed else kernel, o...  5.16 us
    ppermute x5, starting transfers between devices, swap(): return lax.ppermute(x, axis, [(i, i ^ step) for i in range(n)])  3.01 us
    select_n x1, other arithmetic, on_pairs(): pool = jnp.where(here, kv_pool, jnp.zeros_like(kv_pool))  1.59 us
    all_to_all x1, waiting for transfers between devices, trade(): lax.all_to_all(blocks, 'req', 0, 0, tiled=True, axis_index_groups=[group])  0.95 us
  transfers between devices with their start and end apart: 6, of which 5 were waited for; matrix products, arithmetic and copies ran while one was open for 5% of the time, Pallas kernels for 1%

profile of v23, /device:TPU:0, one launch (start us, length us, event | category | flops | bytes accessed | tf_op | source)
XLA Modules:
  0.0 43.2 jit_solution(1923667954378824077)
XLA Ops:
  0.0 1.6 %shard_map.163 = bf16[8,8,256]{2,1,0:T(8,128)(2,1)} custom-call(s32[1,32]{1,0:T(1,128)} %bitcast.7, bf16[4,512]{1,0:T(4,128)(2,1)} %query.1, bf16[4,512]{1,0:T(4,128)(2,1)} %key.1, bf16[4,512]{1,0:T(4,128)(2,1)} %value.1, bf16[4,512]{1,0:T(4,128)(2,1)} %resid.1), custom_call_target="tpu_custom_call" | custom-call | bytes 16512 | tf_op jit(solution)/shard_map/pallas_call | solution.py:221
  1.6 7.9 %all-to-all-start = ((bf16[8,8,256]{2,1,0:T(8,128)(2,1)}), bf16[8,8,256]{2,1,0:T(8,128)(2,1)S(1)}, u32[]{:S(2)}, u32[]{:S(2)}) async-start(bf16[8,8,256]{2,1,0:T(8,128)(2,1)} %shard_map.163), calls=%async_computation | async-start | bytes 65536 | tf_op jit(solution)/shard_map/all_to_all | solution.py:233
  9.4 0.1 pad.60
  9.5 1.6 %broadcast_select_fusion.pool = bf16[2,22,32,512]{3,2,1,0:T(8,128)(2,1)S(1)} fusion(bf16[2,22,32,512]{3,2,1,0:T(8,128)(2,1)} %param.24, pred[]{:T(512)S(6)} %ge.3), kind=kLoop, calls=%fused_computation.1 | loop fusion | flops 720896 | bytes 2883585 | tf_op jit(solution)/shard_map/jit(_where)/select_n | solution.py:299
  11.1 0.3 copy-done.2
  11.5 0.0 copy-start.5
  11.5 0.0 copy-start.6
  11.5 0.0 copy-start.7
  11.5 0.0 copy-start.8
  11.5 0.1 slice_select_fusion.upper
  11.6 0.1 pad_add_fusion.1
  11.7 0.4 copy-done.3
  12.2 0.1 pad_add_fusion.numbers
  12.2 0.1 broadcast_in_dim.25.place
  12.3 0.4 shard_map.164
  12.8 1.0 %all-to-all-done.arrived = bf16[8,8,256]{2,1,0:T(8,128)(2,1)S(1)} async-done(((bf16[8,8,256]{2,1,0:T(8,128)(2,1)}), bf16[8,8,256]{2,1,0:T(8,128)(2,1)S(1)}, u32[]{:S(2)}, u32[]{:S(2)}) %all-to-all-start) | async-done | bytes 32800 | tf_op jit(solution)/shard_map/all_to_all | solution.py:233
  13.8 1.6 %shard_map.165 = (f32[4,2048]{1,0:T(4,128)S(1)}, bf16[4,2048]{1,0:T(4,128)(2,1)S(1)}) custom-call(s32[2,128]{1,0:T(2,128)S(1)} %broadcast_in_dim.25.place, bf16[8,8,256]{2,1,0:T(8,128)(2,1)S(1)} %all-to-all-done.arrived, bf16[56,64]{1,0:T(8,128)(2,1)S(1)} %get-tuple-element.13.pick, f32[16,704]{1,0:T(8,128)S(1)} %get-tuple-element.14.valid, ...), custom_call_target="tpu_custom_call" | custom-call | bytes 5210112 | tf_op jit(solution)/shard_map/pallas_call | solution.py:221
  15.4 0.1 collective-permute-start.2
  15.5 1.6 %collective-permute-start.1 = (bf16[4,2048]{1,0:T(4,128)(2,1)S(1)}, bf16[4,2048]{1,0:T(4,128)(2,1)S(1)}, u32[]{:S(2)}, u32[]{:S(2)}) collective-permute-start(bf16[4,2048]{1,0:T(4,128)(2,1)S(1)} %get-tuple-element.16), channel_id=1, source_target_pairs={{0,2},{1,3},{2,0},{3,1},{4,6},{5,7},{6,4},{7,5},{8,10},{9,11},{10,... | collective-permute-start | bytes 49160 | tf_op jit(solution)/shard_map/ppermute | solution.py:338
  17.0 0.3 collective-permute-start
  17.3 1.4 %collective-permute-done.2.far_sibling = bf16[4,2048]{1,0:T(4,128)(2,1)S(1)} collective-permute-done((bf16[4,2048]{1,0:T(4,128)(2,1)S(1)}, bf16[4,2048]{1,0:T(4,128)(2,1)S(1)}, u32[]{:S(2)}, u32[]{:S(2)}) %collective-permute-start.2) | collective-permute-done | bytes 16416 | tf_op jit(solution)/shard_map/ppermute | solution.py:338
  18.7 0.5 %collective-permute-done.1.far = bf16[4,2048]{1,0:T(4,128)(2,1)S(1)} collective-permute-done((bf16[4,2048]{1,0:T(4,128)(2,1)S(1)}, bf16[4,2048]{1,0:T(4,128)(2,1)S(1)}, u32[]{:S(2)}, u32[]{:S(2)}) %collective-permute-start.1) | collective-permute-done | bytes 16416 | tf_op jit(solution)/shard_map/ppermute | solution.py:338
  19.3 0.2 shard_map.166
  19.5 8.4 %all_to_all.15.rows_in = bf16[8,4,512]{2,1,0:T(4,128)(2,1)S(1)} all-to-all(bf16[8,4,512]{2,1,0:T(4,128)(2,1)S(1)} %get-tuple-element.17), channel_id=1, replica_groups={{12,16,4,24,8,20,0,28},{13,17,5,25,9,21,1,29},{14,18,6,26,10,22,2,30},{..., dimensions={0} | all-to-all | bytes 65536 | tf_op jit(solution)/shard_map/all_to_all | solution.py:233
  27.9 0.5 %shard_map.167 = bf16[32,1024]{1,0:T(8,128)(2,1)S(1)} custom-call(bf16[8,4,512]{2,1,0:T(4,128)(2,1)S(1)} %all_to_all.15.rows_in, bf16[32,32]{1,0:T(8,128)(2,1)S(1)} %get-tuple-element.18.arrange, bf16[1024,512]{1,0:T(8,128)(2,1)S(1)} %copy-done.1), custom_call_target="tpu_custom_call" | custom-call | bytes 1083392 | tf_op jit(solution)/shard_map/pallas_call | solution.py:221
  28.4 0.0 collective-permute-start.3
  28.4 1.2 %collective-permute-done.3 = bf16[32,1024]{1,0:T(8,128)(2,1)S(1)} collective-permute-done((bf16[32,1024]{1,0:T(8,128)(2,1)S(1)}, bf16[32,1024]{1,0:T(8,128)(2,1)S(1)}, u32[]{:S(2)}, u32[]{:S(2)}) %collective-permute-start.3) | collective-permute-done | bytes 65568 | tf_op jit(solution)/shard_map/ppermute | solution.py:338
  29.7 1.1 %collective-permute-start.4 = (bf16[32,1024]{1,0:T(8,128)(2,1)S(1)}, bf16[32,1024]{1,0:T(8,128)(2,1)S(1)}, u32[]{:S(2)}, u32[]{:S(2)}) collective-permute-start(bf16[32,1024]{1,0:T(8,128)(2,1)S(1)} %add_convert_fusion.near), channel_id=1, source_target_pairs={{0,3},{1,2},{2,1},{3,0},{4,7},{5,6},{6,5},{7,4},{8,11},{9,10},{10,... | collective-permute-start | bytes 196616 | tf_op jit(solution)/shard_map/ppermute | solution.py:338
  30.8 3.1 %collective-permute-done.4.far = bf16[32,1024]{1,0:T(8,128)(2,1)S(1)} collective-permute-done((bf16[32,1024]{1,0:T(8,128)(2,1)S(1)}, bf16[32,1024]{1,0:T(8,128)(2,1)S(1)}, u32[]{:S(2)}, u32[]{:S(2)}) %collective-permute-start.4) | collective-permute-done | bytes 65568 | tf_op jit(solution)/shard_map/ppermute | solution.py:338
  33.8 0.3 shard_map.168
  34.1 8.5 %all_to_all.16.pieces = bf16[8,4,512]{2,1,0:T(4,128)(2,1)S(1)} all-to-all(bf16[8,4,512]{2,1,0:T(4,128)(2,1)S(1)} %shard_map.168), channel_id=1, replica_groups={{28,24,20,16,12,8,4,0},{29,25,21,17,13,9,5,1},{30,26,22,18,14,10,6,2},{..., dimensions={0} | all-to-all | bytes 65536 | tf_op jit(solution)/shard_map/all_to_all | solution.py:233
  42.6 0.6 %shard_map.169 = bf16[4,512]{1,0:T(4,128)(2,1)} custom-call(bf16[8,4,512]{2,1,0:T(4,128)(2,1)S(1)} %all_to_all.16.pieces, f32[3072]{0:T(1024)S(1)} %convert_add_fusion.vectors), custom_call_target="tpu_custom_call" | custom-call | bytes 45056 | tf_op jit(solution)/shard_map/pallas_call | solution.py:221
  (22 shorter events, 0.1 us)
Async XLA Ops:
  1.6 12.2 %all-to-all-start = ((bf16[8,8,256]{2,1,0:T(8,128)(2,1)}), bf16[8,8,256]{2,1,0:T(8,128)(2,1)S(1)}, u32[]{:S(2)}, u32[]{:S(2)}) async-start(bf16[8,8,256]{2,1,0:T(8,128)(2,1)} %shard_map.163), calls=%async_computation | async-start | bytes 65536 | tf_op jit(solution)/shard_map/all_to_all | solution.py:233
  9.4 2.0 %copy-start.2 = (bf16[512,2048]{1,0:T(8,128)(2,1)S(1)}, bf16[512,2048]{1,0:T(8,128)(2,1)}, u32[]{:S(2)}) copy-start(bf16[512,2048]{1,0:T(8,128)(2,1)} %weight.3) | copy-start | bytes 6291460
  11.5 0.7 %copy-start.3 = (s32[32,16]{0,1:T(8,128)S(1)}, s32[32,16]{0,1:T(8,128)}, u32[]{:S(2)}) copy-start(s32[32,16]{0,1:T(8,128)} %param.23) | copy-start | bytes 6148
  11.5 0.7 %copy-start.4 = (s32[32]{0:T(128)S(1)}, s32[32]{0:T(128)}, u32[]{:S(2)}) copy-start(s32[32]{0:T(128)} %param.22) | copy-start | bytes 388
  11.5 0.7 %copy-start.10 = (s32[32]{0:T(128)S(1)}, s32[32]{0:T(128)}, u32[]{:S(2)}) copy-start(s32[32]{0:T(128)} %param.21) | copy-start | bytes 388
  11.5 0.7 %copy-start.11 = (s32[32]{0:T(128)S(1)}, s32[32]{0:T(128)}, u32[]{:S(2)}) copy-start(s32[32]{0:T(128)} %param.33) | copy-start | bytes 388
  11.5 1.3 %copy-start.5 = (bf16[1024]{0:T(1024)(128)(2,1)S(1)}, bf16[1024]{0:T(1024)(128)(2,1)}, u32[]{:S(2)}) copy-start(bf16[1024]{0:T(1024)(128)(2,1)} %param.30) | copy-start | bytes 6148
  11.5 1.3 %copy-start.6 = (bf16[512]{0:T(512)(128)(2,1)S(1)}, bf16[512]{0:T(512)(128)(2,1)}, u32[]{:S(2)}) copy-start(bf16[512]{0:T(512)(128)(2,1)} %param.32) | copy-start | bytes 3076
  11.5 1.3 %copy-start.7 = (bf16[512]{0:T(512)(128)(2,1)S(1)}, bf16[512]{0:T(512)(128)(2,1)}, u32[]{:S(2)}) copy-start(bf16[512]{0:T(512)(128)(2,1)} %param.28) | copy-start | bytes 3076
  11.5 1.3 %copy-start.8 = (bf16[512]{0:T(512)(128)(2,1)S(1)}, bf16[512]{0:T(512)(128)(2,1)}, u32[]{:S(2)}) copy-start(bf16[512]{0:T(512)(128)(2,1)} %param.27) | copy-start | bytes 3076
  11.5 1.3 %copy-start.9 = (bf16[512]{0:T(512)(128)(2,1)S(1)}, bf16[512]{0:T(512)(128)(2,1)}, u32[]{:S(2)}) copy-start(bf16[512]{0:T(512)(128)(2,1)} %param.26) | copy-start | bytes 3076
  13.8 14.2 %copy-start.1 = (bf16[1024,512]{1,0:T(8,128)(2,1)S(1)}, bf16[1024,512]{1,0:T(8,128)(2,1)}, u32[]{:S(2)}) copy-start(bf16[1024,512]{1,0:T(8,128)(2,1)} %weight.4) | copy-start | bytes 3145732
  15.4 18.4 %copy-start = (bf16[1024,512]{1,0:T(8,128)(2,1)S(1)}, bf16[1024,512]{1,0:T(8,128)(2,1)}, u32[]{:S(2)}) copy-start(bf16[1024,512]{1,0:T(8,128)(2,1)} %weight.5) | copy-start | bytes 3145732
  15.4 3.4 %collective-permute-start.2 = (bf16[4,2048]{1,0:T(4,128)(2,1)S(1)}, bf16[4,2048]{1,0:T(4,128)(2,1)S(1)}, u32[]{:S(2)}, u32[]{:S(2)}) collective-permute-start(bf16[4,2048]{1,0:T(4,128)(2,1)S(1)} %get-tuple-element.16), channel_id=1, source_target_pairs={{0,3},{1,2},{2,1},{3,0},{4,7},{5,6},{6,5},{7,4},{8,11},{9,10},{10,... | collective-permute-start | bytes 49160 | tf_op jit(solution)/shard_map/ppermute | solution.py:338
  15.5 3.8 %collective-permute-start.1 = (bf16[4,2048]{1,0:T(4,128)(2,1)S(1)}, bf16[4,2048]{1,0:T(4,128)(2,1)S(1)}, u32[]{:S(2)}, u32[]{:S(2)}) collective-permute-start(bf16[4,2048]{1,0:T(4,128)(2,1)S(1)} %get-tuple-element.16), channel_id=1, source_target_pairs={{0,2},{1,3},{2,0},{3,1},{4,6},{5,7},{6,4},{7,5},{8,10},{9,11},{10,... | collective-permute-start | bytes 49160 | tf_op jit(solution)/shard_map/ppermute | solution.py:338
  17.0 2.3 %collective-permute-start = (bf16[4,2048]{1,0:T(4,128)(2,1)S(1)}, bf16[4,2048]{1,0:T(4,128)(2,1)S(1)}, u32[]{:S(2)}, u32[]{:S(2)}) collective-permute-start(bf16[4,2048]{1,0:T(4,128)(2,1)S(1)} %get-tuple-element.16), channel_id=1, source_target_pairs={{0,1},{1,0},{2,3},{3,2},{4,5},{5,4},{6,7},{7,6},{8,9},{9,8},{10,11... | collective-permute-start | bytes 49160 | tf_op jit(solution)/shard_map/ppermute | solution.py:338
  28.4 1.3 %collective-permute-start.3 = (bf16[32,1024]{1,0:T(8,128)(2,1)S(1)}, bf16[32,1024]{1,0:T(8,128)(2,1)S(1)}, u32[]{:S(2)}, u32[]{:S(2)}) collective-permute-start(bf16[32,1024]{1,0:T(8,128)(2,1)S(1)} %shard_map.167), channel_id=1, source_target_pairs={{0,1},{1,0},{2,3},{3,2},{4,5},{5,4},{6,7},{7,6},{8,9},{9,8},{10,11... | collective-permute-start | bytes 196616 | tf_op jit(solution)/shard_map/ppermute | solution.py:338
  29.7 4.1 %collective-permute-start.4 = (bf16[32,1024]{1,0:T(8,128)(2,1)S(1)}, bf16[32,1024]{1,0:T(8,128)(2,1)S(1)}, u32[]{:S(2)}, u32[]{:S(2)}) collective-permute-start(bf16[32,1024]{1,0:T(8,128)(2,1)S(1)} %add_convert_fusion.near), channel_id=1, source_target_pairs={{0,3},{1,2},{2,1},{3,0},{4,7},{5,6},{6,5},{7,4},{8,11},{9,10},{10,... | collective-permute-start | bytes 196616 | tf_op jit(solution)/shard_map/ppermute | solution.py:338

commit v24 on v22

--- a/solution.py
+++ b/solution.py
@@ -199,8 +199,9 @@
     out[...] = nt_dot(ordered, weight[...]).astype(BF16)
 
 
-def down_kernel(near, far, vectors, weight, arrange_own, stream_own, out):
-    hidden = near[...].astype(F32) + far[...].astype(F32)
+def down_kernel(part, near, far, far_near, vectors, weight, arrange_own, stream_own, out):
+    hidden = part[...].astype(F32) + near[...].astype(F32)
+    hidden = hidden + (far[...].astype(F32) + far_near[...].astype(F32))
     hidden = hidden + vectors[vectors.shape[0] - hidden.shape[1] :][None, :]
     activated = (0.5 * hidden * (1.0 + lax.erf(hidden * math.sqrt(0.5)))).astype(BF16)
     feed = onto_mxu(activated, weight[...]) + onto_mxu(arrange_own[...], stream_own[...])
@@ -320,12 +321,13 @@
         [VMEM] * 3,
         [trade(blocks), arrange, up_weight_t],
     )
-    part = (part.astype(F32) + swap(part, "tp", 1).astype(F32)).astype(BF16)
     (feed,) = call(
         down_kernel,
         [arr((REQ, rows, cols))],
-        [VMEM] * 6,
-        [part, swap(part, "tp", 3), vectors, down_weight, arrange_own, stream_own],
+        [VMEM] * 8,
+        [part]
+        + [swap(part, "tp", step) for step in (1, 2, 3)]
+        + [vectors, down_weight, arrange_own, stream_own],
     )
     (out,) = call(finish_kernel, [arr((rows, cols))], [VMEM] * 2, [trade(feed), vectors])
     return out

time: 43.4 us -> 43.5 us (level)
  starting transfers between devices: 10.9 us -> 11.7 us
  waiting for transfers between devices: 7.03 us -> 6.38 us
    ppermute x5 -> x6, starting transfers between devices: 3.06 us -> 3.8 us  [swap(): return lax.ppermute(x, axis, [(i, i ^ step) for i in range(n)])]
    ppermute x5 -> x6, waiting for transfers between devices: 6.21 us -> 5.56 us  [swap(): return lax.ppermute(x, axis, [(i, i ^ step) for i in range(n)])]
  transfers between devices with their start and end apart: 6 -> 7, of which waited for: 5 -> 5; matrix products, arithmetic and copies ran while one was open for 5% -> 5% of each run, Pallas kernels for 1% -> 1%
where the time goes in v24:
time: 43.5 us; the launch traced here: 43.1 us
  blocking collectives  16.9 us (39%)
  starting transfers between devices  11.7 us (27%)
  waiting for transfers between devices  6.38 us (15%)
  Pallas kernels  5.15 us (12%)
  other arithmetic  1.86 us (4%)
  local copies, waits for them, and re-layouts  0.98 us (2%)
    all_to_all x2, blocking collectives, trade(): lax.all_to_all(blocks, 'req', 0, 0, tiled=True, axis_index_groups=[ORDER])  16.9 us
    all_to_all x1, starting transfers between devices, trade(): lax.all_to_all(blocks, 'req', 0, 0, tiled=True, axis_index_groups=[ORDER])  7.85 us
    ppermute x6, waiting for transfers between devices, swap(): return lax.ppermute(x, axis, [(i, i ^ step) for i in range(n)])  5.56 us
    pallas_call x7, Pallas kernels, call(): pl.pallas_call(functools.partial(kernel, **fixed) if fixed else kernel, o...  5.15 us
    ppermute x6, starting transfers between devices, swap(): return lax.ppermute(x, axis, [(i, i ^ step) for i in range(n)])  3.8 us
    select_n x1, other arithmetic, on_pairs(): pool = jnp.where(here, kv_pool, jnp.zeros_like(kv_pool))  1.59 us
  transfers between devices with their start and end apart: 7, of which 5 were waited for; matrix products, arithmetic and copies ran while one was open for 5% of the time, Pallas kernels for 1%

profile of v24, /device:TPU:0, one launch (start us, length us, event | category | flops | bytes accessed | tf_op | source)
XLA Modules:
  0.0 43.1 jit_solution(1510719296023026713)
XLA Ops:
  0.0 1.6 %shard_map.163 = bf16[8,8,256]{2,1,0:T(8,128)(2,1)} custom-call(s32[1,32]{1,0:T(1,128)} %bitcast.7, bf16[4,512]{1,0:T(4,128)(2,1)} %query.1, bf16[4,512]{1,0:T(4,128)(2,1)} %key.1, bf16[4,512]{1,0:T(4,128)(2,1)} %value.1, bf16[4,512]{1,0:T(4,128)(2,1)} %resid.1), custom_call_target="tpu_custom_call" | custom-call | bytes 16512 | tf_op jit(solution)/shard_map/pallas_call | solution.py:220
  1.6 7.9 %all-to-all-start = ((bf16[8,8,256]{2,1,0:T(8,128)(2,1)}), bf16[8,8,256]{2,1,0:T(8,128)(2,1)S(1)}, u32[]{:S(2)}, u32[]{:S(2)}) async-start(bf16[8,8,256]{2,1,0:T(8,128)(2,1)} %shard_map.163), calls=%async_computation | async-start | bytes 65536 | tf_op jit(solution)/shard_map/all_to_all | solution.py:232
  9.4 0.1 pad.60
  9.5 1.6 %broadcast_select_fusion.pool = bf16[2,22,32,512]{3,2,1,0:T(8,128)(2,1)S(1)} fusion(bf16[2,22,32,512]{3,2,1,0:T(8,128)(2,1)} %param.24, pred[]{:T(512)S(6)} %ge.3), kind=kLoop, calls=%fused_computation.1 | loop fusion | flops 720896 | bytes 2883585 | tf_op jit(solution)/shard_map/jit(_where)/select_n | solution.py:298
  11.1 0.3 copy-done.2
  11.5 0.0 copy-start.6
  11.5 0.0 copy-start.7
  11.5 0.1 slice_select_fusion.upper
  11.6 0.1 pad_add_fusion.1
  11.7 0.4 copy-done.3
  12.2 0.1 pad_add_fusion.numbers
  12.2 0.1 broadcast_in_dim.25.place
  12.3 0.4 shard_map.164
  12.8 0.8 %all-to-all-done.arrived = bf16[8,8,256]{2,1,0:T(8,128)(2,1)S(1)} async-done(((bf16[8,8,256]{2,1,0:T(8,128)(2,1)}), bf16[8,8,256]{2,1,0:T(8,128)(2,1)S(1)}, u32[]{:S(2)}, u32[]{:S(2)}) %all-to-all-start) | async-done | bytes 32800 | tf_op jit(solution)/shard_map/all_to_all | solution.py:232
  13.6 1.6 %shard_map.165 = (f32[4,2048]{1,0:T(4,128)S(1)}, bf16[4,2048]{1,0:T(4,128)(2,1)S(1)}) custom-call(s32[2,128]{1,0:T(2,128)S(1)} %broadcast_in_dim.25.place, bf16[8,8,256]{2,1,0:T(8,128)(2,1)S(1)} %all-to-all-done.arrived, bf16[56,64]{1,0:T(8,128)(2,1)S(1)} %get-tuple-element.13.pick, f32[16,704]{1,0:T(8,128)S(1)} %get-tuple-element.14.valid, ...), custom_call_target="tpu_custom_call" | custom-call | bytes 5210112 | tf_op jit(solution)/shard_map/pallas_call | solution.py:220
  15.2 0.0 copy-start.1
  15.3 0.1 collective-permute-start.2
  15.3 1.6 %collective-permute-start.1 = (bf16[4,2048]{1,0:T(4,128)(2,1)S(1)}, bf16[4,2048]{1,0:T(4,128)(2,1)S(1)}, u32[]{:S(2)}, u32[]{:S(2)}) collective-permute-start(bf16[4,2048]{1,0:T(4,128)(2,1)S(1)} %get-tuple-element.16), channel_id=1, source_target_pairs={{0,2},{1,3},{2,0},{3,1},{4,6},{5,7},{6,4},{7,5},{8,10},{9,11},{10,... | collective-permute-start | bytes 49160 | tf_op jit(solution)/shard_map/ppermute | solution.py:338
  16.9 0.3 collective-permute-start
  17.2 1.4 %collective-permute-done.2.far_sibling = bf16[4,2048]{1,0:T(4,128)(2,1)S(1)} collective-permute-done((bf16[4,2048]{1,0:T(4,128)(2,1)S(1)}, bf16[4,2048]{1,0:T(4,128)(2,1)S(1)}, u32[]{:S(2)}, u32[]{:S(2)}) %collective-permute-start.2) | collective-permute-done | bytes 16416 | tf_op jit(solution)/shard_map/ppermute | solution.py:338
  18.6 0.5 %collective-permute-done.1.far = bf16[4,2048]{1,0:T(4,128)(2,1)S(1)} collective-permute-done((bf16[4,2048]{1,0:T(4,128)(2,1)S(1)}, bf16[4,2048]{1,0:T(4,128)(2,1)S(1)}, u32[]{:S(2)}, u32[]{:S(2)}) %collective-permute-start.1) | collective-permute-done | bytes 16416 | tf_op jit(solution)/shard_map/ppermute | solution.py:338
  19.1 0.2 shard_map.166
  19.4 8.6 %all_to_all.15.rows_in = bf16[8,4,512]{2,1,0:T(4,128)(2,1)S(1)} all-to-all(bf16[8,4,512]{2,1,0:T(4,128)(2,1)S(1)} %get-tuple-element.17), channel_id=1, replica_groups={{12,16,4,24,8,20,0,28},{13,17,5,25,9,21,1,29},{14,18,6,26,10,22,2,30},{..., dimensions={0} | all-to-all | bytes 65536 | tf_op jit(solution)/shard_map/all_to_all | solution.py:232
  27.9 0.5 %shard_map.167.part = bf16[32,1024]{1,0:T(8,128)(2,1)S(1)} custom-call(bf16[8,4,512]{2,1,0:T(4,128)(2,1)S(1)} %all_to_all.15.rows_in, bf16[32,32]{1,0:T(8,128)(2,1)S(1)} %get-tuple-element.18.arrange, bf16[1024,512]{1,0:T(8,128)(2,1)S(1)} %copy-done), custom_call_target="tpu_custom_call" | custom-call | bytes 1083392 | tf_op jit(solution)/shard_map/pallas_call | solution.py:220
  28.4 0.0 collective-permute-start.5
  28.4 1.3 %collective-permute-start.4 = (bf16[32,1024]{1,0:T(8,128)(2,1)S(1)}, bf16[32,1024]{1,0:T(8,128)(2,1)S(1)}, u32[]{:S(2)}, u32[]{:S(2)}) collective-permute-start(bf16[32,1024]{1,0:T(8,128)(2,1)S(1)} %shard_map.167.part), channel_id=1, source_target_pairs={{0,2},{1,3},{2,0},{3,1},{4,6},{5,7},{6,4},{7,5},{8,10},{9,11},{10,... | collective-permute-start | bytes 196616 | tf_op jit(solution)/shard_map/ppermute | solution.py:338
  29.8 0.5 %collective-permute-start.3 = (bf16[32,1024]{1,0:T(8,128)(2,1)S(1)}, bf16[32,1024]{1,0:T(8,128)(2,1)S(1)}, u32[]{:S(2)}, u32[]{:S(2)}) collective-permute-start(bf16[32,1024]{1,0:T(8,128)(2,1)S(1)} %shard_map.167.part), channel_id=1, source_target_pairs={{0,1},{1,0},{2,3},{3,2},{4,5},{5,4},{6,7},{7,6},{8,9},{9,8},{10,11... | collective-permute-start | bytes 196616 | tf_op jit(solution)/shard_map/ppermute | solution.py:338
  30.3 2.5 %collective-permute-done.5.far_near = bf16[32,1024]{1,0:T(8,128)(2,1)S(1)} collective-permute-done((bf16[32,1024]{1,0:T(8,128)(2,1)S(1)}, bf16[32,1024]{1,0:T(8,128)(2,1)S(1)}, u32[]{:S(2)}, u32[]{:S(2)}) %collective-permute-start.5) | collective-permute-done | bytes 65568 | tf_op jit(solution)/shard_map/ppermute | solution.py:338
  32.8 1.1 %collective-permute-done.4.far = bf16[32,1024]{1,0:T(8,128)(2,1)S(1)} collective-permute-done((bf16[32,1024]{1,0:T(8,128)(2,1)S(1)}, bf16[32,1024]{1,0:T(8,128)(2,1)S(1)}, u32[]{:S(2)}, u32[]{:S(2)}) %collective-permute-start.4) | collective-permute-done | bytes 65568 | tf_op jit(solution)/shard_map/ppermute | solution.py:338
  33.9 0.3 shard_map.168
  34.2 8.4 %all_to_all.16.pieces = bf16[8,4,512]{2,1,0:T(4,128)(2,1)S(1)} all-to-all(bf16[8,4,512]{2,1,0:T(4,128)(2,1)S(1)} %shard_map.168), channel_id=1, replica_groups={{12,16,4,24,8,20,0,28},{13,17,5,25,9,21,1,29},{14,18,6,26,10,22,2,30},{..., dimensions={0} | all-to-all | bytes 65536 | tf_op jit(solution)/shard_map/all_to_all | solution.py:232
  42.5 0.6 %shard_map.169 = bf16[4,512]{1,0:T(4,128)(2,1)} custom-call(bf16[8,4,512]{2,1,0:T(4,128)(2,1)S(1)} %all_to_all.16.pieces, f32[3072]{0:T(1024)S(1)} %convert_add_fusion.vectors), custom_call_target="tpu_custom_call" | custom-call | bytes 45056 | tf_op jit(solution)/shard_map/pallas_call | solution.py:220
  (23 shorter events, 0.1 us)
Async XLA Ops:
  1.6 12.0 %all-to-all-start = ((bf16[8,8,256]{2,1,0:T(8,128)(2,1)}), bf16[8,8,256]{2,1,0:T(8,128)(2,1)S(1)}, u32[]{:S(2)}, u32[]{:S(2)}) async-start(bf16[8,8,256]{2,1,0:T(8,128)(2,1)} %shard_map.163), calls=%async_computation | async-start | bytes 65536 | tf_op jit(solution)/shard_map/all_to_all | solution.py:232
  9.4 2.0 %copy-start.2 = (bf16[512,2048]{1,0:T(8,128)(2,1)S(1)}, bf16[512,2048]{1,0:T(8,128)(2,1)}, u32[]{:S(2)}) copy-start(bf16[512,2048]{1,0:T(8,128)(2,1)} %weight.3) | copy-start | bytes 6291460
  11.5 0.7 %copy-start.3 = (s32[32,16]{0,1:T(8,128)S(1)}, s32[32,16]{0,1:T(8,128)}, u32[]{:S(2)}) copy-start(s32[32,16]{0,1:T(8,128)} %param.23) | copy-start | bytes 6148
  11.5 0.7 %copy-start.4 = (s32[32]{0:T(128)S(1)}, s32[32]{0:T(128)}, u32[]{:S(2)}) copy-start(s32[32]{0:T(128)} %param.22) | copy-start | bytes 388
  11.5 0.7 %copy-start.10 = (s32[32]{0:T(128)S(1)}, s32[32]{0:T(128)}, u32[]{:S(2)}) copy-start(s32[32]{0:T(128)} %param.21) | copy-start | bytes 388
  11.5 0.7 %copy-start.11 = (s32[32]{0:T(128)S(1)}, s32[32]{0:T(128)}, u32[]{:S(2)}) copy-start(s32[32]{0:T(128)} %param.33) | copy-start | bytes 388
  11.5 1.3 %copy-start.5 = (bf16[1024]{0:T(1024)(128)(2,1)S(1)}, bf16[1024]{0:T(1024)(128)(2,1)}, u32[]{:S(2)}) copy-start(bf16[1024]{0:T(1024)(128)(2,1)} %param.30) | copy-start | bytes 6148
  11.5 1.3 %copy-start.6 = (bf16[512]{0:T(512)(128)(2,1)S(1)}, bf16[512]{0:T(512)(128)(2,1)}, u32[]{:S(2)}) copy-start(bf16[512]{0:T(512)(128)(2,1)} %param.32) | copy-start | bytes 3076
  11.5 1.3 %copy-start.7 = (bf16[512]{0:T(512)(128)(2,1)S(1)}, bf16[512]{0:T(512)(128)(2,1)}, u32[]{:S(2)}) copy-start(bf16[512]{0:T(512)(128)(2,1)} %param.28) | copy-start | bytes 3076
  11.5 1.3 %copy-start.8 = (bf16[512]{0:T(512)(128)(2,1)S(1)}, bf16[512]{0:T(512)(128)(2,1)}, u32[]{:S(2)}) copy-start(bf16[512]{0:T(512)(128)(2,1)} %param.27) | copy-start | bytes 3076
  11.5 1.3 %copy-start.9 = (bf16[512]{0:T(512)(128)(2,1)S(1)}, bf16[512]{0:T(512)(128)(2,1)}, u32[]{:S(2)}) copy-start(bf16[512]{0:T(512)(128)(2,1)} %param.26) | copy-start | bytes 3076
  13.6 14.3 %copy-start = (bf16[1024,512]{1,0:T(8,128)(2,1)S(1)}, bf16[1024,512]{1,0:T(8,128)(2,1)}, u32[]{:S(2)}) copy-start(bf16[1024,512]{1,0:T(8,128)(2,1)} %weight.4) | copy-start | bytes 3145732
  15.2 18.6 %copy-start.1 = (bf16[1024,512]{1,0:T(8,128)(2,1)S(1)}, bf16[1024,512]{1,0:T(8,128)(2,1)}, u32[]{:S(2)}) copy-start(bf16[1024,512]{1,0:T(8,128)(2,1)} %weight.5) | copy-start | bytes 3145732
  15.3 3.4 %collective-permute-start.2 = (bf16[4,2048]{1,0:T(4,128)(2,1)S(1)}, bf16[4,2048]{1,0:T(4,128)(2,1)S(1)}, u32[]{:S(2)}, u32[]{:S(2)}) collective-permute-start(bf16[4,2048]{1,0:T(4,128)(2,1)S(1)} %get-tuple-element.16), channel_id=1, source_target_pairs={{0,3},{1,2},{2,1},{3,0},{4,7},{5,6},{6,5},{7,4},{8,11},{9,10},{10,... | collective-permute-start | bytes 49160 | tf_op jit(solution)/shard_map/ppermute | solution.py:338
  15.3 3.8 %collective-permute-start.1 = (bf16[4,2048]{1,0:T(4,128)(2,1)S(1)}, bf16[4,2048]{1,0:T(4,128)(2,1)S(1)}, u32[]{:S(2)}, u32[]{:S(2)}) collective-permute-start(bf16[4,2048]{1,0:T(4,128)(2,1)S(1)} %get-tuple-element.16), channel_id=1, source_target_pairs={{0,2},{1,3},{2,0},{3,1},{4,6},{5,7},{6,4},{7,5},{8,10},{9,11},{10,... | collective-permute-start | bytes 49160 | tf_op jit(solution)/shard_map/ppermute | solution.py:338
  16.9 2.3 %collective-permute-start = (bf16[4,2048]{1,0:T(4,128)(2,1)S(1)}, bf16[4,2048]{1,0:T(4,128)(2,1)S(1)}, u32[]{:S(2)}, u32[]{:S(2)}) collective-permute-start(bf16[4,2048]{1,0:T(4,128)(2,1)S(1)} %get-tuple-element.16), channel_id=1, source_target_pairs={{0,1},{1,0},{2,3},{3,2},{4,5},{5,4},{6,7},{7,6},{8,9},{9,8},{10,11... | collective-permute-start | bytes 49160 | tf_op jit(solution)/shard_map/ppermute | solution.py:338
  28.4 4.4 %collective-permute-start.5 = (bf16[32,1024]{1,0:T(8,128)(2,1)S(1)}, bf16[32,1024]{1,0:T(8,128)(2,1)S(1)}, u32[]{:S(2)}, u32[]{:S(2)}) collective-permute-start(bf16[32,1024]{1,0:T(8,128)(2,1)S(1)} %shard_map.167.part), channel_id=1, source_target_pairs={{0,3},{1,2},{2,1},{3,0},{4,7},{5,6},{6,5},{7,4},{8,11},{9,10},{10,... | collective-permute-start | bytes 196616 | tf_op jit(solution)/shard_map/ppermute | solution.py:338
  28.4 5.4 %collective-permute-start.4 = (bf16[32,1024]{1,0:T(8,128)(2,1)S(1)}, bf16[32,1024]{1,0:T(8,128)(2,1)S(1)}, u32[]{:S(2)}, u32[]{:S(2)}) collective-permute-start(bf16[32,1024]{1,0:T(8,128)(2,1)S(1)} %shard_map.167.part), channel_id=1, source_target_pairs={{0,2},{1,3},{2,0},{3,1},{4,6},{5,7},{6,4},{7,5},{8,10},{9,11},{10,... | collective-permute-start | bytes 196616 | tf_op jit(solution)/shard_map/ppermute | solution.py:338
  29.8 4.1 %collective-permute-start.3 = (bf16[32,1024]{1,0:T(8,128)(2,1)S(1)}, bf16[32,1024]{1,0:T(8,128)(2,1)S(1)}, u32[]{:S(2)}, u32[]{:S(2)}) collective-permute-start(bf16[32,1024]{1,0:T(8,128)(2,1)S(1)} %shard_map.167.part), channel_id=1, source_target_pairs={{0,1},{1,0},{2,3},{3,2},{4,5},{5,4},{6,7},{7,6},{8,9},{9,8},{10,11... | collective-permute-start | bytes 196616 | tf_op jit(solution)/shard_map/ppermute | solution.py:338

commit v25 on v20

--- a/solution.py
+++ b/solution.py
@@ -67,13 +67,13 @@
         copy.start()
     rows, cols = q.shape
     fields = 4
-    count = REQ * rows
     shape = (REQ * fields, fields * rows)
     down, across = iota(shape, 0), iota(shape, 1)
-    here = (count, fields * rows)
-    of_mine = hot(iota(here, 0) == lax.axis_index("req") * rows + iota(here, 1) % rows)
+    me = lax.axis_index("req")
     copies[0].wait()
-    owner_of = onto_mxu(owner[...].astype(F32).astype(BF16), of_mine).astype(I32)
+    owner_of = jnp.full(shape, owner[me * rows], I32)
+    for i in range(1, rows):
+        owner_of = jnp.where(across % rows == i, owner[me * rows + i], owner_of)
     pick = hot((down % fields == across // rows) & (owner_of == down // fields))
     for copy in copies[1:]:
         copy.wait()
@@ -270,8 +270,8 @@
         pack_kernel,
         [arr((REQ, 8, cols // 2))],
         [HBM] * 5,
-        [owner[None, :], query, key_new, value_new, resid],
-        [pltpu.VMEM((1, count), I32)]
+        [owner, query, key_new, value_new, resid],
+        [pltpu.SMEM((count,), I32)]
         + [pltpu.VMEM((rows, cols), BF16)] * 4
         + [pltpu.SemaphoreType.DMA((5,))],
         room=ALL_ROOM,

time: 43.5 us -> 43.4 us (level)
  no operation moved by 1% of the time
where the time goes in v25:
time: 43.4 us; the launch traced here: 43 us
  blocking collectives  16.7 us (38%)
  starting transfers between devices  11.1 us (26%)
  waiting for transfers between devices  7.32 us (17%)
  Pallas kernels  5.28 us (12%)
  other arithmetic  1.67 us (4%)
  local copies, waits for them, and re-layouts  0.84 us (2%)
    all_to_all x2, blocking collectives, trade(): lax.all_to_all(blocks, 'req', 0, 0, tiled=True, axis_index_groups=[group])  16.7 us
    all_to_all x1, starting transfers between devices, trade(): lax.all_to_all(blocks, 'req', 0, 0, tiled=True, axis_index_groups=[group])  7.85 us
    ppermute x5, waiting for transfers between devices, swap(): return lax.ppermute(x, axis, [(i, i ^ step) for i in range(n)])  6.02 us
    pallas_call x7, Pallas kernels, call(): pl.pallas_call(functools.partial(kernel, **fixed) if fixed else kernel, o...  5.28 us
    ppermute x5, starting transfers between devices, swap(): return lax.ppermute(x, axis, [(i, i ^ step) for i in range(n)])  3.25 us
    select_n x1, other arithmetic, on_pairs(): upper = jnp.where(here, upper, jnp.zeros_like(upper))  1.39 us
    all_to_all x1, waiting for transfers between devices, trade(): lax.all_to_all(blocks, 'req', 0, 0, tiled=True, axis_index_groups=[group])  1.3 us
  transfers between devices with their start and end apart: 6, of which 5 were waited for; matrix products, arithmetic and copies ran while one was open for 4% of the time, Pallas kernels for 1%

profile of v25, /device:TPU:0, one launch (start us, length us, event | category | flops | bytes accessed | tf_op | source)
XLA Modules:
  0.0 43.0 jit_solution(13809968224073853011)
XLA Ops:
  0.0 1.5 %shard_map.163 = bf16[8,8,256]{2,1,0:T(8,128)(2,1)} custom-call(s32[32]{0:T(128)} %owner_in.1, bf16[4,512]{1,0:T(4,128)(2,1)} %query.1, bf16[4,512]{1,0:T(4,128)(2,1)} %key.1, bf16[4,512]{1,0:T(4,128)(2,1)} %value.1, bf16[4,512]{1,0:T(4,128)(2,1)} %resid.1), custom_call_target="tpu_custom_call" | custom-call | bytes 16512 | tf_op jit(solution)/shard_map/pallas_call | solution.py:221
  1.5 7.9 %all-to-all-start = ((bf16[8,8,256]{2,1,0:T(8,128)(2,1)}), bf16[8,8,256]{2,1,0:T(8,128)(2,1)S(1)}, u32[]{:S(2)}, u32[]{:S(2)}) async-start(bf16[8,8,256]{2,1,0:T(8,128)(2,1)} %shard_map.163), calls=%async_computation | async-start | bytes 65536 | tf_op jit(solution)/shard_map/all_to_all | solution.py:233
  9.4 0.1 pad.60
  9.5 1.4 %slice_select_fusion.upper = bf16[256,2048]{1,0:T(8,128)(2,1)S(1)} fusion(bf16[512,2048]{1,0:T(8,128)(2,1)} %weight.3, pred[]{:T(512)S(6)} %ge.3), kind=kLoop, calls=%fused_computation.1 | loop fusion | flops 524288 | bytes 2097153 | tf_op jit(solution)/shard_map/jit(_where)/select_n | solution.py:301
  10.9 0.2 copy-done.2
  11.1 0.0 copy-start.5
  11.1 0.0 copy-start.7
  11.1 0.0 copy-start.8
  11.1 0.1 broadcast_select_fusion.pool
  11.2 0.1 pad_add_fusion.1
  11.3 0.4 %copy-done.3 = s32[32,16]{0,1:T(8,128)S(1)} copy-done((s32[32,16]{0,1:T(8,128)S(1)}, s32[32,16]{0,1:T(8,128)}, u32[]{:S(2)}) %copy-start.3) | copy-done | bytes 2072
  11.8 0.1 pad_add_fusion.numbers
  11.8 0.1 broadcast_in_dim.24.place
  11.9 0.4 shard_map.164
  12.4 1.3 %all-to-all-done.arrived = bf16[8,8,256]{2,1,0:T(8,128)(2,1)S(1)} async-done(((bf16[8,8,256]{2,1,0:T(8,128)(2,1)}), bf16[8,8,256]{2,1,0:T(8,128)(2,1)S(1)}, u32[]{:S(2)}, u32[]{:S(2)}) %all-to-all-start) | async-done | bytes 32800 | tf_op jit(solution)/shard_map/all_to_all | solution.py:233
  13.7 1.8 %shard_map.165 = (f32[4,2048]{1,0:T(4,128)S(1)}, bf16[4,2048]{1,0:T(4,128)(2,1)S(1)}) custom-call(s32[2,128]{1,0:T(2,128)S(1)} %broadcast_in_dim.24.place, bf16[8,8,256]{2,1,0:T(8,128)(2,1)S(1)} %all-to-all-done.arrived, bf16[56,64]{1,0:T(8,128)(2,1)S(1)} %get-tuple-element.13.pick, f32[16,704]{1,0:T(8,128)S(1)} %get-tuple-element.14.valid, ...), custom_call_target="tpu_custom_call" | custom-call | bytes 4685824 | tf_op jit(solution)/shard_map/pallas_call | solution.py:221
  15.5 0.0 copy-start
  15.5 0.1 collective-permute-start.2
  15.6 1.6 %collective-permute-start.1 = (bf16[4,2048]{1,0:T(4,128)(2,1)S(1)}, bf16[4,2048]{1,0:T(4,128)(2,1)S(1)}, u32[]{:S(2)}, u32[]{:S(2)}) collective-permute-start(bf16[4,2048]{1,0:T(4,128)(2,1)S(1)} %get-tuple-element.16), channel_id=1, source_target_pairs={{0,2},{1,3},{2,0},{3,1},{4,6},{5,7},{6,4},{7,5},{8,10},{9,11},{10,... | collective-permute-start | bytes 49160 | tf_op jit(solution)/shard_map/ppermute | solution.py:338
  17.1 0.3 collective-permute-start
  17.4 1.4 %collective-permute-done.2.far_sibling = bf16[4,2048]{1,0:T(4,128)(2,1)S(1)} collective-permute-done((bf16[4,2048]{1,0:T(4,128)(2,1)S(1)}, bf16[4,2048]{1,0:T(4,128)(2,1)S(1)}, u32[]{:S(2)}, u32[]{:S(2)}) %collective-permute-start.2) | collective-permute-done | bytes 16416 | tf_op jit(solution)/shard_map/ppermute | solution.py:338
  18.9 0.5 %collective-permute-done.1.far = bf16[4,2048]{1,0:T(4,128)(2,1)S(1)} collective-permute-done((bf16[4,2048]{1,0:T(4,128)(2,1)S(1)}, bf16[4,2048]{1,0:T(4,128)(2,1)S(1)}, u32[]{:S(2)}, u32[]{:S(2)}) %collective-permute-start.1) | collective-permute-done | bytes 16416 | tf_op jit(solution)/shard_map/ppermute | solution.py:338
  19.4 0.2 shard_map.166
  19.6 8.2 %all_to_all.15.rows_in = bf16[8,4,512]{2,1,0:T(4,128)(2,1)S(1)} all-to-all(bf16[8,4,512]{2,1,0:T(4,128)(2,1)S(1)} %get-tuple-element.17), channel_id=1, replica_groups={{12,16,4,24,8,20,0,28},{13,17,5,25,9,21,1,29},{14,18,6,26,10,22,2,30},{..., dimensions={0} | all-to-all | bytes 65536 | tf_op jit(solution)/shard_map/all_to_all | solution.py:233
  27.8 0.5 %shard_map.167 = bf16[32,1024]{1,0:T(8,128)(2,1)S(1)} custom-call(bf16[8,4,512]{2,1,0:T(4,128)(2,1)S(1)} %all_to_all.15.rows_in, bf16[32,32]{1,0:T(8,128)(2,1)S(1)} %get-tuple-element.18.arrange, bf16[1024,512]{1,0:T(8,128)(2,1)S(1)} %copy-done.1), custom_call_target="tpu_custom_call" | custom-call | bytes 1083392 | tf_op jit(solution)/shard_map/pallas_call | solution.py:221
  28.3 0.0 collective-permute-start.3
  28.3 1.2 %collective-permute-done.3 = bf16[32,1024]{1,0:T(8,128)(2,1)S(1)} collective-permute-done((bf16[32,1024]{1,0:T(8,128)(2,1)S(1)}, bf16[32,1024]{1,0:T(8,128)(2,1)S(1)}, u32[]{:S(2)}, u32[]{:S(2)}) %collective-permute-start.3) | collective-permute-done | bytes 65568 | tf_op jit(solution)/shard_map/ppermute | solution.py:338
  29.6 1.3 %collective-permute-start.4 = (bf16[32,1024]{1,0:T(8,128)(2,1)S(1)}, bf16[32,1024]{1,0:T(8,128)(2,1)S(1)}, u32[]{:S(2)}, u32[]{:S(2)}) collective-permute-start(bf16[32,1024]{1,0:T(8,128)(2,1)S(1)} %add_convert_fusion.near), channel_id=1, source_target_pairs={{0,3},{1,2},{2,1},{3,0},{4,7},{5,6},{6,5},{7,4},{8,11},{9,10},{10,... | collective-permute-start | bytes 196616 | tf_op jit(solution)/shard_map/ppermute | solution.py:338
  30.9 2.8 %collective-permute-done.4.far = bf16[32,1024]{1,0:T(8,128)(2,1)S(1)} collective-permute-done((bf16[32,1024]{1,0:T(8,128)(2,1)S(1)}, bf16[32,1024]{1,0:T(8,128)(2,1)S(1)}, u32[]{:S(2)}, u32[]{:S(2)}) %collective-permute-start.4) | collective-permute-done | bytes 65568 | tf_op jit(solution)/shard_map/ppermute | solution.py:338
  33.7 0.3 shard_map.168
  34.0 8.5 %all_to_all.16.pieces = bf16[8,4,512]{2,1,0:T(4,128)(2,1)S(1)} all-to-all(bf16[8,4,512]{2,1,0:T(4,128)(2,1)S(1)} %shard_map.168), channel_id=1, replica_groups={{28,24,20,16,12,8,4,0},{29,25,21,17,13,9,5,1},{30,26,22,18,14,10,6,2},{..., dimensions={0} | all-to-all | bytes 65536 | tf_op jit(solution)/shard_map/all_to_all | solution.py:233
  42.4 0.6 %shard_map.169 = bf16[4,512]{1,0:T(4,128)(2,1)} custom-call(bf16[8,4,512]{2,1,0:T(4,128)(2,1)S(1)} %all_to_all.16.pieces, f32[3072]{0:T(1024)S(1)} %convert_add_fusion.vectors), custom_call_target="tpu_custom_call" | custom-call | bytes 45056 | tf_op jit(solution)/shard_map/pallas_call | solution.py:221
  (22 shorter events, 0.1 us)
Async XLA Ops:
  1.5 12.2 %all-to-all-start = ((bf16[8,8,256]{2,1,0:T(8,128)(2,1)}), bf16[8,8,256]{2,1,0:T(8,128)(2,1)S(1)}, u32[]{:S(2)}, u32[]{:S(2)}) async-start(bf16[8,8,256]{2,1,0:T(8,128)(2,1)} %shard_map.163), calls=%async_computation | async-start | bytes 65536 | tf_op jit(solution)/shard_map/all_to_all | solution.py:233
  9.4 1.7 %copy-start.2 = (bf16[2,22,32,512]{3,2,1,0:T(8,128)(2,1)S(1)}, bf16[2,22,32,512]{3,2,1,0:T(8,128)(2,1)}, u32[]{:S(2)}) copy-start(bf16[2,22,32,512]{3,2,1,0:T(8,128)(2,1)} %param.24) | copy-start | bytes 4325380
  11.1 0.7 %copy-start.3 = (s32[32,16]{0,1:T(8,128)S(1)}, s32[32,16]{0,1:T(8,128)}, u32[]{:S(2)}) copy-start(s32[32,16]{0,1:T(8,128)} %param.23) | copy-start | bytes 6148
  11.1 0.7 %copy-start.4 = (s32[32]{0:T(128)S(1)}, s32[32]{0:T(128)}, u32[]{:S(2)}) copy-start(s32[32]{0:T(128)} %owner_in.1) | copy-start | bytes 388
  11.1 0.7 %copy-start.10 = (s32[32]{0:T(128)S(1)}, s32[32]{0:T(128)}, u32[]{:S(2)}) copy-start(s32[32]{0:T(128)} %param.21) | copy-start | bytes 388
  11.1 0.7 %copy-start.11 = (s32[32]{0:T(128)S(1)}, s32[32]{0:T(128)}, u32[]{:S(2)}) copy-start(s32[32]{0:T(128)} %param.33) | copy-start | bytes 388
  11.1 1.3 %copy-start.5 = (bf16[1024]{0:T(1024)(128)(2,1)S(1)}, bf16[1024]{0:T(1024)(128)(2,1)}, u32[]{:S(2)}) copy-start(bf16[1024]{0:T(1024)(128)(2,1)} %param.30) | copy-start | bytes 6148
  11.1 1.3 %copy-start.6 = (bf16[512]{0:T(512)(128)(2,1)S(1)}, bf16[512]{0:T(512)(128)(2,1)}, u32[]{:S(2)}) copy-start(bf16[512]{0:T(512)(128)(2,1)} %param.32) | copy-start | bytes 3076
  11.1 1.3 %copy-start.7 = (bf16[512]{0:T(512)(128)(2,1)S(1)}, bf16[512]{0:T(512)(128)(2,1)}, u32[]{:S(2)}) copy-start(bf16[512]{0:T(512)(128)(2,1)} %param.28) | copy-start | bytes 3076
  11.1 1.3 %copy-start.8 = (bf16[512]{0:T(512)(128)(2,1)S(1)}, bf16[512]{0:T(512)(128)(2,1)}, u32[]{:S(2)}) copy-start(bf16[512]{0:T(512)(128)(2,1)} %param.27) | copy-start | bytes 3076
  11.1 1.3 %copy-start.9 = (bf16[512]{0:T(512)(128)(2,1)S(1)}, bf16[512]{0:T(512)(128)(2,1)}, u32[]{:S(2)}) copy-start(bf16[512]{0:T(512)(128)(2,1)} %param.26) | copy-start | bytes 3076
  13.7 14.1 %copy-start.1 = (bf16[1024,512]{1,0:T(8,128)(2,1)S(1)}, bf16[1024,512]{1,0:T(8,128)(2,1)}, u32[]{:S(2)}) copy-start(bf16[1024,512]{1,0:T(8,128)(2,1)} %weight.4) | copy-start | bytes 3145732
  15.5 18.2 %copy-start = (bf16[1024,512]{1,0:T(8,128)(2,1)S(1)}, bf16[1024,512]{1,0:T(8,128)(2,1)}, u32[]{:S(2)}) copy-start(bf16[1024,512]{1,0:T(8,128)(2,1)} %weight.5) | copy-start | bytes 3145732
  15.5 3.4 %collective-permute-start.2 = (bf16[4,2048]{1,0:T(4,128)(2,1)S(1)}, bf16[4,2048]{1,0:T(4,128)(2,1)S(1)}, u32[]{:S(2)}, u32[]{:S(2)}) collective-permute-start(bf16[4,2048]{1,0:T(4,128)(2,1)S(1)} %get-tuple-element.16), channel_id=1, source_target_pairs={{0,3},{1,2},{2,1},{3,0},{4,7},{5,6},{6,5},{7,4},{8,11},{9,10},{10,... | collective-permute-start | bytes 49160 | tf_op jit(solution)/shard_map/ppermute | solution.py:338
  15.6 3.8 %collective-permute-start.1 = (bf16[4,2048]{1,0:T(4,128)(2,1)S(1)}, bf16[4,2048]{1,0:T(4,128)(2,1)S(1)}, u32[]{:S(2)}, u32[]{:S(2)}) collective-permute-start(bf16[4,2048]{1,0:T(4,128)(2,1)S(1)} %get-tuple-element.16), channel_id=1, source_target_pairs={{0,2},{1,3},{2,0},{3,1},{4,6},{5,7},{6,4},{7,5},{8,10},{9,11},{10,... | collective-permute-start | bytes 49160 | tf_op jit(solution)/shard_map/ppermute | solution.py:338
  17.1 2.3 %collective-permute-start = (bf16[4,2048]{1,0:T(4,128)(2,1)S(1)}, bf16[4,2048]{1,0:T(4,128)(2,1)S(1)}, u32[]{:S(2)}, u32[]{:S(2)}) collective-permute-start(bf16[4,2048]{1,0:T(4,128)(2,1)S(1)} %get-tuple-element.16), channel_id=1, source_target_pairs={{0,1},{1,0},{2,3},{3,2},{4,5},{5,4},{6,7},{7,6},{8,9},{9,8},{10,11... | collective-permute-start | bytes 49160 | tf_op jit(solution)/shard_map/ppermute | solution.py:338
  28.3 1.3 %collective-permute-start.3 = (bf16[32,1024]{1,0:T(8,128)(2,1)S(1)}, bf16[32,1024]{1,0:T(8,128)(2,1)S(1)}, u32[]{:S(2)}, u32[]{:S(2)}) collective-permute-start(bf16[32,1024]{1,0:T(8,128)(2,1)S(1)} %shard_map.167), channel_id=1, source_target_pairs={{0,1},{1,0},{2,3},{3,2},{4,5},{5,4},{6,7},{7,6},{8,9},{9,8},{10,11... | collective-permute-start | bytes 196616 | tf_op jit(solution)/shard_map/ppermute | solution.py:338
  29.6 4.1 %collective-permute-start.4 = (bf16[32,1024]{1,0:T(8,128)(2,1)S(1)}, bf16[32,1024]{1,0:T(8,128)(2,1)S(1)}, u32[]{:S(2)}, u32[]{:S(2)}) collective-permute-start(bf16[32,1024]{1,0:T(8,128)(2,1)S(1)} %add_convert_fusion.near), channel_id=1, source_target_pairs={{0,3},{1,2},{2,1},{3,0},{4,7},{5,6},{6,5},{7,4},{8,11},{9,10},{10,... | collective-permute-start | bytes 196616 | tf_op jit(solution)/shard_map/ppermute | solution.py:338

commit v26 on v25

--- a/solution.py
+++ b/solution.py
@@ -12,7 +12,7 @@
 NORM_EPS = 1e-05
 PAIRWISE = 16
 REQ, TP = 8, 4
-ATTENTION_ROOM = 51.2
+ATTENTION_ROOM = 50.6
 ALL_ROOM = 58
 F32, BF16, I32 = jnp.float32, jnp.bfloat16, jnp.int32
 VMEM = pl.BlockSpec(memory_space=pltpu.VMEM)
@@ -136,7 +136,7 @@
     place, arrived, pick, valid, vectors, pool, upper, weight, partial, rounded, lower, sem, *, rows
 ):
     deep = upper.shape[0]
-    copy = pltpu.make_async_copy(weight.at[pl.ds(deep, deep)], lower, sem)
+    copy = pltpu.make_async_copy(weight.at[pl.ds(deep, lower.shape[0])], lower, sem)
     copy.start()
     half = arrived.shape[2]
     cols = 2 * half
@@ -297,7 +297,7 @@
 
     here = position[0] >= 0
     pool = jnp.where(here, kv_pool, jnp.zeros_like(kv_pool))
-    upper = out_weight[: cols // 2]
+    upper = out_weight[: 3 * cols // 4]
     upper = jnp.where(here, upper, jnp.zeros_like(upper))
 
     partial, rounded = call(
@@ -305,7 +305,7 @@
         [arr((rows, width), F32), arr((rows, width))],
         [VMEM] * 7 + [HBM],
         [place, arrived, pick, valid, vectors, pool, upper, out_weight],
-        [pltpu.VMEM(upper.shape, BF16), pltpu.SemaphoreType.DMA],
+        [pltpu.VMEM((cols - upper.shape[0], width), BF16), pltpu.SemaphoreType.DMA],
         room=ATTENTION_ROOM,
         rows=rows,
     )

time: 43.4 us -> 43.5 us (level)
    select_n x1, other arithmetic: 0.1 us -> 1.59 us  [on_pairs(): pool = jnp.where(here, kv_pool, jnp.zeros_like(kv_pool))]
    select_n x1, other arithmetic: 1.39 us -> 0.11 us  [on_pairs(): upper = jnp.where(here, upper, jnp.zeros_like(upper))]
  transfers between devices with their start and end apart: 6 -> 6, of which waited for: 5 -> 5; matrix products, arithmetic and copies ran while one was open for 4% -> 5% of each run, Pallas kernels for 1% -> 1%
where the time goes in v26:
time: 43.5 us; the launch traced here: 43.1 us
  blocking collectives  16.9 us (39%)
  starting transfers between devices  10.9 us (25%)
  waiting for transfers between devices  7.21 us (17%)
  Pallas kernels  5.11 us (12%)
  other arithmetic  1.88 us (4%)
  local copies, waits for them, and re-layouts  0.98 us (2%)
    all_to_all x2, blocking collectives, trade(): lax.all_to_all(blocks, 'req', 0, 0, tiled=True, axis_index_groups=[group])  16.9 us
    all_to_all x1, starting transfers between devices, trade(): lax.all_to_all(blocks, 'req', 0, 0, tiled=True, axis_index_groups=[group])  7.85 us
    ppermute x5, waiting for transfers between devices, swap(): return lax.ppermute(x, axis, [(i, i ^ step) for i in range(n)])  6.26 us
    pallas_call x7, Pallas kernels, call(): pl.pallas_call(functools.partial(kernel, **fixed) if fixed else kernel, o...  5.11 us
    ppermute x5, starting transfers between devices, swap(): return lax.ppermute(x, axis, [(i, i ^ step) for i in range(n)])  3.01 us
    select_n x1, other arithmetic, on_pairs(): pool = jnp.where(here, kv_pool, jnp.zeros_like(kv_pool))  1.59 us
    all_to_all x1, waiting for transfers between devices, trade(): lax.all_to_all(blocks, 'req', 0, 0, tiled=True, axis_index_groups=[group])  0.95 us
  transfers between devices with their start and end apart: 6, of which 5 were waited for; matrix products, arithmetic and copies ran while one was open for 5% of the time, Pallas kernels for 1%

profile of v26, /device:TPU:0, one launch (start us, length us, event | category | flops | bytes accessed | tf_op | source)
XLA Modules:
  0.0 43.1 jit_solution(17914586384097564845)
XLA Ops:
  0.0 1.5 %shard_map.163 = bf16[8,8,256]{2,1,0:T(8,128)(2,1)} custom-call(s32[32]{0:T(128)} %owner_in.1, bf16[4,512]{1,0:T(4,128)(2,1)} %query.1, bf16[4,512]{1,0:T(4,128)(2,1)} %key.1, bf16[4,512]{1,0:T(4,128)(2,1)} %value.1, bf16[4,512]{1,0:T(4,128)(2,1)} %resid.1), custom_call_target="tpu_custom_call" | custom-call | bytes 16512 | tf_op jit(solution)/shard_map/pallas_call | solution.py:221
  1.5 7.9 %all-to-all-start = ((bf16[8,8,256]{2,1,0:T(8,128)(2,1)}), bf16[8,8,256]{2,1,0:T(8,128)(2,1)S(1)}, u32[]{:S(2)}, u32[]{:S(2)}) async-start(bf16[8,8,256]{2,1,0:T(8,128)(2,1)} %shard_map.163), calls=%async_computation | async-start | bytes 65536 | tf_op jit(solution)/shard_map/all_to_all | solution.py:233
  9.4 0.1 pad.60
  9.5 1.6 %broadcast_select_fusion.pool = bf16[2,22,32,512]{3,2,1,0:T(8,128)(2,1)S(1)} fusion(bf16[2,22,32,512]{3,2,1,0:T(8,128)(2,1)} %param.24, pred[]{:T(512)S(6)} %ge.3), kind=kLoop, calls=%fused_computation.1 | loop fusion | flops 720896 | bytes 2883585 | tf_op jit(solution)/shard_map/jit(_where)/select_n | solution.py:299
  11.1 0.3 copy-done.2
  11.4 0.0 copy-start.5
  11.4 0.0 copy-start.6
  11.5 0.0 copy-start.9
  11.5 0.1 slice_select_fusion.upper
  11.6 0.1 pad_add_fusion.1
  11.7 0.4 copy-done.3
  12.1 0.1 pad_add_fusion.numbers
  12.2 0.1 broadcast_in_dim.24.place
  12.3 0.4 shard_map.164
  12.7 1.0 %all-to-all-done.arrived = bf16[8,8,256]{2,1,0:T(8,128)(2,1)S(1)} async-done(((bf16[8,8,256]{2,1,0:T(8,128)(2,1)}), bf16[8,8,256]{2,1,0:T(8,128)(2,1)S(1)}, u32[]{:S(2)}, u32[]{:S(2)}) %all-to-all-start) | async-done | bytes 32800 | tf_op jit(solution)/shard_map/all_to_all | solution.py:233
  13.7 1.6 %shard_map.165 = (f32[4,2048]{1,0:T(4,128)S(1)}, bf16[4,2048]{1,0:T(4,128)(2,1)S(1)}) custom-call(s32[2,128]{1,0:T(2,128)S(1)} %broadcast_in_dim.24.place, bf16[8,8,256]{2,1,0:T(8,128)(2,1)S(1)} %all-to-all-done.arrived, bf16[56,64]{1,0:T(8,128)(2,1)S(1)} %get-tuple-element.13.pick, f32[16,704]{1,0:T(8,128)S(1)} %get-tuple-element.14.valid, ...), custom_call_target="tpu_custom_call" | custom-call | bytes 5210112 | tf_op jit(solution)/shard_map/pallas_call | solution.py:221
  15.3 0.0 copy-start
  15.3 0.1 collective-permute-start.2
  15.4 1.6 %collective-permute-start.1 = (bf16[4,2048]{1,0:T(4,128)(2,1)S(1)}, bf16[4,2048]{1,0:T(4,128)(2,1)S(1)}, u32[]{:S(2)}, u32[]{:S(2)}) collective-permute-start(bf16[4,2048]{1,0:T(4,128)(2,1)S(1)} %get-tuple-element.16), channel_id=1, source_target_pairs={{0,2},{1,3},{2,0},{3,1},{4,6},{5,7},{6,4},{7,5},{8,10},{9,11},{10,... | collective-permute-start | bytes 49160 | tf_op jit(solution)/shard_map/ppermute | solution.py:338
  17.0 0.3 collective-permute-start
  17.3 1.4 %collective-permute-done.2.far_sibling = bf16[4,2048]{1,0:T(4,128)(2,1)S(1)} collective-permute-done((bf16[4,2048]{1,0:T(4,128)(2,1)S(1)}, bf16[4,2048]{1,0:T(4,128)(2,1)S(1)}, u32[]{:S(2)}, u32[]{:S(2)}) %collective-permute-start.2) | collective-permute-done | bytes 16416 | tf_op jit(solution)/shard_map/ppermute | solution.py:338
  18.7 0.5 %collective-permute-done.1.far = bf16[4,2048]{1,0:T(4,128)(2,1)S(1)} collective-permute-done((bf16[4,2048]{1,0:T(4,128)(2,1)S(1)}, bf16[4,2048]{1,0:T(4,128)(2,1)S(1)}, u32[]{:S(2)}, u32[]{:S(2)}) %collective-permute-start.1) | collective-permute-done | bytes 16416 | tf_op jit(solution)/shard_map/ppermute | solution.py:338
  19.2 0.2 shard_map.166
  19.4 8.4 %all_to_all.15.rows_in = bf16[8,4,512]{2,1,0:T(4,128)(2,1)S(1)} all-to-all(bf16[8,4,512]{2,1,0:T(4,128)(2,1)S(1)} %get-tuple-element.17), channel_id=1, replica_groups={{12,16,4,24,8,20,0,28},{13,17,5,25,9,21,1,29},{14,18,6,26,10,22,2,30},{..., dimensions={0} | all-to-all | bytes 65536 | tf_op jit(solution)/shard_map/all_to_all | solution.py:233
  27.9 0.5 %shard_map.167 = bf16[32,1024]{1,0:T(8,128)(2,1)S(1)} custom-call(bf16[8,4,512]{2,1,0:T(4,128)(2,1)S(1)} %all_to_all.15.rows_in, bf16[32,32]{1,0:T(8,128)(2,1)S(1)} %get-tuple-element.18.arrange, bf16[1024,512]{1,0:T(8,128)(2,1)S(1)} %copy-done.1), custom_call_target="tpu_custom_call" | custom-call | bytes 1083392 | tf_op jit(solution)/shard_map/pallas_call | solution.py:221
  28.3 0.0 collective-permute-start.3
  28.4 1.2 %collective-permute-done.3 = bf16[32,1024]{1,0:T(8,128)(2,1)S(1)} collective-permute-done((bf16[32,1024]{1,0:T(8,128)(2,1)S(1)}, bf16[32,1024]{1,0:T(8,128)(2,1)S(1)}, u32[]{:S(2)}, u32[]{:S(2)}) %collective-permute-start.3) | collective-permute-done | bytes 65568 | tf_op jit(solution)/shard_map/ppermute | solution.py:338
  29.6 1.1 %collective-permute-start.4 = (bf16[32,1024]{1,0:T(8,128)(2,1)S(1)}, bf16[32,1024]{1,0:T(8,128)(2,1)S(1)}, u32[]{:S(2)}, u32[]{:S(2)}) collective-permute-start(bf16[32,1024]{1,0:T(8,128)(2,1)S(1)} %add_convert_fusion.near), channel_id=1, source_target_pairs={{0,3},{1,2},{2,1},{3,0},{4,7},{5,6},{6,5},{7,4},{8,11},{9,10},{10,... | collective-permute-start | bytes 196616 | tf_op jit(solution)/shard_map/ppermute | solution.py:338
  30.7 3.1 %collective-permute-done.4.far = bf16[32,1024]{1,0:T(8,128)(2,1)S(1)} collective-permute-done((bf16[32,1024]{1,0:T(8,128)(2,1)S(1)}, bf16[32,1024]{1,0:T(8,128)(2,1)S(1)}, u32[]{:S(2)}, u32[]{:S(2)}) %collective-permute-start.4) | collective-permute-done | bytes 65568 | tf_op jit(solution)/shard_map/ppermute | solution.py:338
  33.8 0.3 shard_map.168
  34.0 8.5 %all_to_all.16.pieces = bf16[8,4,512]{2,1,0:T(4,128)(2,1)S(1)} all-to-all(bf16[8,4,512]{2,1,0:T(4,128)(2,1)S(1)} %shard_map.168), channel_id=1, replica_groups={{28,24,20,16,12,8,4,0},{29,25,21,17,13,9,5,1},{30,26,22,18,14,10,6,2},{..., dimensions={0} | all-to-all | bytes 65536 | tf_op jit(solution)/shard_map/all_to_all | solution.py:233
  42.5 0.6 %shard_map.169 = bf16[4,512]{1,0:T(4,128)(2,1)} custom-call(bf16[8,4,512]{2,1,0:T(4,128)(2,1)S(1)} %all_to_all.16.pieces, f32[3072]{0:T(1024)S(1)} %convert_add_fusion.vectors), custom_call_target="tpu_custom_call" | custom-call | bytes 45056 | tf_op jit(solution)/shard_map/pallas_call | solution.py:221
  (22 shorter events, 0.1 us)
Async XLA Ops:
  1.5 12.2 %all-to-all-start = ((bf16[8,8,256]{2,1,0:T(8,128)(2,1)}), bf16[8,8,256]{2,1,0:T(8,128)(2,1)S(1)}, u32[]{:S(2)}, u32[]{:S(2)}) async-start(bf16[8,8,256]{2,1,0:T(8,128)(2,1)} %shard_map.163), calls=%async_computation | async-start | bytes 65536 | tf_op jit(solution)/shard_map/all_to_all | solution.py:233
  9.4 2.0 %copy-start.2 = (bf16[512,2048]{1,0:T(8,128)(2,1)S(1)}, bf16[512,2048]{1,0:T(8,128)(2,1)}, u32[]{:S(2)}) copy-start(bf16[512,2048]{1,0:T(8,128)(2,1)} %weight.3) | copy-start | bytes 6291460
  11.4 0.7 %copy-start.3 = (s32[32,16]{0,1:T(8,128)S(1)}, s32[32,16]{0,1:T(8,128)}, u32[]{:S(2)}) copy-start(s32[32,16]{0,1:T(8,128)} %param.23) | copy-start | bytes 6148
  11.4 0.7 %copy-start.4 = (s32[32]{0:T(128)S(1)}, s32[32]{0:T(128)}, u32[]{:S(2)}) copy-start(s32[32]{0:T(128)} %owner_in.1) | copy-start | bytes 388
  11.4 0.7 %copy-start.10 = (s32[32]{0:T(128)S(1)}, s32[32]{0:T(128)}, u32[]{:S(2)}) copy-start(s32[32]{0:T(128)} %param.21) | copy-start | bytes 388
  11.4 0.7 %copy-start.11 = (s32[32]{0:T(128)S(1)}, s32[32]{0:T(128)}, u32[]{:S(2)}) copy-start(s32[32]{0:T(128)} %param.33) | copy-start | bytes 388
  11.4 1.3 %copy-start.5 = (bf16[1024]{0:T(1024)(128)(2,1)S(1)}, bf16[1024]{0:T(1024)(128)(2,1)}, u32[]{:S(2)}) copy-start(bf16[1024]{0:T(1024)(128)(2,1)} %param.30) | copy-start | bytes 6148
  11.4 1.3 %copy-start.6 = (bf16[512]{0:T(512)(128)(2,1)S(1)}, bf16[512]{0:T(512)(128)(2,1)}, u32[]{:S(2)}) copy-start(bf16[512]{0:T(512)(128)(2,1)} %param.32) | copy-start | bytes 3076
  11.4 1.3 %copy-start.7 = (bf16[512]{0:T(512)(128)(2,1)S(1)}, bf16[512]{0:T(512)(128)(2,1)}, u32[]{:S(2)}) copy-start(bf16[512]{0:T(512)(128)(2,1)} %param.28) | copy-start | bytes 3076
  11.5 1.3 %copy-start.8 = (bf16[512]{0:T(512)(128)(2,1)S(1)}, bf16[512]{0:T(512)(128)(2,1)}, u32[]{:S(2)}) copy-start(bf16[512]{0:T(512)(128)(2,1)} %param.27) | copy-start | bytes 3076
  11.5 1.3 %copy-start.9 = (bf16[512]{0:T(512)(128)(2,1)S(1)}, bf16[512]{0:T(512)(128)(2,1)}, u32[]{:S(2)}) copy-start(bf16[512]{0:T(512)(128)(2,1)} %param.26) | copy-start | bytes 3076
  13.7 14.2 %copy-start.1 = (bf16[1024,512]{1,0:T(8,128)(2,1)S(1)}, bf16[1024,512]{1,0:T(8,128)(2,1)}, u32[]{:S(2)}) copy-start(bf16[1024,512]{1,0:T(8,128)(2,1)} %weight.4) | copy-start | bytes 3145732
  15.3 18.4 %copy-start = (bf16[1024,512]{1,0:T(8,128)(2,1)S(1)}, bf16[1024,512]{1,0:T(8,128)(2,1)}, u32[]{:S(2)}) copy-start(bf16[1024,512]{1,0:T(8,128)(2,1)} %weight.5) | copy-start | bytes 3145732
  15.3 3.4 %collective-permute-start.2 = (bf16[4,2048]{1,0:T(4,128)(2,1)S(1)}, bf16[4,2048]{1,0:T(4,128)(2,1)S(1)}, u32[]{:S(2)}, u32[]{:S(2)}) collective-permute-start(bf16[4,2048]{1,0:T(4,128)(2,1)S(1)} %get-tuple-element.16), channel_id=1, source_target_pairs={{0,3},{1,2},{2,1},{3,0},{4,7},{5,6},{6,5},{7,4},{8,11},{9,10},{10,... | collective-permute-start | bytes 49160 | tf_op jit(solution)/shard_map/ppermute | solution.py:338
  15.4 3.8 %collective-permute-start.1 = (bf16[4,2048]{1,0:T(4,128)(2,1)S(1)}, bf16[4,2048]{1,0:T(4,128)(2,1)S(1)}, u32[]{:S(2)}, u32[]{:S(2)}) collective-permute-start(bf16[4,2048]{1,0:T(4,128)(2,1)S(1)} %get-tuple-element.16), channel_id=1, source_target_pairs={{0,2},{1,3},{2,0},{3,1},{4,6},{5,7},{6,4},{7,5},{8,10},{9,11},{10,... | collective-permute-start | bytes 49160 | tf_op jit(solution)/shard_map/ppermute | solution.py:338
  17.0 2.3 %collective-permute-start = (bf16[4,2048]{1,0:T(4,128)(2,1)S(1)}, bf16[4,2048]{1,0:T(4,128)(2,1)S(1)}, u32[]{:S(2)}, u32[]{:S(2)}) collective-permute-start(bf16[4,2048]{1,0:T(4,128)(2,1)S(1)} %get-tuple-element.16), channel_id=1, source_target_pairs={{0,1},{1,0},{2,3},{3,2},{4,5},{5,4},{6,7},{7,6},{8,9},{9,8},{10,11... | collective-permute-start | bytes 49160 | tf_op jit(solution)/shard_map/ppermute | solution.py:338
  28.3 1.3 %collective-permute-start.3 = (bf16[32,1024]{1,0:T(8,128)(2,1)S(1)}, bf16[32,1024]{1,0:T(8,128)(2,1)S(1)}, u32[]{:S(2)}, u32[]{:S(2)}) collective-permute-start(bf16[32,1024]{1,0:T(8,128)(2,1)S(1)} %shard_map.167), channel_id=1, source_target_pairs={{0,1},{1,0},{2,3},{3,2},{4,5},{5,4},{6,7},{7,6},{8,9},{9,8},{10,11... | collective-permute-start | bytes 196616 | tf_op jit(solution)/shard_map/ppermute | solution.py:338
  29.6 4.1 %collective-permute-start.4 = (bf16[32,1024]{1,0:T(8,128)(2,1)S(1)}, bf16[32,1024]{1,0:T(8,128)(2,1)S(1)}, u32[]{:S(2)}, u32[]{:S(2)}) collective-permute-start(bf16[32,1024]{1,0:T(8,128)(2,1)S(1)} %add_convert_fusion.near), channel_id=1, source_target_pairs={{0,3},{1,2},{2,1},{3,0},{4,7},{5,6},{6,5},{7,4},{8,11},{9,10},{10,... | collective-permute-start | bytes 196616 | tf_op jit(solution)/shard_map/ppermute | solution.py:338

commit v27 on v25

--- a/solution.py
+++ b/solution.py
@@ -18,8 +18,8 @@
 VMEM = pl.BlockSpec(memory_space=pltpu.VMEM)
 HBM = pl.BlockSpec(memory_space=pltpu.HBM)
 
-FIRST_ORDER = [3, 5, 2, 4, 1, 7, 0, 6]
-MIDDLE_ORDER = [3, 4, 1, 6, 2, 5, 0, 7]
+FIRST_ORDER = [4, 2, 5, 3, 6, 0, 7, 1]
+MIDDLE_ORDER = [4, 3, 6, 1, 5, 2, 7, 0]
 LAST_ORDER = [7, 6, 5, 4, 3, 2, 1, 0]
 
 

time: 43.4 us -> 43.6 us (level)
  no operation moved by 1% of the time
where the time goes in v27:
time: 43.6 us; the launch traced here: 43.2 us
  blocking collectives  17 us (39%)
  starting transfers between devices  11.1 us (25%)
  waiting for transfers between devices  7.14 us (16%)
  Pallas kernels  5.28 us (12%)
  other arithmetic  1.67 us (4%)
  local copies, waits for them, and re-layouts  0.84 us (2%)
    all_to_all x2, blocking collectives, trade(): lax.all_to_all(blocks, 'req', 0, 0, tiled=True, axis_index_groups=[group])  17 us
    all_to_all x1, starting transfers between devices, trade(): lax.all_to_all(blocks, 'req', 0, 0, tiled=True, axis_index_groups=[group])  7.85 us
    ppermute x5, waiting for transfers between devices, swap(): return lax.ppermute(x, axis, [(i, i ^ step) for i in range(n)])  6.02 us
    pallas_call x7, Pallas kernels, call(): pl.pallas_call(functools.partial(kernel, **fixed) if fixed else kernel, o...  5.28 us
    ppermute x5, starting transfers between devices, swap(): return lax.ppermute(x, axis, [(i, i ^ step) for i in range(n)])  3.25 us
    select_n x1, other arithmetic, on_pairs(): upper = jnp.where(here, upper, jnp.zeros_like(upper))  1.39 us
    all_to_all x1, waiting for transfers between devices, trade(): lax.all_to_all(blocks, 'req', 0, 0, tiled=True, axis_index_groups=[group])  1.13 us
  transfers between devices with their start and end apart: 6, of which 5 were waited for; matrix products, arithmetic and copies ran while one was open for 4% of the time, Pallas kernels for 1%

profile of v27, /device:TPU:0, one launch (start us, length us, event | category | flops | bytes accessed | tf_op | source)
XLA Modules:
  0.0 43.2 jit_solution(17329775654164246969)
XLA Ops:
  0.0 1.5 %shard_map.163 = bf16[8,8,256]{2,1,0:T(8,128)(2,1)} custom-call(s32[32]{0:T(128)} %owner_in.1, bf16[4,512]{1,0:T(4,128)(2,1)} %query.1, bf16[4,512]{1,0:T(4,128)(2,1)} %key.1, bf16[4,512]{1,0:T(4,128)(2,1)} %value.1, bf16[4,512]{1,0:T(4,128)(2,1)} %resid.1), custom_call_target="tpu_custom_call" | custom-call | bytes 16512 | tf_op jit(solution)/shard_map/pallas_call | solution.py:221
  1.5 7.9 %all-to-all-start = ((bf16[8,8,256]{2,1,0:T(8,128)(2,1)}), bf16[8,8,256]{2,1,0:T(8,128)(2,1)S(1)}, u32[]{:S(2)}, u32[]{:S(2)}) async-start(bf16[8,8,256]{2,1,0:T(8,128)(2,1)} %shard_map.163), calls=%async_computation | async-start | bytes 65536 | tf_op jit(solution)/shard_map/all_to_all | solution.py:233
  9.4 0.1 pad.60
  9.5 1.4 %slice_select_fusion.upper = bf16[256,2048]{1,0:T(8,128)(2,1)S(1)} fusion(bf16[512,2048]{1,0:T(8,128)(2,1)} %weight.3, pred[]{:T(512)S(6)} %ge.3), kind=kLoop, calls=%fused_computation.1 | loop fusion | flops 524288 | bytes 2097153 | tf_op jit(solution)/shard_map/jit(_where)/select_n | solution.py:301
  10.9 0.2 copy-done.2
  11.1 0.0 copy-start.5
  11.1 0.0 copy-start.8
  11.1 0.0 copy-start.9
  11.1 0.1 broadcast_select_fusion.pool
  11.2 0.1 pad_add_fusion.1
  11.3 0.4 %copy-done.3 = s32[32,16]{0,1:T(8,128)S(1)} copy-done((s32[32,16]{0,1:T(8,128)S(1)}, s32[32,16]{0,1:T(8,128)}, u32[]{:S(2)}) %copy-start.3) | copy-done | bytes 2072
  11.8 0.1 pad_add_fusion.numbers
  11.8 0.1 broadcast_in_dim.24.place
  11.9 0.4 shard_map.164
  12.4 1.1 %all-to-all-done.arrived = bf16[8,8,256]{2,1,0:T(8,128)(2,1)S(1)} async-done(((bf16[8,8,256]{2,1,0:T(8,128)(2,1)}), bf16[8,8,256]{2,1,0:T(8,128)(2,1)S(1)}, u32[]{:S(2)}, u32[]{:S(2)}) %all-to-all-start) | async-done | bytes 32800 | tf_op jit(solution)/shard_map/all_to_all | solution.py:233
  13.5 1.8 %shard_map.165 = (f32[4,2048]{1,0:T(4,128)S(1)}, bf16[4,2048]{1,0:T(4,128)(2,1)S(1)}) custom-call(s32[2,128]{1,0:T(2,128)S(1)} %broadcast_in_dim.24.place, bf16[8,8,256]{2,1,0:T(8,128)(2,1)S(1)} %all-to-all-done.arrived, bf16[56,64]{1,0:T(8,128)(2,1)S(1)} %get-tuple-element.13.pick, f32[16,704]{1,0:T(8,128)S(1)} %get-tuple-element.14.valid, ...), custom_call_target="tpu_custom_call" | custom-call | bytes 4685824 | tf_op jit(solution)/shard_map/pallas_call | solution.py:221
  15.3 0.0 copy-start
  15.3 0.1 collective-permute-start.2
  15.4 1.6 %collective-permute-start.1 = (bf16[4,2048]{1,0:T(4,128)(2,1)S(1)}, bf16[4,2048]{1,0:T(4,128)(2,1)S(1)}, u32[]{:S(2)}, u32[]{:S(2)}) collective-permute-start(bf16[4,2048]{1,0:T(4,128)(2,1)S(1)} %get-tuple-element.16), channel_id=1, source_target_pairs={{0,2},{1,3},{2,0},{3,1},{4,6},{5,7},{6,4},{7,5},{8,10},{9,11},{10,... | collective-permute-start | bytes 49160 | tf_op jit(solution)/shard_map/ppermute | solution.py:338
  17.0 0.3 collective-permute-start
  17.3 1.4 %collective-permute-done.2.far_sibling = bf16[4,2048]{1,0:T(4,128)(2,1)S(1)} collective-permute-done((bf16[4,2048]{1,0:T(4,128)(2,1)S(1)}, bf16[4,2048]{1,0:T(4,128)(2,1)S(1)}, u32[]{:S(2)}, u32[]{:S(2)}) %collective-permute-start.2) | collective-permute-done | bytes 16416 | tf_op jit(solution)/shard_map/ppermute | solution.py:338
  18.7 0.5 %collective-permute-done.1.far = bf16[4,2048]{1,0:T(4,128)(2,1)S(1)} collective-permute-done((bf16[4,2048]{1,0:T(4,128)(2,1)S(1)}, bf16[4,2048]{1,0:T(4,128)(2,1)S(1)}, u32[]{:S(2)}, u32[]{:S(2)}) %collective-permute-start.1) | collective-permute-done | bytes 16416 | tf_op jit(solution)/shard_map/ppermute | solution.py:338
  19.2 0.2 shard_map.166
  19.4 8.6 %all_to_all.15.rows_in = bf16[8,4,512]{2,1,0:T(4,128)(2,1)S(1)} all-to-all(bf16[8,4,512]{2,1,0:T(4,128)(2,1)S(1)} %get-tuple-element.17), channel_id=1, replica_groups={{16,12,24,4,20,8,28,0},{17,13,25,5,21,9,29,1},{18,14,26,6,22,10,30,2},{..., dimensions={0} | all-to-all | bytes 65536 | tf_op jit(solution)/shard_map/all_to_all | solution.py:233
  28.0 0.5 %shard_map.167 = bf16[32,1024]{1,0:T(8,128)(2,1)S(1)} custom-call(bf16[8,4,512]{2,1,0:T(4,128)(2,1)S(1)} %all_to_all.15.rows_in, bf16[32,32]{1,0:T(8,128)(2,1)S(1)} %get-tuple-element.18.arrange, bf16[1024,512]{1,0:T(8,128)(2,1)S(1)} %copy-done.1), custom_call_target="tpu_custom_call" | custom-call | bytes 1083392 | tf_op jit(solution)/shard_map/pallas_call | solution.py:221
  28.4 0.0 collective-permute-start.3
  28.5 1.2 %collective-permute-done.3 = bf16[32,1024]{1,0:T(8,128)(2,1)S(1)} collective-permute-done((bf16[32,1024]{1,0:T(8,128)(2,1)S(1)}, bf16[32,1024]{1,0:T(8,128)(2,1)S(1)}, u32[]{:S(2)}, u32[]{:S(2)}) %collective-permute-start.3) | collective-permute-done | bytes 65568 | tf_op jit(solution)/shard_map/ppermute | solution.py:338
  29.7 1.3 %collective-permute-start.4 = (bf16[32,1024]{1,0:T(8,128)(2,1)S(1)}, bf16[32,1024]{1,0:T(8,128)(2,1)S(1)}, u32[]{:S(2)}, u32[]{:S(2)}) collective-permute-start(bf16[32,1024]{1,0:T(8,128)(2,1)S(1)} %add_convert_fusion.near), channel_id=1, source_target_pairs={{0,3},{1,2},{2,1},{3,0},{4,7},{5,6},{6,5},{7,4},{8,11},{9,10},{10,... | collective-permute-start | bytes 196616 | tf_op jit(solution)/shard_map/ppermute | solution.py:338
  31.0 2.8 %collective-permute-done.4.far = bf16[32,1024]{1,0:T(8,128)(2,1)S(1)} collective-permute-done((bf16[32,1024]{1,0:T(8,128)(2,1)S(1)}, bf16[32,1024]{1,0:T(8,128)(2,1)S(1)}, u32[]{:S(2)}, u32[]{:S(2)}) %collective-permute-start.4) | collective-permute-done | bytes 65568 | tf_op jit(solution)/shard_map/ppermute | solution.py:338
  33.9 0.3 shard_map.168
  34.1 8.5 %all_to_all.16.pieces = bf16[8,4,512]{2,1,0:T(4,128)(2,1)S(1)} all-to-all(bf16[8,4,512]{2,1,0:T(4,128)(2,1)S(1)} %shard_map.168), channel_id=1, replica_groups={{28,24,20,16,12,8,4,0},{29,25,21,17,13,9,5,1},{30,26,22,18,14,10,6,2},{..., dimensions={0} | all-to-all | bytes 65536 | tf_op jit(solution)/shard_map/all_to_all | solution.py:233
  42.6 0.6 %shard_map.169 = bf16[4,512]{1,0:T(4,128)(2,1)} custom-call(bf16[8,4,512]{2,1,0:T(4,128)(2,1)S(1)} %all_to_all.16.pieces, f32[3072]{0:T(1024)S(1)} %convert_add_fusion.vectors), custom_call_target="tpu_custom_call" | custom-call | bytes 45056 | tf_op jit(solution)/shard_map/pallas_call | solution.py:221
  (22 shorter events, 0.1 us)
Async XLA Ops:
  1.5 12.0 %all-to-all-start = ((bf16[8,8,256]{2,1,0:T(8,128)(2,1)}), bf16[8,8,256]{2,1,0:T(8,128)(2,1)S(1)}, u32[]{:S(2)}, u32[]{:S(2)}) async-start(bf16[8,8,256]{2,1,0:T(8,128)(2,1)} %shard_map.163), calls=%async_computation | async-start | bytes 65536 | tf_op jit(solution)/shard_map/all_to_all | solution.py:233
  9.4 1.7 %copy-start.2 = (bf16[2,22,32,512]{3,2,1,0:T(8,128)(2,1)S(1)}, bf16[2,22,32,512]{3,2,1,0:T(8,128)(2,1)}, u32[]{:S(2)}) copy-start(bf16[2,22,32,512]{3,2,1,0:T(8,128)(2,1)} %param.24) | copy-start | bytes 4325380
  11.1 0.7 %copy-start.3 = (s32[32,16]{0,1:T(8,128)S(1)}, s32[32,16]{0,1:T(8,128)}, u32[]{:S(2)}) copy-start(s32[32,16]{0,1:T(8,128)} %param.23) | copy-start | bytes 6148
  11.1 0.7 %copy-start.4 = (s32[32]{0:T(128)S(1)}, s32[32]{0:T(128)}, u32[]{:S(2)}) copy-start(s32[32]{0:T(128)} %owner_in.1) | copy-start | bytes 388
  11.1 0.7 %copy-start.10 = (s32[32]{0:T(128)S(1)}, s32[32]{0:T(128)}, u32[]{:S(2)}) copy-start(s32[32]{0:T(128)} %param.21) | copy-start | bytes 388
  11.1 0.7 %copy-start.11 = (s32[32]{0:T(128)S(1)}, s32[32]{0:T(128)}, u32[]{:S(2)}) copy-start(s32[32]{0:T(128)} %param.33) | copy-start | bytes 388
  11.1 1.3 %copy-start.5 = (bf16[1024]{0:T(1024)(128)(2,1)S(1)}, bf16[1024]{0:T(1024)(128)(2,1)}, u32[]{:S(2)}) copy-start(bf16[1024]{0:T(1024)(128)(2,1)} %param.30) | copy-start | bytes 6148
  11.1 1.3 %copy-start.6 = (bf16[512]{0:T(512)(128)(2,1)S(1)}, bf16[512]{0:T(512)(128)(2,1)}, u32[]{:S(2)}) copy-start(bf16[512]{0:T(512)(128)(2,1)} %param.32) | copy-start | bytes 3076
  11.1 1.3 %copy-start.7 = (bf16[512]{0:T(512)(128)(2,1)S(1)}, bf16[512]{0:T(512)(128)(2,1)}, u32[]{:S(2)}) copy-start(bf16[512]{0:T(512)(128)(2,1)} %param.28) | copy-start | bytes 3076
  11.1 1.3 %copy-start.8 = (bf16[512]{0:T(512)(128)(2,1)S(1)}, bf16[512]{0:T(512)(128)(2,1)}, u32[]{:S(2)}) copy-start(bf16[512]{0:T(512)(128)(2,1)} %param.27) | copy-start | bytes 3076
  11.1 1.3 %copy-start.9 = (bf16[512]{0:T(512)(128)(2,1)S(1)}, bf16[512]{0:T(512)(128)(2,1)}, u32[]{:S(2)}) copy-start(bf16[512]{0:T(512)(128)(2,1)} %param.26) | copy-start | bytes 3076
  13.5 14.4 %copy-start.1 = (bf16[1024,512]{1,0:T(8,128)(2,1)S(1)}, bf16[1024,512]{1,0:T(8,128)(2,1)}, u32[]{:S(2)}) copy-start(bf16[1024,512]{1,0:T(8,128)(2,1)} %weight.4) | copy-start | bytes 3145732
  15.3 18.5 %copy-start = (bf16[1024,512]{1,0:T(8,128)(2,1)S(1)}, bf16[1024,512]{1,0:T(8,128)(2,1)}, u32[]{:S(2)}) copy-start(bf16[1024,512]{1,0:T(8,128)(2,1)} %weight.5) | copy-start | bytes 3145732
  15.3 3.4 %collective-permute-start.2 = (bf16[4,2048]{1,0:T(4,128)(2,1)S(1)}, bf16[4,2048]{1,0:T(4,128)(2,1)S(1)}, u32[]{:S(2)}, u32[]{:S(2)}) collective-permute-start(bf16[4,2048]{1,0:T(4,128)(2,1)S(1)} %get-tuple-element.16), channel_id=1, source_target_pairs={{0,3},{1,2},{2,1},{3,0},{4,7},{5,6},{6,5},{7,4},{8,11},{9,10},{10,... | collective-permute-start | bytes 49160 | tf_op jit(solution)/shard_map/ppermute | solution.py:338
  15.4 3.8 %collective-permute-start.1 = (bf16[4,2048]{1,0:T(4,128)(2,1)S(1)}, bf16[4,2048]{1,0:T(4,128)(2,1)S(1)}, u32[]{:S(2)}, u32[]{:S(2)}) collective-permute-start(bf16[4,2048]{1,0:T(4,128)(2,1)S(1)} %get-tuple-element.16), channel_id=1, source_target_pairs={{0,2},{1,3},{2,0},{3,1},{4,6},{5,7},{6,4},{7,5},{8,10},{9,11},{10,... | collective-permute-start | bytes 49160 | tf_op jit(solution)/shard_map/ppermute | solution.py:338
  17.0 2.3 %collective-permute-start = (bf16[4,2048]{1,0:T(4,128)(2,1)S(1)}, bf16[4,2048]{1,0:T(4,128)(2,1)S(1)}, u32[]{:S(2)}, u32[]{:S(2)}) collective-permute-start(bf16[4,2048]{1,0:T(4,128)(2,1)S(1)} %get-tuple-element.16), channel_id=1, source_target_pairs={{0,1},{1,0},{2,3},{3,2},{4,5},{5,4},{6,7},{7,6},{8,9},{9,8},{10,11... | collective-permute-start | bytes 49160 | tf_op jit(solution)/shard_map/ppermute | solution.py:338
  28.4 1.3 %collective-permute-start.3 = (bf16[32,1024]{1,0:T(8,128)(2,1)S(1)}, bf16[32,1024]{1,0:T(8,128)(2,1)S(1)}, u32[]{:S(2)}, u32[]{:S(2)}) collective-permute-start(bf16[32,1024]{1,0:T(8,128)(2,1)S(1)} %shard_map.167), channel_id=1, source_target_pairs={{0,1},{1,0},{2,3},{3,2},{4,5},{5,4},{6,7},{7,6},{8,9},{9,8},{10,11... | collective-permute-start | bytes 196616 | tf_op jit(solution)/shard_map/ppermute | solution.py:338
  29.7 4.1 %collective-permute-start.4 = (bf16[32,1024]{1,0:T(8,128)(2,1)S(1)}, bf16[32,1024]{1,0:T(8,128)(2,1)S(1)}, u32[]{:S(2)}, u32[]{:S(2)}) collective-permute-start(bf16[32,1024]{1,0:T(8,128)(2,1)S(1)} %add_convert_fusion.near), channel_id=1, source_target_pairs={{0,3},{1,2},{2,1},{3,0},{4,7},{5,6},{6,5},{7,4},{8,11},{9,10},{10,... | collective-permute-start | bytes 196616 | tf_op jit(solution)/shard_map/ppermute | solution.py:338
